TPU v7x, 32 devices: a whole 2x2x4 slice. The times are simulated.
32 devices in a mesh: groups: 2 (over y), seq: 4 (over z), head: 2 (over x), rep: 2 (over core).
Axes of the slice: x: 2, y: 2, z: 4, core: 2. Of those that a mesh axis runs over, the one named last changes fastest.
Arguments:
- prefill_kv: bfloat16 [8, 8, 512, 256], P('groups', ('head', 'rep'), 'seq'), parts along dimension 0, may hold values from -6 to 6
- kept_blocks: int32 [8, 8, 2], P('groups'), parts along dimension 0, may hold values from 0 to 3, as said below
- kept_counts: int32 [8, 8], P('groups'), parts along dimension 0, may hold values from 1 to 2, as said below
- queries: bfloat16 [2, 8, 64, 128], P(None, ('groups', 'seq'), 'head'), parts along dimension 1, may hold values from -6 to 6
- new_kv: bfloat16 [2, 8, 8, 256], P(None, ('groups', 'seq'), 'head'), parts along dimension 1, may hold values from -6 to 6
- out_weight: bfloat16 [8192, 8192], P('head', ('seq', 'rep')), may hold values from -0.0625 to 0.0625
- prefill_state: float32 [8, 16, 16384], P('groups', None, ('head', 'seq')), parts along dimension 0, may hold values from -6 to 6
- a_log: float32 [16, 16384], P(None, 'head'), may hold values from 0 to 2.77
- step_input: bfloat16 [2, 8, 16384], P(None, ('groups', 'seq'), 'head'), parts along dimension 1, may hold values from -6 to 6
- step_dt: float32 [2, 8, 16384], P(None, ('groups', 'seq'), 'head'), parts along dimension 1, may hold values from 0.01 to 0.3
- step_bc: float32 [2, 8, 2, 16], P(None, ('groups', 'seq')), parts along dimension 1, may hold values from -3 to 3
- skip_gain: float32 [16384], P('head'), may hold values from 0.5 to 1.5
Outputs:
- handoff: bfloat16 [8, 8, 2, 128, 256], P(('groups', 'seq'), 'head', 'rep'), parts along dimension 0
- proj_out: bfloat16 [2, 8, 8192], P(None, ('groups', 'head'), ('seq', 'rep')), parts along dimension 1
- mamba_out: float32 [2, 8, 16384], P(None, ('groups', 'seq'), 'head'), parts along dimension 1
There are 2 independent parts, one for each index of `groups`. A program takes and returns all parts, laid end to end along the dimension named above; an argument that names none is the same for every part. Nothing has to cross between parts.
Inputs may be any that keep to these rules, and one draw needn't show every extreme that they name: `kept_blocks`: for each request and kv head, 2 distinct block indices; only the first kept_counts of them are used. `kept_counts`: every request has a kv head with exactly 2 kept blocks.
All inputs are finite; a program needn't handle non-finite values.
Results may differ from a plain program's by a relative error of at most 0.01.
Values may be sent and summed in bfloat16 or wider, within the bound.
No kernel may reach another device: no remote copies, remote signals or barrier semaphores. Data moves between devices by JAX's collectives and lax.ppermute only.
A program may use at most 64 MiB of HBM per device.

v0:
```python
import jax
import jax.numpy as jnp
from jax import lax
from jax.sharding import PartitionSpec as P

BLOCK = 128


def joined(shard, axis, combine):
    everything = jax.tree.map(lambda part: lax.all_gather(part, axis), shard)
    leading = jax.tree.map(lambda part: part[0], everything)

    def hop(k, so_far):
        return combine(so_far, jax.tree.map(lambda part: part[k], everything))

    return lax.fori_loop(1, lax.axis_size(axis), hop, leading)


def merge_partials(first, second):
    merged_top = jnp.maximum(first[0], second[0])
    first_weight = jnp.exp(first[0] - merged_top)
    second_weight = jnp.exp(second[0] - merged_top)
    return (
        merged_top,
        first[1] * first_weight + second[1] * second_weight,
        first[2] * first_weight[..., None] + second[2] * second_weight[..., None],
    )


def per_device(
    prefill_kv,
    kept_blocks,
    kept_counts,
    queries,
    new_kv,
    out_weight,
    prefill_state,
    a_log,
    step_input,
    step_dt,
    step_bc,
    skip_gain,
):
    seq_count = lax.axis_size("seq")
    rep_count = lax.axis_size("rep")
    seq_index = lax.axis_index("seq")
    head_index = lax.axis_index("head")
    rep_index = lax.axis_index("rep")
    req_all, heads_pre, tokens_dev, width = prefill_kv.shape
    head_dim = width // 2
    req_dev = req_all // seq_count
    blk_dev = tokens_dev // BLOCK
    keep_all = kept_blocks.shape[2]
    keep_rep = keep_all // rep_count
    heads_dec = heads_pre * rep_count
    dec_first = head_index * heads_dec
    zero_bf = jnp.zeros((), jnp.bfloat16)
    blocks = prefill_kv.reshape(req_all, heads_pre, blk_dev, BLOCK, width)
    dec_counts = lax.dynamic_slice(
        kept_counts, (seq_index * req_dev, dec_first), (req_dev, heads_dec)
    )
    slot_live = (
        rep_index * keep_rep + jnp.arange(keep_rep, dtype=jnp.int32)[None, None, :]
        < dec_counts[:, :, None]
    )
    received = lax.all_to_all(blocks, "seq", split_axis=0, concat_axis=2, tiled=True)
    own_first = dec_first + rep_index * heads_pre
    block_lists = lax.dynamic_slice(
        kept_blocks, (seq_index * req_dev, own_first, 0), (req_dev, heads_pre, keep_all)
    )
    own_counts = lax.dynamic_slice(
        kept_counts, (seq_index * req_dev, own_first), (req_dev, heads_pre)
    )
    picked = jnp.take_along_axis(received, block_lists[:, :, :, None, None], axis=2)
    entry_live = jnp.arange(keep_all, dtype=jnp.int32)[None, None, :] < own_counts[:, :, None]
    picked = jnp.where(entry_live[:, :, :, None, None], picked, zero_bf)
    handoff = lax.all_to_all(picked, "rep", split_axis=2, concat_axis=1, tiled=True)
    cache_keys = handoff[..., :head_dim].reshape(req_dev, heads_dec, keep_rep * BLOCK, head_dim)
    cache_values = handoff[..., head_dim:].reshape(req_dev, heads_dec, keep_rep * BLOCK, head_dim)
    token_live = jnp.broadcast_to(
        slot_live[..., None], (req_dev, heads_dec, keep_rep, BLOCK)
    ).reshape(req_dev, heads_dec, keep_rep * BLOCK)[:, :, None, :]
    steps_count, _, local_heads, _ = queries.shape
    group_size = local_heads // heads_dec
    grouped = queries.reshape(steps_count, req_dev, heads_dec, group_size, head_dim)
    new_keys = new_kv[..., :head_dim]
    new_values = new_kv[..., head_dim:]
    own_new = rep_index == 0
    score_scale = head_dim ** (-0.5)
    top_list, total_list, weighted_list = ([], [], [])
    for step_index in range(steps_count):
        query_step = grouped[step_index]
        cache_scores = (
            jnp.einsum(
                "rhgd,rhkd->rhgk", query_step, cache_keys, preferred_element_type=jnp.float32
            )
            * score_scale
        )
        cache_scores = jnp.where(token_live, cache_scores, -1e30)
        fresh_scores = (
            jnp.einsum(
                "rhgd,srhd->rhgs",
                query_step,
                new_keys[: step_index + 1],
                preferred_element_type=jnp.float32,
            )
            * score_scale
        )
        fresh_scores = jnp.where(own_new, fresh_scores, -1e30)
        score_top = jnp.maximum(jnp.max(cache_scores, axis=-1), jnp.max(fresh_scores, axis=-1))
        cache_weights = jnp.where(token_live, jnp.exp(cache_scores - score_top[..., None]), 0.0)
        fresh_weights = jnp.where(own_new, jnp.exp(fresh_scores - score_top[..., None]), 0.0)
        softmax_total = jnp.sum(cache_weights, axis=-1) + jnp.sum(fresh_weights, axis=-1)
        weighted = jnp.einsum(
            "rhgk,rhkd->rhgd",
            cache_weights.astype(jnp.bfloat16),
            cache_values,
            preferred_element_type=jnp.float32,
        )
        weighted = weighted + jnp.einsum(
            "rhgs,srhd->rhgd",
            fresh_weights.astype(jnp.bfloat16),
            new_values[: step_index + 1],
            preferred_element_type=jnp.float32,
        )
        top_list.append(score_top)
        total_list.append(softmax_total)
        weighted_list.append(weighted)
    tops = jnp.stack(top_list)
    totals = jnp.stack(total_list)
    weighted_all = jnp.stack(weighted_list)
    query_width = local_heads * head_dim
    merged_top, merged_total, merged_sum = joined(
        (tops, totals, weighted_all), "rep", merge_partials
    )
    attn_rows = (
        (merged_sum / merged_total[..., None])
        .astype(jnp.bfloat16)
        .reshape(steps_count, req_dev, query_width)
    )
    partial_terms = jnp.einsum(
        "trk,kd->trd",
        lax.all_gather(attn_rows, "seq", axis=1, tiled=True),
        out_weight,
        preferred_element_type=jnp.float32,
    )
    proj_out = lax.psum_scatter(
        partial_terms.astype(jnp.bfloat16), "head", scatter_dimension=1, tiled=True
    )
    moved = lax.all_to_all(
        prefill_state.astype(jnp.bfloat16), "seq", split_axis=0, concat_axis=2, tiled=True
    )
    mamba_state = moved.astype(jnp.float32)
    decay_rate = -jnp.exp(a_log)
    mamba_steps = []
    for step_index in range(steps_count):
        step_rate = step_dt[step_index]
        inputs = step_input[step_index].astype(jnp.float32)
        drive_b = step_bc[step_index, :, 0, :]
        read_c = step_bc[step_index, :, 1, :]
        mamba_state = (
            jnp.exp(step_rate[:, None, :] * decay_rate[None]) * mamba_state
            + step_rate[:, None, :] * drive_b[:, :, None] * inputs[:, None, :]
        )
        mamba_steps.append(
            jnp.sum(read_c[:, :, None] * mamba_state, axis=1) + skip_gain[None, :] * inputs
        )
    mamba_out = jnp.stack(mamba_steps)
    return (handoff, proj_out, mamba_out)


def solution(mesh):
    return jax.shard_map(
        per_device,
        mesh=mesh,
        in_specs=(
            P("groups", ("head", "rep"), "seq", None),
            P("groups", None, None),
            P("groups", None),
            P(None, ("groups", "seq"), "head", None),
            P(None, ("groups", "seq"), "head", None),
            P("head", ("seq", "rep")),
            P("groups", None, ("head", "seq")),
            P(None, "head"),
            P(None, ("groups", "seq"), "head"),
            P(None, ("groups", "seq"), "head"),
            P(None, ("groups", "seq"), None, None),
            P("head"),
        ),
        out_specs=(
            P(("groups", "seq"), "head", "rep", None, None),
            P(None, ("groups", "head"), ("seq", "rep")),
            P(None, ("groups", "seq"), "head"),
        ),
        check_vma=False,
    )
```

profile of v0, /device:TPU:0, one launch (start us, length us, event | category | flops | bytes accessed | tf_op | source)
XLA Modules:
  0.0 76.3 jit_solution(10699189310708518143)
XLA Ops:
  0.7 1.8 %convert_element_type.63 = bf16[4,16,2048]{2,1,0:T(8,128)(2,1)} convert(f32[4,16,2048]{2,1,0:T(8,128)} %param.18) | non-fusion elementwise | flops 131072 | bytes 786432 | tf_op jit(solution)/shard_map/convert_element_type | solution.py:151
  2.4 6.3 %all-to-all-start.2 = ((bf16[4,16,2048]{2,1,0:T(8,128)(2,1)}), bf16[4,16,2048]{2,1,0:T(8,128)(2,1)S(1)}, u32[]{:S(2)}, u32[]{:S(2)}) async-start(bf16[4,16,2048]{2,1,0:T(8,128)(2,1)} %convert_element_type.63), calls=%async_computation.2 | async-start | bytes 524288 | tf_op jit(solution)/shard_map/all_to_all | solution.py:150
  9.0 0.7 bitcast_convert_fusion
  9.7 0.7 fusion.56
  10.5 0.8 dynamic-slice_bitcast_fusion
  11.3 0.8 compare_bitcast_fusion
  12.1 0.9 %slice_convert_fusion = (f32[1,1,8192]{2,0,1:T(1,128)S(1)}, f32[1,1,8192]{2,0,1:T(1,128)S(1)}) fusion(bf16[2,1,8192]{2,0,1:T(2,128)(2,1)} %param.20), kind=kLoop, calls=%fused_computation.30 | loop fusion | flops 16384 | bytes 98304 | tf_op jit(solution)/shard_map/mul | solution.py:163
  13.0 0.8 %slice_bitcast_fusion.12 = (f32[16]{0:T(128)S(1)}, f32[16]{0:T(128)S(1)}, f32[16]{0:T(128)S(1)}, f32[16]{0:T(128)S(1)}) fusion(f32[2,1,2,16]{3,2,1,0:T(2,128)} %param.22), kind=kLoop, calls=%fused_computation.92 | loop fusion | bytes 512 | tf_op jit(solution)/shard_map/mul | solution.py:166
  13.7 0.8 %fusion.54 = (f32[1,1,8192]{2,1,0:T(1,128)S(1)}, f32[1,1,8192]{2,1,0:T(1,128)S(1)}) fusion(f32[2,1,8192]{2,1,0:T(1,128)} %param.21), kind=kLoop, calls=%fused_computation.100 | loop fusion | bytes 131072 | tf_op jit(solution)/shard_map/slice | solution.py:157
  14.5 0.8 %fusion.24 = f32[4,1,8]{2,1,0:T(1,128)S(1)} fusion(bf16[2,1,32,128]{3,2,1,0:T(8,128)(2,1)} %param.15, bf16[4,128,1]{1,0,2:T(4,128)(2,1)S(1)} %get-tuple-element.51), kind=kOutput, calls=%fused_computation.43 | convolution fusion | flops 8192 | bytes 9344 | tf_op jit(solution)/shard_map/rhgd,srhd->rhgs/dot_general | solution.py:101
  15.3 1.2 %dynamic-slice = u32[1]{0:T(128)} dynamic-slice(u32[32]{0:T(128)} %constant.75, u32[]{:T(128)S(6)} %add.137), dynamic_slice_sizes={1} | dynamic-slice | bytes 12
  17.2 0.8 %fusion.59 = (f32[4,8]{1,0:T(4,128)S(1)}, f32[4,8,2]{1,2,0:T(2,128)S(1)}) fusion(bf16[2,1,4,128]{3,2,1,0:T(4,128)(2,1)S(1)} %get-tuple-element.53, bf16[2,1,32,128]{3,2,1,0:T(8,128)(2,1)} %param.15, pred[]{:T(512)S(6)} %eq.3), kind=kOutput, calls=%fused_computation.105 | convolution fusion | flops 16544 | bytes 10625 | tf_op jit(solution)/shard_map/rhgd,srhd->rhgs/dot_general | solution.py:101
  18.1 5.1 %all-to-all-start = ((bf16[4,2,1,128,256]{4,3,1,2,0:T(8,128)(2,1)}), bf16[4,2,1,128,256]{4,3,1,2,0:T(8,128)(2,1)S(1)}, u32[]{:S(2)}, u32[]{:S(2)}) async-start(bf16[4,2,1,128,256]{4,3,1,2,0:T(8,128)(2,1)} %bitcast.160), calls=%async_computation | async-start | bytes 1048576 | tf_op jit(solution)/shard_map/all_to_all | solution.py:66
  23.2 0.3 copy.32
  23.5 0.3 copy.40
  23.9 1.6 %multiply_reduce_fusion.1 = (f32[8192]{0:T(1024)S(1)}, f32[8192]{0:T(1024)S(1)}) fusion(f32[16,8192]{1,0:T(8,128)S(1)} %bitcast.151, f32[16,8192]{1,0:T(8,128)} %param.19, f32[8192]{0:T(1024)S(1)} %bitcast.163, f32[16]{0:T(128)S(1)} %get-tuple-element.55, f32[8192]{0:T(1024)S(1)} %bitcast.166, f32[16]{0:T(128)S(1)} %get-tuple-element.56, ...), kind=kLoop, calls=%fused_computation.18 | loop fusion | flops 1949696 | bytes 1245440 | tf_op jit(solution)/shard_map/reduce_sum | solution.py:166
  25.4 0.8 %multiply_add_fusion.2 = (f32[8192]{0:T(1024)S(1)}, f32[8192]{0:T(1024)S(1)}) fusion(f32[8192]{0:T(1024)S(1)} %get-tuple-element.33, f32[8192]{0:T(1024)} %param.23, f32[8192]{0:T(1024)S(1)} %bitcast.164, f32[8192]{0:T(1024)S(1)} %get-tuple-element.34, f32[8192]{0:T(1024)S(1)} %bitcast.162), kind=kLoop, calls=%fused_computation.31 | loop fusion | flops 32768 | bytes 229376 | tf_op jit(solution)/shard_map/add | solution.py:166
  26.2 0.7 pad_maximum_fusion
  26.9 10.2 %all-to-all-done = bf16[4,2,1,128,256]{4,3,1,2,0:T(8,128)(2,1)S(1)} async-done(((bf16[4,2,1,128,256]{4,3,1,2,0:T(8,128)(2,1)}), bf16[4,2,1,128,256]{4,3,1,2,0:T(8,128)(2,1)S(1)}, u32[]{:S(2)}, u32[]{:S(2)}) %all-to-all-start) | async-done | bytes 524320 | tf_op jit(solution)/shard_map/all_to_all | solution.py:66
  37.1 0.6 gather_fusion
  37.8 3.9 %all_to_all.45 = bf16[1,2,2,128,256]{4,3,1,0,2:T(8,128)(2,1)S(1)} all-to-all(bf16[1,2,2,128,256]{4,3,1,0,2:T(8,128)(2,1)S(1)} %fusion.12), channel_id=1, replica_groups=mesh['groups'=2,'seq'=4,'head'=2,'rep'=2] {'rep'}, dimensions={2} | all-to-all | bytes 524288 | tf_op jit(solution)/shard_map/all_to_all | solution.py:77
  41.7 0.3 fusion.57
  42.0 0.3 fusion.58
  42.7 1.8 %all-gather.2 = f32[4,1,4,8]{3,2,1,0:T(4,128)S(1)} all-gather(f32[2,1,4,8]{3,2,1,0:T(4,128)S(1)} %pad_maximum_fusion.3), channel_id=4, replica_groups=mesh['groups'=2,'seq'=4,'head'=2,'rep'=2] {'rep'}, dimensions={0}, use_global_device_ids=true | all-gather | bytes 768 | tf_op jit(solution)/shard_map/all_gather | solution.py:10
  44.5 1.8 %all-gather.1 = f32[4,1,4,8]{3,2,1,0:T(4,128)S(1)} all-gather(f32[2,1,4,8]{3,2,1,0:T(4,128)S(1)} %pad_maximum_fusion.2), channel_id=3, replica_groups=mesh['groups'=2,'seq'=4,'head'=2,'rep'=2] {'rep'}, dimensions={0}, use_global_device_ids=true | all-gather | bytes 768 | tf_op jit(solution)/shard_map/all_gather | solution.py:10
  46.6 0.2 fusion.8
  46.8 1.9 %all-gather = f32[4,1,4,8,128]{4,3,2,1,0:T(8,128)S(1)} all-gather(f32[2,1,4,8,128]{4,3,2,1,0:T(8,128)S(1)} %pad_maximum_fusion.1), channel_id=2, replica_groups=mesh['groups'=2,'seq'=4,'head'=2,'rep'=2] {'rep'}, dimensions={0}, use_global_device_ids=true | all-gather | bytes 98304 | tf_op jit(solution)/shard_map/all_gather | solution.py:10
  49.0 13.1 %all_gather.27 = bf16[2,4,4096]{2,0,1:T(2,128)(2,1)S(1)} all-gather(bf16[2,1,4096]{2,0,1:T(2,128)(2,1)S(1)} %fusion.15), channel_id=1, replica_groups=mesh['groups'=2,'seq'=4,'head'=2,'rep'=2] {'seq'}, dimensions={1}, use_global_device_ids=true | all-gather | bytes 81920 | tf_op jit(solution)/shard_map/all_gather | solution.py:143
  62.1 4.7 %fusion.2 = bf16[2,4,1024]{2,1,0:T(4,128)(2,1)S(1)} fusion(bf16[4096,1024]{1,0:T(8,128)(2,1)} %param.17, bf16[2,4,4096]{2,0,1:T(2,128)(2,1)S(1)} %all_gather.27), kind=kOutput, calls=%fused_computation.3 | convolution fusion | flops 67117056 | bytes 8470528 | tf_op jit(solution)/shard_map/trk,kd->trd/dot_general | solution.py:141
  66.8 8.2 %all-reduce = bf16[2,4,1024]{2,1,0:T(4,128)(2,1)S(1)} all-reduce(bf16[2,4,1024]{2,1,0:T(4,128)(2,1)S(1)} %fusion.2), channel_id=5, replica_groups=mesh['groups'=2,'seq'=4,'head'=2,'rep'=2] {'head'}, use_global_device_ids=true, to_apply=%region_6.7.clone | all-reduce | flops 8192 | bytes 32768
  75.0 0.6 constant_dynamic-slice_fusion
  75.6 0.7 copy.55
  (35 shorter events, 1.6 us)
Async XLA Ops:
  0.6 8.1 %copy-start = (s32[4,8,2]{1,2,0:T(2,128)S(1)}, s32[4,8,2]{1,2,0:T(2,128)}, u32[]{:S(2)}) copy-start(s32[4,8,2]{1,2,0:T(2,128)} %param.13) | copy-start | bytes 772
  0.6 41.1 %copy-start.1 = (bf16[2,1,32,128]{3,2,1,0:T(8,128)(2,1)S(1)}, bf16[2,1,32,128]{3,2,1,0:T(8,128)(2,1)}, u32[]{:S(2)}) copy-start(bf16[2,1,32,128]{3,2,1,0:T(8,128)(2,1)} %param.15) | copy-start | bytes 49156
  2.4 15.6 %all-to-all-start.2 = ((bf16[4,16,2048]{2,1,0:T(8,128)(2,1)}), bf16[4,16,2048]{2,1,0:T(8,128)(2,1)S(1)}, u32[]{:S(2)}, u32[]{:S(2)}) async-start(bf16[4,16,2048]{2,1,0:T(8,128)(2,1)} %convert_element_type.63), calls=%async_computation.2 | async-start | bytes 524288 | tf_op jit(solution)/shard_map/all_to_all | solution.py:150
  18.1 19.0 %all-to-all-start = ((bf16[4,2,1,128,256]{4,3,1,2,0:T(8,128)(2,1)}), bf16[4,2,1,128,256]{4,3,1,2,0:T(8,128)(2,1)S(1)}, u32[]{:S(2)}, u32[]{:S(2)}) async-start(bf16[4,2,1,128,256]{4,3,1,2,0:T(8,128)(2,1)} %bitcast.160), calls=%async_computation | async-start | bytes 1048576 | tf_op jit(solution)/shard_map/all_to_all | solution.py:66
where the time goes:
time: 77.2 us; the launch traced here: 76.3 us
  blocking collectives  30.7 us (40%)
  starting transfers between devices  11.4 us (15%)
  waiting for transfers between devices  10.2 us (13%)
  other arithmetic  7.63 us (10%)
  local copies, waits for them, and re-layouts  7.48 us (10%)
  matrix products  7.44 us (10%)
  between operations  1.44 us (2%)
    all_gather x1, blocking collectives, per_device(): lax.all_gather(attn_rows, 'seq', axis=1, tiled=True)  13.1 us
    all_to_all x1, waiting for transfers between devices, per_device(): lax.all_to_all(blocks, 'seq', split_axis=0, concat_axis=2, tiled=True)  10.2 us
    unnamed x1, blocking collectives  8.16 us
    all_to_all x1, starting transfers between devices, per_device(): lax.all_to_all(prefill_state.astype(jnp.bfloat16), 'seq', split_axis=0, c...  6.32 us
    all_gather x3, blocking collectives, joined(): everything = jax.tree.map(lambda part: lax.all_gather(part, axis), shard)  5.43 us
    all_to_all x1, starting transfers between devices, per_device(): lax.all_to_all(blocks, 'seq', split_axis=0, concat_axis=2, tiled=True)  5.1 us
    dot_general x1, matrix products, per_device(): jnp.einsum('trk,kd->trd', lax.all_gather(attn_rows, 'seq', axis=1, tiled=...  4.67 us
    all_to_all x1, blocking collectives, per_device(): lax.all_to_all(picked, 'rep', split_axis=2, concat_axis=1, tiled=True)  3.94 us
  transfers between devices with their start and end apart: 2, of which 1 were waited for; matrix products, arithmetic and copies ran while one was open for 16% of the time, Pallas kernels for 0%

commit v1 on v0

v1 whole, which is shorter than its diff:
```python
import functools

import jax
import jax.numpy as jnp
from jax import lax
from jax.experimental import pallas as pl
from jax.experimental.pallas import tpu as pltpu
from jax.sharding import PartitionSpec as P

BLOCK = 128
NEG = -1e30
BF = jnp.bfloat16
F32 = jnp.float32
VM = pl.BlockSpec(memory_space=pltpu.VMEM)
SM = pl.BlockSpec(memory_space=pltpu.SMEM)
ANY = pl.BlockSpec(memory_space=pl.ANY)


def shift(x, axis, c):
    count = lax.axis_size(axis)
    return lax.ppermute(x, axis, [(i, i ^ c) for i in range(count)])


def call(body, out_shape, in_specs, out_specs, scratch=(), cost=(0, 0)):
    return pl.pallas_call(
        body,
        out_shape=out_shape,
        in_specs=in_specs,
        out_specs=out_specs,
        scratch_shapes=list(scratch),
        cost_estimate=pl.CostEstimate(flops=cost[0], bytes_accessed=cost[1], transcendentals=0),
        compiler_params=pltpu.CompilerParams(vmem_limit_bytes=32 * 1024 * 1024),
    )


def stage_kv(count, kv_ref, *rest):
    outs, sems = rest[:count], rest[count]
    me = lax.axis_index("seq")
    copies = [
        pltpu.make_async_copy(kv_ref.at[me ^ c], outs[c], sems.at[c]) for c in range(count)
    ]
    for copy in copies:
        copy.start()
    for copy in copies:
        copy.wait()


def stage_state(count, split, state_ref, *outs):
    me = lax.axis_index("seq")
    rep = lax.axis_index("rep")
    part = outs[0].shape[-1]
    for c in range(count):
        if split:
            piece = state_ref[me ^ c, :, pl.ds(pl.multiple_of(rep * part, 128), part)]
        else:
            piece = state_ref[me ^ c]
        outs[c][...] = piece.astype(BF)


def attend(count, blocks_ref, counts_ref, kv_ref, new_ref, *rest):
    q_refs, out_ref = rest[:count], rest[count]
    me = lax.axis_index("seq")
    head_first = lax.axis_index("head") * new_ref.shape[2]
    rep = lax.axis_index("rep")
    heads = kv_ref.shape[1]
    hd = kv_ref.shape[3] // 2
    steps, _, q_heads, _ = q_refs[0].shape
    keep = blocks_ref.shape[2]
    own_q = q_heads // 2
    group = own_q // heads
    rows = steps * group
    scale = hd ** (-0.5)
    fresh = []
    for step in range(steps):
        both = new_ref[step, 0].astype(F32)
        fresh.append(jnp.where(rep == 0, both[:heads], both[heads:]))
    pieces, lses = [], []
    for c in range(count):
        request = me ^ c
        q_all = [q_refs[c][step, 0].astype(F32) for step in range(steps)]
        q_all = [jnp.where(rep == 0, q[:own_q], q[own_q:]) for q in q_all]
        for j in range(heads):
            head = head_first + rep * heads + j
            live_count = counts_ref[request, head]
            live = jnp.int32(0)
            for slot in range(keep):
                hit = (blocks_ref[request, head, slot] == me) & (slot < live_count)
                live = live | hit.astype(jnp.int32)
            dead = jnp.where(live > 0, 0.0, NEG).astype(F32)
            q = jnp.concatenate([x[j * group : (j + 1) * group] for x in q_all], axis=0)
            keys = kv_ref[request, j, :, :hd]
            values = kv_ref[request, j, :, hd:]
            scores = lax.dot_general(
                q.astype(BF), keys, (((1,), (1,)), ((), ())), preferred_element_type=F32
            )
            scores = jnp.where(live > 0, scores * scale, dead)
            top = jnp.max(scores, axis=1, keepdims=True)
            fresh_scores = []
            if c == 0:
                row_step = lax.broadcasted_iota(jnp.int32, (rows, 1), 0) // group
                for step in range(steps):
                    dots = jnp.sum(q * fresh[step][j : j + 1, :hd], axis=1, keepdims=True)
                    dots = jnp.where(row_step >= step, dots * scale, NEG)
                    fresh_scores.append(dots)
                    top = jnp.maximum(top, dots)
            weights = jnp.where(live > 0, jnp.exp(scores - top), 0.0)
            total = jnp.sum(weights, axis=1, keepdims=True)
            summed = jnp.dot(weights.astype(BF), values, preferred_element_type=F32)
            for step, dots in enumerate(fresh_scores):
                weight = jnp.where(row_step >= step, jnp.exp(dots - top), 0.0)
                total = total + weight
                summed = summed + weight.astype(BF).astype(F32) * fresh[step][j : j + 1, hd:]
            safe = jnp.where(total > 0.0, total, 1.0)
            pieces.append(summed / safe)
            lses.append(jnp.where(total > 0.0, top + jnp.log(safe), NEG))
    all_rows = jnp.concatenate(pieces, axis=0)
    all_lse = jnp.concatenate(lses, axis=0)
    chunks = out_ref.shape[0]
    line = lax.broadcasted_iota(jnp.int32, (16, 128), 0)
    for k in range(chunks):
        out_ref[k, :128, :] = all_rows[k * 128 : (k + 1) * 128].astype(BF)
        flat = jnp.transpose(jnp.broadcast_to(all_lse[k * 128 : (k + 1) * 128], (128, 128)))[:16]
        high = flat.astype(BF).astype(F32)
        middle = (flat - high).astype(BF).astype(F32)
        low = flat - high - middle
        stats = jnp.where(line == 0, high, jnp.where(line == 1, middle, jnp.where(line == 2, low, 0.0)))
        out_ref[k, 128:, :] = stats.astype(BF)


def merge(count, heads, steps, group, *rest):
    parts, out_ref, scratch = rest[:count], rest[count], rest[count + 1]
    me = lax.axis_index("seq")
    rows = steps * group
    chunks = parts[0].shape[0]
    lse = []
    for c in range(count):
        columns = []
        for k in range(chunks):
            stats = parts[c][k, 128:, :].astype(F32)
            line = jnp.sum(stats[:8], axis=0, keepdims=True)
            columns.append(jnp.transpose(jnp.broadcast_to(line, (128, 128))))
        lse.append(columns)
    for e in range(count):
        for j in range(heads):
            tops, values = [], []
            for c in range(count):
                base = ((e ^ c) * heads + j) * rows
                k, at = base // 128, base % 128
                tops.append(lse[c][k][at : at + rows])
                values.append(parts[c][k, at : at + rows, :].astype(F32))
            top = functools.reduce(jnp.maximum, tops)
            total = jnp.zeros_like(top)
            summed = jnp.zeros_like(top)
            for c in range(count):
                weight = jnp.exp(tops[c] - top)
                total = total + weight
                summed = summed + weight * values[c]
            result = summed / total
            for step in range(steps):
                at = pl.multiple_of((step * count + (me ^ e)) * group, group)
                scratch[j, pl.ds(at, group), :] = result[step * group : (step + 1) * group]
    for j in range(heads):
        for g in range(group):
            at = (j * group + g) * 128
            tile = scratch[j, pl.ds(g, steps * count, stride=group), :]
            out_ref[:, at : at + 128] = tile.astype(BF)


def load_weight(weight_ref, out_ref, sem):
    copy = pltpu.make_async_copy(weight_ref, out_ref, sem)
    copy.start()
    copy.wait()


def project_own(attn_ref, weight_ref, out_ref):
    half = attn_ref.shape[1]
    first = pl.multiple_of(lax.axis_index("rep") * half, half)
    out_ref[...] = jnp.dot(
        attn_ref[...], weight_ref[pl.ds(first, half), :], preferred_element_type=F32
    )


def pick(options, index):
    chosen = options[0]
    for i in range(1, len(options)):
        chosen = jnp.where(index == i, options[i], chosen)
    return chosen


def project_other(heads_count, count, acc_ref, attn_ref, weight_ref, *outs):
    half = attn_ref.shape[1]
    first = pl.multiple_of((1 - lax.axis_index("rep")) * half, half)
    total = acc_ref[...] + jnp.dot(
        attn_ref[...], weight_ref[pl.ds(first, half), :], preferred_element_type=F32
    )
    head = lax.axis_index("head")
    steps = total.shape[0] // count
    share = count // heads_count
    for step in range(steps):
        slices = [
            total[step * count + x * share : step * count + (x + 1) * share]
            for x in range(heads_count)
        ]
        for c in range(heads_count):
            outs[c][step] = pick(slices, head ^ c)


def add_up(*refs):
    total = refs[0][...]
    for ref in refs[1:-1]:
        total = total + ref[...]
    refs[-1][...] = total.astype(BF)


def scan_steps(count, split, dt_ref, x_ref, bc_ref, gain_ref, log_ref, *rest):
    states, out_ref = rest[:count], rest[count]
    me = lax.axis_index("seq")
    rep = lax.axis_index("rep")
    ns, part = states[0].shape
    block = part * 2 if split else part
    steps = dt_ref.shape[0]
    diagonal = lax.broadcasted_iota(jnp.int32, (ns, ns), 0) == lax.broadcasted_iota(
        jnp.int32, (ns, ns), 1
    )

    def column(row):
        return jnp.sum(jnp.where(diagonal, row, 0.0), axis=1, keepdims=True)

    drive = [column(bc_ref[step, 0, 0:1, :]) for step in range(steps)]
    read = [column(bc_ref[step, 0, 1:2, :]) for step in range(steps)]
    for c in range(count):
        place = me ^ c
        first = place * block + (rep * part if split else 0)
        lanes = pl.ds(pl.multiple_of(first, 128), part)
        state = states[c][...].astype(F32)
        rate = -jnp.exp(log_ref[:, lanes])
        gain = gain_ref[:, lanes]
        for step in range(steps):
            dt = dt_ref[step, :, lanes]
            inputs = x_ref[step, :, lanes].astype(F32)
            state = jnp.exp(dt * rate) * state + drive[step] * (dt * inputs)
            out_ref[step, pl.ds(place, 1), :] = (
                jnp.sum(read[step] * state, axis=0, keepdims=True) + gain * inputs
            )


def join_halves(own_ref, other_ref, out_ref):
    rep = lax.axis_index("rep")
    steps, count, part = own_ref.shape
    for step in range(steps):
        for b in range(count):
            own, other = own_ref[step, b : b + 1, :], other_ref[step, b : b + 1, :]
            at = b * 2 * part
            out_ref[step, :, at : at + part] = jnp.where(rep == 0, own, other)
            out_ref[step, :, at + part : at + 2 * part] = jnp.where(rep == 0, other, own)


def assemble(count, blocks_ref, counts_ref, *rest):
    own, other = rest[:count], rest[count : 2 * count]
    out_ref, zeros, sems = rest[2 * count :]
    me = lax.axis_index("seq")
    rep = lax.axis_index("rep")
    heads = own[0].shape[0]
    _, dec_heads, keep_rep, _, _ = out_ref.shape
    head_first = lax.axis_index("head") * dec_heads
    zeros[...] = jnp.zeros_like(zeros)
    for side in range(2):
        pieces = own if side == 0 else other
        owner = rep if side == 0 else 1 - rep
        for j in range(heads):
            local = owner * heads + j
            head = head_first + local
            live_count = counts_ref[me, head]
            for k in range(keep_rep):
                slot = rep * keep_rep + k
                source = blocks_ref[me, head, slot] ^ me
                live = slot < live_count
                sem = sems.at[side, j, k]
                for c in range(count):

                    @pl.when(live & (source == c))
                    def _():
                        pltpu.make_async_copy(pieces[c].at[j], out_ref.at[0, local, k], sem).start()

                @pl.when(jnp.logical_not(live))
                def _():
                    pltpu.make_async_copy(zeros, out_ref.at[0, local, k], sem).start()

    for side in range(2):
        owner = rep if side == 0 else 1 - rep
        for j in range(heads):
            for k in range(keep_rep):
                pltpu.make_async_copy(
                    zeros, out_ref.at[0, owner * heads + j, k], sems.at[side, j, k]
                ).wait()


def per_device(
    prefill_kv,
    kept_blocks,
    kept_counts,
    queries,
    new_kv,
    out_weight,
    prefill_state,
    a_log,
    step_input,
    step_dt,
    step_bc,
    skip_gain,
):
    count = lax.axis_size("seq")
    reps = lax.axis_size("rep")
    heads_count = lax.axis_size("head")
    requests, heads, tokens, width = prefill_kv.shape
    assert requests == count and tokens == BLOCK and reps == 2 and width == 256
    assert count & (count - 1) == 0 and heads_count & (heads_count - 1) == 0
    keep = kept_blocks.shape[2]
    steps, _, q_heads, hd = queries.shape
    dec_heads = new_kv.shape[2]
    group = q_heads // dec_heads
    _, ns, block = prefill_state.shape
    split = block % (reps * 128) == 0
    part = block // reps if split else block
    all_rows = count * heads * steps * group
    chunks = all_rows // 128
    shape = jax.ShapeDtypeStruct

    asked = [queries] + [shift(queries, "seq", c) for c in range(1, count)]

    kv = call(
        functools.partial(stage_kv, count),
        [shape((heads, BLOCK, width), BF)] * count,
        [ANY],
        [ANY] * count,
        [pltpu.SemaphoreType.DMA((count,))],
    )(prefill_kv)
    state = call(
        functools.partial(stage_state, count, split),
        [shape((ns, part), BF)] * count,
        [VM],
        [VM] * count,
    )(prefill_state)
    kv_own = [kv[0]] + [shift(kv[c], "seq", c) for c in range(1, count)]
    kv_other = [shift(piece, "rep", 1) for piece in kv_own]
    state = [state[0]] + [shift(state[c], "seq", c) for c in range(1, count)]

    weight = call(
        load_weight, pltpu.VMEM(out_weight.shape, BF), [ANY], VM, [pltpu.SemaphoreType.DMA]
    )(out_weight)

    partial_sums = call(
        functools.partial(attend, count),
        shape((chunks, 144, 128), BF),
        [SM, SM, VM, VM] + [VM] * count,
        VM,
    )(kept_blocks, kept_counts, prefill_kv, new_kv, *asked)
    gathered = [partial_sums] + [shift(partial_sums, "seq", c) for c in range(1, count)]
    half = heads * group * hd
    attn = call(
        functools.partial(merge, count, heads, steps, group),
        shape((steps * count, half), BF),
        [VM] * count,
        VM,
        [pltpu.VMEM((heads, steps * count * group, hd), F32)],
    )(*gathered)
    attn_other = shift(attn, "rep", 1)
    columns = out_weight.shape[1]
    own_sum = call(project_own, shape((steps * count, columns), F32), [VM, VM], VM)(attn, weight)
    share = count // heads_count
    sums = call(
        functools.partial(project_other, heads_count, count),
        [shape((steps, share, columns), F32)] * heads_count,
        [VM, VM, VM],
        [VM] * heads_count,
    )(own_sum, attn_other, weight)
    sums = [sums[0]] + [shift(sums[c], "head", c) for c in range(1, heads_count)]
    proj_out = call(
        add_up, shape((steps, share, columns), BF), [VM] * heads_count, VM
    )(*sums)

    mamba = call(
        functools.partial(scan_steps, count, split),
        shape((steps, count, part), F32),
        [VM] * 5 + [VM] * count,
        VM,
    )(step_dt, step_input, step_bc, skip_gain.reshape(1, -1), a_log, *state)
    if split:
        mamba_out = call(
            join_halves, shape((steps, 1, count * block), F32), [VM, VM], VM
        )(mamba, shift(mamba, "rep", 1))
    else:
        mamba_out = mamba.reshape(steps, 1, count * block)

    keep_rep = keep // reps
    handoff = call(
        functools.partial(assemble, count),
        shape((1, dec_heads, keep_rep, BLOCK, width), BF),
        [SM, SM] + [ANY] * (2 * count),
        ANY,
        [pltpu.VMEM((BLOCK, width), BF), pltpu.SemaphoreType.DMA((2, heads, keep_rep))],
    )(kept_blocks, kept_counts, *kv_own, *kv_other)
    return handoff, proj_out, mamba_out


def solution(mesh):
    return jax.shard_map(
        per_device,
        mesh=mesh,
        in_specs=(
            P("groups", ("head", "rep"), "seq", None),
            P("groups", None, None),
            P("groups", None),
            P(None, ("groups", "seq"), "head", None),
            P(None, ("groups", "seq"), "head", None),
            P("head", ("seq", "rep")),
            P("groups", None, ("head", "seq")),
            P(None, "head"),
            P(None, ("groups", "seq"), "head"),
            P(None, ("groups", "seq"), "head"),
            P(None, ("groups", "seq"), None, None),
            P("head"),
        ),
        out_specs=(
            P(("groups", "seq"), "head", "rep", None, None),
            P(None, ("groups", "head"), ("seq", "rep")),
            P(None, ("groups", "seq"), "head"),
        ),
        check_vma=False,
    )
```

time: 77.2 us -> 66.9 us (0.87)
  blocking collectives: 30.7 us -> 0 us
  starting transfers between devices: 11.4 us -> 24.5 us
  Pallas kernels: 0 us -> 8.87 us
  waiting for transfers between devices: 10.2 us -> 18.6 us
  other arithmetic: 7.63 us -> 0 us
  matrix products: 7.44 us -> 0 us
  local copies, waits for them, and re-layouts: 7.48 us -> 13.5 us
    ppermute x0 -> x19, starting transfers between devices: none -> 24.5 us  [shift(): return lax.ppermute(x, axis, [(i, i ^ c) for i in range(count)])]
    ppermute x0 -> x19, waiting for transfers between devices: none -> 18.6 us  [shift(): return lax.ppermute(x, axis, [(i, i ^ c) for i in range(count)])]
    all_gather x4 -> x0, blocking collectives: 18.6 us -> none  [the longest x1 13.1 us: per_device(): lax.all_gather(attn_rows, 'seq', axis=1, tiled=True)]
    all_to_all x2 -> x0, starting transfers between devices: 11.4 us -> none  [the longest x1 6.32 us: per_device(): lax.all_to_all(prefill_state.astype(jnp.bfloat16), 'seq', split_axis=0, c...]
    unnamed x8 -> x26, local copies, waits for them, and re-layouts: 2.88 us -> 13.5 us
    all_to_all x2 -> x0, waiting for transfers between devices: 10.2 us -> none  [the longest x1 10.2 us: per_device(): lax.all_to_all(blocks, 'seq', split_axis=0, concat_axis=2, tiled=True)]
    pallas_call x0 -> x11, Pallas kernels: none -> 8.87 us  [the longest x1 2.94 us: per_device(): call(functools.partial(attend, count), shape((chunks, 144, 128), BF), [SM...]
    unnamed x1 -> x0, blocking collectives: 8.16 us -> none
  transfers between devices with their start and end apart: 2 -> 19, of which waited for: 1 -> 8; matrix products, arithmetic and copies ran while one was open for 16% -> 2% of each run, Pallas kernels for 0% -> 10%
where the time goes in v1:
time: 66.9 us; the launch traced here: 66.2 us
  starting transfers between devices  24.5 us (37%)
  waiting for transfers between devices  18.6 us (28%)
  local copies, waits for them, and re-layouts  13.5 us (20%)
  Pallas kernels  8.87 us (13%)
  between operations  0.76 us (1%)
    ppermute x19, starting transfers between devices, shift(): return lax.ppermute(x, axis, [(i, i ^ c) for i in range(count)])  24.5 us
    ppermute x19, waiting for transfers between devices, shift(): return lax.ppermute(x, axis, [(i, i ^ c) for i in range(count)])  18.6 us
    unnamed x26, local copies, waits for them, and re-layouts  13.5 us
    pallas_call x1, Pallas kernels, per_device(): call(functools.partial(attend, count), shape((chunks, 144, 128), BF), [SM...  2.94 us
    pallas_call x1, Pallas kernels, per_device(): call(functools.partial(assemble, count), shape((1, dec_heads, keep_rep, B...  1.59 us
  transfers between devices with their start and end apart: 19, of which 8 were waited for; matrix products, arithmetic and copies ran while one was open for 2% of the time, Pallas kernels for 10%

profile of v1, /device:TPU:0, one launch (start us, length us, event | category | flops | bytes accessed | tf_op | source)
XLA Modules:
  0.0 66.2 jit_solution(2181951325844904767)
XLA Ops:
  0.6 1.0 %copy-done.1 = bf16[4,2,128,256]{3,2,1,0:T(8,128)(2,1)S(1)} copy-done((bf16[4,2,128,256]{3,2,1,0:T(8,128)(2,1)S(1)}, bf16[4,2,128,256]{3,2,1,0:T(8,128)(2,1)}, u32[]{:S(2)}) %copy-start.1) | copy-done | bytes 524312
  1.7 0.7 %shard_map.139 = (bf16[2,128,256]{2,1,0:T(8,128)(2,1)S(1)}, bf16[2,128,256]{2,1,0:T(8,128)(2,1)S(1)}, bf16[2,128,256]{2,1,0:T(8,128)(2,1)S(1)}, bf16[2,128,256]{2,1,0:T(8,128)(2,1)S(1)}) custom-call(bf16[4,2,128,256]{3,2,1,0:T(8,128)(2,1)S(1)} %copy-done.1), custom_call_target="tpu_custom_call" | custom-call | tf_op jit(solution)/shard_map/pallas_call | solution.py:331
  2.4 3.1 %collective-permute-start = (bf16[2,128,256]{2,1,0:T(8,128)(2,1)S(1)}, bf16[2,128,256]{2,1,0:T(8,128)(2,1)S(1)}, u32[]{:S(2)}, u32[]{:S(2)}) collective-permute-start(bf16[2,128,256]{2,1,0:T(8,128)(2,1)S(1)} %get-tuple-element.14), channel_id=1, source_target_pairs={{0,4},{4,0},{8,12},{12,8},{1,5},{5,1},{9,13},{13,9},{2,6},{6,2},{1... | collective-permute-start | bytes 393224 | tf_op jit(solution)/shard_map/ppermute | solution.py:21
  5.5 2.6 %collective-permute-start.1 = (bf16[2,128,256]{2,1,0:T(8,128)(2,1)S(1)}, bf16[2,128,256]{2,1,0:T(8,128)(2,1)S(1)}, u32[]{:S(2)}, u32[]{:S(2)}) collective-permute-start(bf16[2,128,256]{2,1,0:T(8,128)(2,1)S(1)} %get-tuple-element.15), channel_id=1, source_target_pairs={{0,8},{4,12},{8,0},{12,4},{1,9},{5,13},{9,1},{13,5},{2,10},{6,14},... | collective-permute-start | bytes 393224 | tf_op jit(solution)/shard_map/ppermute | solution.py:21
  8.0 0.9 %collective-permute-start.7 = (bf16[2,1,32,128]{3,2,1,0:T(8,128)(2,1)}, bf16[2,1,32,128]{3,2,1,0:T(8,128)(2,1)S(1)}, u32[]{:S(2)}, u32[]{:S(2)}) collective-permute-start(bf16[2,1,32,128]{3,2,1,0:T(8,128)(2,1)} %rest_0_.1), channel_id=1, source_target_pairs={{0,4},{4,0},{8,12},{12,8},{1,5},{5,1},{9,13},{13,9},{2,6},{6,2},{1... | collective-permute-start | bytes 49160 | tf_op jit(solution)/shard_map/ppermute | solution.py:21
  8.9 3.5 %collective-permute-start.8 = (bf16[2,1,32,128]{3,2,1,0:T(8,128)(2,1)}, bf16[2,1,32,128]{3,2,1,0:T(8,128)(2,1)S(1)}, u32[]{:S(2)}, u32[]{:S(2)}) collective-permute-start(bf16[2,1,32,128]{3,2,1,0:T(8,128)(2,1)} %rest_0_.1), channel_id=1, source_target_pairs={{0,8},{4,12},{8,0},{12,4},{1,9},{5,13},{9,1},{13,5},{2,10},{6,14},... | collective-permute-start | bytes 49160 | tf_op jit(solution)/shard_map/ppermute | solution.py:21
  12.4 1.0 %copy-done.3 = f32[4,16,2048]{2,1,0:T(8,128)S(1)} copy-done((f32[4,16,2048]{2,1,0:T(8,128)S(1)}, f32[4,16,2048]{2,1,0:T(8,128)}, u32[]{:S(2)}) %copy-start.3) | copy-done | bytes 524312
  13.5 0.9 %collective-permute-done.7.rest_1_ = bf16[2,1,32,128]{3,2,1,0:T(8,128)(2,1)S(1)} collective-permute-done((bf16[2,1,32,128]{3,2,1,0:T(8,128)(2,1)}, bf16[2,1,32,128]{3,2,1,0:T(8,128)(2,1)S(1)}, u32[]{:S(2)}, u32[]{:S(2)}) %collective-permute-start.7) | collective-permute-done | bytes 16416 | tf_op jit(solution)/shard_map/ppermute | solution.py:21
  14.4 2.5 %collective-permute-start.15 = (bf16[16,1024]{1,0:T(8,128)(2,1)S(1)}, bf16[16,1024]{1,0:T(8,128)(2,1)S(1)}, u32[]{:S(2)}, u32[]{:S(2)}) collective-permute-start(bf16[16,1024]{1,0:T(8,128)(2,1)S(1)} %get-tuple-element.20), channel_id=1, source_target_pairs={{0,4},{4,0},{8,12},{12,8},{1,5},{5,1},{9,13},{13,9},{2,6},{6,2},{1... | collective-permute-start | bytes 98312 | tf_op jit(solution)/shard_map/ppermute | solution.py:21
  16.9 3.6 %collective-permute-done.8.rest_2_ = bf16[2,1,32,128]{3,2,1,0:T(8,128)(2,1)S(1)} collective-permute-done((bf16[2,1,32,128]{3,2,1,0:T(8,128)(2,1)}, bf16[2,1,32,128]{3,2,1,0:T(8,128)(2,1)S(1)}, u32[]{:S(2)}, u32[]{:S(2)}) %collective-permute-start.8) | collective-permute-done | bytes 16416 | tf_op jit(solution)/shard_map/ppermute | solution.py:21
  20.5 2.6 %collective-permute-start.9 = (bf16[2,1,32,128]{3,2,1,0:T(8,128)(2,1)}, bf16[2,1,32,128]{3,2,1,0:T(8,128)(2,1)S(1)}, u32[]{:S(2)}, u32[]{:S(2)}) collective-permute-start(bf16[2,1,32,128]{3,2,1,0:T(8,128)(2,1)} %rest_0_.1), channel_id=1, source_target_pairs={{0,12},{4,8},{8,4},{12,0},{1,13},{5,9},{9,5},{13,1},{2,14},{6,10},... | collective-permute-start | bytes 49160 | tf_op jit(solution)/shard_map/ppermute | solution.py:21
  23.1 3.1 %collective-permute-done.9.rest_3_ = bf16[2,1,32,128]{3,2,1,0:T(8,128)(2,1)S(1)} collective-permute-done((bf16[2,1,32,128]{3,2,1,0:T(8,128)(2,1)}, bf16[2,1,32,128]{3,2,1,0:T(8,128)(2,1)S(1)}, u32[]{:S(2)}, u32[]{:S(2)}) %collective-permute-start.9) | collective-permute-done | bytes 16416 | tf_op jit(solution)/shard_map/ppermute | solution.py:21
  26.2 0.8 %copy.15.blocks_ref = s32[4,8,2]{2,1,0:T(8,128)S(1)} copy(s32[4,8,2]{1,2,0:T(2,128)} %param.13) | data formatting | bytes 512 | tf_op args[1]
  27.0 1.0 %copy-done.2 = bf16[4,2,128,256]{3,2,1,0:T(8,128)(2,1)S(1)} copy-done((bf16[4,2,128,256]{3,2,1,0:T(8,128)(2,1)S(1)}, bf16[4,2,128,256]{3,2,1,0:T(8,128)(2,1)}, u32[]{:S(2)}) %copy-start.2) | copy-done | bytes 524312
  28.1 0.7 %copy-done.7 = bf16[2,1,32,128]{3,2,1,0:T(8,128)(2,1)S(1)} copy-done((bf16[2,1,32,128]{3,2,1,0:T(8,128)(2,1)S(1)}, bf16[2,1,32,128]{3,2,1,0:T(8,128)(2,1)}, u32[]{:S(2)}) %copy-start.7) | copy-done | bytes 16408
  29.5 0.7 %copy-done.10 = bf16[2,1,4,256]{3,2,1,0:T(4,128)(2,1)S(1)} copy-done((bf16[2,1,4,256]{3,2,1,0:T(4,128)(2,1)S(1)}, bf16[2,1,4,256]{3,2,1,0:T(4,128)(2,1)}, u32[]{:S(2)}) %copy-start.10) | copy-done | bytes 4120
  30.1 2.9 %shard_map.141.rest_0_ = bf16[1,144,128]{2,1,0:T(8,128)(2,1)S(1)} custom-call(s32[4,8,2]{2,1,0:T(8,128)S(1)} %copy.15.blocks_ref, s32[4,8]{1,0:T(4,128)S(1)} %copy-done.8, bf16[4,2,128,256]{3,2,1,0:T(8,128)(2,1)S(1)} %copy-done.2, bf16[2,1,4,256]{3,2,1,0:T(4,128)(2,1)S(1)} %copy-done.10, bf16[2,1,32,128]{3,2,1,0:T(8,128)(2,1)S(1)} %copy-done.7, ...), custom_call_target="tpu_custom_call" | custom-call | tf_op jit(solution)/shard_map/pallas_call | solution.py:352
  33.1 3.3 %collective-permute-start.10 = (bf16[1,144,128]{2,1,0:T(8,128)(2,1)S(1)}, bf16[1,144,128]{2,1,0:T(8,128)(2,1)S(1)}, u32[]{:S(2)}, u32[]{:S(2)}) collective-permute-start(bf16[1,144,128]{2,1,0:T(8,128)(2,1)S(1)} %shard_map.141.rest_0_), channel_id=1, source_target_pairs={{0,4},{4,0},{8,12},{12,8},{1,5},{5,1},{9,13},{13,9},{2,6},{6,2},{1... | collective-permute-start | bytes 110600 | tf_op jit(solution)/shard_map/ppermute | solution.py:21
  36.4 1.9 %collective-permute-done.10.rest_1_ = bf16[1,144,128]{2,1,0:T(8,128)(2,1)S(1)} collective-permute-done((bf16[1,144,128]{2,1,0:T(8,128)(2,1)S(1)}, bf16[1,144,128]{2,1,0:T(8,128)(2,1)S(1)}, u32[]{:S(2)}, u32[]{:S(2)}) %collective-permute-start.10) | collective-permute-done | bytes 36896 | tf_op jit(solution)/shard_map/ppermute | solution.py:21
  38.3 1.5 %collective-permute-start.12 = (bf16[1,144,128]{2,1,0:T(8,128)(2,1)S(1)}, bf16[1,144,128]{2,1,0:T(8,128)(2,1)S(1)}, u32[]{:S(2)}, u32[]{:S(2)}) collective-permute-start(bf16[1,144,128]{2,1,0:T(8,128)(2,1)S(1)} %shard_map.141.rest_0_), channel_id=1, source_target_pairs={{0,12},{4,8},{8,4},{12,0},{1,13},{5,9},{9,5},{13,1},{2,14},{6,10},... | collective-permute-start | bytes 110600 | tf_op jit(solution)/shard_map/ppermute | solution.py:21
  39.8 1.5 %collective-permute-done.11.rest_2_ = bf16[1,144,128]{2,1,0:T(8,128)(2,1)S(1)} collective-permute-done((bf16[1,144,128]{2,1,0:T(8,128)(2,1)S(1)}, bf16[1,144,128]{2,1,0:T(8,128)(2,1)S(1)}, u32[]{:S(2)}, u32[]{:S(2)}) %collective-permute-start.11) | collective-permute-done | bytes 36896 | tf_op jit(solution)/shard_map/ppermute | solution.py:21
  42.3 1.9 %collective-permute-done.12.rest_3_ = bf16[1,144,128]{2,1,0:T(8,128)(2,1)S(1)} collective-permute-done((bf16[1,144,128]{2,1,0:T(8,128)(2,1)S(1)}, bf16[1,144,128]{2,1,0:T(8,128)(2,1)S(1)}, u32[]{:S(2)}, u32[]{:S(2)}) %collective-permute-start.12) | collective-permute-done | bytes 36896 | tf_op jit(solution)/shard_map/ppermute | solution.py:21
  44.1 1.4 %collective-permute-start.17 = (bf16[16,1024]{1,0:T(8,128)(2,1)S(1)}, bf16[16,1024]{1,0:T(8,128)(2,1)S(1)}, u32[]{:S(2)}, u32[]{:S(2)}) collective-permute-start(bf16[16,1024]{1,0:T(8,128)(2,1)S(1)} %get-tuple-element.22), channel_id=1, source_target_pairs={{0,12},{4,8},{8,4},{12,0},{1,13},{5,9},{9,5},{13,1},{2,14},{6,10},... | collective-permute-start | bytes 98312 | tf_op jit(solution)/shard_map/ppermute | solution.py:21
  45.7 4.1 %collective-permute-done.17.rest_3_ = bf16[16,1024]{1,0:T(8,128)(2,1)S(1)} collective-permute-done((bf16[16,1024]{1,0:T(8,128)(2,1)S(1)}, bf16[16,1024]{1,0:T(8,128)(2,1)S(1)}, u32[]{:S(2)}, u32[]{:S(2)}) %collective-permute-start.17) | collective-permute-done | bytes 32800 | tf_op jit(solution)/shard_map/ppermute | solution.py:21
  49.8 0.8 %copy.17.x_ref = bf16[2,1,8192]{2,1,0:T(2,128)(2,1)S(1)} copy(bf16[2,1,8192]{2,0,1:T(2,128)(2,1)} %param.20) | data formatting | bytes 65536 | tf_op args[8]
  50.7 1.0 %copy-done.4 = f32[16,8192]{1,0:T(8,128)S(1)} copy-done((f32[16,8192]{1,0:T(8,128)S(1)}, f32[16,8192]{1,0:T(8,128)}, u32[]{:S(2)}) %copy-start.4) | copy-done | bytes 524312
  51.7 0.8 %copy-done.5 = f32[2,1,8192]{2,1,0:T(1,128)S(1)} copy-done((f32[2,1,8192]{2,1,0:T(1,128)S(1)}, f32[2,1,8192]{2,1,0:T(1,128)}, u32[]{:S(2)}) %copy-start.5) | copy-done | bytes 65560
  52.5 0.8 %copy-done.6 = f32[8192]{0:T(1024)S(1)} copy-done((f32[8192]{0:T(1024)S(1)}, f32[8192]{0:T(1024)}, u32[]{:S(2)}) %copy-start.6) | copy-done | bytes 32792
  54.9 3.4 %copy-done = bf16[4096,1024]{1,0:T(8,128)(2,1)S(1)} copy-done((bf16[4096,1024]{1,0:T(8,128)(2,1)S(1)}, bf16[4096,1024]{1,0:T(8,128)(2,1)}, u32[]{:S(2)}) %copy-start) | copy-done | bytes 8388632
  60.2 1.6 %collective-permute-start.14 = (f32[2,2,1024]{2,1,0:T(2,128)S(1)}, f32[2,2,1024]{2,1,0:T(2,128)S(1)}, u32[]{:S(2)}, u32[]{:S(2)}) collective-permute-start(f32[2,2,1024]{2,1,0:T(2,128)S(1)} %get-tuple-element.18), channel_id=1, source_target_pairs={{0,2},{2,0},{1,3},{3,1},{4,6},{6,4},{5,7},{7,5},{8,10},{10,8},{9,1... | collective-permute-start | bytes 49160 | tf_op jit(solution)/shard_map/ppermute | solution.py:21
  62.4 1.6 %collective-permute-done.14.refs_1_ = f32[2,2,1024]{2,1,0:T(2,128)S(1)} collective-permute-done((f32[2,2,1024]{2,1,0:T(2,128)S(1)}, f32[2,2,1024]{2,1,0:T(2,128)S(1)}, u32[]{:S(2)}, u32[]{:S(2)}) %collective-permute-start.14) | collective-permute-done | bytes 16416 | tf_op jit(solution)/shard_map/ppermute | solution.py:21
  64.6 1.6 %shard_map.140 = bf16[1,4,1,128,256]{4,3,2,1,0:T(8,128)(2,1)} custom-call(s32[4,8,2]{2,1,0:T(8,128)S(1)} %copy.15.blocks_ref, s32[4,8]{1,0:T(4,128)S(1)} %copy-done.9, bf16[2,128,256]{2,1,0:T(8,128)(2,1)S(1)} %get-tuple-element.13.rest_0_, bf16[2,128,256]{2,1,0:T(8,128)(2,1)S(1)} %collective-permute-done.rest_1_, ...), custom_call_target="tpu_custom_call" | custom-call | tf_op jit(solution)/shard_map/pallas_call | solution.py:396
  (43 shorter events, 6.7 us)
Async XLA Ops:
  0.6 1.0 %copy-start.1 = (bf16[4,2,128,256]{3,2,1,0:T(8,128)(2,1)S(1)}, bf16[4,2,128,256]{3,2,1,0:T(8,128)(2,1)}, u32[]{:S(2)}) copy-start(bf16[4,2,128,256]{3,2,1,0:T(8,128)(2,1)} %kv_ref.3) | copy-start | bytes 1572868
  2.4 38.9 %collective-permute-start = (bf16[2,128,256]{2,1,0:T(8,128)(2,1)S(1)}, bf16[2,128,256]{2,1,0:T(8,128)(2,1)S(1)}, u32[]{:S(2)}, u32[]{:S(2)}) collective-permute-start(bf16[2,128,256]{2,1,0:T(8,128)(2,1)S(1)} %get-tuple-element.14), channel_id=1, source_target_pairs={{0,4},{4,0},{8,12},{12,8},{1,5},{5,1},{9,13},{13,9},{2,6},{6,2},{1... | collective-permute-start | bytes 393224 | tf_op jit(solution)/shard_map/ppermute | solution.py:21
  5.5 36.3 %collective-permute-start.1 = (bf16[2,128,256]{2,1,0:T(8,128)(2,1)S(1)}, bf16[2,128,256]{2,1,0:T(8,128)(2,1)S(1)}, u32[]{:S(2)}, u32[]{:S(2)}) collective-permute-start(bf16[2,128,256]{2,1,0:T(8,128)(2,1)S(1)} %get-tuple-element.15), channel_id=1, source_target_pairs={{0,8},{4,12},{8,0},{12,4},{1,9},{5,13},{9,1},{13,5},{2,10},{6,14},... | collective-permute-start | bytes 393224 | tf_op jit(solution)/shard_map/ppermute | solution.py:21
  8.0 33.8 %collective-permute-start.2 = (bf16[2,128,256]{2,1,0:T(8,128)(2,1)S(1)}, bf16[2,128,256]{2,1,0:T(8,128)(2,1)S(1)}, u32[]{:S(2)}, u32[]{:S(2)}) collective-permute-start(bf16[2,128,256]{2,1,0:T(8,128)(2,1)S(1)} %get-tuple-element.16), channel_id=1, source_target_pairs={{0,12},{4,8},{8,4},{12,0},{1,13},{5,9},{9,5},{13,1},{2,14},{6,10},... | collective-permute-start | bytes 393224 | tf_op jit(solution)/shard_map/ppermute | solution.py:21
  8.0 6.4 %collective-permute-start.7 = (bf16[2,1,32,128]{3,2,1,0:T(8,128)(2,1)}, bf16[2,1,32,128]{3,2,1,0:T(8,128)(2,1)S(1)}, u32[]{:S(2)}, u32[]{:S(2)}) collective-permute-start(bf16[2,1,32,128]{3,2,1,0:T(8,128)(2,1)} %rest_0_.1), channel_id=1, source_target_pairs={{0,4},{4,0},{8,12},{12,8},{1,5},{5,1},{9,13},{13,9},{2,6},{6,2},{1... | collective-permute-start | bytes 49160 | tf_op jit(solution)/shard_map/ppermute | solution.py:21
  8.9 11.5 %collective-permute-start.8 = (bf16[2,1,32,128]{3,2,1,0:T(8,128)(2,1)}, bf16[2,1,32,128]{3,2,1,0:T(8,128)(2,1)S(1)}, u32[]{:S(2)}, u32[]{:S(2)}) collective-permute-start(bf16[2,1,32,128]{3,2,1,0:T(8,128)(2,1)} %rest_0_.1), channel_id=1, source_target_pairs={{0,8},{4,12},{8,0},{12,4},{1,9},{5,13},{9,1},{13,5},{2,10},{6,14},... | collective-permute-start | bytes 49160 | tf_op jit(solution)/shard_map/ppermute | solution.py:21
  12.4 1.0 %copy-start.3 = (f32[4,16,2048]{2,1,0:T(8,128)S(1)}, f32[4,16,2048]{2,1,0:T(8,128)}, u32[]{:S(2)}) copy-start(f32[4,16,2048]{2,1,0:T(8,128)} %state_ref.1) | copy-start | bytes 1572868
  14.4 18.7 %collective-permute-start.15 = (bf16[16,1024]{1,0:T(8,128)(2,1)S(1)}, bf16[16,1024]{1,0:T(8,128)(2,1)S(1)}, u32[]{:S(2)}, u32[]{:S(2)}) collective-permute-start(bf16[16,1024]{1,0:T(8,128)(2,1)S(1)} %get-tuple-element.20), channel_id=1, source_target_pairs={{0,4},{4,0},{8,12},{12,8},{1,5},{5,1},{9,13},{13,9},{2,6},{6,2},{1... | collective-permute-start | bytes 98312 | tf_op jit(solution)/shard_map/ppermute | solution.py:21
  20.5 5.7 %collective-permute-start.9 = (bf16[2,1,32,128]{3,2,1,0:T(8,128)(2,1)}, bf16[2,1,32,128]{3,2,1,0:T(8,128)(2,1)S(1)}, u32[]{:S(2)}, u32[]{:S(2)}) collective-permute-start(bf16[2,1,32,128]{3,2,1,0:T(8,128)(2,1)} %rest_0_.1), channel_id=1, source_target_pairs={{0,12},{4,8},{8,4},{12,0},{1,13},{5,9},{9,5},{13,1},{2,14},{6,10},... | collective-permute-start | bytes 49160 | tf_op jit(solution)/shard_map/ppermute | solution.py:21
  26.2 10.1 %collective-permute-start.16 = (bf16[16,1024]{1,0:T(8,128)(2,1)S(1)}, bf16[16,1024]{1,0:T(8,128)(2,1)S(1)}, u32[]{:S(2)}, u32[]{:S(2)}) collective-permute-start(bf16[16,1024]{1,0:T(8,128)(2,1)S(1)} %get-tuple-element.21), channel_id=1, source_target_pairs={{0,8},{4,12},{8,0},{12,4},{1,9},{5,13},{9,1},{13,5},{2,10},{6,14},... | collective-permute-start | bytes 98312 | tf_op jit(solution)/shard_map/ppermute | solution.py:21
  27.0 1.0 %copy-start.2 = (bf16[4,2,128,256]{3,2,1,0:T(8,128)(2,1)S(1)}, bf16[4,2,128,256]{3,2,1,0:T(8,128)(2,1)}, u32[]{:S(2)}) copy-start(bf16[4,2,128,256]{3,2,1,0:T(8,128)(2,1)} %kv_ref.3) | copy-start | bytes 1572868
  28.1 0.7 %copy-start.7 = (bf16[2,1,32,128]{3,2,1,0:T(8,128)(2,1)S(1)}, bf16[2,1,32,128]{3,2,1,0:T(8,128)(2,1)}, u32[]{:S(2)}) copy-start(bf16[2,1,32,128]{3,2,1,0:T(8,128)(2,1)} %rest_0_.1) | copy-start | bytes 49156
  28.8 0.7 %copy-start.8 = (s32[4,8]{1,0:T(4,128)S(1)}, s32[4,8]{1,0:T(4,128)}, u32[]{:S(2)}) copy-start(s32[4,8]{1,0:T(4,128)} %counts_ref.3) | copy-start | bytes 388
  29.5 0.7 %copy-start.10 = (bf16[2,1,4,256]{3,2,1,0:T(4,128)(2,1)S(1)}, bf16[2,1,4,256]{3,2,1,0:T(4,128)(2,1)}, u32[]{:S(2)}) copy-start(bf16[2,1,4,256]{3,2,1,0:T(4,128)(2,1)} %new_ref.1) | copy-start | bytes 12292
  33.1 5.2 %collective-permute-start.10 = (bf16[1,144,128]{2,1,0:T(8,128)(2,1)S(1)}, bf16[1,144,128]{2,1,0:T(8,128)(2,1)S(1)}, u32[]{:S(2)}, u32[]{:S(2)}) collective-permute-start(bf16[1,144,128]{2,1,0:T(8,128)(2,1)S(1)} %shard_map.141.rest_0_), channel_id=1, source_target_pairs={{0,4},{4,0},{8,12},{12,8},{1,5},{5,1},{9,13},{13,9},{2,6},{6,2},{1... | collective-permute-start | bytes 110600 | tf_op jit(solution)/shard_map/ppermute | solution.py:21
  36.4 4.9 %collective-permute-start.11 = (bf16[1,144,128]{2,1,0:T(8,128)(2,1)S(1)}, bf16[1,144,128]{2,1,0:T(8,128)(2,1)S(1)}, u32[]{:S(2)}, u32[]{:S(2)}) collective-permute-start(bf16[1,144,128]{2,1,0:T(8,128)(2,1)S(1)} %shard_map.141.rest_0_), channel_id=1, source_target_pairs={{0,8},{4,12},{8,0},{12,4},{1,9},{5,13},{9,1},{13,5},{2,10},{6,14},... | collective-permute-start | bytes 110600 | tf_op jit(solution)/shard_map/ppermute | solution.py:21
  38.3 5.8 %collective-permute-start.12 = (bf16[1,144,128]{2,1,0:T(8,128)(2,1)S(1)}, bf16[1,144,128]{2,1,0:T(8,128)(2,1)S(1)}, u32[]{:S(2)}, u32[]{:S(2)}) collective-permute-start(bf16[1,144,128]{2,1,0:T(8,128)(2,1)S(1)} %shard_map.141.rest_0_), channel_id=1, source_target_pairs={{0,12},{4,8},{8,4},{12,0},{1,13},{5,9},{9,5},{13,1},{2,14},{6,10},... | collective-permute-start | bytes 110600 | tf_op jit(solution)/shard_map/ppermute | solution.py:21
  41.2 23.4 %collective-permute-start.3 = (bf16[2,128,256]{2,1,0:T(8,128)(2,1)S(1)}, bf16[2,128,256]{2,1,0:T(8,128)(2,1)S(1)}, u32[]{:S(2)}, u32[]{:S(2)}) collective-permute-start(bf16[2,128,256]{2,1,0:T(8,128)(2,1)S(1)} %get-tuple-element.13.rest_0_), channel_id=1, source_target_pairs={{0,1},{1,0},{2,3},{3,2},{4,5},{5,4},{6,7},{7,6},{8,9},{9,8},{10,11... | collective-permute-start | bytes 393224 | tf_op jit(solution)/shard_map/ppermute | solution.py:21
  41.2 23.4 %collective-permute-start.4 = (bf16[2,128,256]{2,1,0:T(8,128)(2,1)S(1)}, bf16[2,128,256]{2,1,0:T(8,128)(2,1)S(1)}, u32[]{:S(2)}, u32[]{:S(2)}) collective-permute-start(bf16[2,128,256]{2,1,0:T(8,128)(2,1)S(1)} %collective-permute-done.rest_1_), channel_id=1, source_target_pairs={{0,1},{1,0},{2,3},{3,2},{4,5},{5,4},{6,7},{7,6},{8,9},{9,8},{10,11... | collective-permute-start | bytes 393224 | tf_op jit(solution)/shard_map/ppermute | solution.py:21
  41.8 22.8 %collective-permute-start.5 = (bf16[2,128,256]{2,1,0:T(8,128)(2,1)S(1)}, bf16[2,128,256]{2,1,0:T(8,128)(2,1)S(1)}, u32[]{:S(2)}, u32[]{:S(2)}) collective-permute-start(bf16[2,128,256]{2,1,0:T(8,128)(2,1)S(1)} %collective-permute-done.1.rest_2_), channel_id=1, source_target_pairs={{0,1},{1,0},{2,3},{3,2},{4,5},{5,4},{6,7},{7,6},{8,9},{9,8},{10,11... | collective-permute-start | bytes 393224 | tf_op jit(solution)/shard_map/ppermute | solution.py:21
  41.8 22.8 %collective-permute-start.6 = (bf16[2,128,256]{2,1,0:T(8,128)(2,1)S(1)}, bf16[2,128,256]{2,1,0:T(8,128)(2,1)S(1)}, u32[]{:S(2)}, u32[]{:S(2)}) collective-permute-start(bf16[2,128,256]{2,1,0:T(8,128)(2,1)S(1)} %collective-permute-done.2.rest_3_), channel_id=1, source_target_pairs={{0,1},{1,0},{2,3},{3,2},{4,5},{5,4},{6,7},{7,6},{8,9},{9,8},{10,11... | collective-permute-start | bytes 393224 | tf_op jit(solution)/shard_map/ppermute | solution.py:21
  44.1 5.7 %collective-permute-start.17 = (bf16[16,1024]{1,0:T(8,128)(2,1)S(1)}, bf16[16,1024]{1,0:T(8,128)(2,1)S(1)}, u32[]{:S(2)}, u32[]{:S(2)}) collective-permute-start(bf16[16,1024]{1,0:T(8,128)(2,1)S(1)} %get-tuple-element.22), channel_id=1, source_target_pairs={{0,12},{4,8},{8,4},{12,0},{1,13},{5,9},{9,5},{13,1},{2,14},{6,10},... | collective-permute-start | bytes 98312 | tf_op jit(solution)/shard_map/ppermute | solution.py:21
  49.8 4.4 %collective-permute-start.13 = (bf16[8,2048]{1,0:T(8,128)(2,1)S(1)}, bf16[8,2048]{1,0:T(8,128)(2,1)S(1)}, u32[]{:S(2)}, u32[]{:S(2)}) collective-permute-start(bf16[8,2048]{1,0:T(8,128)(2,1)S(1)} %shard_map.142.attn_ref), channel_id=1, source_target_pairs={{0,1},{1,0},{2,3},{3,2},{4,5},{5,4},{6,7},{7,6},{8,9},{9,8},{10,11... | collective-permute-start | bytes 98312 | tf_op jit(solution)/shard_map/ppermute | solution.py:21
  50.7 1.0 %copy-start.4 = (f32[16,8192]{1,0:T(8,128)S(1)}, f32[16,8192]{1,0:T(8,128)}, u32[]{:S(2)}) copy-start(f32[16,8192]{1,0:T(8,128)} %log_ref.1) | copy-start | bytes 1572868
  51.7 0.8 %copy-start.5 = (f32[2,1,8192]{2,1,0:T(1,128)S(1)}, f32[2,1,8192]{2,1,0:T(1,128)}, u32[]{:S(2)}) copy-start(f32[2,1,8192]{2,1,0:T(1,128)} %dt_ref.1) | copy-start | bytes 196612
  52.5 0.8 %copy-start.6 = (f32[8192]{0:T(1024)S(1)}, f32[8192]{0:T(1024)}, u32[]{:S(2)}) copy-start(f32[8192]{0:T(1024)} %param.23) | copy-start | bytes 98308
  53.3 0.7 %copy-start.11 = (f32[2,1,2,16]{3,2,1,0:T(2,128)S(1)}, f32[2,1,2,16]{3,2,1,0:T(2,128)}, u32[]{:S(2)}) copy-start(f32[2,1,2,16]{3,2,1,0:T(2,128)} %bc_ref.1) | copy-start | bytes 772
  54.3 5.9 %collective-permute-start.18 = (f32[2,4,1024]{2,1,0:T(4,128)S(1)}, f32[2,4,1024]{2,1,0:T(4,128)S(1)}, u32[]{:S(2)}, u32[]{:S(2)}) collective-permute-start(f32[2,4,1024]{2,1,0:T(4,128)S(1)} %shard_map.148.own_ref), channel_id=1, source_target_pairs={{0,1},{1,0},{2,3},{3,2},{4,5},{5,4},{6,7},{7,6},{8,9},{9,8},{10,11... | collective-permute-start | bytes 98312 | tf_op jit(solution)/shard_map/ppermute | solution.py:21
  54.9 3.4 %copy-start = (bf16[4096,1024]{1,0:T(8,128)(2,1)S(1)}, bf16[4096,1024]{1,0:T(8,128)(2,1)}, u32[]{:S(2)}) copy-start(bf16[4096,1024]{1,0:T(8,128)(2,1)} %weight_ref.1) | copy-start | bytes 25165828
  58.8 5.8 %copy-start.9 = (s32[4,8]{1,0:T(4,128)S(1)}, s32[4,8]{1,0:T(4,128)}, u32[]{:S(2)}) copy-start(s32[4,8]{1,0:T(4,128)} %counts_ref.3) | copy-start | bytes 388
  60.2 3.8 %collective-permute-start.14 = (f32[2,2,1024]{2,1,0:T(2,128)S(1)}, f32[2,2,1024]{2,1,0:T(2,128)S(1)}, u32[]{:S(2)}, u32[]{:S(2)}) collective-permute-start(f32[2,2,1024]{2,1,0:T(2,128)S(1)} %get-tuple-element.18), channel_id=1, source_target_pairs={{0,2},{2,0},{1,3},{3,1},{4,6},{6,4},{5,7},{7,5},{8,10},{10,8},{9,1... | collective-permute-start | bytes 49160 | tf_op jit(solution)/shard_map/ppermute | solution.py:21

commit v2 on v1

v2 whole, which is shorter than its diff:
```python
import functools

import jax
import jax.numpy as jnp
from jax import lax
from jax.experimental import pallas as pl
from jax.experimental.pallas import tpu as pltpu
from jax.sharding import PartitionSpec as P

BLOCK = 128
NEG = -1e30
BF = jnp.bfloat16
F32 = jnp.float32
VM = pl.BlockSpec(memory_space=pltpu.VMEM)
HB = pl.BlockSpec(memory_space=pltpu.HBM)
DMA = pltpu.SemaphoreType.DMA


def shift(x, axis, c):
    size = lax.axis_size(axis)
    return lax.ppermute(x, axis, [(i, i ^ c) for i in range(size)])


def call(body, out_shape, in_specs, out_specs, scratch=(), us=1.0):
    return pl.pallas_call(
        body,
        out_shape=out_shape,
        in_specs=in_specs,
        out_specs=out_specs,
        scratch_shapes=list(scratch),
        cost_estimate=pl.CostEstimate(
            flops=0, bytes_accessed=int(us * 3.6e6), transcendentals=0
        ),
        compiler_params=pltpu.CompilerParams(vmem_limit_bytes=32 * 1024 * 1024),
    )


def in_hbm(x):
    return pltpu.with_memory_space_constraint(x, pltpu.HBM)


def after(arrays, *earlier):
    return lax.optimization_barrier((*arrays, *earlier))[: len(arrays)]


def run_all(copies):
    for copy in copies:
        copy.start()
    for copy in copies:
        copy.wait()


def copier(sems):
    position = iter(range(sems.shape[0]))
    return lambda src, dst: pltpu.make_async_copy(src, dst, sems.at[next(position)])


def state_rows(part):
    return 16 * pl.cdiv(part, 256)


def pack_state(piece, out_ref, first):
    ns, part = piece.shape
    for i in range(pl.cdiv(part, 256)):
        cut = piece[:, i * 256 : (i + 1) * 256]
        if cut.shape[1] < 256:
            cut = jnp.concatenate([cut, jnp.zeros((ns, 256 - cut.shape[1]), F32)], axis=1)
        out_ref[first + i * 16 : first + (i + 1) * 16, :] = cut.astype(BF)


def stage(count, split, kv_ref, state_ref, q_ref, new_ref, blocks_ref, counts_ref, *rest):
    sends = rest[: count - 1]
    own_state, kv_out, q_out, new_out, bias_out = rest[count - 1 : count + 4]
    loaded, blocks, counts, sems, early = rest[count + 4 :]
    me, rep = lax.axis_index("seq"), lax.axis_index("rep")
    heads = kv_ref.shape[1]
    part = loaded.shape[2]
    copy = copier(early)
    first = [copy(blocks_ref, blocks), copy(counts_ref, counts)]
    for c in range(count):
        if split:
            src = state_ref.at[me ^ c, :, pl.ds(pl.multiple_of(rep * part, 128), part)]
        else:
            src = state_ref.at[me ^ c]
        first.append(copy(src, loaded.at[c]))
    copy = copier(sems)
    moves = []
    for c in range(1, count):
        for j in range(heads):
            rows = pl.ds(j * BLOCK, BLOCK)
            moves.append(copy(kv_ref.at[me ^ c, j], sends[c - 1].at[rows]))
    moves += [copy(kv_ref, kv_out), copy(q_ref, q_out), copy(new_ref, new_out)]
    for move in first + moves:
        move.start()
    for move in first:
        move.wait()
    pack_state(loaded[0], own_state, 0)
    for c in range(1, count):
        pack_state(loaded[c], sends[c - 1], heads * BLOCK)
    head_first = lax.axis_index("head") * new_ref.shape[2] + rep * heads
    rows = bias_out.shape[0] // (count * heads)
    for c in range(count):
        for j in range(heads):
            live = jnp.int32(0)
            for slot in range(blocks.shape[1]):
                hit = blocks[me ^ c, slot, head_first + j] == me
                live = live | (hit & (slot < counts[me ^ c, head_first + j])).astype(jnp.int32)
            at = (c * heads + j) * rows
            dead = jnp.where(live > 0, 0.0, NEG).astype(F32)
            bias_out[at : at + rows, :] = jnp.full((rows, 128), dead, F32)
    for move in moves:
        move.wait()


def dot_f32(a, b, contract):
    return lax.dot_general(a, b, (contract, ((), ())), preferred_element_type=F32)


def attend(count, kv_ref, new_ref, bias_ref, *rest):
    q_refs, out_ref = rest[:count], rest[count]
    me, rep = lax.axis_index("seq"), lax.axis_index("rep")
    heads = kv_ref.shape[1]
    hd = kv_ref.shape[3] // 2
    steps, _, q_heads, _ = q_refs[0].shape
    own_q = q_heads // 2
    group = own_q // heads
    rows = steps * group
    scale = hd ** (-0.5)
    fresh = []
    for step in range(steps):
        both = new_ref[step, 0].astype(F32)
        fresh.append(jnp.where(rep == 0, both[:heads], both[heads:]))
    queries = []
    for c in range(count):
        q_all = [q_refs[c][step, 0].astype(F32) for step in range(steps)]
        q_all = [jnp.where(rep == 0, q[:own_q], q[own_q:]) for q in q_all]
        for j in range(heads):
            queries.append(
                jnp.concatenate([x[j * group : (j + 1) * group] for x in q_all], axis=0)
            )
    scores = []
    for c in range(count):
        for j in range(heads):
            keys = kv_ref[me ^ c, j, :, :hd]
            scores.append(dot_f32(queries[c * heads + j].astype(BF), keys, ((1,), (1,))))
    scores = jnp.concatenate(scores, axis=0)
    alive = bias_ref[...] == 0.0
    scores = jnp.where(alive, scores * scale, NEG)
    top = jnp.max(scores, axis=1, keepdims=True)
    own_rows = heads * rows
    own_q_rows = jnp.concatenate(queries[:heads], axis=0)
    row_step = (lax.broadcasted_iota(jnp.int32, (own_rows, 1), 0) // group) % steps
    own_top = top[:own_rows]
    dots = []
    for step in range(steps):
        wide = jnp.concatenate(
            [jnp.broadcast_to(fresh[step][j : j + 1, :hd], (rows, hd)) for j in range(heads)],
            axis=0,
        )
        dot = jnp.sum(own_q_rows * wide, axis=1, keepdims=True)
        dots.append(jnp.where(row_step >= step, dot * scale, NEG))
        own_top = jnp.maximum(own_top, dots[-1])
    top = jnp.concatenate([own_top, top[own_rows:]], axis=0)
    weights = jnp.where(alive, jnp.exp(scores - top), 0.0)
    total = jnp.sum(weights, axis=1, keepdims=True)
    weights = weights.astype(BF)
    summed = []
    for c in range(count):
        for j in range(heads):
            at = (c * heads + j) * rows
            values = kv_ref[me ^ c, j, :, hd:]
            summed.append(dot_f32(weights[at : at + rows], values, ((1,), (0,))))
    own_sum = jnp.concatenate(summed[:heads], axis=0)
    own_total = total[:own_rows]
    for step in range(steps):
        weight = jnp.where(row_step >= step, jnp.exp(dots[step] - own_top), 0.0)
        own_total = own_total + weight
        wide = jnp.concatenate(
            [jnp.broadcast_to(fresh[step][j : j + 1, hd:], (rows, hd)) for j in range(heads)],
            axis=0,
        )
        own_sum = own_sum + weight.astype(BF).astype(F32) * wide
    total = jnp.concatenate([own_total, total[own_rows:]], axis=0)
    summed = jnp.concatenate([own_sum] + summed[heads:], axis=0)
    chunks = out_ref.shape[0]
    line = lax.broadcasted_iota(jnp.int32, (16, 128), 0)
    for k in range(chunks):
        cut = slice(k * 128, (k + 1) * 128)
        out_ref[k, :128, :] = summed[cut].astype(BF)
        stats = jnp.zeros((16, 128), F32)
        for kind, column in ((0, top[cut]), (3, total[cut])):
            flat = jnp.transpose(jnp.broadcast_to(column, (128, 128)))[:16]
            high = flat.astype(BF).astype(F32)
            middle = (flat - high).astype(BF).astype(F32)
            low = flat - high - middle
            for at, piece in ((kind, high), (kind + 1, middle), (kind + 2, low)):
                stats = jnp.where(line == at, piece, stats)
        out_ref[k, 128:, :] = stats.astype(BF)


def merge(count, heads, steps, group, *rest):
    parts, out_ref, scratch = rest[:count], rest[count], rest[count + 1]
    me = lax.axis_index("seq")
    rows = steps * group
    chunks = parts[0].shape[0]
    line = lax.broadcasted_iota(jnp.int32, (16, 128), 0)
    top_all, total_all = [], []
    for c in range(count):
        tops, totals = [], []
        for k in range(chunks):
            stats = parts[c][k, 128:, :].astype(F32)
            for kind, out in ((0, tops), (3, totals)):
                mine = (line >= kind) & (line < kind + 3)
                row = jnp.sum(jnp.where(mine, stats, 0.0), axis=0, keepdims=True)
                out.append(jnp.transpose(jnp.broadcast_to(row, (128, 128))))
        top_all.append(tops)
        total_all.append(totals)
    for e in range(count):
        for j in range(heads):
            places = [divmod(((e ^ c) * heads + j) * rows, 128) for c in range(count)]
            tops = [top_all[c][k][at : at + rows] for c, (k, at) in enumerate(places)]
            top = functools.reduce(jnp.maximum, tops)
            total = jnp.zeros_like(top)
            summed = jnp.zeros_like(top)
            for c, (k, at) in enumerate(places):
                weight = jnp.exp(tops[c] - top)
                total = total + weight * total_all[c][k][at : at + rows]
                summed = summed + weight * parts[c][k, at : at + rows, :].astype(F32)
            result = summed / total
            for step in range(steps):
                at = pl.multiple_of((step * count + (me ^ e)) * group, group)
                scratch[j, pl.ds(at, group), :] = result[step * group : (step + 1) * group]
    for j in range(heads):
        for g in range(group):
            at = (j * group + g) * 128
            tile = scratch[j, pl.ds(g, steps * count, stride=group), :]
            out_ref[:, at : at + 128] = tile.astype(BF)


def load_weight(weight_ref, out_ref, sems):
    pieces = sems.shape[0]
    rows = weight_ref.shape[0] // pieces
    copy = copier(sems)
    cuts = [pl.ds(i * rows, rows) for i in range(pieces)]
    run_all([copy(weight_ref.at[cut], out_ref.at[cut]) for cut in cuts])


def project_own(attn_ref, weight_ref, out_ref):
    half = attn_ref.shape[1]
    first = pl.multiple_of(lax.axis_index("rep") * half, half)
    out_ref[...] = dot_f32(attn_ref[...], weight_ref[pl.ds(first, half), :], ((1,), (0,)))


def pick(options, index):
    chosen = options[0]
    for i in range(1, len(options)):
        chosen = jnp.where(index == i, options[i], chosen)
    return chosen


def project_other(heads_count, count, acc_ref, attn_ref, weight_ref, *outs):
    half = attn_ref.shape[1]
    first = pl.multiple_of((1 - lax.axis_index("rep")) * half, half)
    total = acc_ref[...] + dot_f32(
        attn_ref[...], weight_ref[pl.ds(first, half), :], ((1,), (0,))
    )
    head = lax.axis_index("head")
    steps = total.shape[0] // count
    share = count // heads_count
    for step in range(steps):
        slices = [
            total[step * count + x * share : step * count + (x + 1) * share]
            for x in range(heads_count)
        ]
        for c in range(heads_count):
            outs[c][step] = pick(slices, head ^ c)


def add_up(*refs):
    total = refs[0][...]
    for ref in refs[1:-1]:
        total = total + ref[...]
    refs[-1][...] = total.astype(BF)


def coefficients(count, split, dt_hbm, x_hbm, bc_hbm, gain_hbm, log_hbm, slope_ref, base_ref,
                 dt_ref, x_ref, bc_ref, gain_ref, log_ref, sems):
    copy = copier(sems)
    run_all(
        [
            copy(dt_hbm, dt_ref),
            copy(x_hbm, x_ref),
            copy(bc_hbm, bc_ref),
            copy(gain_hbm, gain_ref),
            copy(log_hbm, log_ref),
        ]
    )
    me, rep = lax.axis_index("seq"), lax.axis_index("rep")
    _, steps, ns, part = slope_ref.shape
    block = part * 2 if split else part
    diagonal = lax.broadcasted_iota(jnp.int32, (ns, ns), 0) == lax.broadcasted_iota(
        jnp.int32, (ns, ns), 1
    )

    def column(row):
        return jnp.sum(jnp.where(diagonal, row, 0.0), axis=1, keepdims=True)

    drive = [column(bc_ref[step, 0, 0:1, :]) for step in range(steps)]
    read = [column(bc_ref[step, 0, 1:2, :]) for step in range(steps)]
    for c in range(count):
        first = (me ^ c) * block + (rep * part if split else 0)
        lanes = pl.ds(pl.multiple_of(first, 128), part)
        rate = -jnp.exp(log_ref[:, lanes])
        gain = gain_ref[:, lanes]
        kept = jnp.ones((ns, part), F32)
        added = jnp.zeros((ns, part), F32)
        for step in range(steps):
            dt = dt_ref[step, :, lanes]
            inputs = x_ref[step : step + 1, lanes].astype(F32)
            decay = jnp.exp(dt * rate)
            kept = kept * decay
            added = added * decay + drive[step] * (dt * inputs)
            slope_ref[c, step] = read[step] * kept
            base_ref[c, step] = (
                jnp.sum(read[step] * added, axis=0, keepdims=True) + gain * inputs
            )


def select(count, blocks_ref, counts_ref, kv_ref, state_ref, slope_ref, base_ref, *rest):
    received = rest[: count - 1]
    kept_ref, sent_ref, mamba_ref, blocks, counts, zeros, sems, early = rest[count - 1 :]
    me, rep = lax.axis_index("seq"), lax.axis_index("rep")
    heads, keep_rep = kept_ref.shape[:2]
    copy = copier(early)
    scalars = [copy(blocks_ref, blocks), copy(counts_ref, counts)]
    for move in scalars:
        move.start()
    zeros[...] = jnp.zeros_like(zeros)
    _, steps, ns, part = slope_ref.shape
    for c in range(count):
        source, first = (state_ref, 0) if c == 0 else (received[c - 1], heads * BLOCK)
        rows = [
            source[first + 16 * i : first + 16 * (i + 1), :].astype(F32)
            for i in range(pl.cdiv(part, 256))
        ]
        state = jnp.concatenate(rows, axis=1)[:, :part]
        for step in range(steps):
            mamba_ref[step, me ^ c] = base_ref[c, step] + jnp.sum(
                slope_ref[c, step] * state, axis=0, keepdims=True
            )
    for move in scalars:
        move.wait()
    head_first = lax.axis_index("head") * (2 * heads) + rep * heads
    for side, out in ((0, kept_ref), (1, sent_ref)):
        owner = rep if side == 0 else 1 - rep
        for j in range(heads):
            live_count = counts[me, head_first + j]
            for k in range(keep_rep):
                slot = owner * keep_rep + k
                source = blocks[me, slot, head_first + j] ^ me
                live = slot < live_count
                sem = sems.at[side, j, k]
                for c in range(count):
                    piece = kv_ref.at[me, j] if c == 0 else received[c - 1].at[pl.ds(j * BLOCK, BLOCK)]

                    @pl.when(live & (source == c))
                    def _():
                        pltpu.make_async_copy(piece, out.at[j, k], sem).start()

                @pl.when(jnp.logical_not(live))
                def _():
                    pltpu.make_async_copy(zeros, out.at[j, k], sem).start()

    for side, out in ((0, kept_ref), (1, sent_ref)):
        for j in range(heads):
            for k in range(keep_rep):
                pltpu.make_async_copy(zeros, out.at[j, k], sems.at[side, j, k]).wait()


def assemble(split, kept_ref, got_ref, mamba_ref, *rest):
    rep = lax.axis_index("rep")
    if split:
        other_ref, handoff_ref, out_ref, sems = rest
    else:
        handoff_ref, out_ref, sems = rest
    heads = kept_ref.shape[0]
    copy = copier(sems)
    moves = [
        copy(kept_ref, handoff_ref.at[0, pl.ds(rep * heads, heads)]),
        copy(got_ref, handoff_ref.at[0, pl.ds((1 - rep) * heads, heads)]),
    ]
    steps, count, _, part = mamba_ref.shape
    for step in range(steps):
        for b in range(count):
            if split:
                for ref, side in ((mamba_ref, rep), (other_ref, 1 - rep)):
                    lanes = pl.ds(pl.multiple_of((2 * b + side) * part, 128), part)
                    moves.append(copy(ref.at[step, b], out_ref.at[step, :, lanes]))
            else:
                moves.append(copy(mamba_ref.at[step, b], out_ref.at[step, :, pl.ds(b * part, part)]))
    run_all(moves)


def per_device(
    prefill_kv,
    kept_blocks,
    kept_counts,
    queries,
    new_kv,
    out_weight,
    prefill_state,
    a_log,
    step_input,
    step_dt,
    step_bc,
    skip_gain,
):
    count = lax.axis_size("seq")
    reps = lax.axis_size("rep")
    heads_count = lax.axis_size("head")
    requests, heads, tokens, width = prefill_kv.shape
    assert requests == count and tokens == BLOCK and reps == 2 and width == 256
    assert count & (count - 1) == 0 and heads_count & (heads_count - 1) == 0
    keep = kept_blocks.shape[2]
    keep_rep = keep // reps
    steps, _, q_heads, hd = queries.shape
    dec_heads = new_kv.shape[2]
    group = q_heads // dec_heads
    _, ns, block = prefill_state.shape
    split = block % (reps * 128) == 0
    part = block // reps if split else block
    all_rows = count * heads * steps * group
    chunks = all_rows // 128
    channels = count * block
    shape = jax.ShapeDtypeStruct
    smem = pltpu.SMEM
    blocks = jnp.swapaxes(kept_blocks, 1, 2)

    asked = [shift(queries, "seq", c) for c in range(1, count)]
    prefill_kv, prefill_state, queries, new_kv = map(in_hbm, (prefill_kv, prefill_state, queries, new_kv))
    step_dt, step_bc, a_log, out_weight = map(in_hbm, (step_dt, step_bc, a_log, out_weight))
    step_input = in_hbm(step_input.reshape(steps, channels))
    skip_gain = in_hbm(skip_gain.reshape(1, -1))
    blocks, kept_counts = in_hbm(blocks), in_hbm(kept_counts)

    packed = heads * BLOCK + state_rows(part)
    staged = call(
        functools.partial(stage, count, split),
        [shape((packed, width), BF)] * (count - 1)
        + [
            shape((state_rows(part), width), BF),
            shape(prefill_kv.shape, BF),
            shape(queries.shape, BF),
            shape(new_kv.shape, BF),
            shape((all_rows, 128), F32),
        ],
        [HB] * 6,
        [VM] * (count + 4),
        [
            pltpu.VMEM((count, ns, part), F32),
            smem(blocks.shape, jnp.int32),
            smem(kept_counts.shape, jnp.int32),
            DMA(((count - 1) * heads + 3,)),
            DMA((count + 2,)),
        ],
        us=1.5,
    )(prefill_kv, prefill_state, queries, new_kv, blocks, kept_counts)
    sends = staged[: count - 1]
    own_state, kv_near, q_near, new_near, bias = staged[count - 1 :]
    far = after(sends[1:], *asked)
    received = [shift(far[c - 2], "seq", c) for c in range(2, count)]

    slope, base = call(
        functools.partial(coefficients, count, split),
        [shape((count, steps, ns, part), F32), shape((count, steps, 1, part), F32)],
        [HB] * 5,
        [VM] * 2,
        [
            pltpu.VMEM((steps, 1, channels), F32),
            pltpu.VMEM((steps, channels), BF),
            pltpu.VMEM(step_bc.shape, F32),
            pltpu.VMEM((1, channels), F32),
            pltpu.VMEM(a_log.shape, F32),
            DMA((5,)),
        ],
        us=2.0,
    )(step_dt, step_input, step_bc, skip_gain, a_log)

    partial_sums = call(
        functools.partial(attend, count),
        shape((chunks, 144, 128), BF),
        [VM] * (3 + count),
        VM,
        us=1.5,
    )(kv_near, new_near, bias, q_near, *asked)
    weight = call(load_weight, pltpu.VMEM(out_weight.shape, BF), [HB], VM, [DMA((8,))], us=3.4)(
        *after([out_weight], partial_sums)
    )
    gathered = [partial_sums] + [shift(partial_sums, "seq", c) for c in range(1, count)]
    half = heads * group * hd
    attn = call(
        functools.partial(merge, count, heads, steps, group),
        shape((steps * count, half), BF),
        [VM] * count,
        VM,
        [pltpu.VMEM((heads, steps * count * group, hd), F32)],
        us=0.3,
    )(*gathered)
    attn_other = shift(attn, "rep", 1)
    received = [shift(after(sends[:1], attn)[0], "seq", 1)] + received
    columns = out_weight.shape[1]
    own_sum = call(
        project_own, shape((steps * count, columns), F32), [VM, VM], VM, us=0.7
    )(attn, weight)
    share = count // heads_count
    sums = call(
        functools.partial(project_other, heads_count, count),
        [shape((steps, share, columns), F32)] * heads_count,
        [VM, VM, VM],
        [VM] * heads_count,
        us=0.7,
    )(own_sum, attn_other, weight)
    sums = [sums[0]] + [shift(sums[c], "head", c) for c in range(1, heads_count)]
    proj_out = call(
        add_up, shape((steps, share, columns), BF), [VM] * heads_count, VM, us=0.6
    )(*sums)

    received = after(received, proj_out)
    half_shape = (heads, keep_rep, BLOCK, width)
    kept, sent, mamba = call(
        functools.partial(select, count),
        [shape(half_shape, BF), shape(half_shape, BF), shape((steps, count, 1, part), F32)],
        [HB] * 3 + [VM] * (3 + count - 1),
        [VM] * 3,
        [
            smem(blocks.shape, jnp.int32),
            smem(kept_counts.shape, jnp.int32),
            pltpu.VMEM((BLOCK, width), BF),
            DMA((2, heads, keep_rep)),
            DMA((2,)),
        ],
        us=1.0,
    )(blocks, kept_counts, prefill_kv, own_state, slope, base, *received)
    got = shift(sent, "rep", 1)
    operands = [kept, got, mamba] + ([shift(mamba, "rep", 1)] if split else [])
    handoff, mamba_out = call(
        functools.partial(assemble, split),
        [
            shape((1, dec_heads, keep_rep, BLOCK, width), BF),
            shape((steps, 1, channels), F32),
        ],
        [VM] * len(operands),
        [HB] * 2,
        [DMA((2 + steps * count * (2 if split else 1),))],
        us=1.0,
    )(*operands)
    return handoff, proj_out, mamba_out


def solution(mesh):
    return jax.shard_map(
        per_device,
        mesh=mesh,
        in_specs=(
            P("groups", ("head", "rep"), "seq", None),
            P("groups", None, None),
            P("groups", None),
            P(None, ("groups", "seq"), "head", None),
            P(None, ("groups", "seq"), "head", None),
            P("head", ("seq", "rep")),
            P("groups", None, ("head", "seq")),
            P(None, "head"),
            P(None, ("groups", "seq"), "head"),
            P(None, ("groups", "seq"), "head"),
            P(None, ("groups", "seq"), None, None),
            P("head"),
        ),
        out_specs=(
            P(("groups", "seq"), "head", "rep", None, None),
            P(None, ("groups", "head"), ("seq", "rep")),
            P(None, ("groups", "seq"), "head"),
        ),
        check_vma=False,
    )
```

time: 66.9 us -> 39.5 us (0.59)
  local copies, waits for them, and re-layouts: 13.5 us -> 0 us
  starting transfers between devices: 24.5 us -> 16 us
  waiting for transfers between devices: 18.6 us -> 10.7 us
  Pallas kernels: 8.87 us -> 11.8 us
    unnamed x26 -> x0, local copies, waits for them, and re-layouts: 13.5 us -> none
    ppermute x19 -> x13, starting transfers between devices: 24.5 us -> 16 us  [shift(): return lax.ppermute(x, axis, [(i, i ^ c) for i in range(size)])]
    ppermute x19 -> x13, waiting for transfers between devices: 18.6 us -> 10.7 us  [shift(): return lax.ppermute(x, axis, [(i, i ^ c) for i in range(size)])]
    pallas_call x9 -> x8, Pallas kernels: 7.99 us -> 10.9 us  [the longest x1 3.47 us: per_device(): call(load_weight, pltpu.VMEM(out_weight.shape, BF), [HB], VM, [DMA((8,))]...]
  transfers between devices with their start and end apart: 19 -> 13, of which waited for: 8 -> 5; matrix products, arithmetic and copies ran while one was open for 2% -> 0% of each run, Pallas kernels for 10% -> 22%
where the time goes in v2:
time: 39.5 us; the launch traced here: 39.2 us
  starting transfers between devices  16 us (41%)
  Pallas kernels  11.8 us (30%)
  waiting for transfers between devices  10.7 us (27%)
  between operations  0.72 us (2%)
    ppermute x13, starting transfers between devices, shift(): return lax.ppermute(x, axis, [(i, i ^ c) for i in range(size)])  16 us
    ppermute x13, waiting for transfers between devices, shift(): return lax.ppermute(x, axis, [(i, i ^ c) for i in range(size)])  10.7 us
    pallas_call x1, Pallas kernels, per_device(): call(load_weight, pltpu.VMEM(out_weight.shape, BF), [HB], VM, [DMA((8,))]...  3.47 us
    pallas_call x1, Pallas kernels, per_device(): call(functools.partial(select, count), [shape(half_shape, BF), shape(half...  1.67 us
    pallas_call x1, Pallas kernels, per_device(): call(functools.partial(coefficients, count, split), [shape((count, steps,...  1.51 us
    pallas_call x1, Pallas kernels, per_device(): call(functools.partial(stage, count, split), [shape((packed, width), BF)]...  1.48 us
    pallas_call x1, Pallas kernels, per_device(): call(functools.partial(assemble, split), [shape((1, dec_heads, keep_rep,...  0.89 us
  transfers between devices with their start and end apart: 13, of which 5 were waited for; matrix products, arithmetic and copies ran while one was open for 0% of the time, Pallas kernels for 22%

profile of v2, /device:TPU:0, one launch (start us, length us, event | category | flops | bytes accessed | tf_op | source)
XLA Modules:
  0.0 39.2 jit_solution(6039465381698494627)
XLA Ops:
  0.6 3.1 %collective-permute-start = (bf16[2,1,32,128]{3,2,1,0:T(8,128)(2,1)}, bf16[2,1,32,128]{3,2,1,0:T(8,128)(2,1)S(1)}, u32[]{:S(2)}, u32[]{:S(2)}) collective-permute-start(bf16[2,1,32,128]{3,2,1,0:T(8,128)(2,1)} %q_ref.1), channel_id=1, source_target_pairs={{0,4},{4,0},{8,12},{12,8},{1,5},{5,1},{9,13},{13,9},{2,6},{6,2},{1... | collective-permute-start | bytes 49160 | tf_op jit(solution)/shard_map/ppermute | solution.py:21
  3.7 2.6 %collective-permute-start.1 = (bf16[2,1,32,128]{3,2,1,0:T(8,128)(2,1)}, bf16[2,1,32,128]{3,2,1,0:T(8,128)(2,1)S(1)}, u32[]{:S(2)}, u32[]{:S(2)}) collective-permute-start(bf16[2,1,32,128]{3,2,1,0:T(8,128)(2,1)} %q_ref.1), channel_id=1, source_target_pairs={{0,8},{4,12},{8,0},{12,4},{1,9},{5,13},{9,1},{13,5},{2,10},{6,14},... | collective-permute-start | bytes 49160 | tf_op jit(solution)/shard_map/ppermute | solution.py:21
  6.3 0.0 collective-permute-start.2
  6.3 1.5 %shard_map.139 = (bf16[320,256]{1,0:T(8,128)(2,1)S(1)}, bf16[320,256]{1,0:T(8,128)(2,1)S(1)}, bf16[320,256]{1,0:T(8,128)(2,1)S(1)}, bf16[64,256]{1,0:T(8,128)(2,...) custom-call(bf16[4,2,128,256]{3,2,1,0:T(8,128)(2,1)} %kv_ref.3, ...), custom_call_target="tpu_custom_call" | custom-call | bytes 5400000 | tf_op jit(solution)/shard_map/pallas_call | solution.py:447
  7.8 0.0 collective-permute-done.rest_1_
  7.8 0.8 %collective-permute-done.1.rest_2_ = bf16[2,1,32,128]{3,2,1,0:T(8,128)(2,1)S(1)} collective-permute-done((bf16[2,1,32,128]{3,2,1,0:T(8,128)(2,1)}, bf16[2,1,32,128]{3,2,1,0:T(8,128)(2,1)S(1)}, u32[]{:S(2)}, u32[]{:S(2)}) %collective-permute-start.1) | collective-permute-done | bytes 16416 | tf_op jit(solution)/shard_map/ppermute | solution.py:21
  8.6 3.4 %collective-permute-done.2.rest_3_ = bf16[2,1,32,128]{3,2,1,0:T(8,128)(2,1)S(1)} collective-permute-done((bf16[2,1,32,128]{3,2,1,0:T(8,128)(2,1)}, bf16[2,1,32,128]{3,2,1,0:T(8,128)(2,1)S(1)}, u32[]{:S(2)}, u32[]{:S(2)}) %collective-permute-start.2) | collective-permute-done | bytes 16416 | tf_op jit(solution)/shard_map/ppermute | solution.py:21
  12.1 0.6 %shard_map.141.rest_0_ = bf16[1,144,128]{2,1,0:T(8,128)(2,1)S(1)} custom-call(bf16[4,2,128,256]{3,2,1,0:T(8,128)(2,1)S(1)} %get-tuple-element.31.kv_ref, bf16[2,1,4,256]{3,2,1,0:T(4,128)(2,1)S(1)} %get-tuple-element.32.new_ref, f32[128,128]{1,0:T(8,128)S(1)} %get-tuple-element.33.bias_ref, bf16[2,1,32,128]{3,2,1,0:T(8,128)(2,1)S(1)} %get-tuple-element.34.rest_0_, ...), custom_call_target="tpu_custom_call" | custom-call | bytes 5400000 | tf_op jit(solution)/shard_map/pallas_call | solution.py:489
  12.7 0.1 collective-permute-start.3
  12.8 0.7 %collective-permute-start.4 = (bf16[1,144,128]{2,1,0:T(8,128)(2,1)S(1)}, bf16[1,144,128]{2,1,0:T(8,128)(2,1)S(1)}, u32[]{:S(2)}, u32[]{:S(2)}) collective-permute-start(bf16[1,144,128]{2,1,0:T(8,128)(2,1)S(1)} %shard_map.141.rest_0_), channel_id=1, source_target_pairs={{0,8},{4,12},{8,0},{12,4},{1,9},{5,13},{9,1},{13,5},{2,10},{6,14},... | collective-permute-start | bytes 110600 | tf_op jit(solution)/shard_map/ppermute | solution.py:21
  13.5 3.6 %collective-permute-start.5 = (bf16[1,144,128]{2,1,0:T(8,128)(2,1)S(1)}, bf16[1,144,128]{2,1,0:T(8,128)(2,1)S(1)}, u32[]{:S(2)}, u32[]{:S(2)}) collective-permute-start(bf16[1,144,128]{2,1,0:T(8,128)(2,1)S(1)} %shard_map.141.rest_0_), channel_id=1, source_target_pairs={{0,12},{4,8},{8,4},{12,0},{1,13},{5,9},{9,5},{13,1},{2,14},{6,10},... | collective-permute-start | bytes 110600 | tf_op jit(solution)/shard_map/ppermute | solution.py:21
  17.1 1.5 %collective-permute-start.8 = (bf16[320,256]{1,0:T(8,128)(2,1)S(1)}, bf16[320,256]{1,0:T(8,128)(2,1)S(1)}, u32[]{:S(2)}, u32[]{:S(2)}) collective-permute-start(bf16[320,256]{1,0:T(8,128)(2,1)S(1)} %get-tuple-element.39), channel_id=1, source_target_pairs={{0,12},{4,8},{8,4},{12,0},{1,13},{5,9},{9,5},{13,1},{2,14},{6,10},... | collective-permute-start | bytes 491528 | tf_op jit(solution)/shard_map/ppermute | solution.py:21
  18.7 4.8 %collective-permute-done.4.rest_2_ = bf16[1,144,128]{2,1,0:T(8,128)(2,1)S(1)} collective-permute-done((bf16[1,144,128]{2,1,0:T(8,128)(2,1)S(1)}, bf16[1,144,128]{2,1,0:T(8,128)(2,1)S(1)}, u32[]{:S(2)}, u32[]{:S(2)}) %collective-permute-start.4) | collective-permute-done | bytes 36896 | tf_op jit(solution)/shard_map/ppermute | solution.py:21
  23.5 0.2 shard_map.142.attn_ref
  23.7 2.2 %collective-permute-start.6 = (bf16[320,256]{1,0:T(8,128)(2,1)S(1)}, bf16[320,256]{1,0:T(8,128)(2,1)S(1)}, u32[]{:S(2)}, u32[]{:S(2)}) collective-permute-start(bf16[320,256]{1,0:T(8,128)(2,1)S(1)} %get-tuple-element.35), channel_id=1, source_target_pairs={{0,4},{4,0},{8,12},{12,8},{1,5},{5,1},{9,13},{13,9},{2,6},{6,2},{1... | collective-permute-start | bytes 491528 | tf_op jit(solution)/shard_map/ppermute | solution.py:21
  25.9 0.0 collective-permute-start.9
  25.9 3.5 %shard_map.143.weight_ref = bf16[4096,1024]{1,0:T(8,128)(2,1)S(1)} custom-call(bf16[4096,1024]{1,0:T(8,128)(2,1)} %weight_ref), custom_call_target="tpu_custom_call" | custom-call | bytes 12240000 | tf_op jit(solution)/shard_map/pallas_call | solution.py:496
  29.4 0.7 %shard_map.144.acc_ref = f32[8,1024]{1,0:T(8,128)S(1)} custom-call(bf16[8,2048]{1,0:T(8,128)(2,1)S(1)} %shard_map.142.attn_ref, bf16[4096,1024]{1,0:T(8,128)(2,1)S(1)} %shard_map.143.weight_ref), custom_call_target="tpu_custom_call" | custom-call | bytes 2520000 | tf_op jit(solution)/shard_map/pallas_call | solution.py:512
  30.1 0.0 collective-permute-done.9.attn_ref
  30.1 0.7 %shard_map.145 = (f32[2,2,1024]{2,1,0:T(2,128)S(1)}, f32[2,2,1024]{2,1,0:T(2,128)S(1)}) custom-call(f32[8,1024]{1,0:T(8,128)S(1)} %shard_map.144.acc_ref, bf16[8,2048]{1,0:T(8,128)(2,1)S(1)} %collective-permute-done.9.attn_ref, bf16[4096,1024]{1,0:T(8,128)(2,1)S(1)} %shard_map.143.weight_ref), custom_call_target="tpu_custom_call" | custom-call | bytes 2520000 | tf_op jit(solution)/shard_map/pallas_call | solution.py:516
  30.8 1.5 %collective-permute-start.10 = (f32[2,2,1024]{2,1,0:T(2,128)S(1)}, f32[2,2,1024]{2,1,0:T(2,128)S(1)}, u32[]{:S(2)}, u32[]{:S(2)}) collective-permute-start(f32[2,2,1024]{2,1,0:T(2,128)S(1)} %get-tuple-element.42), channel_id=1, source_target_pairs={{0,2},{2,0},{1,3},{3,1},{4,6},{6,4},{5,7},{7,5},{8,10},{10,8},{9,1... | collective-permute-start | bytes 49160 | tf_op jit(solution)/shard_map/ppermute | solution.py:21
  32.3 1.5 %shard_map.140 = (f32[4,2,16,1024]{3,2,1,0:T(8,128)S(1)}, f32[4,2,1,1024]{3,2,1,0:T(1,128)S(1)}) custom-call(f32[2,1,8192]{2,1,0:T(1,128)} %dt_hbm.1, bf16[2,8192]{1,0:T(2,128)(2,1)} %bitcast.3, f32[2,1,2,16]{3,2,1,0:T(2,128)} %bc_hbm.1, f32[1,8192]{1,0:T(1,128)} %bitcast.4, f32[16,8192]{1,0:T(8,128)} %log_hbm.1), custom_call_target="tpu_custom_call" | custom-call | bytes 7200000 | tf_op jit(solution)/shard_map/pallas_call | solution.py:473
  33.8 0.7 %collective-permute-done.10.refs_1_ = f32[2,2,1024]{2,1,0:T(2,128)S(1)} collective-permute-done((f32[2,2,1024]{2,1,0:T(2,128)S(1)}, f32[2,2,1024]{2,1,0:T(2,128)S(1)}, u32[]{:S(2)}, u32[]{:S(2)}) %collective-permute-start.10) | collective-permute-done | bytes 16416 | tf_op jit(solution)/shard_map/ppermute | solution.py:21
  34.6 0.6 %shard_map.146 = bf16[2,2,1024]{2,1,0:T(2,128)(2,1)} custom-call(f32[2,2,1024]{2,1,0:T(2,128)S(1)} %get-tuple-element.41.refs_0_, f32[2,2,1024]{2,1,0:T(2,128)S(1)} %collective-permute-done.10.refs_1_), custom_call_target="tpu_custom_call" | custom-call | bytes 2160000 | tf_op jit(solution)/shard_map/pallas_call | solution.py:524
  35.2 0.0 collective-permute-done.7.rest_1_
  35.2 0.0 collective-permute-done.8.rest_2_
  35.2 1.7 %shard_map.147 = (bf16[2,1,128,256]{3,2,1,0:T(8,128)(2,1)S(1)}, bf16[2,1,128,256]{3,2,1,0:T(8,128)(2,1)S(1)}, f32[2,4,1,1024]{3,2,1,0:T(1,128)S(1)}) custom-call(s32[4,2,8]{2,1,0:T(2,128)} %bitcast.6, s32[4,8]{1,0:T(4,128)} %counts_ref.3, bf16[4,2,128,256]{3,2,1,0:T(8,128)(2,1)} %kv_ref.3, bf16[64,256]{1,0:T(8,128)(2,1)S(1)} %get-tuple-element.27.state_ref, ...), custom_call_target="tpu_custom_call" | custom-call | bytes 3600000 | tf_op jit(solution)/shard_map/pallas_call | solution.py:530
  36.9 0.1 collective-permute-start.11
  36.9 0.5 %collective-permute-start.12 = (f32[2,4,1,1024]{3,2,1,0:T(1,128)S(1)}, f32[2,4,1,1024]{3,2,1,0:T(1,128)S(1)}, u32[]{:S(2)}, u32[]{:S(2)}) collective-permute-start(f32[2,4,1,1024]{3,2,1,0:T(1,128)S(1)} %get-tuple-element.48.mamba_ref), channel_id=1, source_target_pairs={{0,1},{1,0},{2,3},{3,2},{4,5},{5,4},{6,7},{7,6},{8,9},{9,8},{10,11... | collective-permute-start | bytes 98312 | tf_op jit(solution)/shard_map/ppermute | solution.py:21
  37.4 0.9 %collective-permute-done.12.rest_0_ = f32[2,4,1,1024]{3,2,1,0:T(1,128)S(1)} collective-permute-done((f32[2,4,1,1024]{3,2,1,0:T(1,128)S(1)}, f32[2,4,1,1024]{3,2,1,0:T(1,128)S(1)}, u32[]{:S(2)}, u32[]{:S(2)}) %collective-permute-start.12) | collective-permute-done | bytes 32800 | tf_op jit(solution)/shard_map/ppermute | solution.py:21
  38.3 0.0 collective-permute-done.11.got_ref
  38.3 0.9 %shard_map.148 = (bf16[1,4,1,128,256]{4,3,2,1,0:T(8,128)(2,1)}, f32[2,1,8192]{2,1,0:T(1,128)}) custom-call(bf16[2,1,128,256]{3,2,1,0:T(8,128)(2,1)S(1)} %get-tuple-element.46.kept_ref, bf16[2,1,128,256]{3,2,1,0:T(8,128)(2,1)S(1)} %collective-permute-done.11.got_ref, f32[2,4,1,1024]{3,2,1,0:T(1,128)S(1)} %get-tuple-element.48.mamba_ref, ...), custom_call_target="tpu_custom_call" | custom-call | bytes 3600000 | tf_op jit(solution)/shard_map/pallas_call | solution.py:546
  (4 shorter events, 0.0 us)
Async XLA Ops:
  0.6 7.2 %collective-permute-start = (bf16[2,1,32,128]{3,2,1,0:T(8,128)(2,1)}, bf16[2,1,32,128]{3,2,1,0:T(8,128)(2,1)S(1)}, u32[]{:S(2)}, u32[]{:S(2)}) collective-permute-start(bf16[2,1,32,128]{3,2,1,0:T(8,128)(2,1)} %q_ref.1), channel_id=1, source_target_pairs={{0,4},{4,0},{8,12},{12,8},{1,5},{5,1},{9,13},{13,9},{2,6},{6,2},{1... | collective-permute-start | bytes 49160 | tf_op jit(solution)/shard_map/ppermute | solution.py:21
  3.7 4.9 %collective-permute-start.1 = (bf16[2,1,32,128]{3,2,1,0:T(8,128)(2,1)}, bf16[2,1,32,128]{3,2,1,0:T(8,128)(2,1)S(1)}, u32[]{:S(2)}, u32[]{:S(2)}) collective-permute-start(bf16[2,1,32,128]{3,2,1,0:T(8,128)(2,1)} %q_ref.1), channel_id=1, source_target_pairs={{0,8},{4,12},{8,0},{12,4},{1,9},{5,13},{9,1},{13,5},{2,10},{6,14},... | collective-permute-start | bytes 49160 | tf_op jit(solution)/shard_map/ppermute | solution.py:21
  6.3 5.7 %collective-permute-start.2 = (bf16[2,1,32,128]{3,2,1,0:T(8,128)(2,1)}, bf16[2,1,32,128]{3,2,1,0:T(8,128)(2,1)S(1)}, u32[]{:S(2)}, u32[]{:S(2)}) collective-permute-start(bf16[2,1,32,128]{3,2,1,0:T(8,128)(2,1)} %q_ref.1), channel_id=1, source_target_pairs={{0,12},{4,8},{8,4},{12,0},{1,13},{5,9},{9,5},{13,1},{2,14},{6,10},... | collective-permute-start | bytes 49160 | tf_op jit(solution)/shard_map/ppermute | solution.py:21
  12.7 6.0 %collective-permute-start.3 = (bf16[1,144,128]{2,1,0:T(8,128)(2,1)S(1)}, bf16[1,144,128]{2,1,0:T(8,128)(2,1)S(1)}, u32[]{:S(2)}, u32[]{:S(2)}) collective-permute-start(bf16[1,144,128]{2,1,0:T(8,128)(2,1)S(1)} %shard_map.141.rest_0_), channel_id=1, source_target_pairs={{0,4},{4,0},{8,12},{12,8},{1,5},{5,1},{9,13},{13,9},{2,6},{6,2},{1... | collective-permute-start | bytes 110600 | tf_op jit(solution)/shard_map/ppermute | solution.py:21
  12.8 10.7 %collective-permute-start.4 = (bf16[1,144,128]{2,1,0:T(8,128)(2,1)S(1)}, bf16[1,144,128]{2,1,0:T(8,128)(2,1)S(1)}, u32[]{:S(2)}, u32[]{:S(2)}) collective-permute-start(bf16[1,144,128]{2,1,0:T(8,128)(2,1)S(1)} %shard_map.141.rest_0_), channel_id=1, source_target_pairs={{0,8},{4,12},{8,0},{12,4},{1,9},{5,13},{9,1},{13,5},{2,10},{6,14},... | collective-permute-start | bytes 110600 | tf_op jit(solution)/shard_map/ppermute | solution.py:21
  13.5 10.0 %collective-permute-start.5 = (bf16[1,144,128]{2,1,0:T(8,128)(2,1)S(1)}, bf16[1,144,128]{2,1,0:T(8,128)(2,1)S(1)}, u32[]{:S(2)}, u32[]{:S(2)}) collective-permute-start(bf16[1,144,128]{2,1,0:T(8,128)(2,1)S(1)} %shard_map.141.rest_0_), channel_id=1, source_target_pairs={{0,12},{4,8},{8,4},{12,0},{1,13},{5,9},{9,5},{13,1},{2,14},{6,10},... | collective-permute-start | bytes 110600 | tf_op jit(solution)/shard_map/ppermute | solution.py:21
  17.1 18.0 %collective-permute-start.7 = (bf16[320,256]{1,0:T(8,128)(2,1)S(1)}, bf16[320,256]{1,0:T(8,128)(2,1)S(1)}, u32[]{:S(2)}, u32[]{:S(2)}) collective-permute-start(bf16[320,256]{1,0:T(8,128)(2,1)S(1)} %get-tuple-element.38), channel_id=1, source_target_pairs={{0,8},{4,12},{8,0},{12,4},{1,9},{5,13},{9,1},{13,5},{2,10},{6,14},... | collective-permute-start | bytes 491528 | tf_op jit(solution)/shard_map/ppermute | solution.py:21
  17.1 18.0 %collective-permute-start.8 = (bf16[320,256]{1,0:T(8,128)(2,1)S(1)}, bf16[320,256]{1,0:T(8,128)(2,1)S(1)}, u32[]{:S(2)}, u32[]{:S(2)}) collective-permute-start(bf16[320,256]{1,0:T(8,128)(2,1)S(1)} %get-tuple-element.39), channel_id=1, source_target_pairs={{0,12},{4,8},{8,4},{12,0},{1,13},{5,9},{9,5},{13,1},{2,14},{6,10},... | collective-permute-start | bytes 491528 | tf_op jit(solution)/shard_map/ppermute | solution.py:21
  23.7 11.4 %collective-permute-start.6 = (bf16[320,256]{1,0:T(8,128)(2,1)S(1)}, bf16[320,256]{1,0:T(8,128)(2,1)S(1)}, u32[]{:S(2)}, u32[]{:S(2)}) collective-permute-start(bf16[320,256]{1,0:T(8,128)(2,1)S(1)} %get-tuple-element.35), channel_id=1, source_target_pairs={{0,4},{4,0},{8,12},{12,8},{1,5},{5,1},{9,13},{13,9},{2,6},{6,2},{1... | collective-permute-start | bytes 491528 | tf_op jit(solution)/shard_map/ppermute | solution.py:21
  25.9 4.1 %collective-permute-start.9 = (bf16[8,2048]{1,0:T(8,128)(2,1)S(1)}, bf16[8,2048]{1,0:T(8,128)(2,1)S(1)}, u32[]{:S(2)}, u32[]{:S(2)}) collective-permute-start(bf16[8,2048]{1,0:T(8,128)(2,1)S(1)} %shard_map.142.attn_ref), channel_id=1, source_target_pairs={{0,1},{1,0},{2,3},{3,2},{4,5},{5,4},{6,7},{7,6},{8,9},{9,8},{10,11... | collective-permute-start | bytes 98312 | tf_op jit(solution)/shard_map/ppermute | solution.py:21
  30.8 3.8 %collective-permute-start.10 = (f32[2,2,1024]{2,1,0:T(2,128)S(1)}, f32[2,2,1024]{2,1,0:T(2,128)S(1)}, u32[]{:S(2)}, u32[]{:S(2)}) collective-permute-start(f32[2,2,1024]{2,1,0:T(2,128)S(1)} %get-tuple-element.42), channel_id=1, source_target_pairs={{0,2},{2,0},{1,3},{3,1},{4,6},{6,4},{5,7},{7,5},{8,10},{10,8},{9,1... | collective-permute-start | bytes 49160 | tf_op jit(solution)/shard_map/ppermute | solution.py:21
  36.9 1.5 %collective-permute-start.11 = (bf16[2,1,128,256]{3,2,1,0:T(8,128)(2,1)S(1)}, bf16[2,1,128,256]{3,2,1,0:T(8,128)(2,1)S(1)}, u32[]{:S(2)}, u32[]{:S(2)}) collective-permute-start(bf16[2,1,128,256]{3,2,1,0:T(8,128)(2,1)S(1)} %get-tuple-element.47), channel_id=1, source_target_pairs={{0,1},{1,0},{2,3},{3,2},{4,5},{5,4},{6,7},{7,6},{8,9},{9,8},{10,11... | collective-permute-start | bytes 393224 | tf_op jit(solution)/shard_map/ppermute | solution.py:21
  36.9 1.4 %collective-permute-start.12 = (f32[2,4,1,1024]{3,2,1,0:T(1,128)S(1)}, f32[2,4,1,1024]{3,2,1,0:T(1,128)S(1)}, u32[]{:S(2)}, u32[]{:S(2)}) collective-permute-start(f32[2,4,1,1024]{3,2,1,0:T(1,128)S(1)} %get-tuple-element.48.mamba_ref), channel_id=1, source_target_pairs={{0,1},{1,0},{2,3},{3,2},{4,5},{5,4},{6,7},{7,6},{8,9},{9,8},{10,11... | collective-permute-start | bytes 98312 | tf_op jit(solution)/shard_map/ppermute | solution.py:21

commit v3 on v2

--- a/solution.py
+++ b/solution.py
@@ -8,6 +8,7 @@
 from jax.sharding import PartitionSpec as P
 
 BLOCK = 128
+PIECES = 4
 NEG = -1e30
 BF = jnp.bfloat16
 F32 = jnp.float32
@@ -29,7 +30,7 @@
         out_specs=out_specs,
         scratch_shapes=list(scratch),
         cost_estimate=pl.CostEstimate(
-            flops=0, bytes_accessed=int(us * 3.6e6), transcendentals=0
+            flops=0, bytes_accessed=int(us * 3.6e4), transcendentals=0
         ),
         compiler_params=pltpu.CompilerParams(vmem_limit_bytes=32 * 1024 * 1024),
     )
@@ -68,10 +69,10 @@
         out_ref[first + i * 16 : first + (i + 1) * 16, :] = cut.astype(BF)
 
 
-def stage(count, split, kv_ref, state_ref, q_ref, new_ref, blocks_ref, counts_ref, *rest):
+def stage(count, split, kv_ref, state_ref, q_ref, new_ref, blocks_ref, counts_ref, weight_ref, *rest):
     sends = rest[: count - 1]
-    own_state, kv_out, q_out, new_out, bias_out = rest[count - 1 : count + 4]
-    loaded, blocks, counts, sems, early = rest[count + 4 :]
+    own_state, kv_out, q_out, new_out, bias_out, weight_out = rest[count - 1 : count + 5]
+    loaded, blocks, counts, sems, early = rest[count + 5 :]
     me, rep = lax.axis_index("seq"), lax.axis_index("rep")
     heads = kv_ref.shape[1]
     part = loaded.shape[2]
@@ -90,6 +91,7 @@
             rows = pl.ds(j * BLOCK, BLOCK)
             moves.append(copy(kv_ref.at[me ^ c, j], sends[c - 1].at[rows]))
     moves += [copy(kv_ref, kv_out), copy(q_ref, q_out), copy(new_ref, new_out)]
+    moves += weight_half(weight_ref, weight_out, rep, copy)
     for move in first + moves:
         move.start()
     for move in first:
@@ -117,7 +119,7 @@
 
 
 def attend(count, kv_ref, new_ref, bias_ref, *rest):
-    q_refs, out_ref = rest[:count], rest[count]
+    q_refs, out_ref = rest[:1] + rest[1:count][::-1], rest[count]
     me, rep = lax.axis_index("seq"), lax.axis_index("rep")
     heads = kv_ref.shape[1]
     hd = kv_ref.shape[3] // 2
@@ -199,7 +201,8 @@
 
 
 def merge(count, heads, steps, group, *rest):
-    parts, out_ref, scratch = rest[:count], rest[count], rest[count + 1]
+    parts = rest[:1] + rest[1:count][::-1]
+    out_ref, scratch = rest[count:]
     me = lax.axis_index("seq")
     rows = steps * group
     chunks = parts[0].shape[0]
@@ -237,18 +240,19 @@
             out_ref[:, at : at + 128] = tile.astype(BF)
 
 
+def weight_half(weight_ref, out_ref, which, copy):
+    half = out_ref.shape[0]
+    rows = half // PIECES
+    cuts = [(pl.ds(which * half + i * rows, rows), pl.ds(i * rows, rows)) for i in range(PIECES)]
+    return [copy(weight_ref.at[src], out_ref.at[dst]) for src, dst in cuts]
+
+
 def load_weight(weight_ref, out_ref, sems):
-    pieces = sems.shape[0]
-    rows = weight_ref.shape[0] // pieces
-    copy = copier(sems)
-    cuts = [pl.ds(i * rows, rows) for i in range(pieces)]
-    run_all([copy(weight_ref.at[cut], out_ref.at[cut]) for cut in cuts])
+    run_all(weight_half(weight_ref, out_ref, 1 - lax.axis_index("rep"), copier(sems)))
 
 
 def project_own(attn_ref, weight_ref, out_ref):
-    half = attn_ref.shape[1]
-    first = pl.multiple_of(lax.axis_index("rep") * half, half)
-    out_ref[...] = dot_f32(attn_ref[...], weight_ref[pl.ds(first, half), :], ((1,), (0,)))
+    out_ref[...] = dot_f32(attn_ref[...], weight_ref[...], ((1,), (0,)))
 
 
 def pick(options, index):
@@ -259,11 +263,7 @@
 
 
 def project_other(heads_count, count, acc_ref, attn_ref, weight_ref, *outs):
-    half = attn_ref.shape[1]
-    first = pl.multiple_of((1 - lax.axis_index("rep")) * half, half)
-    total = acc_ref[...] + dot_f32(
-        attn_ref[...], weight_ref[pl.ds(first, half), :], ((1,), (0,))
-    )
+    total = acc_ref[...] + dot_f32(attn_ref[...], weight_ref[...], ((1,), (0,)))
     head = lax.axis_index("head")
     steps = total.shape[0] // count
     share = count // heads_count
@@ -436,13 +436,16 @@
     smem = pltpu.SMEM
     blocks = jnp.swapaxes(kept_blocks, 1, 2)
 
-    asked = [shift(queries, "seq", c) for c in range(1, count)]
+    asked = [shift(queries, "seq", c) for c in range(count - 1, 0, -1)][::-1]
     prefill_kv, prefill_state, queries, new_kv = map(in_hbm, (prefill_kv, prefill_state, queries, new_kv))
     step_dt, step_bc, a_log, out_weight = map(in_hbm, (step_dt, step_bc, a_log, out_weight))
     step_input = in_hbm(step_input.reshape(steps, channels))
     skip_gain = in_hbm(skip_gain.reshape(1, -1))
     blocks, kept_counts = in_hbm(blocks), in_hbm(kept_counts)
 
+    columns = out_weight.shape[1]
+    half = heads * group * hd
+    half_weight = pltpu.VMEM((half, columns), BF)
     packed = heads * BLOCK + state_rows(part)
     staged = call(
         functools.partial(stage, count, split),
@@ -453,22 +456,22 @@
             shape(queries.shape, BF),
             shape(new_kv.shape, BF),
             shape((all_rows, 128), F32),
+            half_weight,
         ],
-        [HB] * 6,
-        [VM] * (count + 4),
+        [HB] * 7,
+        [VM] * (count + 5),
         [
             pltpu.VMEM((count, ns, part), F32),
             smem(blocks.shape, jnp.int32),
             smem(kept_counts.shape, jnp.int32),
-            DMA(((count - 1) * heads + 3,)),
+            DMA(((count - 1) * heads + 3 + PIECES,)),
             DMA((count + 2,)),
         ],
         us=1.5,
-    )(prefill_kv, prefill_state, queries, new_kv, blocks, kept_counts)
+    )(prefill_kv, prefill_state, queries, new_kv, blocks, kept_counts, out_weight)
     sends = staged[: count - 1]
-    own_state, kv_near, q_near, new_near, bias = staged[count - 1 :]
-    far = after(sends[1:], *asked)
-    received = [shift(far[c - 2], "seq", c) for c in range(2, count)]
+    own_state, kv_near, q_near, new_near, bias, own_weight = staged[count - 1 :]
+    early = shift(after(sends[-1:], *asked)[0], "seq", count - 1)
 
     slope, base = call(
         functools.partial(coefficients, count, split),
@@ -492,12 +495,15 @@
         [VM] * (3 + count),
         VM,
         us=1.5,
-    )(kv_near, new_near, bias, q_near, *asked)
-    weight = call(load_weight, pltpu.VMEM(out_weight.shape, BF), [HB], VM, [DMA((8,))], us=3.4)(
+    )(kv_near, new_near, bias, q_near, *asked[::-1])
+    other_weight = call(load_weight, half_weight, [HB], VM, [DMA((PIECES,))], us=1.7)(
         *after([out_weight], partial_sums)
     )
-    gathered = [partial_sums] + [shift(partial_sums, "seq", c) for c in range(1, count)]
-    half = heads * group * hd
+    middle = after(sends[1:-1], partial_sums)
+    middle = [shift(middle[c - 2], "seq", c) for c in range(count - 2, 1, -1)][::-1]
+    gathered = [partial_sums] + [shift(partial_sums, "seq", c) for c in range(count - 1, 0, -1)][::-1]
+    *gathered, early, other_weight = after([*gathered[::-1], early, other_weight])
+    gathered = gathered[::-1]
     attn = call(
         functools.partial(merge, count, heads, steps, group),
         shape((steps * count, half), BF),
@@ -505,13 +511,12 @@
         VM,
         [pltpu.VMEM((heads, steps * count * group, hd), F32)],
         us=0.3,
-    )(*gathered)
+    )(*gathered[:1], *gathered[:0:-1])
     attn_other = shift(attn, "rep", 1)
-    received = [shift(after(sends[:1], attn)[0], "seq", 1)] + received
-    columns = out_weight.shape[1]
+    received = [shift(after(sends[:1], attn)[0], "seq", 1), *middle, early]
     own_sum = call(
         project_own, shape((steps * count, columns), F32), [VM, VM], VM, us=0.7
-    )(attn, weight)
+    )(attn, own_weight)
     share = count // heads_count
     sums = call(
         functools.partial(project_other, heads_count, count),
@@ -519,7 +524,7 @@
         [VM, VM, VM],
         [VM] * heads_count,
         us=0.7,
-    )(own_sum, attn_other, weight)
+    )(own_sum, attn_other, other_weight)
     sums = [sums[0]] + [shift(sums[c], "head", c) for c in range(1, heads_count)]
     proj_out = call(
         add_up, shape((steps, share, columns), BF), [VM] * heads_count, VM, us=0.6

time: 39.5 us -> 37.9 us (0.959)
  waiting for transfers between devices: 10.7 us -> 7.75 us
  starting transfers between devices: 16 us -> 17.3 us
    ppermute x13, waiting for transfers between devices: 10.7 us -> 7.75 us  [shift(): return lax.ppermute(x, axis, [(i, i ^ c) for i in range(size)])]
    ppermute x13, starting transfers between devices: 16 us -> 17.3 us  [shift(): return lax.ppermute(x, axis, [(i, i ^ c) for i in range(size)])]
    pallas_call x1, Pallas kernels: 1.48 us -> 2.81 us  [per_device(): call(functools.partial(stage, count, split), [shape((packed, width), BF)]...]
    pallas_call x1, Pallas kernels: 3.47 us -> 2.2 us  [per_device(): call(load_weight, half_weight, [HB], VM, [DMA((PIECES,))], us=1.7)]
  transfers between devices with their start and end apart: 13 -> 13, of which waited for: 5 -> 5; matrix products, arithmetic and copies ran while one was open for 0% -> 0% of each run, Pallas kernels for 22% -> 25%
where the time goes in v3:
time: 37.9 us; the launch traced here: 37.7 us
  starting transfers between devices  17.3 us (46%)
  Pallas kernels  11.9 us (31%)
  waiting for transfers between devices  7.75 us (20%)
  between operations  0.72 us (2%)
    ppermute x13, starting transfers between devices, shift(): return lax.ppermute(x, axis, [(i, i ^ c) for i in range(size)])  17.3 us
    ppermute x13, waiting for transfers between devices, shift(): return lax.ppermute(x, axis, [(i, i ^ c) for i in range(size)])  7.75 us
    pallas_call x1, Pallas kernels, per_device(): call(functools.partial(stage, count, split), [shape((packed, width), BF)]...  2.81 us
    pallas_call x1, Pallas kernels, per_device(): call(load_weight, half_weight, [HB], VM, [DMA((PIECES,))], us=1.7)  2.2 us
    pallas_call x1, Pallas kernels, per_device(): call(functools.partial(select, count), [shape(half_shape, BF), shape(half...  1.67 us
    pallas_call x1, Pallas kernels, per_device(): call(functools.partial(coefficients, count, split), [shape((count, steps,...  1.51 us
    pallas_call x1, Pallas kernels, per_device(): call(functools.partial(assemble, split), [shape((1, dec_heads, keep_rep,...  0.89 us
  transfers between devices with their start and end apart: 13, of which 5 were waited for; matrix products, arithmetic and copies ran while one was open for 0% of the time, Pallas kernels for 25%

profile of v3, /device:TPU:0, one launch (start us, length us, event | category | flops | bytes accessed | tf_op | source)
XLA Modules:
  0.0 37.7 jit_solution(14036745596384791411)
XLA Ops:
  0.6 5.1 %collective-permute-start = (bf16[2,1,32,128]{3,2,1,0:T(8,128)(2,1)}, bf16[2,1,32,128]{3,2,1,0:T(8,128)(2,1)S(1)}, u32[]{:S(2)}, u32[]{:S(2)}) collective-permute-start(bf16[2,1,32,128]{3,2,1,0:T(8,128)(2,1)} %q_ref.1), channel_id=1, source_target_pairs={{0,12},{4,8},{8,4},{12,0},{1,13},{5,9},{9,5},{13,1},{2,14},{6,10},... | collective-permute-start | bytes 49160 | tf_op jit(solution)/shard_map/ppermute | solution.py:22
  5.7 0.0 collective-permute-start.1
  5.7 0.6 %collective-permute-start.2 = (bf16[2,1,32,128]{3,2,1,0:T(8,128)(2,1)}, bf16[2,1,32,128]{3,2,1,0:T(8,128)(2,1)S(1)}, u32[]{:S(2)}, u32[]{:S(2)}) collective-permute-start(bf16[2,1,32,128]{3,2,1,0:T(8,128)(2,1)} %q_ref.1), channel_id=1, source_target_pairs={{0,4},{4,0},{8,12},{12,8},{1,5},{5,1},{9,13},{13,9},{2,6},{6,2},{1... | collective-permute-start | bytes 49160 | tf_op jit(solution)/shard_map/ppermute | solution.py:22
  6.4 2.8 %shard_map.139 = (bf16[320,256]{1,0:T(8,128)(2,1)S(1)}, bf16[320,256]{1,0:T(8,128)(2,1)S(1)}, bf16[320,256]{1,0:T(8,128)(2,1)S(1)}, bf16[64,256]{1,0:T(8,128)(2,...) custom-call(bf16[4,2,128,256]{3,2,1,0:T(8,128)(2,1)} %kv_ref.3, ...), custom_call_target="tpu_custom_call" | custom-call | bytes 54000 | tf_op jit(solution)/shard_map/pallas_call | solution.py:450
  9.2 0.0 collective-permute-done.rest_1_
  9.2 1.4 %collective-permute-done.1.rest_2_ = bf16[2,1,32,128]{3,2,1,0:T(8,128)(2,1)S(1)} collective-permute-done((bf16[2,1,32,128]{3,2,1,0:T(8,128)(2,1)}, bf16[2,1,32,128]{3,2,1,0:T(8,128)(2,1)S(1)}, u32[]{:S(2)}, u32[]{:S(2)}) %collective-permute-start.1) | collective-permute-done | bytes 16416 | tf_op jit(solution)/shard_map/ppermute | solution.py:22
  10.6 2.4 %collective-permute-start.6 = (bf16[320,256]{1,0:T(8,128)(2,1)S(1)}, bf16[320,256]{1,0:T(8,128)(2,1)S(1)}, u32[]{:S(2)}, u32[]{:S(2)}) collective-permute-start(bf16[320,256]{1,0:T(8,128)(2,1)S(1)} %get-tuple-element.43), channel_id=1, source_target_pairs={{0,12},{4,8},{8,4},{12,0},{1,13},{5,9},{9,5},{13,1},{2,14},{6,10},... | collective-permute-start | bytes 491528 | tf_op jit(solution)/shard_map/ppermute | solution.py:22
  13.0 0.6 %shard_map.141.rest_0_ = bf16[1,144,128]{2,1,0:T(8,128)(2,1)S(1)} custom-call(bf16[4,2,128,256]{3,2,1,0:T(8,128)(2,1)S(1)} %get-tuple-element.38.kv_ref, bf16[2,1,4,256]{3,2,1,0:T(4,128)(2,1)S(1)} %get-tuple-element.39.new_ref, f32[128,128]{1,0:T(8,128)S(1)} %get-tuple-element.40.bias_ref, bf16[2,1,32,128]{3,2,1,0:T(8,128)(2,1)S(1)} %get-tuple-element.41.rest_0_, ...), custom_call_target="tpu_custom_call" | custom-call | bytes 54000 | tf_op jit(solution)/shard_map/pallas_call | solution.py:492
  13.7 1.4 %collective-permute-start.3 = (bf16[1,144,128]{2,1,0:T(8,128)(2,1)S(1)}, bf16[1,144,128]{2,1,0:T(8,128)(2,1)S(1)}, u32[]{:S(2)}, u32[]{:S(2)}) collective-permute-start(bf16[1,144,128]{2,1,0:T(8,128)(2,1)S(1)} %shard_map.141.rest_0_), channel_id=1, source_target_pairs={{0,12},{4,8},{8,4},{12,0},{1,13},{5,9},{9,5},{13,1},{2,14},{6,10},... | collective-permute-start | bytes 110600 | tf_op jit(solution)/shard_map/ppermute | solution.py:22
  15.1 0.2 collective-permute-start.4
  15.3 2.8 %collective-permute-start.5 = (bf16[1,144,128]{2,1,0:T(8,128)(2,1)S(1)}, bf16[1,144,128]{2,1,0:T(8,128)(2,1)S(1)}, u32[]{:S(2)}, u32[]{:S(2)}) collective-permute-start(bf16[1,144,128]{2,1,0:T(8,128)(2,1)S(1)} %shard_map.141.rest_0_), channel_id=1, source_target_pairs={{0,4},{4,0},{8,12},{12,8},{1,5},{5,1},{9,13},{13,9},{2,6},{6,2},{1... | collective-permute-start | bytes 110600 | tf_op jit(solution)/shard_map/ppermute | solution.py:22
  18.1 2.2 %shard_map.142.weight_ref = bf16[2048,1024]{1,0:T(8,128)(2,1)S(1)} custom-call(bf16[4096,1024]{1,0:T(8,128)(2,1)} %weight_ref.2), custom_call_target="tpu_custom_call" | custom-call | bytes 61200 | tf_op jit(solution)/shard_map/pallas_call | solution.py:499
  20.3 0.1 collective-permute-start.8
  20.4 0.0 collective-permute-done.3.rest_1_
  20.4 4.2 %collective-permute-done.4.rest_2_ = bf16[1,144,128]{2,1,0:T(8,128)(2,1)S(1)} collective-permute-done((bf16[1,144,128]{2,1,0:T(8,128)(2,1)S(1)}, bf16[1,144,128]{2,1,0:T(8,128)(2,1)S(1)}, u32[]{:S(2)}, u32[]{:S(2)}) %collective-permute-start.4) | collective-permute-done | bytes 36896 | tf_op jit(solution)/shard_map/ppermute | solution.py:22
  24.6 0.3 shard_map.143.attn_ref
  24.9 2.5 %collective-permute-start.7 = (bf16[320,256]{1,0:T(8,128)(2,1)S(1)}, bf16[320,256]{1,0:T(8,128)(2,1)S(1)}, u32[]{:S(2)}, u32[]{:S(2)}) collective-permute-start(bf16[320,256]{1,0:T(8,128)(2,1)S(1)} %get-tuple-element.49), channel_id=1, source_target_pairs={{0,4},{4,0},{8,12},{12,8},{1,5},{5,1},{9,13},{13,9},{2,6},{6,2},{1... | collective-permute-start | bytes 491528 | tf_op jit(solution)/shard_map/ppermute | solution.py:22
  27.3 0.0 collective-permute-start.9
  27.3 0.6 %shard_map.144.acc_ref = f32[8,1024]{1,0:T(8,128)S(1)} custom-call(bf16[8,2048]{1,0:T(8,128)(2,1)S(1)} %shard_map.143.attn_ref, bf16[2048,1024]{1,0:T(8,128)(2,1)S(1)} %get-tuple-element.53.weight_ref), custom_call_target="tpu_custom_call" | custom-call | bytes 25200 | tf_op jit(solution)/shard_map/pallas_call | solution.py:517
  28.0 0.6 %collective-permute-done.9.attn_ref = bf16[8,2048]{1,0:T(8,128)(2,1)S(1)} collective-permute-done((bf16[8,2048]{1,0:T(8,128)(2,1)S(1)}, bf16[8,2048]{1,0:T(8,128)(2,1)S(1)}, u32[]{:S(2)}, u32[]{:S(2)}) %collective-permute-start.9) | collective-permute-done | bytes 32800 | tf_op jit(solution)/shard_map/ppermute | solution.py:22
  28.5 0.7 %shard_map.145 = (f32[2,2,1024]{2,1,0:T(2,128)S(1)}, f32[2,2,1024]{2,1,0:T(2,128)S(1)}) custom-call(f32[8,1024]{1,0:T(8,128)S(1)} %shard_map.144.acc_ref, bf16[8,2048]{1,0:T(8,128)(2,1)S(1)} %collective-permute-done.9.attn_ref, bf16[2048,1024]{1,0:T(8,128)(2,1)S(1)} %shard_map.142.weight_ref), custom_call_target="tpu_custom_call" | custom-call | bytes 25200 | tf_op jit(solution)/shard_map/pallas_call | solution.py:521
  29.2 1.5 %collective-permute-start.10 = (f32[2,2,1024]{2,1,0:T(2,128)S(1)}, f32[2,2,1024]{2,1,0:T(2,128)S(1)}, u32[]{:S(2)}, u32[]{:S(2)}) collective-permute-start(f32[2,2,1024]{2,1,0:T(2,128)S(1)} %get-tuple-element.56), channel_id=1, source_target_pairs={{0,2},{2,0},{1,3},{3,1},{4,6},{6,4},{5,7},{7,5},{8,10},{10,8},{9,1... | collective-permute-start | bytes 49160 | tf_op jit(solution)/shard_map/ppermute | solution.py:22
  30.8 1.5 %shard_map.140 = (f32[4,2,16,1024]{3,2,1,0:T(8,128)S(1)}, f32[4,2,1,1024]{3,2,1,0:T(1,128)S(1)}) custom-call(f32[2,1,8192]{2,1,0:T(1,128)} %dt_hbm.1, bf16[2,8192]{1,0:T(2,128)(2,1)} %bitcast.3, f32[2,1,2,16]{3,2,1,0:T(2,128)} %bc_hbm.1, f32[1,8192]{1,0:T(1,128)} %bitcast.4, f32[16,8192]{1,0:T(8,128)} %log_hbm.1), custom_call_target="tpu_custom_call" | custom-call | bytes 72000 | tf_op jit(solution)/shard_map/pallas_call | solution.py:476
  32.3 0.7 %collective-permute-done.10.refs_1_ = f32[2,2,1024]{2,1,0:T(2,128)S(1)} collective-permute-done((f32[2,2,1024]{2,1,0:T(2,128)S(1)}, f32[2,2,1024]{2,1,0:T(2,128)S(1)}, u32[]{:S(2)}, u32[]{:S(2)}) %collective-permute-start.10) | collective-permute-done | bytes 16416 | tf_op jit(solution)/shard_map/ppermute | solution.py:22
  33.0 0.6 %shard_map.146 = bf16[2,2,1024]{2,1,0:T(2,128)(2,1)} custom-call(f32[2,2,1024]{2,1,0:T(2,128)S(1)} %get-tuple-element.55.refs_0_, f32[2,2,1024]{2,1,0:T(2,128)S(1)} %collective-permute-done.10.refs_1_), custom_call_target="tpu_custom_call" | custom-call | bytes 21600 | tf_op jit(solution)/shard_map/pallas_call | solution.py:529
  33.6 0.0 collective-permute-done.8.rest_1_
  33.6 0.0 collective-permute-done.7.rest_0_
  33.6 1.7 %shard_map.147 = (bf16[2,1,128,256]{3,2,1,0:T(8,128)(2,1)S(1)}, bf16[2,1,128,256]{3,2,1,0:T(8,128)(2,1)S(1)}, f32[2,4,1,1024]{3,2,1,0:T(1,128)S(1)}) custom-call(s32[4,2,8]{2,1,0:T(2,128)} %bitcast.6, s32[4,8]{1,0:T(4,128)} %counts_ref.3, bf16[4,2,128,256]{3,2,1,0:T(8,128)(2,1)} %kv_ref.3, bf16[64,256]{1,0:T(8,128)(2,1)S(1)} %get-tuple-element.34.state_ref, ...), custom_call_target="tpu_custom_call" | custom-call | bytes 36000 | tf_op jit(solution)/shard_map/pallas_call | solution.py:535
  35.3 0.1 collective-permute-start.11
  35.4 0.5 %collective-permute-start.12 = (f32[2,4,1,1024]{3,2,1,0:T(1,128)S(1)}, f32[2,4,1,1024]{3,2,1,0:T(1,128)S(1)}, u32[]{:S(2)}, u32[]{:S(2)}) collective-permute-start(f32[2,4,1,1024]{3,2,1,0:T(1,128)S(1)} %get-tuple-element.62.mamba_ref), channel_id=1, source_target_pairs={{0,1},{1,0},{2,3},{3,2},{4,5},{5,4},{6,7},{7,6},{8,9},{9,8},{10,11... | collective-permute-start | bytes 98312 | tf_op jit(solution)/shard_map/ppermute | solution.py:22
  35.9 0.9 %collective-permute-done.12.rest_0_ = f32[2,4,1,1024]{3,2,1,0:T(1,128)S(1)} collective-permute-done((f32[2,4,1,1024]{3,2,1,0:T(1,128)S(1)}, f32[2,4,1,1024]{3,2,1,0:T(1,128)S(1)}, u32[]{:S(2)}, u32[]{:S(2)}) %collective-permute-start.12) | collective-permute-done | bytes 32800 | tf_op jit(solution)/shard_map/ppermute | solution.py:22
  36.8 0.9 %shard_map.148 = (bf16[1,4,1,128,256]{4,3,2,1,0:T(8,128)(2,1)}, f32[2,1,8192]{2,1,0:T(1,128)}) custom-call(bf16[2,1,128,256]{3,2,1,0:T(8,128)(2,1)S(1)} %get-tuple-element.60.kept_ref, bf16[2,1,128,256]{3,2,1,0:T(8,128)(2,1)S(1)} %collective-permute-done.11.got_ref, f32[2,4,1,1024]{3,2,1,0:T(1,128)S(1)} %get-tuple-element.62.mamba_ref, ...), custom_call_target="tpu_custom_call" | custom-call | bytes 36000 | tf_op jit(solution)/shard_map/pallas_call | solution.py:551
  (4 shorter events, 0.0 us)
Async XLA Ops:
  0.6 8.6 %collective-permute-start = (bf16[2,1,32,128]{3,2,1,0:T(8,128)(2,1)}, bf16[2,1,32,128]{3,2,1,0:T(8,128)(2,1)S(1)}, u32[]{:S(2)}, u32[]{:S(2)}) collective-permute-start(bf16[2,1,32,128]{3,2,1,0:T(8,128)(2,1)} %q_ref.1), channel_id=1, source_target_pairs={{0,12},{4,8},{8,4},{12,0},{1,13},{5,9},{9,5},{13,1},{2,14},{6,10},... | collective-permute-start | bytes 49160 | tf_op jit(solution)/shard_map/ppermute | solution.py:22
  5.7 4.8 %collective-permute-start.1 = (bf16[2,1,32,128]{3,2,1,0:T(8,128)(2,1)}, bf16[2,1,32,128]{3,2,1,0:T(8,128)(2,1)S(1)}, u32[]{:S(2)}, u32[]{:S(2)}) collective-permute-start(bf16[2,1,32,128]{3,2,1,0:T(8,128)(2,1)} %q_ref.1), channel_id=1, source_target_pairs={{0,8},{4,12},{8,0},{12,4},{1,9},{5,13},{9,1},{13,5},{2,10},{6,14},... | collective-permute-start | bytes 49160 | tf_op jit(solution)/shard_map/ppermute | solution.py:22
  5.7 4.8 %collective-permute-start.2 = (bf16[2,1,32,128]{3,2,1,0:T(8,128)(2,1)}, bf16[2,1,32,128]{3,2,1,0:T(8,128)(2,1)S(1)}, u32[]{:S(2)}, u32[]{:S(2)}) collective-permute-start(bf16[2,1,32,128]{3,2,1,0:T(8,128)(2,1)} %q_ref.1), channel_id=1, source_target_pairs={{0,4},{4,0},{8,12},{12,8},{1,5},{5,1},{9,13},{13,9},{2,6},{6,2},{1... | collective-permute-start | bytes 49160 | tf_op jit(solution)/shard_map/ppermute | solution.py:22
  10.6 14.0 %collective-permute-start.6 = (bf16[320,256]{1,0:T(8,128)(2,1)S(1)}, bf16[320,256]{1,0:T(8,128)(2,1)S(1)}, u32[]{:S(2)}, u32[]{:S(2)}) collective-permute-start(bf16[320,256]{1,0:T(8,128)(2,1)S(1)} %get-tuple-element.43), channel_id=1, source_target_pairs={{0,12},{4,8},{8,4},{12,0},{1,13},{5,9},{9,5},{13,1},{2,14},{6,10},... | collective-permute-start | bytes 491528 | tf_op jit(solution)/shard_map/ppermute | solution.py:22
  13.7 6.7 %collective-permute-start.3 = (bf16[1,144,128]{2,1,0:T(8,128)(2,1)S(1)}, bf16[1,144,128]{2,1,0:T(8,128)(2,1)S(1)}, u32[]{:S(2)}, u32[]{:S(2)}) collective-permute-start(bf16[1,144,128]{2,1,0:T(8,128)(2,1)S(1)} %shard_map.141.rest_0_), channel_id=1, source_target_pairs={{0,12},{4,8},{8,4},{12,0},{1,13},{5,9},{9,5},{13,1},{2,14},{6,10},... | collective-permute-start | bytes 110600 | tf_op jit(solution)/shard_map/ppermute | solution.py:22
  15.1 9.5 %collective-permute-start.4 = (bf16[1,144,128]{2,1,0:T(8,128)(2,1)S(1)}, bf16[1,144,128]{2,1,0:T(8,128)(2,1)S(1)}, u32[]{:S(2)}, u32[]{:S(2)}) collective-permute-start(bf16[1,144,128]{2,1,0:T(8,128)(2,1)S(1)} %shard_map.141.rest_0_), channel_id=1, source_target_pairs={{0,8},{4,12},{8,0},{12,4},{1,9},{5,13},{9,1},{13,5},{2,10},{6,14},... | collective-permute-start | bytes 110600 | tf_op jit(solution)/shard_map/ppermute | solution.py:22
  15.3 9.3 %collective-permute-start.5 = (bf16[1,144,128]{2,1,0:T(8,128)(2,1)S(1)}, bf16[1,144,128]{2,1,0:T(8,128)(2,1)S(1)}, u32[]{:S(2)}, u32[]{:S(2)}) collective-permute-start(bf16[1,144,128]{2,1,0:T(8,128)(2,1)S(1)} %shard_map.141.rest_0_), channel_id=1, source_target_pairs={{0,4},{4,0},{8,12},{12,8},{1,5},{5,1},{9,13},{13,9},{2,6},{6,2},{1... | collective-permute-start | bytes 110600 | tf_op jit(solution)/shard_map/ppermute | solution.py:22
  20.3 13.3 %collective-permute-start.8 = (bf16[320,256]{1,0:T(8,128)(2,1)S(1)}, bf16[320,256]{1,0:T(8,128)(2,1)S(1)}, u32[]{:S(2)}, u32[]{:S(2)}) collective-permute-start(bf16[320,256]{1,0:T(8,128)(2,1)S(1)} %get-tuple-element.51), channel_id=1, source_target_pairs={{0,8},{4,12},{8,0},{12,4},{1,9},{5,13},{9,1},{13,5},{2,10},{6,14},... | collective-permute-start | bytes 491528 | tf_op jit(solution)/shard_map/ppermute | solution.py:22
  24.9 8.8 %collective-permute-start.7 = (bf16[320,256]{1,0:T(8,128)(2,1)S(1)}, bf16[320,256]{1,0:T(8,128)(2,1)S(1)}, u32[]{:S(2)}, u32[]{:S(2)}) collective-permute-start(bf16[320,256]{1,0:T(8,128)(2,1)S(1)} %get-tuple-element.49), channel_id=1, source_target_pairs={{0,4},{4,0},{8,12},{12,8},{1,5},{5,1},{9,13},{13,9},{2,6},{6,2},{1... | collective-permute-start | bytes 491528 | tf_op jit(solution)/shard_map/ppermute | solution.py:22
  27.3 1.2 %collective-permute-start.9 = (bf16[8,2048]{1,0:T(8,128)(2,1)S(1)}, bf16[8,2048]{1,0:T(8,128)(2,1)S(1)}, u32[]{:S(2)}, u32[]{:S(2)}) collective-permute-start(bf16[8,2048]{1,0:T(8,128)(2,1)S(1)} %shard_map.143.attn_ref), channel_id=1, source_target_pairs={{0,1},{1,0},{2,3},{3,2},{4,5},{5,4},{6,7},{7,6},{8,9},{9,8},{10,11... | collective-permute-start | bytes 98312 | tf_op jit(solution)/shard_map/ppermute | solution.py:22
  29.2 3.8 %collective-permute-start.10 = (f32[2,2,1024]{2,1,0:T(2,128)S(1)}, f32[2,2,1024]{2,1,0:T(2,128)S(1)}, u32[]{:S(2)}, u32[]{:S(2)}) collective-permute-start(f32[2,2,1024]{2,1,0:T(2,128)S(1)} %get-tuple-element.56), channel_id=1, source_target_pairs={{0,2},{2,0},{1,3},{3,1},{4,6},{6,4},{5,7},{7,5},{8,10},{10,8},{9,1... | collective-permute-start | bytes 49160 | tf_op jit(solution)/shard_map/ppermute | solution.py:22
  35.3 1.5 %collective-permute-start.11 = (bf16[2,1,128,256]{3,2,1,0:T(8,128)(2,1)S(1)}, bf16[2,1,128,256]{3,2,1,0:T(8,128)(2,1)S(1)}, u32[]{:S(2)}, u32[]{:S(2)}) collective-permute-start(bf16[2,1,128,256]{3,2,1,0:T(8,128)(2,1)S(1)} %get-tuple-element.61), channel_id=1, source_target_pairs={{0,1},{1,0},{2,3},{3,2},{4,5},{5,4},{6,7},{7,6},{8,9},{9,8},{10,11... | collective-permute-start | bytes 393224 | tf_op jit(solution)/shard_map/ppermute | solution.py:22
  35.4 1.4 %collective-permute-start.12 = (f32[2,4,1,1024]{3,2,1,0:T(1,128)S(1)}, f32[2,4,1,1024]{3,2,1,0:T(1,128)S(1)}, u32[]{:S(2)}, u32[]{:S(2)}) collective-permute-start(f32[2,4,1,1024]{3,2,1,0:T(1,128)S(1)} %get-tuple-element.62.mamba_ref), channel_id=1, source_target_pairs={{0,1},{1,0},{2,3},{3,2},{4,5},{5,4},{6,7},{7,6},{8,9},{9,8},{10,11... | collective-permute-start | bytes 98312 | tf_op jit(solution)/shard_map/ppermute | solution.py:22

commit v4 on v3

--- a/solution.py
+++ b/solution.py
@@ -69,10 +69,10 @@
         out_ref[first + i * 16 : first + (i + 1) * 16, :] = cut.astype(BF)
 
 
-def stage(count, split, kv_ref, state_ref, q_ref, new_ref, blocks_ref, counts_ref, weight_ref, *rest):
+def stage(count, split, kv_ref, state_ref, q_ref, new_ref, blocks_ref, counts_ref, *rest):
     sends = rest[: count - 1]
-    own_state, kv_out, q_out, new_out, bias_out, weight_out = rest[count - 1 : count + 5]
-    loaded, blocks, counts, sems, early = rest[count + 5 :]
+    own_state, kv_out, q_out, new_out, bias_out = rest[count - 1 : count + 4]
+    loaded, blocks, counts, sems, early = rest[count + 4 :]
     me, rep = lax.axis_index("seq"), lax.axis_index("rep")
     heads = kv_ref.shape[1]
     part = loaded.shape[2]
@@ -91,7 +91,6 @@
             rows = pl.ds(j * BLOCK, BLOCK)
             moves.append(copy(kv_ref.at[me ^ c, j], sends[c - 1].at[rows]))
     moves += [copy(kv_ref, kv_out), copy(q_ref, q_out), copy(new_ref, new_out)]
-    moves += weight_half(weight_ref, weight_out, rep, copy)
     for move in first + moves:
         move.start()
     for move in first:
@@ -247,10 +246,6 @@
     return [copy(weight_ref.at[src], out_ref.at[dst]) for src, dst in cuts]
 
 
-def load_weight(weight_ref, out_ref, sems):
-    run_all(weight_half(weight_ref, out_ref, 1 - lax.axis_index("rep"), copier(sems)))
-
-
 def project_own(attn_ref, weight_ref, out_ref):
     out_ref[...] = dot_f32(attn_ref[...], weight_ref[...], ((1,), (0,)))
 
@@ -283,18 +278,24 @@
     refs[-1][...] = total.astype(BF)
 
 
-def coefficients(count, split, dt_hbm, x_hbm, bc_hbm, gain_hbm, log_hbm, slope_ref, base_ref,
-                 dt_ref, x_ref, bc_ref, gain_ref, log_ref, sems):
+def prepare(count, split, weight_hbm, dt_hbm, x_hbm, bc_hbm, gain_hbm, log_hbm, own_ref, other_ref,
+            slope_ref, base_ref, dt_ref, x_ref, bc_ref, gain_ref, log_ref, sems, weight_sems):
     copy = copier(sems)
-    run_all(
-        [
-            copy(dt_hbm, dt_ref),
-            copy(x_hbm, x_ref),
-            copy(bc_hbm, bc_ref),
-            copy(gain_hbm, gain_ref),
-            copy(log_hbm, log_ref),
-        ]
-    )
+    first = [
+        copy(dt_hbm, dt_ref),
+        copy(x_hbm, x_ref),
+        copy(bc_hbm, bc_ref),
+        copy(gain_hbm, gain_ref),
+        copy(log_hbm, log_ref),
+    ]
+    copy = copier(weight_sems)
+    which = lax.axis_index("rep")
+    weights = weight_half(weight_hbm, own_ref, which, copy)
+    weights += weight_half(weight_hbm, other_ref, 1 - which, copy)
+    for move in first + weights:
+        move.start()
+    for move in first:
+        move.wait()
     me, rep = lax.axis_index("seq"), lax.axis_index("rep")
     _, steps, ns, part = slope_ref.shape
     block = part * 2 if split else part
@@ -324,6 +325,8 @@
             base_ref[c, step] = (
                 jnp.sum(read[step] * added, axis=0, keepdims=True) + gain * inputs
             )
+    for move in weights:
+        move.wait()
 
 
 def select(count, blocks_ref, counts_ref, kv_ref, state_ref, slope_ref, base_ref, *rest):
@@ -456,28 +459,40 @@
             shape(queries.shape, BF),
             shape(new_kv.shape, BF),
             shape((all_rows, 128), F32),
-            half_weight,
         ],
-        [HB] * 7,
-        [VM] * (count + 5),
+        [HB] * 6,
+        [VM] * (count + 4),
         [
             pltpu.VMEM((count, ns, part), F32),
             smem(blocks.shape, jnp.int32),
             smem(kept_counts.shape, jnp.int32),
-            DMA(((count - 1) * heads + 3 + PIECES,)),
+            DMA(((count - 1) * heads + 3,)),
             DMA((count + 2,)),
         ],
         us=1.5,
-    )(prefill_kv, prefill_state, queries, new_kv, blocks, kept_counts, out_weight)
+    )(prefill_kv, prefill_state, queries, new_kv, blocks, kept_counts)
     sends = staged[: count - 1]
-    own_state, kv_near, q_near, new_near, bias, own_weight = staged[count - 1 :]
-    early = shift(after(sends[-1:], *asked)[0], "seq", count - 1)
-
-    slope, base = call(
-        functools.partial(coefficients, count, split),
-        [shape((count, steps, ns, part), F32), shape((count, steps, 1, part), F32)],
-        [HB] * 5,
-        [VM] * 2,
+    own_state, kv_near, q_near, new_near, bias = staged[count - 1 :]
+    far = after(sends[1:], *asked)
+    far = [shift(far[c - 2], "seq", c) for c in range(count - 1, 1, -1)][::-1]
+
+    partial_sums = call(
+        functools.partial(attend, count),
+        shape((chunks, 144, 128), BF),
+        [VM] * (3 + count),
+        VM,
+        us=1.5,
+    )(kv_near, new_near, bias, q_near, *asked[::-1])
+    own_weight, other_weight, slope, base = call(
+        functools.partial(prepare, count, split),
+        [
+            half_weight,
+            half_weight,
+            shape((count, steps, ns, part), F32),
+            shape((count, steps, 1, part), F32),
+        ],
+        [HB] * 6,
+        [VM] * 4,
         [
             pltpu.VMEM((steps, 1, channels), F32),
             pltpu.VMEM((steps, channels), BF),
@@ -485,25 +500,13 @@
             pltpu.VMEM((1, channels), F32),
             pltpu.VMEM(a_log.shape, F32),
             DMA((5,)),
+            DMA((2 * PIECES,)),
         ],
-        us=2.0,
-    )(step_dt, step_input, step_bc, skip_gain, a_log)
-
-    partial_sums = call(
-        functools.partial(attend, count),
-        shape((chunks, 144, 128), BF),
-        [VM] * (3 + count),
-        VM,
-        us=1.5,
-    )(kv_near, new_near, bias, q_near, *asked[::-1])
-    other_weight = call(load_weight, half_weight, [HB], VM, [DMA((PIECES,))], us=1.7)(
-        *after([out_weight], partial_sums)
-    )
-    middle = after(sends[1:-1], partial_sums)
-    middle = [shift(middle[c - 2], "seq", c) for c in range(count - 2, 1, -1)][::-1]
+        us=3.6,
+    )(*after([out_weight], partial_sums), step_dt, step_input, step_bc, skip_gain, a_log)
     gathered = [partial_sums] + [shift(partial_sums, "seq", c) for c in range(count - 1, 0, -1)][::-1]
-    *gathered, early, other_weight = after([*gathered[::-1], early, other_weight])
-    gathered = gathered[::-1]
+    joint = after([*gathered, *far, other_weight])
+    gathered, far, other_weight = joint[:count], joint[count:-1], joint[-1]
     attn = call(
         functools.partial(merge, count, heads, steps, group),
         shape((steps * count, half), BF),
@@ -513,7 +516,7 @@
         us=0.3,
     )(*gathered[:1], *gathered[:0:-1])
     attn_other = shift(attn, "rep", 1)
-    received = [shift(after(sends[:1], attn)[0], "seq", 1), *middle, early]
+    received = [shift(after(sends[:1], attn)[0], "seq", 1), *far]
     own_sum = call(
         project_own, shape((steps * count, columns), F32), [VM, VM], VM, us=0.7
     )(attn, own_weight)
@@ -526,11 +529,7 @@
         us=0.7,
     )(own_sum, attn_other, other_weight)
     sums = [sums[0]] + [shift(sums[c], "head", c) for c in range(1, heads_count)]
-    proj_out = call(
-        add_up, shape((steps, share, columns), BF), [VM] * heads_count, VM, us=0.6
-    )(*sums)
-
-    received = after(received, proj_out)
+    received = after(received, sums[0])
     half_shape = (heads, keep_rep, BLOCK, width)
     kept, sent, mamba = call(
         functools.partial(select, count),
@@ -547,6 +546,11 @@
         us=1.0,
     )(blocks, kept_counts, prefill_kv, own_state, slope, base, *received)
     got = shift(sent, "rep", 1)
+    sums[1:] = after(sums[1:], kept)
+    proj_out = call(
+        add_up, shape((steps, share, columns), BF), [VM] * heads_count, VM, us=0.6
+    )(*sums)
+
     operands = [kept, got, mamba] + ([shift(mamba, "rep", 1)] if split else [])
     handoff, mamba_out = call(
         functools.partial(assemble, split),

time: 37.9 us -> 42.7 us (1.13)
  waiting for transfers between devices: 7.75 us -> 14.1 us
  Pallas kernels: 11.9 us -> 10.2 us
    ppermute x13, waiting for transfers between devices: 7.75 us -> 14.1 us  [shift(): return lax.ppermute(x, axis, [(i, i ^ c) for i in range(size)])]
    pallas_call x1, Pallas kernels: 2.81 us -> 1.48 us  [per_device(): call(functools.partial(stage, count, split), [shape((packed, width), BF)]...]
    pallas_call x2 -> x1, Pallas kernels: 3.71 us -> 3.74 us  [per_device(): call(functools.partial(prepare, count, split), [half_weight, half_weight,...]
  transfers between devices with their start and end apart: 13 -> 13, of which waited for: 5 -> 6; matrix products, arithmetic and copies ran while one was open for 0% -> 0% of each run, Pallas kernels for 25% -> 18%
where the time goes in v4:
time: 42.7 us; the launch traced here: 42.6 us
  starting transfers between devices  17.6 us (41%)
  waiting for transfers between devices  14.1 us (33%)
  Pallas kernels  10.2 us (24%)
  between operations  0.71 us (2%)
    ppermute x13, starting transfers between devices, shift(): return lax.ppermute(x, axis, [(i, i ^ c) for i in range(size)])  17.6 us
    ppermute x13, waiting for transfers between devices, shift(): return lax.ppermute(x, axis, [(i, i ^ c) for i in range(size)])  14.1 us
    pallas_call x1, Pallas kernels, per_device(): call(functools.partial(prepare, count, split), [half_weight, half_weight,...  3.74 us
    pallas_call x1, Pallas kernels, per_device(): call(functools.partial(stage, count, split), [shape((packed, width), BF)]...  1.48 us
    pallas_call x1, Pallas kernels, per_device(): call(functools.partial(select, count), [shape(half_shape, BF), shape(half...  1.26 us
    pallas_call x1, Pallas kernels, per_device(): call(functools.partial(assemble, split), [shape((1, dec_heads, keep_rep,...  0.89 us
  transfers between devices with their start and end apart: 13, of which 6 were waited for; matrix products, arithmetic and copies ran while one was open for 0% of the time, Pallas kernels for 18%

profile of v4, /device:TPU:0, one launch (start us, length us, event | category | flops | bytes accessed | tf_op | source)
XLA Modules:
  0.0 42.6 jit_solution(3465489383773620438)
XLA Ops:
  0.6 5.1 %collective-permute-start = (bf16[2,1,32,128]{3,2,1,0:T(8,128)(2,1)}, bf16[2,1,32,128]{3,2,1,0:T(8,128)(2,1)S(1)}, u32[]{:S(2)}, u32[]{:S(2)}) collective-permute-start(bf16[2,1,32,128]{3,2,1,0:T(8,128)(2,1)} %q_ref.1), channel_id=1, source_target_pairs={{0,12},{4,8},{8,4},{12,0},{1,13},{5,9},{9,5},{13,1},{2,14},{6,10},... | collective-permute-start | bytes 49160 | tf_op jit(solution)/shard_map/ppermute | solution.py:22
  5.7 0.6 %collective-permute-start.1 = (bf16[2,1,32,128]{3,2,1,0:T(8,128)(2,1)}, bf16[2,1,32,128]{3,2,1,0:T(8,128)(2,1)S(1)}, u32[]{:S(2)}, u32[]{:S(2)}) collective-permute-start(bf16[2,1,32,128]{3,2,1,0:T(8,128)(2,1)} %q_ref.1), channel_id=1, source_target_pairs={{0,8},{4,12},{8,0},{12,4},{1,9},{5,13},{9,1},{13,5},{2,10},{6,14},... | collective-permute-start | bytes 49160 | tf_op jit(solution)/shard_map/ppermute | solution.py:22
  6.4 1.5 %shard_map.139 = (bf16[320,256]{1,0:T(8,128)(2,1)S(1)}, bf16[320,256]{1,0:T(8,128)(2,1)S(1)}, bf16[320,256]{1,0:T(8,128)(2,1)S(1)}, bf16[64,256]{1,0:T(8,128)(2,...) custom-call(bf16[4,2,128,256]{3,2,1,0:T(8,128)(2,1)} %kv_ref.3, ...), custom_call_target="tpu_custom_call" | custom-call | bytes 54000 | tf_op jit(solution)/shard_map/pallas_call | solution.py:453
  7.9 1.8 %collective-permute-done.2.rest_3_ = bf16[2,1,32,128]{3,2,1,0:T(8,128)(2,1)S(1)} collective-permute-done((bf16[2,1,32,128]{3,2,1,0:T(8,128)(2,1)}, bf16[2,1,32,128]{3,2,1,0:T(8,128)(2,1)S(1)}, u32[]{:S(2)}, u32[]{:S(2)}) %collective-permute-start.2) | collective-permute-done | bytes 16416 | tf_op jit(solution)/shard_map/ppermute | solution.py:22
  9.7 0.9 %collective-permute-done.1.rest_2_ = bf16[2,1,32,128]{3,2,1,0:T(8,128)(2,1)S(1)} collective-permute-done((bf16[2,1,32,128]{3,2,1,0:T(8,128)(2,1)}, bf16[2,1,32,128]{3,2,1,0:T(8,128)(2,1)S(1)}, u32[]{:S(2)}, u32[]{:S(2)}) %collective-permute-start.1) | collective-permute-done | bytes 16416 | tf_op jit(solution)/shard_map/ppermute | solution.py:22
  10.6 0.7 %collective-permute-start.6 = (bf16[320,256]{1,0:T(8,128)(2,1)S(1)}, bf16[320,256]{1,0:T(8,128)(2,1)S(1)}, u32[]{:S(2)}, u32[]{:S(2)}) collective-permute-start(bf16[320,256]{1,0:T(8,128)(2,1)S(1)} %get-tuple-element.48), channel_id=1, source_target_pairs={{0,8},{4,12},{8,0},{12,4},{1,9},{5,13},{9,1},{13,5},{2,10},{6,14},... | collective-permute-start | bytes 491528 | tf_op jit(solution)/shard_map/ppermute | solution.py:22
  11.3 3.6 %collective-permute-start.7 = (bf16[320,256]{1,0:T(8,128)(2,1)S(1)}, bf16[320,256]{1,0:T(8,128)(2,1)S(1)}, u32[]{:S(2)}, u32[]{:S(2)}) collective-permute-start(bf16[320,256]{1,0:T(8,128)(2,1)S(1)} %get-tuple-element.49), channel_id=1, source_target_pairs={{0,12},{4,8},{8,4},{12,0},{1,13},{5,9},{9,5},{13,1},{2,14},{6,10},... | collective-permute-start | bytes 491528 | tf_op jit(solution)/shard_map/ppermute | solution.py:22
  15.0 0.6 %shard_map.140.rest_0_ = bf16[1,144,128]{2,1,0:T(8,128)(2,1)S(1)} custom-call(bf16[4,2,128,256]{3,2,1,0:T(8,128)(2,1)S(1)} %get-tuple-element.38.kv_ref, bf16[2,1,4,256]{3,2,1,0:T(4,128)(2,1)S(1)} %get-tuple-element.39.new_ref, f32[128,128]{1,0:T(8,128)S(1)} %get-tuple-element.40.bias_ref, bf16[2,1,32,128]{3,2,1,0:T(8,128)(2,1)S(1)} %get-tuple-element.41.rest_0_, ...), custom_call_target="tpu_custom_call" | custom-call | bytes 54000 | tf_op jit(solution)/shard_map/pallas_call | solution.py:479
  15.6 0.2 collective-permute-start.5
  15.9 0.4 collective-permute-start.4
  16.2 3.8 %collective-permute-start.3 = (bf16[1,144,128]{2,1,0:T(8,128)(2,1)S(1)}, bf16[1,144,128]{2,1,0:T(8,128)(2,1)S(1)}, u32[]{:S(2)}, u32[]{:S(2)}) collective-permute-start(bf16[1,144,128]{2,1,0:T(8,128)(2,1)S(1)} %shard_map.140.rest_0_), channel_id=1, source_target_pairs={{0,4},{4,0},{8,12},{12,8},{1,5},{5,1},{9,13},{13,9},{2,6},{6,2},{1... | collective-permute-start | bytes 110600 | tf_op jit(solution)/shard_map/ppermute | solution.py:22
  20.1 3.7 %shard_map.141 = (bf16[2048,1024]{1,0:T(8,128)(2,1)S(1)}, bf16[2048,1024]{1,0:T(8,128)(2,1)S(1)}, f32[4,2,16,1024]{3,2,1,0:T(8,128)S(1)}, f32[4,2,1,1024]{3,2,1,0:T(1,128)S(1)}) custom-call(bf16[4096,1024]{1,0:T(8,128)(2,1)} %weight_hbm, f32[2,1,8192]{2,1,0:T(1,128)} %dt_hbm.1, bf16[2,8192]{1,0:T(2,128)(2,1)} %bitcast.3, f32[2,1,2,16]{3,2,1,0:T(2,128)} %bc_hbm.1, ...), custom_call_target="tpu_custom_call" | custom-call | bytes 129600 | tf_op jit(solution)/shard_map/pallas_call | solution.py:486
  23.8 0.0 collective-permute-done.5.rest_1_
  23.8 5.9 %collective-permute-done.4.rest_2_ = bf16[1,144,128]{2,1,0:T(8,128)(2,1)S(1)} collective-permute-done((bf16[1,144,128]{2,1,0:T(8,128)(2,1)S(1)}, bf16[1,144,128]{2,1,0:T(8,128)(2,1)S(1)}, u32[]{:S(2)}, u32[]{:S(2)}) %collective-permute-start.4) | collective-permute-done | bytes 36896 | tf_op jit(solution)/shard_map/ppermute | solution.py:22
  29.7 0.0 collective-permute-done.3.rest_3_
  29.7 0.0 collective-permute-done.6.rest_1_
  29.7 0.0 collective-permute-done.7.rest_2_
  29.7 0.2 shard_map.142.attn_ref
  30.0 0.2 collective-permute-start.8
  30.2 0.0 collective-permute-start.9
  30.2 0.6 %shard_map.143.acc_ref = f32[8,1024]{1,0:T(8,128)S(1)} custom-call(bf16[8,2048]{1,0:T(8,128)(2,1)S(1)} %shard_map.142.attn_ref, bf16[2048,1024]{1,0:T(8,128)(2,1)S(1)} %get-tuple-element.58.weight_ref), custom_call_target="tpu_custom_call" | custom-call | bytes 25200 | tf_op jit(solution)/shard_map/pallas_call | solution.py:520
  30.9 0.6 %collective-permute-done.9.attn_ref = bf16[8,2048]{1,0:T(8,128)(2,1)S(1)} collective-permute-done((bf16[8,2048]{1,0:T(8,128)(2,1)S(1)}, bf16[8,2048]{1,0:T(8,128)(2,1)S(1)}, u32[]{:S(2)}, u32[]{:S(2)}) %collective-permute-start.9) | collective-permute-done | bytes 32800 | tf_op jit(solution)/shard_map/ppermute | solution.py:22
  31.4 0.7 %shard_map.144 = (f32[2,2,1024]{2,1,0:T(2,128)S(1)}, f32[2,2,1024]{2,1,0:T(2,128)S(1)}) custom-call(f32[8,1024]{1,0:T(8,128)S(1)} %shard_map.143.acc_ref, bf16[8,2048]{1,0:T(8,128)(2,1)S(1)} %collective-permute-done.9.attn_ref, bf16[2048,1024]{1,0:T(8,128)(2,1)S(1)} %get-tuple-element.59.weight_ref), custom_call_target="tpu_custom_call" | custom-call | bytes 25200 | tf_op jit(solution)/shard_map/pallas_call | solution.py:524
  32.1 3.3 %collective-permute-done.8.rest_0_ = bf16[320,256]{1,0:T(8,128)(2,1)S(1)} collective-permute-done((bf16[320,256]{1,0:T(8,128)(2,1)S(1)}, bf16[320,256]{1,0:T(8,128)(2,1)S(1)}, u32[]{:S(2)}, u32[]{:S(2)}) %collective-permute-start.8) | collective-permute-done | bytes 163872 | tf_op jit(solution)/shard_map/ppermute | solution.py:22
  35.4 1.3 %shard_map.145 = (bf16[2,1,128,256]{3,2,1,0:T(8,128)(2,1)S(1)}, bf16[2,1,128,256]{3,2,1,0:T(8,128)(2,1)S(1)}, f32[2,4,1,1024]{3,2,1,0:T(1,128)S(1)}) custom-call(s32[4,2,8]{2,1,0:T(2,128)} %bitcast.6, s32[4,8]{1,0:T(4,128)} %counts_ref.3, bf16[4,2,128,256]{3,2,1,0:T(8,128)(2,1)} %kv_ref.3, bf16[64,256]{1,0:T(8,128)(2,1)S(1)} %get-tuple-element.37.state_ref, ...), custom_call_target="tpu_custom_call" | custom-call | bytes 36000 | tf_op jit(solution)/shard_map/pallas_call | solution.py:534
  36.6 0.1 collective-permute-start.10
  36.7 0.5 %collective-permute-start.11 = (f32[2,4,1,1024]{3,2,1,0:T(1,128)S(1)}, f32[2,4,1,1024]{3,2,1,0:T(1,128)S(1)}, u32[]{:S(2)}, u32[]{:S(2)}) collective-permute-start(f32[2,4,1,1024]{3,2,1,0:T(1,128)S(1)} %get-tuple-element.66.mamba_ref), channel_id=1, source_target_pairs={{0,1},{1,0},{2,3},{3,2},{4,5},{5,4},{6,7},{7,6},{8,9},{9,8},{10,11... | collective-permute-start | bytes 98312 | tf_op jit(solution)/shard_map/ppermute | solution.py:22
  37.2 2.2 %collective-permute-start.12 = (f32[2,2,1024]{2,1,0:T(2,128)S(1)}, f32[2,2,1024]{2,1,0:T(2,128)S(1)}, u32[]{:S(2)}, u32[]{:S(2)}) collective-permute-start(f32[2,2,1024]{2,1,0:T(2,128)S(1)} %get-tuple-element.68), channel_id=1, source_target_pairs={{0,2},{2,0},{1,3},{3,1},{4,6},{6,4},{5,7},{7,5},{8,10},{10,8},{9,1... | collective-permute-start | bytes 49160 | tf_op jit(solution)/shard_map/ppermute | solution.py:22
  39.3 1.7 %collective-permute-done.12.refs_1_ = f32[2,2,1024]{2,1,0:T(2,128)S(1)} collective-permute-done((f32[2,2,1024]{2,1,0:T(2,128)S(1)}, f32[2,2,1024]{2,1,0:T(2,128)S(1)}, u32[]{:S(2)}, u32[]{:S(2)}) %collective-permute-start.12) | collective-permute-done | bytes 16416 | tf_op jit(solution)/shard_map/ppermute | solution.py:22
  41.1 0.6 %shard_map.147 = bf16[2,2,1024]{2,1,0:T(2,128)(2,1)} custom-call(f32[2,2,1024]{2,1,0:T(2,128)S(1)} %get-tuple-element.60.refs_0_, f32[2,2,1024]{2,1,0:T(2,128)S(1)} %collective-permute-done.12.refs_1_), custom_call_target="tpu_custom_call" | custom-call | bytes 21600 | tf_op jit(solution)/shard_map/pallas_call | solution.py:550
  41.7 0.0 collective-permute-done.11.rest_0_
  41.7 0.9 %shard_map.146 = (bf16[1,4,1,128,256]{4,3,2,1,0:T(8,128)(2,1)}, f32[2,1,8192]{2,1,0:T(1,128)}) custom-call(bf16[2,1,128,256]{3,2,1,0:T(8,128)(2,1)S(1)} %get-tuple-element.64.kept_ref, bf16[2,1,128,256]{3,2,1,0:T(8,128)(2,1)S(1)} %collective-permute-done.10.got_ref, f32[2,4,1,1024]{3,2,1,0:T(1,128)S(1)} %get-tuple-element.66.mamba_ref, ...), custom_call_target="tpu_custom_call" | custom-call | bytes 36000 | tf_op jit(solution)/shard_map/pallas_call | solution.py:555
  (3 shorter events, 0.0 us)
Async XLA Ops:
  0.6 7.2 %collective-permute-start = (bf16[2,1,32,128]{3,2,1,0:T(8,128)(2,1)}, bf16[2,1,32,128]{3,2,1,0:T(8,128)(2,1)S(1)}, u32[]{:S(2)}, u32[]{:S(2)}) collective-permute-start(bf16[2,1,32,128]{3,2,1,0:T(8,128)(2,1)} %q_ref.1), channel_id=1, source_target_pairs={{0,12},{4,8},{8,4},{12,0},{1,13},{5,9},{9,5},{13,1},{2,14},{6,10},... | collective-permute-start | bytes 49160 | tf_op jit(solution)/shard_map/ppermute | solution.py:22
  5.7 3.9 %collective-permute-start.2 = (bf16[2,1,32,128]{3,2,1,0:T(8,128)(2,1)}, bf16[2,1,32,128]{3,2,1,0:T(8,128)(2,1)S(1)}, u32[]{:S(2)}, u32[]{:S(2)}) collective-permute-start(bf16[2,1,32,128]{3,2,1,0:T(8,128)(2,1)} %q_ref.1), channel_id=1, source_target_pairs={{0,4},{4,0},{8,12},{12,8},{1,5},{5,1},{9,13},{13,9},{2,6},{6,2},{1... | collective-permute-start | bytes 49160 | tf_op jit(solution)/shard_map/ppermute | solution.py:22
  5.7 4.8 %collective-permute-start.1 = (bf16[2,1,32,128]{3,2,1,0:T(8,128)(2,1)}, bf16[2,1,32,128]{3,2,1,0:T(8,128)(2,1)S(1)}, u32[]{:S(2)}, u32[]{:S(2)}) collective-permute-start(bf16[2,1,32,128]{3,2,1,0:T(8,128)(2,1)} %q_ref.1), channel_id=1, source_target_pairs={{0,8},{4,12},{8,0},{12,4},{1,9},{5,13},{9,1},{13,5},{2,10},{6,14},... | collective-permute-start | bytes 49160 | tf_op jit(solution)/shard_map/ppermute | solution.py:22
  10.6 19.1 %collective-permute-start.6 = (bf16[320,256]{1,0:T(8,128)(2,1)S(1)}, bf16[320,256]{1,0:T(8,128)(2,1)S(1)}, u32[]{:S(2)}, u32[]{:S(2)}) collective-permute-start(bf16[320,256]{1,0:T(8,128)(2,1)S(1)} %get-tuple-element.48), channel_id=1, source_target_pairs={{0,8},{4,12},{8,0},{12,4},{1,9},{5,13},{9,1},{13,5},{2,10},{6,14},... | collective-permute-start | bytes 491528 | tf_op jit(solution)/shard_map/ppermute | solution.py:22
  11.3 18.4 %collective-permute-start.7 = (bf16[320,256]{1,0:T(8,128)(2,1)S(1)}, bf16[320,256]{1,0:T(8,128)(2,1)S(1)}, u32[]{:S(2)}, u32[]{:S(2)}) collective-permute-start(bf16[320,256]{1,0:T(8,128)(2,1)S(1)} %get-tuple-element.49), channel_id=1, source_target_pairs={{0,12},{4,8},{8,4},{12,0},{1,13},{5,9},{9,5},{13,1},{2,14},{6,10},... | collective-permute-start | bytes 491528 | tf_op jit(solution)/shard_map/ppermute | solution.py:22
  15.6 8.2 %collective-permute-start.5 = (bf16[1,144,128]{2,1,0:T(8,128)(2,1)S(1)}, bf16[1,144,128]{2,1,0:T(8,128)(2,1)S(1)}, u32[]{:S(2)}, u32[]{:S(2)}) collective-permute-start(bf16[1,144,128]{2,1,0:T(8,128)(2,1)S(1)} %shard_map.140.rest_0_), channel_id=1, source_target_pairs={{0,12},{4,8},{8,4},{12,0},{1,13},{5,9},{9,5},{13,1},{2,14},{6,10},... | collective-permute-start | bytes 110600 | tf_op jit(solution)/shard_map/ppermute | solution.py:22
  15.9 13.8 %collective-permute-start.4 = (bf16[1,144,128]{2,1,0:T(8,128)(2,1)S(1)}, bf16[1,144,128]{2,1,0:T(8,128)(2,1)S(1)}, u32[]{:S(2)}, u32[]{:S(2)}) collective-permute-start(bf16[1,144,128]{2,1,0:T(8,128)(2,1)S(1)} %shard_map.140.rest_0_), channel_id=1, source_target_pairs={{0,8},{4,12},{8,0},{12,4},{1,9},{5,13},{9,1},{13,5},{2,10},{6,14},... | collective-permute-start | bytes 110600 | tf_op jit(solution)/shard_map/ppermute | solution.py:22
  16.2 13.5 %collective-permute-start.3 = (bf16[1,144,128]{2,1,0:T(8,128)(2,1)S(1)}, bf16[1,144,128]{2,1,0:T(8,128)(2,1)S(1)}, u32[]{:S(2)}, u32[]{:S(2)}) collective-permute-start(bf16[1,144,128]{2,1,0:T(8,128)(2,1)S(1)} %shard_map.140.rest_0_), channel_id=1, source_target_pairs={{0,4},{4,0},{8,12},{12,8},{1,5},{5,1},{9,13},{13,9},{2,6},{6,2},{1... | collective-permute-start | bytes 110600 | tf_op jit(solution)/shard_map/ppermute | solution.py:22
  30.0 5.4 %collective-permute-start.8 = (bf16[320,256]{1,0:T(8,128)(2,1)S(1)}, bf16[320,256]{1,0:T(8,128)(2,1)S(1)}, u32[]{:S(2)}, u32[]{:S(2)}) collective-permute-start(bf16[320,256]{1,0:T(8,128)(2,1)S(1)} %get-tuple-element.55), channel_id=1, source_target_pairs={{0,4},{4,0},{8,12},{12,8},{1,5},{5,1},{9,13},{13,9},{2,6},{6,2},{1... | collective-permute-start | bytes 491528 | tf_op jit(solution)/shard_map/ppermute | solution.py:22
  30.2 1.2 %collective-permute-start.9 = (bf16[8,2048]{1,0:T(8,128)(2,1)S(1)}, bf16[8,2048]{1,0:T(8,128)(2,1)S(1)}, u32[]{:S(2)}, u32[]{:S(2)}) collective-permute-start(bf16[8,2048]{1,0:T(8,128)(2,1)S(1)} %shard_map.142.attn_ref), channel_id=1, source_target_pairs={{0,1},{1,0},{2,3},{3,2},{4,5},{5,4},{6,7},{7,6},{8,9},{9,8},{10,11... | collective-permute-start | bytes 98312 | tf_op jit(solution)/shard_map/ppermute | solution.py:22
  36.6 5.1 %collective-permute-start.10 = (bf16[2,1,128,256]{3,2,1,0:T(8,128)(2,1)S(1)}, bf16[2,1,128,256]{3,2,1,0:T(8,128)(2,1)S(1)}, u32[]{:S(2)}, u32[]{:S(2)}) collective-permute-start(bf16[2,1,128,256]{3,2,1,0:T(8,128)(2,1)S(1)} %get-tuple-element.65), channel_id=1, source_target_pairs={{0,1},{1,0},{2,3},{3,2},{4,5},{5,4},{6,7},{7,6},{8,9},{9,8},{10,11... | collective-permute-start | bytes 393224 | tf_op jit(solution)/shard_map/ppermute | solution.py:22
  36.7 5.0 %collective-permute-start.11 = (f32[2,4,1,1024]{3,2,1,0:T(1,128)S(1)}, f32[2,4,1,1024]{3,2,1,0:T(1,128)S(1)}, u32[]{:S(2)}, u32[]{:S(2)}) collective-permute-start(f32[2,4,1,1024]{3,2,1,0:T(1,128)S(1)} %get-tuple-element.66.mamba_ref), channel_id=1, source_target_pairs={{0,1},{1,0},{2,3},{3,2},{4,5},{5,4},{6,7},{7,6},{8,9},{9,8},{10,11... | collective-permute-start | bytes 98312 | tf_op jit(solution)/shard_map/ppermute | solution.py:22
  37.2 3.9 %collective-permute-start.12 = (f32[2,2,1024]{2,1,0:T(2,128)S(1)}, f32[2,2,1024]{2,1,0:T(2,128)S(1)}, u32[]{:S(2)}, u32[]{:S(2)}) collective-permute-start(f32[2,2,1024]{2,1,0:T(2,128)S(1)} %get-tuple-element.68), channel_id=1, source_target_pairs={{0,2},{2,0},{1,3},{3,1},{4,6},{6,4},{5,7},{7,5},{8,10},{10,8},{9,1... | collective-permute-start | bytes 49160 | tf_op jit(solution)/shard_map/ppermute | solution.py:22

commit v5 on v4

v5 whole, which is shorter than its diff:
```python
import functools

import jax
import jax.numpy as jnp
from jax import lax
from jax.experimental import pallas as pl
from jax.experimental.pallas import tpu as pltpu
from jax.sharding import PartitionSpec as P

BLOCK = 128
PIECES = 4
NEG = -1e30
BF = jnp.bfloat16
F32 = jnp.float32
VM = pl.BlockSpec(memory_space=pltpu.VMEM)
HB = pl.BlockSpec(memory_space=pltpu.HBM)
DMA = pltpu.SemaphoreType.DMA


def shift(x, axis, c):
    size = lax.axis_size(axis)
    return lax.ppermute(x, axis, [(i, i ^ c) for i in range(size)])


def call(body, out_shape, in_specs, out_specs, scratch=(), us=1.0):
    return pl.pallas_call(
        body,
        out_shape=out_shape,
        in_specs=in_specs,
        out_specs=out_specs,
        scratch_shapes=list(scratch),
        cost_estimate=pl.CostEstimate(
            flops=0, bytes_accessed=int(us * 3.6e4), transcendentals=0
        ),
        compiler_params=pltpu.CompilerParams(vmem_limit_bytes=32 * 1024 * 1024),
    )


def in_hbm(x):
    return pltpu.with_memory_space_constraint(x, pltpu.HBM)


def after(arrays, *earlier):
    return lax.optimization_barrier((*arrays, *earlier))[: len(arrays)]


def run_all(copies):
    for copy in copies:
        copy.start()
    for copy in copies:
        copy.wait()


def copier(sems):
    position = iter(range(sems.shape[0]))
    return lambda src, dst: pltpu.make_async_copy(src, dst, sems.at[next(position)])


def state_rows(part):
    return 16 * pl.cdiv(part, 256)


def pack_state(piece, out_ref, first):
    ns, part = piece.shape
    for i in range(pl.cdiv(part, 256)):
        cut = piece[:, i * 256 : (i + 1) * 256]
        if cut.shape[1] < 256:
            cut = jnp.concatenate([cut, jnp.zeros((ns, 256 - cut.shape[1]), F32)], axis=1)
        out_ref[first + i * 16 : first + (i + 1) * 16, :] = cut.astype(BF)


def stage(count, kv_ref, q_ref, new_ref, blocks_ref, counts_ref, *rest):
    pieces = rest[:count]
    q_out, new_out, bias_out, blocks, counts, sems, early = rest[count:]
    me, rep = lax.axis_index("seq"), lax.axis_index("rep")
    heads = kv_ref.shape[1]
    copy = copier(sems)
    moves = []
    for c in range(count - 1, -1, -1):
        for j in range(heads):
            moves.append(copy(kv_ref.at[me ^ c, j], pieces[c].at[pl.ds(j * BLOCK, BLOCK)]))
    moves += [copy(q_ref, q_out), copy(new_ref, new_out)]
    copy = copier(early)
    first = [copy(blocks_ref, blocks), copy(counts_ref, counts)]
    for move in moves + first:
        move.start()
    for move in first:
        move.wait()
    head_first = lax.axis_index("head") * new_ref.shape[2] + rep * heads
    rows = bias_out.shape[0] // heads
    for j in range(heads):
        for c in range(count):
            live = jnp.int32(0)
            for slot in range(blocks.shape[1]):
                hit = blocks[me, slot, head_first + j] == (me ^ c)
                live = live | (hit & (slot < counts[me, head_first + j])).astype(jnp.int32)
            dead = jnp.where(live > 0, 0.0, NEG).astype(F32)
            bias_out[j * rows : (j + 1) * rows, c * BLOCK : (c + 1) * BLOCK] = jnp.full(
                (rows, BLOCK), dead, F32
            )
    for move in moves:
        move.wait()


def stage_state(count, split, state_ref, *rest):
    outs, loaded, sems = rest[:count], rest[count], rest[count + 1]
    me, rep = lax.axis_index("seq"), lax.axis_index("rep")
    part = loaded.shape[2]
    copy = copier(sems)
    moves = []
    for c in range(count):
        if split:
            src = state_ref.at[me ^ c, :, pl.ds(pl.multiple_of(rep * part, 128), part)]
        else:
            src = state_ref.at[me ^ c]
        moves.append(copy(src, loaded.at[c]))
    run_all(moves)
    for c in range(count):
        pack_state(loaded[c], outs[c], 0)


def dot_f32(a, b, contract):
    return lax.dot_general(a, b, (contract, ((), ())), preferred_element_type=F32)


def query_rows(q_ref, heads):
    rep = lax.axis_index("rep")
    steps, _, q_heads, _ = q_ref.shape
    own_q = q_heads // 2
    group = own_q // heads
    q_all = [q_ref[step, 0].astype(F32) for step in range(steps)]
    q_all = [jnp.where(rep == 0, q[:own_q], q[own_q:]) for q in q_all]
    return [
        jnp.concatenate([x[j * group : (j + 1) * group] for x in q_all], axis=0)
        for j in range(heads)
    ]


def block_scores(q, piece_ref, j):
    hd = piece_ref.shape[1] // 2
    keys = piece_ref[j * BLOCK : (j + 1) * BLOCK, :hd]
    return dot_f32(q.astype(BF), keys, ((1,), (1,))) * hd ** (-0.5)


def block_sums(weights, piece_ref, j):
    values = piece_ref[j * BLOCK : (j + 1) * BLOCK, piece_ref.shape[1] // 2 :]
    return dot_f32(weights, values, ((1,), (0,)))


def choose(count, pieces, blocks, counts, zeros, sems, kept_ref, sent_ref):
    me, rep = lax.axis_index("seq"), lax.axis_index("rep")
    heads, keep_rep = kept_ref.shape[:2]
    head_first = lax.axis_index("head") * (2 * heads) + rep * heads
    waits = []
    for side, out in ((1, sent_ref), (0, kept_ref)):
        owner = rep if side == 0 else 1 - rep
        for j in range(heads):
            live_count = counts[me, head_first + j]
            for k in range(keep_rep):
                slot = owner * keep_rep + k
                source = blocks[me, slot, head_first + j] ^ me
                live = slot < live_count
                sem = sems.at[side, j, k]
                for c in range(count):
                    piece = pieces[c].at[pl.ds(j * BLOCK, BLOCK)]

                    @pl.when(live & (source == c))
                    def _():
                        pltpu.make_async_copy(piece, out.at[j, k], sem).start()

                @pl.when(jnp.logical_not(live))
                def _():
                    pltpu.make_async_copy(zeros, out.at[j, k], sem).start()

                waits.append(pltpu.make_async_copy(zeros, out.at[j, k], sem))
    return waits


def attend(count, heads, blocks_ref, counts_ref, q_ref, new_ref, bias_ref, *rest):
    pieces, states = rest[:count], rest[count : 2 * count - 1]
    outs, rest = rest[2 * count - 1 : 3 * count - 1], rest[3 * count - 1 :]
    kept_ref, sent_ref, blocks, counts, zeros, sems, early = rest
    copy = copier(early)
    scalars = [copy(blocks_ref, blocks), copy(counts_ref, counts)]
    for move in scalars:
        move.start()
    zeros[...] = jnp.zeros_like(zeros)
    rep = lax.axis_index("rep")
    queries = query_rows(q_ref, heads)
    rows, hd = queries[0].shape
    steps = q_ref.shape[0]
    group = rows // steps
    all_rows = heads * rows
    scale = hd ** (-0.5)
    scores = [
        jnp.concatenate([block_scores(q, piece, j) for piece in pieces], axis=1)
        for j, q in enumerate(queries)
    ]
    scores = jnp.concatenate(scores, axis=0)
    alive = bias_ref[...] == 0.0
    scores = jnp.where(alive, scores, NEG)
    row_step = (lax.broadcasted_iota(jnp.int32, (all_rows, 1), 0) // group) % steps
    wide_q = jnp.concatenate(queries, axis=0)
    dots, fresh_values = [], []
    top = jnp.max(scores, axis=1, keepdims=True)
    for step in range(steps):
        both = new_ref[step, 0].astype(F32)
        fresh = jnp.where(rep == 0, both[:heads], both[heads:])
        wide = jnp.concatenate(
            [jnp.broadcast_to(fresh[j : j + 1], (rows, 2 * hd)) for j in range(heads)], axis=0
        )
        dot = jnp.sum(wide_q * wide[:, :hd], axis=1, keepdims=True) * scale
        dots.append(jnp.where(row_step >= step, dot, NEG))
        fresh_values.append(wide[:, hd:])
        top = jnp.maximum(top, dots[-1])
    weights = jnp.where(alive, jnp.exp(scores - top), 0.0)
    total = jnp.sum(weights, axis=1, keepdims=True)
    weights = weights.astype(BF)
    for move in scalars:
        move.wait()
    waits = choose(count, pieces, blocks, counts, zeros, sems, kept_ref, sent_ref)
    summed = []
    for j in range(heads):
        parts = [
            block_sums(weights[j * rows : (j + 1) * rows, c * BLOCK : (c + 1) * BLOCK], piece, j)
            for c, piece in enumerate(pieces)
        ]
        summed.append(functools.reduce(jnp.add, parts))
    summed = jnp.concatenate(summed, axis=0)
    for step in range(steps):
        weight = jnp.where(row_step >= step, jnp.exp(dots[step] - top), 0.0)
        total = total + weight
        summed = summed + weight.astype(BF).astype(F32) * fresh_values[step]
    result = (summed / total).astype(BF)
    for c in range(count):
        for j in range(2):
            half = result[j * rows : (j + 1) * rows] if j < heads else jnp.zeros((rows, hd), BF)
            outs[c][:rows, j * hd : (j + 1) * hd] = half
        if c:
            outs[c][rows:, :] = states[c - 1][...]
    for move in waits:
        move.wait()


def collect(count, heads, steps, group, *rest):
    parts = rest[:1] + rest[1:count][::-1]
    out_ref, scratch = rest[count:]
    me = lax.axis_index("seq")
    for c in range(count):
        rows = parts[c][: steps * group, :].astype(F32)
        for j in range(heads):
            for step in range(steps):
                at = pl.multiple_of((step * count + (me ^ c)) * group, group)
                cut = rows[step * group : (step + 1) * group, j * 128 : (j + 1) * 128]
                scratch[j, pl.ds(at, group), :] = cut
    for j in range(heads):
        for g in range(group):
            at = (j * group + g) * 128
            tile = scratch[j, pl.ds(g, steps * count, stride=group), :]
            out_ref[:, at : at + 128] = tile.astype(BF)


def weight_half(weight_ref, out_ref, which, copy):
    half = out_ref.shape[0]
    rows = half // PIECES
    cuts = [(pl.ds(which * half + i * rows, rows), pl.ds(i * rows, rows)) for i in range(PIECES)]
    return [copy(weight_ref.at[src], out_ref.at[dst]) for src, dst in cuts]


def project_own(attn_ref, weight_ref, out_ref):
    out_ref[...] = dot_f32(attn_ref[...], weight_ref[...], ((1,), (0,)))


def pick(options, index):
    chosen = options[0]
    for i in range(1, len(options)):
        chosen = jnp.where(index == i, options[i], chosen)
    return chosen


def project_other(heads_count, count, acc_ref, attn_ref, weight_ref, *outs):
    total = acc_ref[...] + dot_f32(attn_ref[...], weight_ref[...], ((1,), (0,)))
    head = lax.axis_index("head")
    steps = total.shape[0] // count
    share = count // heads_count
    for step in range(steps):
        slices = [
            total[step * count + x * share : step * count + (x + 1) * share]
            for x in range(heads_count)
        ]
        for c in range(heads_count):
            outs[c][step] = pick(slices, head ^ c)


def add_up(*refs):
    total = refs[0][...]
    for ref in refs[1:-1]:
        total = total + ref[...]
    refs[-1][...] = total.astype(BF)


def prepare(count, split, weight_hbm, dt_hbm, x_hbm, bc_hbm, gain_hbm, log_hbm, own_ref, other_ref,
            slope_ref, base_ref, dt_ref, x_ref, bc_ref, gain_ref, log_ref, sems, weight_sems):
    copy = copier(sems)
    first = [
        copy(dt_hbm, dt_ref),
        copy(x_hbm, x_ref),
        copy(bc_hbm, bc_ref),
        copy(gain_hbm, gain_ref),
        copy(log_hbm, log_ref),
    ]
    copy, which = copier(weight_sems), lax.axis_index("rep")
    weights = weight_half(weight_hbm, own_ref, which, copy)
    weights += weight_half(weight_hbm, other_ref, 1 - which, copy)
    for move in first + weights:
        move.start()
    for move in first:
        move.wait()
    me, rep = lax.axis_index("seq"), lax.axis_index("rep")
    _, steps, ns, part = slope_ref.shape
    block = part * 2 if split else part
    diagonal = lax.broadcasted_iota(jnp.int32, (ns, ns), 0) == lax.broadcasted_iota(
        jnp.int32, (ns, ns), 1
    )

    def column(row):
        return jnp.sum(jnp.where(diagonal, row, 0.0), axis=1, keepdims=True)

    drive = [column(bc_ref[step, 0, 0:1, :]) for step in range(steps)]
    read = [column(bc_ref[step, 0, 1:2, :]) for step in range(steps)]
    for c in range(count):
        first = (me ^ c) * block + (rep * part if split else 0)
        lanes = pl.ds(pl.multiple_of(first, 128), part)
        rate = -jnp.exp(log_ref[:, lanes])
        gain = gain_ref[:, lanes]
        kept = jnp.ones((ns, part), F32)
        added = jnp.zeros((ns, part), F32)
        for step in range(steps):
            dt = dt_ref[step, :, lanes]
            inputs = x_ref[step : step + 1, lanes].astype(F32)
            decay = jnp.exp(dt * rate)
            kept = kept * decay
            added = added * decay + drive[step] * (dt * inputs)
            slope_ref[c, step] = read[step] * kept
            base_ref[c, step] = (
                jnp.sum(read[step] * added, axis=0, keepdims=True) + gain * inputs
            )
    for move in weights:
        move.wait()


def mamba_steps(count, slope_ref, base_ref, own_ref, *rest):
    parts, out_ref = rest[:-1][::-1], rest[-1]
    me = lax.axis_index("seq")
    _, steps, ns, part = slope_ref.shape
    for c in range(count):
        source = own_ref if c == 0 else parts[c - 1]
        first = source.shape[0] - state_rows(part)
        rows = [
            source[first + 16 * i : first + 16 * (i + 1), :].astype(F32)
            for i in range(pl.cdiv(part, 256))
        ]
        state = jnp.concatenate(rows, axis=1)[:, :part]
        for step in range(steps):
            out_ref[step, me ^ c] = base_ref[c, step] + jnp.sum(
                slope_ref[c, step] * state, axis=0, keepdims=True
            )


def assemble(split, kept_ref, got_ref, mamba_ref, *rest):
    rep = lax.axis_index("rep")
    if split:
        other_ref, handoff_ref, out_ref, sems = rest
    else:
        handoff_ref, out_ref, sems = rest
    heads = kept_ref.shape[0]
    copy = copier(sems)
    moves = [
        copy(kept_ref, handoff_ref.at[0, pl.ds(rep * heads, heads)]),
        copy(got_ref, handoff_ref.at[0, pl.ds((1 - rep) * heads, heads)]),
    ]
    steps, count, _, part = mamba_ref.shape
    for step in range(steps):
        for b in range(count):
            if split:
                for ref, side in ((mamba_ref, rep), (other_ref, 1 - rep)):
                    lanes = pl.ds(pl.multiple_of((2 * b + side) * part, 128), part)
                    moves.append(copy(ref.at[step, b], out_ref.at[step, :, lanes]))
            else:
                moves.append(copy(mamba_ref.at[step, b], out_ref.at[step, :, pl.ds(b * part, part)]))
    run_all(moves)


def per_device(
    prefill_kv,
    kept_blocks,
    kept_counts,
    queries,
    new_kv,
    out_weight,
    prefill_state,
    a_log,
    step_input,
    step_dt,
    step_bc,
    skip_gain,
):
    count = lax.axis_size("seq")
    reps = lax.axis_size("rep")
    heads_count = lax.axis_size("head")
    requests, heads, tokens, width = prefill_kv.shape
    assert requests == count and tokens == BLOCK and reps == 2 and width == 256
    assert count & (count - 1) == 0 and heads_count & (heads_count - 1) == 0
    keep = kept_blocks.shape[2]
    keep_rep = keep // reps
    steps, _, q_heads, hd = queries.shape
    dec_heads = new_kv.shape[2]
    group = q_heads // dec_heads
    _, ns, block = prefill_state.shape
    split = block % (reps * 128) == 0
    part = block // reps if split else block
    all_rows = heads * steps * group
    assert all_rows <= 128
    channels = count * block
    shape = jax.ShapeDtypeStruct
    smem = pltpu.SMEM
    blocks = jnp.swapaxes(kept_blocks, 1, 2)

    prefill_kv, prefill_state, queries, new_kv = map(in_hbm, (prefill_kv, prefill_state, queries, new_kv))
    step_dt, step_bc, a_log, out_weight = map(in_hbm, (step_dt, step_bc, a_log, out_weight))
    step_input = in_hbm(step_input.reshape(steps, channels))
    skip_gain = in_hbm(skip_gain.reshape(1, -1))
    blocks, kept_counts = in_hbm(blocks), in_hbm(kept_counts)

    columns = out_weight.shape[1]
    half = heads * group * hd
    half_weight = pltpu.VMEM((half, columns), BF)
    *pieces, q_near, new_near, bias = call(
        functools.partial(stage, count),
        [shape((heads * BLOCK, width), BF)] * count
        + [
            shape(queries.shape, BF),
            shape(new_kv.shape, BF),
            shape((all_rows, count * BLOCK), F32),
        ],
        [HB] * 5,
        [VM] * (count + 3),
        [
            smem(blocks.shape, jnp.int32),
            smem(kept_counts.shape, jnp.int32),
            DMA((count * heads + 2,)),
            DMA((2,)),
        ],
    )(prefill_kv, queries, new_kv, blocks, kept_counts)
    moved = [shift(pieces[c], "seq", c) for c in range(count - 1, 0, -1)][::-1]
    states = call(
        functools.partial(stage_state, count, split),
        [shape((state_rows(part), width), BF)] * count,
        [HB],
        [VM] * count,
        [pltpu.VMEM((count, ns, part), F32), DMA((count,))],
    )(*after([prefill_state], pieces[0]))
    own_weight, other_weight, slope, base = call(
        functools.partial(prepare, count, split),
        [
            half_weight,
            half_weight,
            shape((count, steps, ns, part), F32),
            shape((count, steps, 1, part), F32),
        ],
        [HB] * 6,
        [VM] * 4,
        [
            pltpu.VMEM((steps, 1, channels), F32),
            pltpu.VMEM((steps, channels), BF),
            pltpu.VMEM(step_bc.shape, F32),
            pltpu.VMEM((1, channels), F32),
            pltpu.VMEM(a_log.shape, F32),
            DMA((5,)),
            DMA((2 * PIECES,)),
        ],
    )(*after([out_weight], pieces[0]), step_dt, step_input, step_bc, skip_gain, a_log)

    *moved, own_weight = after([*moved[::-1], own_weight])
    kv = [pieces[0], *moved[::-1]]
    rows = steps * group
    half_shape = (heads, keep_rep, BLOCK, width)
    *sends, kept, sent = call(
        functools.partial(attend, count, heads),
        [shape((rows, width), BF)]
        + [shape((rows + state_rows(part), width), BF)] * (count - 1)
        + [shape(half_shape, BF)] * 2,
        [HB] * 2 + [VM] * (2 + 2 * count),
        [VM] * (count + 2),
        [
            smem(blocks.shape, jnp.int32),
            smem(kept_counts.shape, jnp.int32),
            pltpu.VMEM((BLOCK, width), BF),
            DMA((2, heads, keep_rep)),
            DMA((2,)),
        ],
    )(blocks, kept_counts, q_near, new_near, bias, *kv, *states[1:])
    gathered = [shift(sends[c], "seq", c) for c in range(count - 1, 0, -1)][::-1]
    attn = call(
        functools.partial(collect, count, heads, steps, group),
        shape((steps * count, half), BF),
        [VM] * count,
        VM,
        [pltpu.VMEM((heads, steps * count * group, hd), F32)],
    )(sends[0], *gathered[::-1])
    attn_other = shift(attn, "rep", 1)
    own_sum = call(
        project_own, shape((steps * count, columns), F32), [VM, VM], VM, us=0.7
    )(attn, own_weight)
    share = count // heads_count
    sums = call(
        functools.partial(project_other, heads_count, count),
        [shape((steps, share, columns), F32)] * heads_count,
        [VM, VM, VM],
        [VM] * heads_count,
        us=0.7,
    )(own_sum, attn_other, other_weight)
    sums = [sums[0]] + [shift(sums[c], "head", c) for c in range(1, heads_count)]
    mamba = call(
        functools.partial(mamba_steps, count),
        shape((steps, count, 1, part), F32),
        [VM] * (2 + count),
        VM,
    )(slope, base, *after(states[:1], attn), *gathered[::-1])
    got = shift(after([sent], mamba)[0], "rep", 1)
    kept = after([kept], sums[0])[0]
    operands = [kept, got, mamba] + ([shift(mamba, "rep", 1)] if split else [])
    handoff, mamba_out = call(
        functools.partial(assemble, split),
        [
            shape((1, dec_heads, keep_rep, BLOCK, width), BF),
            shape((steps, 1, channels), F32),
        ],
        [VM] * len(operands),
        [HB] * 2,
        [DMA((2 + steps * count * (2 if split else 1),))],
    )(*operands)
    sums[1:] = after(sums[1:], handoff)
    proj_out = call(
        add_up, shape((steps, share, columns), BF), [VM] * heads_count, VM, us=0.6
    )(*sums)
    return handoff, proj_out, mamba_out


def solution(mesh):
    return jax.shard_map(
        per_device,
        mesh=mesh,
        in_specs=(
            P("groups", ("head", "rep"), "seq", None),
            P("groups", None, None),
            P("groups", None),
            P(None, ("groups", "seq"), "head", None),
            P(None, ("groups", "seq"), "head", None),
            P("head", ("seq", "rep")),
            P("groups", None, ("head", "seq")),
            P(None, "head"),
            P(None, ("groups", "seq"), "head"),
            P(None, ("groups", "seq"), "head"),
            P(None, ("groups", "seq"), None, None),
            P("head"),
        ),
        out_specs=(
            P(("groups", "seq"), "head", "rep", None, None),
            P(None, ("groups", "head"), ("seq", "rep")),
            P(None, ("groups", "seq"), "head"),
        ),
        check_vma=False,
    )
```

time: 42.7 us -> 34.1 us (0.80)
  starting transfers between devices: 17.6 us -> 12.4 us
  waiting for transfers between devices: 14.1 us -> 10.2 us
    ppermute x13 -> x10, starting transfers between devices: 17.6 us -> 12.4 us  [shift(): return lax.ppermute(x, axis, [(i, i ^ c) for i in range(size)])]
    ppermute x13 -> x10, waiting for transfers between devices: 14.1 us -> 10.2 us  [shift(): return lax.ppermute(x, axis, [(i, i ^ c) for i in range(size)])]
    pallas_call x4 -> x5, Pallas kernels: 3.6 us -> 4.04 us  [the longest x1 1.73 us: per_device(): call(functools.partial(attend, count, heads), [shape((rows, width), BF)]...]
  transfers between devices with their start and end apart: 13 -> 10, of which waited for: 6 -> 5; matrix products, arithmetic and copies ran while one was open for 0% -> 0% of each run, Pallas kernels for 18% -> 20%
where the time goes in v5:
time: 34.1 us; the launch traced here: 33.9 us
  starting transfers between devices  12.4 us (36%)
  Pallas kernels  10.6 us (31%)
  waiting for transfers between devices  10.2 us (30%)
  between operations  0.7 us (2%)
    ppermute x10, starting transfers between devices, shift(): return lax.ppermute(x, axis, [(i, i ^ c) for i in range(size)])  12.4 us
    ppermute x10, waiting for transfers between devices, shift(): return lax.ppermute(x, axis, [(i, i ^ c) for i in range(size)])  10.2 us
    pallas_call x1, Pallas kernels, per_device(): call(functools.partial(prepare, count, split), [half_weight, half_weight,...  3.76 us
    pallas_call x1, Pallas kernels, per_device(): call(functools.partial(attend, count, heads), [shape((rows, width), BF)]...  1.73 us
    pallas_call x1, Pallas kernels, per_device(): call(functools.partial(stage, count), [shape((heads * BLOCK, width), BF)]...  1.18 us
    pallas_call x1, Pallas kernels, per_device(): call(functools.partial(stage_state, count, split), [shape((state_rows(par...  0.98 us
    pallas_call x1, Pallas kernels, per_device(): call(functools.partial(assemble, split), [shape((1, dec_heads, keep_rep,...  0.89 us
  transfers between devices with their start and end apart: 10, of which 5 were waited for; matrix products, arithmetic and copies ran while one was open for 0% of the time, Pallas kernels for 20%

profile of v5, /device:TPU:0, one launch (start us, length us, event | category | flops | bytes accessed | tf_op | source)
XLA Modules:
  0.0 33.9 jit_solution(141951152023259662)
XLA Ops:
  0.6 1.2 %shard_map.139 = (bf16[256,256]{1,0:T(8,128)(2,1)S(1)}, bf16[256,256]{1,0:T(8,128)(2,1)S(1)}, bf16[256,256]{1,0:T(8,128)(2,1)S(1)}, bf16[256,256]{1,0:T(8,128)(2...) custom-call(bf16[4,2,128,256]{3,2,1,0:T(8,128)(2,1)} %kv_ref.1, ...), custom_call_target="tpu_custom_call" | custom-call | bytes 36000 | tf_op jit(solution)/shard_map/pallas_call | solution.py:438
  1.8 5.1 %collective-permute-start = (bf16[256,256]{1,0:T(8,128)(2,1)S(1)}, bf16[256,256]{1,0:T(8,128)(2,1)S(1)}, u32[]{:S(2)}, u32[]{:S(2)}) collective-permute-start(bf16[256,256]{1,0:T(8,128)(2,1)S(1)} %get-tuple-element.42), channel_id=1, source_target_pairs={{0,12},{4,8},{8,4},{12,0},{1,13},{5,9},{9,5},{13,1},{2,14},{6,10},... | collective-permute-start | bytes 393224 | tf_op jit(solution)/shard_map/ppermute | solution.py:22
  6.9 0.0 collective-permute-start.1
  6.9 0.6 %collective-permute-start.2 = (bf16[256,256]{1,0:T(8,128)(2,1)S(1)}, bf16[256,256]{1,0:T(8,128)(2,1)S(1)}, u32[]{:S(2)}, u32[]{:S(2)}) collective-permute-start(bf16[256,256]{1,0:T(8,128)(2,1)S(1)} %get-tuple-element.44), channel_id=1, source_target_pairs={{0,4},{4,0},{8,12},{12,8},{1,5},{5,1},{9,13},{13,9},{2,6},{6,2},{1... | collective-permute-start | bytes 393224 | tf_op jit(solution)/shard_map/ppermute | solution.py:22
  7.6 1.0 %shard_map.141 = (bf16[64,256]{1,0:T(8,128)(2,1)S(1)}, bf16[64,256]{1,0:T(8,128)(2,1)S(1)}, bf16[64,256]{1,0:T(8,128)(2,1)S(1)}, bf16[64,256]{1,0:T(8,128)(2,1)S(1)}) custom-call(f32[4,16,2048]{2,1,0:T(8,128)} %state_ref), custom_call_target="tpu_custom_call" | custom-call | bytes 36000 | tf_op jit(solution)/shard_map/pallas_call | solution.py:456
  8.6 3.8 %shard_map.140 = (bf16[2048,1024]{1,0:T(8,128)(2,1)S(1)}, bf16[2048,1024]{1,0:T(8,128)(2,1)S(1)}, f32[4,2,16,1024]{3,2,1,0:T(8,128)S(1)}, f32[4,2,1,1024]{3,2,1,0:T(1,128)S(1)}) custom-call(bf16[4096,1024]{1,0:T(8,128)(2,1)} %weight_hbm, f32[2,1,8192]{2,1,0:T(1,128)} %dt_hbm.1, bf16[2,8192]{1,0:T(2,128)(2,1)} %bitcast.3, f32[2,1,2,16]{3,2,1,0:T(2,128)} %bc_hbm.1, ...), custom_call_target="tpu_custom_call" | custom-call | bytes 36000 | tf_op jit(solution)/shard_map/pallas_call | solution.py:463
  12.3 0.0 collective-permute-done.rest_3_
  12.3 5.7 %collective-permute-done.1.rest_2_ = bf16[256,256]{1,0:T(8,128)(2,1)S(1)} collective-permute-done((bf16[256,256]{1,0:T(8,128)(2,1)S(1)}, bf16[256,256]{1,0:T(8,128)(2,1)S(1)}, u32[]{:S(2)}, u32[]{:S(2)}) %collective-permute-start.1) | collective-permute-done | bytes 131104 | tf_op jit(solution)/shard_map/ppermute | solution.py:22
  18.0 0.0 collective-permute-done.2.rest_1_
  18.0 1.7 %shard_map.142 = (bf16[16,256]{1,0:T(8,128)(2,1)S(1)}, bf16[80,256]{1,0:T(8,128)(2,1)S(1)}, bf16[80,256]{1,0:T(8,128)(2,1)S(1)}, bf16[80,256]{1,0:T(8,128)(2,1)S...) custom-call(s32[4,2,8]{2,1,0:T(2,128)} %bitcast.6, s32[4,8]{1,0:T(4,128)} %counts_ref.3, ...), custom_call_target="tpu_custom_call" | custom-call | bytes 36000 | tf_op jit(solution)/shard_map/pallas_call | solution.py:488
  19.8 2.5 %collective-permute-start.3 = (bf16[80,256]{1,0:T(8,128)(2,1)S(1)}, bf16[80,256]{1,0:T(8,128)(2,1)S(1)}, u32[]{:S(2)}, u32[]{:S(2)}) collective-permute-start(bf16[80,256]{1,0:T(8,128)(2,1)S(1)} %get-tuple-element.56), channel_id=1, source_target_pairs={{0,12},{4,8},{8,4},{12,0},{1,13},{5,9},{9,5},{13,1},{2,14},{6,10},... | collective-permute-start | bytes 122888 | tf_op jit(solution)/shard_map/ppermute | solution.py:22
  22.3 0.0 collective-permute-start.4
  22.3 1.9 %collective-permute-start.5 = (bf16[80,256]{1,0:T(8,128)(2,1)S(1)}, bf16[80,256]{1,0:T(8,128)(2,1)S(1)}, u32[]{:S(2)}, u32[]{:S(2)}) collective-permute-start(bf16[80,256]{1,0:T(8,128)(2,1)S(1)} %get-tuple-element.58), channel_id=1, source_target_pairs={{0,4},{4,0},{8,12},{12,8},{1,5},{5,1},{9,13},{13,9},{2,6},{6,2},{1... | collective-permute-start | bytes 122888 | tf_op jit(solution)/shard_map/ppermute | solution.py:22
  24.2 1.4 %collective-permute-done.3.rest_1_.rest_0_ = bf16[80,256]{1,0:T(8,128)(2,1)S(1)} collective-permute-done((bf16[80,256]{1,0:T(8,128)(2,1)S(1)}, bf16[80,256]{1,0:T(8,128)(2,1)S(1)}, u32[]{:S(2)}, u32[]{:S(2)}) %collective-permute-start.3) | collective-permute-done | bytes 40992 | tf_op jit(solution)/shard_map/ppermute | solution.py:22
  25.6 1.6 %collective-permute-done.4.rest_2_.rest_1_ = bf16[80,256]{1,0:T(8,128)(2,1)S(1)} collective-permute-done((bf16[80,256]{1,0:T(8,128)(2,1)S(1)}, bf16[80,256]{1,0:T(8,128)(2,1)S(1)}, u32[]{:S(2)}, u32[]{:S(2)}) %collective-permute-start.4) | collective-permute-done | bytes 40992 | tf_op jit(solution)/shard_map/ppermute | solution.py:22
  27.2 0.0 collective-permute-done.5.rest_3_.rest_2_
  27.2 0.1 shard_map.146.mamba_ref
  27.3 0.1 collective-permute-start.7
  27.4 0.5 %collective-permute-start.6 = (bf16[8,2048]{1,0:T(8,128)(2,1)S(1)}, bf16[8,2048]{1,0:T(8,128)(2,1)S(1)}, u32[]{:S(2)}, u32[]{:S(2)}) collective-permute-start(bf16[8,2048]{1,0:T(8,128)(2,1)S(1)} %shard_map.143.attn_ref), channel_id=1, source_target_pairs={{0,1},{1,0},{2,3},{3,2},{4,5},{5,4},{6,7},{7,6},{8,9},{9,8},{10,11... | collective-permute-start | bytes 98312 | tf_op jit(solution)/shard_map/ppermute | solution.py:22
  27.9 0.1 collective-permute-start.8
  28.0 0.6 %shard_map.144.acc_ref = f32[8,1024]{1,0:T(8,128)S(1)} custom-call(bf16[8,2048]{1,0:T(8,128)(2,1)S(1)} %shard_map.143.attn_ref, bf16[2048,1024]{1,0:T(8,128)(2,1)S(1)} %get-tuple-element.59.weight_ref), custom_call_target="tpu_custom_call" | custom-call | bytes 25200 | tf_op jit(solution)/shard_map/pallas_call | solution.py:512
  28.6 0.2 collective-permute-done.6.attn_ref
  28.8 0.7 %shard_map.145 = (f32[2,2,1024]{2,1,0:T(2,128)S(1)}, f32[2,2,1024]{2,1,0:T(2,128)S(1)}) custom-call(f32[8,1024]{1,0:T(8,128)S(1)} %shard_map.144.acc_ref, bf16[8,2048]{1,0:T(8,128)(2,1)S(1)} %collective-permute-done.6.attn_ref, bf16[2048,1024]{1,0:T(8,128)(2,1)S(1)} %get-tuple-element.60.weight_ref), custom_call_target="tpu_custom_call" | custom-call | bytes 25200 | tf_op jit(solution)/shard_map/pallas_call | solution.py:516
  29.5 1.5 %collective-permute-start.9 = (f32[2,2,1024]{2,1,0:T(2,128)S(1)}, f32[2,2,1024]{2,1,0:T(2,128)S(1)}, u32[]{:S(2)}, u32[]{:S(2)}) collective-permute-start(f32[2,2,1024]{2,1,0:T(2,128)S(1)} %get-tuple-element.70), channel_id=1, source_target_pairs={{0,2},{2,0},{1,3},{3,1},{4,6},{6,4},{5,7},{7,5},{8,10},{10,8},{9,1... | collective-permute-start | bytes 49160 | tf_op jit(solution)/shard_map/ppermute | solution.py:22
  31.0 0.0 collective-permute-done.8.rest_0_
  31.0 0.0 collective-permute-done.7.got_ref
  31.0 0.9 %shard_map.147 = (bf16[1,4,1,128,256]{4,3,2,1,0:T(8,128)(2,1)}, f32[2,1,8192]{2,1,0:T(1,128)}) custom-call(bf16[2,1,128,256]{3,2,1,0:T(8,128)(2,1)S(1)} %get-tuple-element.62.kept_ref, bf16[2,1,128,256]{3,2,1,0:T(8,128)(2,1)S(1)} %collective-permute-done.7.got_ref, f32[2,4,1,1024]{3,2,1,0:T(1,128)S(1)} %shard_map.146.mamba_ref, ...), custom_call_target="tpu_custom_call" | custom-call | bytes 36000 | tf_op jit(solution)/shard_map/pallas_call | solution.py:533
  31.9 1.4 %collective-permute-done.9.refs_1_ = f32[2,2,1024]{2,1,0:T(2,128)S(1)} collective-permute-done((f32[2,2,1024]{2,1,0:T(2,128)S(1)}, f32[2,2,1024]{2,1,0:T(2,128)S(1)}, u32[]{:S(2)}, u32[]{:S(2)}) %collective-permute-start.9) | collective-permute-done | bytes 16416 | tf_op jit(solution)/shard_map/ppermute | solution.py:22
  33.2 0.6 %shard_map.148 = bf16[2,2,1024]{2,1,0:T(2,128)(2,1)} custom-call(f32[2,2,1024]{2,1,0:T(2,128)S(1)} %get-tuple-element.61.refs_0_, f32[2,2,1024]{2,1,0:T(2,128)S(1)} %collective-permute-done.9.refs_1_), custom_call_target="tpu_custom_call" | custom-call | bytes 21600 | tf_op jit(solution)/shard_map/pallas_call | solution.py:544
  (1 shorter events, 0.0 us)
Async XLA Ops:
  1.8 10.5 %collective-permute-start = (bf16[256,256]{1,0:T(8,128)(2,1)S(1)}, bf16[256,256]{1,0:T(8,128)(2,1)S(1)}, u32[]{:S(2)}, u32[]{:S(2)}) collective-permute-start(bf16[256,256]{1,0:T(8,128)(2,1)S(1)} %get-tuple-element.42), channel_id=1, source_target_pairs={{0,12},{4,8},{8,4},{12,0},{1,13},{5,9},{9,5},{13,1},{2,14},{6,10},... | collective-permute-start | bytes 393224 | tf_op jit(solution)/shard_map/ppermute | solution.py:22
  6.9 11.1 %collective-permute-start.1 = (bf16[256,256]{1,0:T(8,128)(2,1)S(1)}, bf16[256,256]{1,0:T(8,128)(2,1)S(1)}, u32[]{:S(2)}, u32[]{:S(2)}) collective-permute-start(bf16[256,256]{1,0:T(8,128)(2,1)S(1)} %get-tuple-element.43), channel_id=1, source_target_pairs={{0,8},{4,12},{8,0},{12,4},{1,9},{5,13},{9,1},{13,5},{2,10},{6,14},... | collective-permute-start | bytes 393224 | tf_op jit(solution)/shard_map/ppermute | solution.py:22
  6.9 11.1 %collective-permute-start.2 = (bf16[256,256]{1,0:T(8,128)(2,1)S(1)}, bf16[256,256]{1,0:T(8,128)(2,1)S(1)}, u32[]{:S(2)}, u32[]{:S(2)}) collective-permute-start(bf16[256,256]{1,0:T(8,128)(2,1)S(1)} %get-tuple-element.44), channel_id=1, source_target_pairs={{0,4},{4,0},{8,12},{12,8},{1,5},{5,1},{9,13},{13,9},{2,6},{6,2},{1... | collective-permute-start | bytes 393224 | tf_op jit(solution)/shard_map/ppermute | solution.py:22
  19.8 5.9 %collective-permute-start.3 = (bf16[80,256]{1,0:T(8,128)(2,1)S(1)}, bf16[80,256]{1,0:T(8,128)(2,1)S(1)}, u32[]{:S(2)}, u32[]{:S(2)}) collective-permute-start(bf16[80,256]{1,0:T(8,128)(2,1)S(1)} %get-tuple-element.56), channel_id=1, source_target_pairs={{0,12},{4,8},{8,4},{12,0},{1,13},{5,9},{9,5},{13,1},{2,14},{6,10},... | collective-permute-start | bytes 122888 | tf_op jit(solution)/shard_map/ppermute | solution.py:22
  22.3 4.9 %collective-permute-start.4 = (bf16[80,256]{1,0:T(8,128)(2,1)S(1)}, bf16[80,256]{1,0:T(8,128)(2,1)S(1)}, u32[]{:S(2)}, u32[]{:S(2)}) collective-permute-start(bf16[80,256]{1,0:T(8,128)(2,1)S(1)} %get-tuple-element.57), channel_id=1, source_target_pairs={{0,8},{4,12},{8,0},{12,4},{1,9},{5,13},{9,1},{13,5},{2,10},{6,14},... | collective-permute-start | bytes 122888 | tf_op jit(solution)/shard_map/ppermute | solution.py:22
  22.3 4.9 %collective-permute-start.5 = (bf16[80,256]{1,0:T(8,128)(2,1)S(1)}, bf16[80,256]{1,0:T(8,128)(2,1)S(1)}, u32[]{:S(2)}, u32[]{:S(2)}) collective-permute-start(bf16[80,256]{1,0:T(8,128)(2,1)S(1)} %get-tuple-element.58), channel_id=1, source_target_pairs={{0,4},{4,0},{8,12},{12,8},{1,5},{5,1},{9,13},{13,9},{2,6},{6,2},{1... | collective-permute-start | bytes 122888 | tf_op jit(solution)/shard_map/ppermute | solution.py:22
  27.3 3.7 %collective-permute-start.7 = (bf16[2,1,128,256]{3,2,1,0:T(8,128)(2,1)S(1)}, bf16[2,1,128,256]{3,2,1,0:T(8,128)(2,1)S(1)}, u32[]{:S(2)}, u32[]{:S(2)}) collective-permute-start(bf16[2,1,128,256]{3,2,1,0:T(8,128)(2,1)S(1)} %get-tuple-element.68), channel_id=1, source_target_pairs={{0,1},{1,0},{2,3},{3,2},{4,5},{5,4},{6,7},{7,6},{8,9},{9,8},{10,11... | collective-permute-start | bytes 393224 | tf_op jit(solution)/shard_map/ppermute | solution.py:22
  27.4 1.4 %collective-permute-start.6 = (bf16[8,2048]{1,0:T(8,128)(2,1)S(1)}, bf16[8,2048]{1,0:T(8,128)(2,1)S(1)}, u32[]{:S(2)}, u32[]{:S(2)}) collective-permute-start(bf16[8,2048]{1,0:T(8,128)(2,1)S(1)} %shard_map.143.attn_ref), channel_id=1, source_target_pairs={{0,1},{1,0},{2,3},{3,2},{4,5},{5,4},{6,7},{7,6},{8,9},{9,8},{10,11... | collective-permute-start | bytes 98312 | tf_op jit(solution)/shard_map/ppermute | solution.py:22
  27.9 3.1 %collective-permute-start.8 = (f32[2,4,1,1024]{3,2,1,0:T(1,128)S(1)}, f32[2,4,1,1024]{3,2,1,0:T(1,128)S(1)}, u32[]{:S(2)}, u32[]{:S(2)}) collective-permute-start(f32[2,4,1,1024]{3,2,1,0:T(1,128)S(1)} %shard_map.146.mamba_ref), channel_id=1, source_target_pairs={{0,1},{1,0},{2,3},{3,2},{4,5},{5,4},{6,7},{7,6},{8,9},{9,8},{10,11... | collective-permute-start | bytes 98312 | tf_op jit(solution)/shard_map/ppermute | solution.py:22
  29.5 3.8 %collective-permute-start.9 = (f32[2,2,1024]{2,1,0:T(2,128)S(1)}, f32[2,2,1024]{2,1,0:T(2,128)S(1)}, u32[]{:S(2)}, u32[]{:S(2)}) collective-permute-start(f32[2,2,1024]{2,1,0:T(2,128)S(1)} %get-tuple-element.70), channel_id=1, source_target_pairs={{0,2},{2,0},{1,3},{3,1},{4,6},{6,4},{5,7},{7,5},{8,10},{10,8},{9,1... | collective-permute-start | bytes 49160 | tf_op jit(solution)/shard_map/ppermute | solution.py:22

commit v6 on v5

--- a/solution.py
+++ b/solution.py
@@ -69,9 +69,16 @@
         out_ref[first + i * 16 : first + (i + 1) * 16, :] = cut.astype(BF)
 
 
-def stage(count, kv_ref, q_ref, new_ref, blocks_ref, counts_ref, *rest):
+def own_state(state_ref, c, split, part):
+    me, rep = lax.axis_index("seq"), lax.axis_index("rep")
+    if split:
+        return state_ref.at[me ^ c, :, pl.ds(pl.multiple_of(rep * part, 128), part)]
+    return state_ref.at[me ^ c]
+
+
+def stage(count, split, kv_ref, q_ref, new_ref, state_ref, blocks_ref, counts_ref, *rest):
     pieces = rest[:count]
-    q_out, new_out, bias_out, blocks, counts, sems, early = rest[count:]
+    q_out, new_out, bias_out, pick_out, loaded, blocks, counts, sems, early = rest[count:]
     me, rep = lax.axis_index("seq"), lax.axis_index("rep")
     heads = kv_ref.shape[1]
     copy = copier(sems)
@@ -82,18 +89,26 @@
     moves += [copy(q_ref, q_out), copy(new_ref, new_out)]
     copy = copier(early)
     first = [copy(blocks_ref, blocks), copy(counts_ref, counts)]
+    first.append(copy(own_state(state_ref, 1, split, loaded.shape[1]), loaded))
     for move in moves + first:
         move.start()
     for move in first:
         move.wait()
+    pack_state(loaded[...], pieces[1], heads * BLOCK)
     head_first = lax.axis_index("head") * new_ref.shape[2] + rep * heads
     rows = bias_out.shape[0] // heads
+    keep_rep = pick_out.shape[2]
     for j in range(heads):
+        live_count = counts[me, head_first + j]
         for c in range(count):
             live = jnp.int32(0)
-            for slot in range(blocks.shape[1]):
-                hit = blocks[me, slot, head_first + j] == (me ^ c)
-                live = live | (hit & (slot < counts[me, head_first + j])).astype(jnp.int32)
+            for side in range(2):
+                for k in range(keep_rep):
+                    slot = (rep if side == 0 else 1 - rep) * keep_rep + k
+                    hit = (blocks[me, slot, head_first + j] == (me ^ c)) & (slot < live_count)
+                    one = jnp.where(hit, 1.0, 0.0).astype(F32)
+                    pick_out[side, j, k, c] = jnp.full(pick_out.shape[4:], one, F32).astype(BF)
+                    live = live | hit.astype(jnp.int32)
             dead = jnp.where(live > 0, 0.0, NEG).astype(F32)
             bias_out[j * rows : (j + 1) * rows, c * BLOCK : (c + 1) * BLOCK] = jnp.full(
                 (rows, BLOCK), dead, F32
@@ -103,20 +118,17 @@
 
 
 def stage_state(count, split, state_ref, *rest):
-    outs, loaded, sems = rest[:count], rest[count], rest[count + 1]
-    me, rep = lax.axis_index("seq"), lax.axis_index("rep")
-    part = loaded.shape[2]
+    outs, loaded, sems = rest[: count - 1], rest[count - 1], rest[count]
     copy = copier(sems)
-    moves = []
-    for c in range(count):
-        if split:
-            src = state_ref.at[me ^ c, :, pl.ds(pl.multiple_of(rep * part, 128), part)]
-        else:
-            src = state_ref.at[me ^ c]
-        moves.append(copy(src, loaded.at[c]))
-    run_all(moves)
-    for c in range(count):
-        pack_state(loaded[c], outs[c], 0)
+    steps_away = [0, *range(2, count)]
+    run_all(
+        [
+            copy(own_state(state_ref, c, split, loaded.shape[2]), loaded.at[i])
+            for i, c in enumerate(steps_away)
+        ]
+    )
+    for i in range(count - 1):
+        pack_state(loaded[i], outs[i], 0)
 
 
 def dot_f32(a, b, contract):
@@ -147,44 +159,8 @@
     return dot_f32(weights, values, ((1,), (0,)))
 
 
-def choose(count, pieces, blocks, counts, zeros, sems, kept_ref, sent_ref):
-    me, rep = lax.axis_index("seq"), lax.axis_index("rep")
-    heads, keep_rep = kept_ref.shape[:2]
-    head_first = lax.axis_index("head") * (2 * heads) + rep * heads
-    waits = []
-    for side, out in ((1, sent_ref), (0, kept_ref)):
-        owner = rep if side == 0 else 1 - rep
-        for j in range(heads):
-            live_count = counts[me, head_first + j]
-            for k in range(keep_rep):
-                slot = owner * keep_rep + k
-                source = blocks[me, slot, head_first + j] ^ me
-                live = slot < live_count
-                sem = sems.at[side, j, k]
-                for c in range(count):
-                    piece = pieces[c].at[pl.ds(j * BLOCK, BLOCK)]
-
-                    @pl.when(live & (source == c))
-                    def _():
-                        pltpu.make_async_copy(piece, out.at[j, k], sem).start()
-
-                @pl.when(jnp.logical_not(live))
-                def _():
-                    pltpu.make_async_copy(zeros, out.at[j, k], sem).start()
-
-                waits.append(pltpu.make_async_copy(zeros, out.at[j, k], sem))
-    return waits
-
-
-def attend(count, heads, blocks_ref, counts_ref, q_ref, new_ref, bias_ref, *rest):
-    pieces, states = rest[:count], rest[count : 2 * count - 1]
-    outs, rest = rest[2 * count - 1 : 3 * count - 1], rest[3 * count - 1 :]
-    kept_ref, sent_ref, blocks, counts, zeros, sems, early = rest
-    copy = copier(early)
-    scalars = [copy(blocks_ref, blocks), copy(counts_ref, counts)]
-    for move in scalars:
-        move.start()
-    zeros[...] = jnp.zeros_like(zeros)
+def attend(count, heads, q_ref, new_ref, bias_ref, pick_ref, *rest):
+    pieces, (out_ref, kept_ref, sent_ref) = rest[:count], rest[count:]
     rep = lax.axis_index("rep")
     queries = query_rows(q_ref, heads)
     rows, hd = queries[0].shape
@@ -216,9 +192,6 @@
     weights = jnp.where(alive, jnp.exp(scores - top), 0.0)
     total = jnp.sum(weights, axis=1, keepdims=True)
     weights = weights.astype(BF)
-    for move in scalars:
-        move.wait()
-    waits = choose(count, pieces, blocks, counts, zeros, sems, kept_ref, sent_ref)
     summed = []
     for j in range(heads):
         parts = [
@@ -232,20 +205,38 @@
         total = total + weight
         summed = summed + weight.astype(BF).astype(F32) * fresh_values[step]
     result = (summed / total).astype(BF)
+    for j in range(2):
+        half = result[j * rows : (j + 1) * rows] if j < heads else jnp.zeros((rows, hd), BF)
+        out_ref[:, j * hd : (j + 1) * hd] = half
+    tile = pick_ref.shape[4]
+    for side, ref in ((1, sent_ref), (0, kept_ref)):
+        for j in range(heads):
+            for k in range(ref.shape[1]):
+                total = None
+                for c in range(count):
+                    piece = pieces[c][j * BLOCK : (j + 1) * BLOCK, :].reshape(-1, tile, 2 * hd)
+                    term = piece * pick_ref[side, j, k, c][None]
+                    total = term if total is None else total + term
+                ref[j, k] = total.reshape(BLOCK, 2 * hd)
+
+
+def collect(count, heads, steps, group, slope_ref, base_ref, *rest):
+    parts = rest[:1] + rest[1:count][::-1]
+    states = rest[count : 2 * count]
+    out_ref, mamba_ref, scratch = rest[2 * count :]
+    me = lax.axis_index("seq")
+    ns, part = slope_ref.shape[2:]
     for c in range(count):
-        for j in range(2):
-            half = result[j * rows : (j + 1) * rows] if j < heads else jnp.zeros((rows, hd), BF)
-            outs[c][:rows, j * hd : (j + 1) * hd] = half
-        if c:
-            outs[c][rows:, :] = states[c - 1][...]
-    for move in waits:
-        move.wait()
-
-
-def collect(count, heads, steps, group, *rest):
-    parts = rest[:1] + rest[1:count][::-1]
-    out_ref, scratch = rest[count:]
-    me = lax.axis_index("seq")
+        first = states[c].shape[0] - state_rows(part)
+        rows = [
+            states[c][first + 16 * i : first + 16 * (i + 1), :].astype(F32)
+            for i in range(pl.cdiv(part, 256))
+        ]
+        state = jnp.concatenate(rows, axis=1)[:, :part]
+        for step in range(steps):
+            mamba_ref[step, me ^ c] = base_ref[c, step] + jnp.sum(
+                slope_ref[c, step] * state, axis=0, keepdims=True
+            )
     for c in range(count):
         rows = parts[c][: steps * group, :].astype(F32)
         for j in range(heads):
@@ -347,24 +338,6 @@
             )
     for move in weights:
         move.wait()
-
-
-def mamba_steps(count, slope_ref, base_ref, own_ref, *rest):
-    parts, out_ref = rest[:-1][::-1], rest[-1]
-    me = lax.axis_index("seq")
-    _, steps, ns, part = slope_ref.shape
-    for c in range(count):
-        source = own_ref if c == 0 else parts[c - 1]
-        first = source.shape[0] - state_rows(part)
-        rows = [
-            source[first + 16 * i : first + 16 * (i + 1), :].astype(F32)
-            for i in range(pl.cdiv(part, 256))
-        ]
-        state = jnp.concatenate(rows, axis=1)[:, :part]
-        for step in range(steps):
-            out_ref[step, me ^ c] = base_ref[c, step] + jnp.sum(
-                slope_ref[c, step] * state, axis=0, keepdims=True
-            )
 
 
 def assemble(split, kept_ref, got_ref, mamba_ref, *rest):
@@ -435,30 +408,36 @@
     columns = out_weight.shape[1]
     half = heads * group * hd
     half_weight = pltpu.VMEM((half, columns), BF)
-    *pieces, q_near, new_near, bias = call(
-        functools.partial(stage, count),
-        [shape((heads * BLOCK, width), BF)] * count
+    tall = heads * BLOCK
+    *pieces, q_near, new_near, bias, picks = call(
+        functools.partial(stage, count, split),
+        [
+            shape((tall + (state_rows(part) if c == 1 else 0), width), BF)
+            for c in range(count)
+        ]
         + [
             shape(queries.shape, BF),
             shape(new_kv.shape, BF),
             shape((all_rows, count * BLOCK), F32),
+            shape((reps, heads, keep_rep, count, 16, width), BF),
         ],
-        [HB] * 5,
-        [VM] * (count + 3),
+        [HB] * 6,
+        [VM] * (count + 4),
         [
+            pltpu.VMEM((ns, part), F32),
             smem(blocks.shape, jnp.int32),
             smem(kept_counts.shape, jnp.int32),
             DMA((count * heads + 2,)),
-            DMA((2,)),
+            DMA((3,)),
         ],
-    )(prefill_kv, queries, new_kv, blocks, kept_counts)
+    )(prefill_kv, queries, new_kv, prefill_state, blocks, kept_counts)
     moved = [shift(pieces[c], "seq", c) for c in range(count - 1, 0, -1)][::-1]
-    states = call(
+    home_state, *states = call(
         functools.partial(stage_state, count, split),
-        [shape((state_rows(part), width), BF)] * count,
+        [shape((state_rows(part), width), BF)] * (count - 1),
         [HB],
-        [VM] * count,
-        [pltpu.VMEM((count, ns, part), F32), DMA((count,))],
+        [VM] * (count - 1),
+        [pltpu.VMEM((count - 1, ns, part), F32), DMA((count - 1,))],
     )(*after([prefill_state], pieces[0]))
     own_weight, other_weight, slope, base = call(
         functools.partial(prepare, count, split),
@@ -481,33 +460,25 @@
         ],
     )(*after([out_weight], pieces[0]), step_dt, step_input, step_bc, skip_gain, a_log)
 
+    states = after(states, own_weight)
+    states = [shift(states[c - 2], "seq", c) for c in range(count - 1, 1, -1)][::-1]
     *moved, own_weight = after([*moved[::-1], own_weight])
     kv = [pieces[0], *moved[::-1]]
-    rows = steps * group
     half_shape = (heads, keep_rep, BLOCK, width)
-    *sends, kept, sent = call(
+    rows, kept, sent = call(
         functools.partial(attend, count, heads),
-        [shape((rows, width), BF)]
-        + [shape((rows + state_rows(part), width), BF)] * (count - 1)
-        + [shape(half_shape, BF)] * 2,
-        [HB] * 2 + [VM] * (2 + 2 * count),
-        [VM] * (count + 2),
-        [
-            smem(blocks.shape, jnp.int32),
-            smem(kept_counts.shape, jnp.int32),
-            pltpu.VMEM((BLOCK, width), BF),
-            DMA((2, heads, keep_rep)),
-            DMA((2,)),
-        ],
-    )(blocks, kept_counts, q_near, new_near, bias, *kv, *states[1:])
-    gathered = [shift(sends[c], "seq", c) for c in range(count - 1, 0, -1)][::-1]
-    attn = call(
+        [shape((steps * group, width), BF)] + [shape(half_shape, BF)] * 2,
+        [VM] * (4 + count),
+        [VM] * 3,
+    )(q_near, new_near, bias, picks, *kv)
+    gathered = [shift(rows, "seq", c) for c in range(count - 1, 0, -1)]
+    attn, mamba = call(
         functools.partial(collect, count, heads, steps, group),
-        shape((steps * count, half), BF),
-        [VM] * count,
-        VM,
+        [shape((steps * count, half), BF), shape((steps, count, 1, part), F32)],
+        [VM] * (2 + 2 * count),
+        [VM] * 2,
         [pltpu.VMEM((heads, steps * count * group, hd), F32)],
-    )(sends[0], *gathered[::-1])
+    )(slope, base, rows, *gathered, home_state, kv[1], *states)
     attn_other = shift(attn, "rep", 1)
     own_sum = call(
         project_own, shape((steps * count, columns), F32), [VM, VM], VM, us=0.7
@@ -521,12 +492,6 @@
         us=0.7,
     )(own_sum, attn_other, other_weight)
     sums = [sums[0]] + [shift(sums[c], "head", c) for c in range(1, heads_count)]
-    mamba = call(
-        functools.partial(mamba_steps, count),
-        shape((steps, count, 1, part), F32),
-        [VM] * (2 + count),
-        VM,
-    )(slope, base, *after(states[:1], attn), *gathered[::-1])
     got = shift(after([sent], mamba)[0], "rep", 1)
     kept = after([kept], sums[0])[0]
     operands = [kept, got, mamba] + ([shift(mamba, "rep", 1)] if split else [])

time: 34.1 us -> 36.1 us (1.059)
  starting transfers between devices: 12.4 us -> 16.5 us
  Pallas kernels: 10.6 us -> 9.41 us
  waiting for transfers between devices: 10.2 us -> 9.21 us
    ppermute x10 -> x12, starting transfers between devices: 12.4 us -> 16.5 us  [shift(): return lax.ppermute(x, axis, [(i, i ^ c) for i in range(size)])]
    pallas_call x4 -> x3, Pallas kernels: 3.06 us -> 1.9 us  [the longest x1 1.28 us: per_device(): call(functools.partial(stage, count, split), [shape((tall + (state_rows(p...]
    ppermute x10 -> x12, waiting for transfers between devices: 10.2 us -> 9.21 us  [shift(): return lax.ppermute(x, axis, [(i, i ^ c) for i in range(size)])]
  transfers between devices with their start and end apart: 10 -> 12, of which waited for: 5 -> 5; matrix products, arithmetic and copies ran while one was open for 0% -> 0% of each run, Pallas kernels for 20% -> 21%
where the time goes in v6:
time: 36.1 us; the launch traced here: 35.9 us
  starting transfers between devices  16.5 us (46%)
  Pallas kernels  9.41 us (26%)
  waiting for transfers between devices  9.21 us (26%)
  between operations  0.7 us (2%)
    ppermute x12, starting transfers between devices, shift(): return lax.ppermute(x, axis, [(i, i ^ c) for i in range(size)])  16.5 us
    ppermute x12, waiting for transfers between devices, shift(): return lax.ppermute(x, axis, [(i, i ^ c) for i in range(size)])  9.21 us
    pallas_call x1, Pallas kernels, per_device(): call(functools.partial(prepare, count, split), [half_weight, half_weight,...  3.76 us
    pallas_call x1, Pallas kernels, per_device(): call(functools.partial(stage, count, split), [shape((tall + (state_rows(p...  1.28 us
    pallas_call x1, Pallas kernels, per_device(): call(functools.partial(stage_state, count, split), [shape((state_rows(par...  0.94 us
    pallas_call x1, Pallas kernels, per_device(): call(functools.partial(assemble, split), [shape((1, dec_heads, keep_rep,...  0.89 us
  transfers between devices with their start and end apart: 12, of which 5 were waited for; matrix products, arithmetic and copies ran while one was open for 0% of the time, Pallas kernels for 21%

profile of v6, /device:TPU:0, one launch (start us, length us, event | category | flops | bytes accessed | tf_op | source)
XLA Modules:
  0.0 35.9 jit_solution(10109503278386969196)
XLA Ops:
  0.6 1.3 %shard_map.139 = (bf16[256,256]{1,0:T(8,128)(2,1)S(1)}, bf16[320,256]{1,0:T(8,128)(2,1)S(1)}, bf16[256,256]{1,0:T(8,128)(2,1)S(1)}, bf16[256,256]{1,0:T(8,128)(2...) custom-call(bf16[4,2,128,256]{3,2,1,0:T(8,128)(2,1)} %kv_ref.1, ...), custom_call_target="tpu_custom_call" | custom-call | bytes 36000 | tf_op jit(solution)/shard_map/pallas_call | solution.py:412
  1.9 3.1 %collective-permute-start.2 = (bf16[320,256]{1,0:T(8,128)(2,1)S(1)}, bf16[320,256]{1,0:T(8,128)(2,1)S(1)}, u32[]{:S(2)}, u32[]{:S(2)}) collective-permute-start(bf16[320,256]{1,0:T(8,128)(2,1)S(1)} %get-tuple-element.45), channel_id=1, source_target_pairs={{0,4},{4,0},{8,12},{12,8},{1,5},{5,1},{9,13},{13,9},{2,6},{6,2},{1... | collective-permute-start | bytes 491528 | tf_op jit(solution)/shard_map/ppermute | solution.py:22
  5.0 2.5 %collective-permute-start = (bf16[256,256]{1,0:T(8,128)(2,1)S(1)}, bf16[256,256]{1,0:T(8,128)(2,1)S(1)}, u32[]{:S(2)}, u32[]{:S(2)}) collective-permute-start(bf16[256,256]{1,0:T(8,128)(2,1)S(1)} %get-tuple-element.43), channel_id=1, source_target_pairs={{0,12},{4,8},{8,4},{12,0},{1,13},{5,9},{9,5},{13,1},{2,14},{6,10},... | collective-permute-start | bytes 393224 | tf_op jit(solution)/shard_map/ppermute | solution.py:22
  7.5 0.1 collective-permute-start.1
  7.6 0.9 %shard_map.142 = (bf16[64,256]{1,0:T(8,128)(2,1)S(1)}, bf16[64,256]{1,0:T(8,128)(2,1)S(1)}, bf16[64,256]{1,0:T(8,128)(2,1)S(1)}) custom-call(f32[4,16,2048]{2,1,0:T(8,128)} %state_ref.2), custom_call_target="tpu_custom_call" | custom-call | bytes 36000 | tf_op jit(solution)/shard_map/pallas_call | solution.py:435
  8.6 3.8 %shard_map.140 = (bf16[2048,1024]{1,0:T(8,128)(2,1)S(1)}, bf16[2048,1024]{1,0:T(8,128)(2,1)S(1)}, f32[4,2,16,1024]{3,2,1,0:T(8,128)S(1)}, f32[4,2,1,1024]{3,2,1,0:T(1,128)S(1)}) custom-call(bf16[4096,1024]{1,0:T(8,128)(2,1)} %weight_hbm, f32[2,1,8192]{2,1,0:T(1,128)} %dt_hbm.1, bf16[2,8192]{1,0:T(2,128)(2,1)} %bitcast.3, f32[2,1,2,16]{3,2,1,0:T(2,128)} %bc_hbm.1, ...), custom_call_target="tpu_custom_call" | custom-call | bytes 36000 | tf_op jit(solution)/shard_map/pallas_call | solution.py:442
  12.3 2.9 %collective-permute-start.6 = (bf16[64,256]{1,0:T(8,128)(2,1)S(1)}, bf16[64,256]{1,0:T(8,128)(2,1)S(1)}, u32[]{:S(2)}, u32[]{:S(2)}) collective-permute-start(bf16[64,256]{1,0:T(8,128)(2,1)S(1)} %get-tuple-element.59), channel_id=1, source_target_pairs={{0,8},{4,12},{8,0},{12,4},{1,9},{5,13},{9,1},{13,5},{2,10},{6,14},... | collective-permute-start | bytes 98312 | tf_op jit(solution)/shard_map/ppermute | solution.py:22
  15.2 1.3 %collective-permute-start.7 = (bf16[64,256]{1,0:T(8,128)(2,1)S(1)}, bf16[64,256]{1,0:T(8,128)(2,1)S(1)}, u32[]{:S(2)}, u32[]{:S(2)}) collective-permute-start(bf16[64,256]{1,0:T(8,128)(2,1)S(1)} %get-tuple-element.60), channel_id=1, source_target_pairs={{0,12},{4,8},{8,4},{12,0},{1,13},{5,9},{9,5},{13,1},{2,14},{6,10},... | collective-permute-start | bytes 98312 | tf_op jit(solution)/shard_map/ppermute | solution.py:22
  16.5 0.0 collective-permute-done.rest_3_
  16.5 4.7 %collective-permute-done.1.rest_2_ = bf16[256,256]{1,0:T(8,128)(2,1)S(1)} collective-permute-done((bf16[256,256]{1,0:T(8,128)(2,1)S(1)}, bf16[256,256]{1,0:T(8,128)(2,1)S(1)}, u32[]{:S(2)}, u32[]{:S(2)}) %collective-permute-start.1) | collective-permute-done | bytes 131104 | tf_op jit(solution)/shard_map/ppermute | solution.py:22
  21.2 0.0 collective-permute-done.2.rest_1_.rest_5_
  21.2 0.5 %shard_map.141 = (bf16[16,256]{1,0:T(8,128)(2,1)S(1)}, bf16[2,1,128,256]{3,2,1,0:T(8,128)(2,1)S(1)}, bf16[2,1,128,256]{3,2,1,0:T(8,128)(2,1)S(1)}) custom-call(bf16[2,1,32,128]{3,2,1,0:T(8,128)(2,1)S(1)} %get-tuple-element.38.q_ref, bf16[2,1,4,256]{3,2,1,0:T(4,128)(2,1)S(1)} %get-tuple-element.39.new_ref, f32[32,512]{1,0:T(8,128)S(1)} %get-tuple-element.40.bias_ref, ...), custom_call_target="tpu_custom_call" | custom-call | bytes 36000 | tf_op jit(solution)/shard_map/pallas_call | solution.py:468
  21.7 2.9 %collective-permute-start.3 = (bf16[16,256]{1,0:T(8,128)(2,1)S(1)}, bf16[16,256]{1,0:T(8,128)(2,1)S(1)}, u32[]{:S(2)}, u32[]{:S(2)}) collective-permute-start(bf16[16,256]{1,0:T(8,128)(2,1)S(1)} %get-tuple-element.54.rest_0_), channel_id=1, source_target_pairs={{0,12},{4,8},{8,4},{12,0},{1,13},{5,9},{9,5},{13,1},{2,14},{6,10},... | collective-permute-start | bytes 24584 | tf_op jit(solution)/shard_map/ppermute | solution.py:22
  24.6 0.0 collective-permute-start.4
  24.6 1.5 %collective-permute-start.5 = (bf16[16,256]{1,0:T(8,128)(2,1)S(1)}, bf16[16,256]{1,0:T(8,128)(2,1)S(1)}, u32[]{:S(2)}, u32[]{:S(2)}) collective-permute-start(bf16[16,256]{1,0:T(8,128)(2,1)S(1)} %get-tuple-element.54.rest_0_), channel_id=1, source_target_pairs={{0,4},{4,0},{8,12},{12,8},{1,5},{5,1},{9,13},{13,9},{2,6},{6,2},{1... | collective-permute-start | bytes 24584 | tf_op jit(solution)/shard_map/ppermute | solution.py:22
  26.1 0.0 collective-permute-done.6.rest_6_
  26.2 0.0 collective-permute-done.7.rest_7_
  26.2 1.1 %collective-permute-done.3.rest_1_ = bf16[16,256]{1,0:T(8,128)(2,1)S(1)} collective-permute-done((bf16[16,256]{1,0:T(8,128)(2,1)S(1)}, bf16[16,256]{1,0:T(8,128)(2,1)S(1)}, u32[]{:S(2)}, u32[]{:S(2)}) %collective-permute-start.3) | collective-permute-done | bytes 8224 | tf_op jit(solution)/shard_map/ppermute | solution.py:22
  27.2 2.0 %collective-permute-done.4.rest_2_ = bf16[16,256]{1,0:T(8,128)(2,1)S(1)} collective-permute-done((bf16[16,256]{1,0:T(8,128)(2,1)S(1)}, bf16[16,256]{1,0:T(8,128)(2,1)S(1)}, u32[]{:S(2)}, u32[]{:S(2)}) %collective-permute-start.4) | collective-permute-done | bytes 8224 | tf_op jit(solution)/shard_map/ppermute | solution.py:22
  29.2 0.0 collective-permute-done.5.rest_3_
  29.2 0.1 shard_map.143
  29.3 0.1 collective-permute-start.9
  29.4 0.5 %collective-permute-start.8 = (bf16[8,2048]{1,0:T(8,128)(2,1)S(1)}, bf16[8,2048]{1,0:T(8,128)(2,1)S(1)}, u32[]{:S(2)}, u32[]{:S(2)}) collective-permute-start(bf16[8,2048]{1,0:T(8,128)(2,1)S(1)} %get-tuple-element.61.attn_ref), channel_id=1, source_target_pairs={{0,1},{1,0},{2,3},{3,2},{4,5},{5,4},{6,7},{7,6},{8,9},{9,8},{10,11... | collective-permute-start | bytes 98312 | tf_op jit(solution)/shard_map/ppermute | solution.py:22
  29.9 0.1 collective-permute-start.10
  30.0 0.6 %shard_map.144.acc_ref = f32[8,1024]{1,0:T(8,128)S(1)} custom-call(bf16[8,2048]{1,0:T(8,128)(2,1)S(1)} %get-tuple-element.61.attn_ref, bf16[2048,1024]{1,0:T(8,128)(2,1)S(1)} %get-tuple-element.62.weight_ref), custom_call_target="tpu_custom_call" | custom-call | bytes 25200 | tf_op jit(solution)/shard_map/pallas_call | solution.py:483
  30.6 0.2 collective-permute-done.8.attn_ref
  30.8 0.7 %shard_map.145 = (f32[2,2,1024]{2,1,0:T(2,128)S(1)}, f32[2,2,1024]{2,1,0:T(2,128)S(1)}) custom-call(f32[8,1024]{1,0:T(8,128)S(1)} %shard_map.144.acc_ref, bf16[8,2048]{1,0:T(8,128)(2,1)S(1)} %collective-permute-done.8.attn_ref, bf16[2048,1024]{1,0:T(8,128)(2,1)S(1)} %get-tuple-element.63.weight_ref), custom_call_target="tpu_custom_call" | custom-call | bytes 25200 | tf_op jit(solution)/shard_map/pallas_call | solution.py:487
  31.5 1.5 %collective-permute-start.11 = (f32[2,2,1024]{2,1,0:T(2,128)S(1)}, f32[2,2,1024]{2,1,0:T(2,128)S(1)}, u32[]{:S(2)}, u32[]{:S(2)}) collective-permute-start(f32[2,2,1024]{2,1,0:T(2,128)S(1)} %get-tuple-element.70), channel_id=1, source_target_pairs={{0,2},{2,0},{1,3},{3,1},{4,6},{6,4},{5,7},{7,5},{8,10},{10,8},{9,1... | collective-permute-start | bytes 49160 | tf_op jit(solution)/shard_map/ppermute | solution.py:22
  33.0 0.0 collective-permute-done.10.rest_0_
  33.0 0.9 %shard_map.146 = (bf16[1,4,1,128,256]{4,3,2,1,0:T(8,128)(2,1)}, f32[2,1,8192]{2,1,0:T(1,128)}) custom-call(bf16[2,1,128,256]{3,2,1,0:T(8,128)(2,1)S(1)} %get-tuple-element.65.kept_ref, bf16[2,1,128,256]{3,2,1,0:T(8,128)(2,1)S(1)} %collective-permute-done.9.got_ref, f32[2,4,1,1024]{3,2,1,0:T(1,128)S(1)} %get-tuple-element.67.mamba_ref, ...), custom_call_target="tpu_custom_call" | custom-call | bytes 36000 | tf_op jit(solution)/shard_map/pallas_call | solution.py:498
  33.9 1.3 %collective-permute-done.11.refs_1_ = f32[2,2,1024]{2,1,0:T(2,128)S(1)} collective-permute-done((f32[2,2,1024]{2,1,0:T(2,128)S(1)}, f32[2,2,1024]{2,1,0:T(2,128)S(1)}, u32[]{:S(2)}, u32[]{:S(2)}) %collective-permute-start.11) | collective-permute-done | bytes 16416 | tf_op jit(solution)/shard_map/ppermute | solution.py:22
  35.2 0.6 %shard_map.147 = bf16[2,2,1024]{2,1,0:T(2,128)(2,1)} custom-call(f32[2,2,1024]{2,1,0:T(2,128)S(1)} %get-tuple-element.64.refs_0_, f32[2,2,1024]{2,1,0:T(2,128)S(1)} %collective-permute-done.11.refs_1_), custom_call_target="tpu_custom_call" | custom-call | bytes 21600 | tf_op jit(solution)/shard_map/pallas_call | solution.py:509
  (1 shorter events, 0.0 us)
Async XLA Ops:
  1.9 19.3 %collective-permute-start.2 = (bf16[320,256]{1,0:T(8,128)(2,1)S(1)}, bf16[320,256]{1,0:T(8,128)(2,1)S(1)}, u32[]{:S(2)}, u32[]{:S(2)}) collective-permute-start(bf16[320,256]{1,0:T(8,128)(2,1)S(1)} %get-tuple-element.45), channel_id=1, source_target_pairs={{0,4},{4,0},{8,12},{12,8},{1,5},{5,1},{9,13},{13,9},{2,6},{6,2},{1... | collective-permute-start | bytes 491528 | tf_op jit(solution)/shard_map/ppermute | solution.py:22
  5.0 11.5 %collective-permute-start = (bf16[256,256]{1,0:T(8,128)(2,1)S(1)}, bf16[256,256]{1,0:T(8,128)(2,1)S(1)}, u32[]{:S(2)}, u32[]{:S(2)}) collective-permute-start(bf16[256,256]{1,0:T(8,128)(2,1)S(1)} %get-tuple-element.43), channel_id=1, source_target_pairs={{0,12},{4,8},{8,4},{12,0},{1,13},{5,9},{9,5},{13,1},{2,14},{6,10},... | collective-permute-start | bytes 393224 | tf_op jit(solution)/shard_map/ppermute | solution.py:22
  7.5 13.7 %collective-permute-start.1 = (bf16[256,256]{1,0:T(8,128)(2,1)S(1)}, bf16[256,256]{1,0:T(8,128)(2,1)S(1)}, u32[]{:S(2)}, u32[]{:S(2)}) collective-permute-start(bf16[256,256]{1,0:T(8,128)(2,1)S(1)} %get-tuple-element.44), channel_id=1, source_target_pairs={{0,8},{4,12},{8,0},{12,4},{1,9},{5,13},{9,1},{13,5},{2,10},{6,14},... | collective-permute-start | bytes 393224 | tf_op jit(solution)/shard_map/ppermute | solution.py:22
  12.3 13.8 %collective-permute-start.6 = (bf16[64,256]{1,0:T(8,128)(2,1)S(1)}, bf16[64,256]{1,0:T(8,128)(2,1)S(1)}, u32[]{:S(2)}, u32[]{:S(2)}) collective-permute-start(bf16[64,256]{1,0:T(8,128)(2,1)S(1)} %get-tuple-element.59), channel_id=1, source_target_pairs={{0,8},{4,12},{8,0},{12,4},{1,9},{5,13},{9,1},{13,5},{2,10},{6,14},... | collective-permute-start | bytes 98312 | tf_op jit(solution)/shard_map/ppermute | solution.py:22
  15.2 11.0 %collective-permute-start.7 = (bf16[64,256]{1,0:T(8,128)(2,1)S(1)}, bf16[64,256]{1,0:T(8,128)(2,1)S(1)}, u32[]{:S(2)}, u32[]{:S(2)}) collective-permute-start(bf16[64,256]{1,0:T(8,128)(2,1)S(1)} %get-tuple-element.60), channel_id=1, source_target_pairs={{0,12},{4,8},{8,4},{12,0},{1,13},{5,9},{9,5},{13,1},{2,14},{6,10},... | collective-permute-start | bytes 98312 | tf_op jit(solution)/shard_map/ppermute | solution.py:22
  21.7 5.5 %collective-permute-start.3 = (bf16[16,256]{1,0:T(8,128)(2,1)S(1)}, bf16[16,256]{1,0:T(8,128)(2,1)S(1)}, u32[]{:S(2)}, u32[]{:S(2)}) collective-permute-start(bf16[16,256]{1,0:T(8,128)(2,1)S(1)} %get-tuple-element.54.rest_0_), channel_id=1, source_target_pairs={{0,12},{4,8},{8,4},{12,0},{1,13},{5,9},{9,5},{13,1},{2,14},{6,10},... | collective-permute-start | bytes 24584 | tf_op jit(solution)/shard_map/ppermute | solution.py:22
  24.6 4.5 %collective-permute-start.4 = (bf16[16,256]{1,0:T(8,128)(2,1)S(1)}, bf16[16,256]{1,0:T(8,128)(2,1)S(1)}, u32[]{:S(2)}, u32[]{:S(2)}) collective-permute-start(bf16[16,256]{1,0:T(8,128)(2,1)S(1)} %get-tuple-element.54.rest_0_), channel_id=1, source_target_pairs={{0,8},{4,12},{8,0},{12,4},{1,9},{5,13},{9,1},{13,5},{2,10},{6,14},... | collective-permute-start | bytes 24584 | tf_op jit(solution)/shard_map/ppermute | solution.py:22
  24.6 4.5 %collective-permute-start.5 = (bf16[16,256]{1,0:T(8,128)(2,1)S(1)}, bf16[16,256]{1,0:T(8,128)(2,1)S(1)}, u32[]{:S(2)}, u32[]{:S(2)}) collective-permute-start(bf16[16,256]{1,0:T(8,128)(2,1)S(1)} %get-tuple-element.54.rest_0_), channel_id=1, source_target_pairs={{0,4},{4,0},{8,12},{12,8},{1,5},{5,1},{9,13},{13,9},{2,6},{6,2},{1... | collective-permute-start | bytes 24584 | tf_op jit(solution)/shard_map/ppermute | solution.py:22
  29.3 3.7 %collective-permute-start.9 = (bf16[2,1,128,256]{3,2,1,0:T(8,128)(2,1)S(1)}, bf16[2,1,128,256]{3,2,1,0:T(8,128)(2,1)S(1)}, u32[]{:S(2)}, u32[]{:S(2)}) collective-permute-start(bf16[2,1,128,256]{3,2,1,0:T(8,128)(2,1)S(1)} %get-tuple-element.68), channel_id=1, source_target_pairs={{0,1},{1,0},{2,3},{3,2},{4,5},{5,4},{6,7},{7,6},{8,9},{9,8},{10,11... | collective-permute-start | bytes 393224 | tf_op jit(solution)/shard_map/ppermute | solution.py:22
  29.4 1.4 %collective-permute-start.8 = (bf16[8,2048]{1,0:T(8,128)(2,1)S(1)}, bf16[8,2048]{1,0:T(8,128)(2,1)S(1)}, u32[]{:S(2)}, u32[]{:S(2)}) collective-permute-start(bf16[8,2048]{1,0:T(8,128)(2,1)S(1)} %get-tuple-element.61.attn_ref), channel_id=1, source_target_pairs={{0,1},{1,0},{2,3},{3,2},{4,5},{5,4},{6,7},{7,6},{8,9},{9,8},{10,11... | collective-permute-start | bytes 98312 | tf_op jit(solution)/shard_map/ppermute | solution.py:22
  29.9 3.1 %collective-permute-start.10 = (f32[2,4,1,1024]{3,2,1,0:T(1,128)S(1)}, f32[2,4,1,1024]{3,2,1,0:T(1,128)S(1)}, u32[]{:S(2)}, u32[]{:S(2)}) collective-permute-start(f32[2,4,1,1024]{3,2,1,0:T(1,128)S(1)} %get-tuple-element.67.mamba_ref), channel_id=1, source_target_pairs={{0,1},{1,0},{2,3},{3,2},{4,5},{5,4},{6,7},{7,6},{8,9},{9,8},{10,11... | collective-permute-start | bytes 98312 | tf_op jit(solution)/shard_map/ppermute | solution.py:22
  31.5 3.8 %collective-permute-start.11 = (f32[2,2,1024]{2,1,0:T(2,128)S(1)}, f32[2,2,1024]{2,1,0:T(2,128)S(1)}, u32[]{:S(2)}, u32[]{:S(2)}) collective-permute-start(f32[2,2,1024]{2,1,0:T(2,128)S(1)} %get-tuple-element.70), channel_id=1, source_target_pairs={{0,2},{2,0},{1,3},{3,1},{4,6},{6,4},{5,7},{7,5},{8,10},{10,8},{9,1... | collective-permute-start | bytes 49160 | tf_op jit(solution)/shard_map/ppermute | solution.py:22

commit v7 on v6

--- a/solution.py
+++ b/solution.py
@@ -76,9 +76,9 @@
     return state_ref.at[me ^ c]
 
 
-def stage(count, split, kv_ref, q_ref, new_ref, state_ref, blocks_ref, counts_ref, *rest):
+def stage(count, kv_ref, q_ref, new_ref, blocks_ref, counts_ref, *rest):
     pieces = rest[:count]
-    q_out, new_out, bias_out, pick_out, loaded, blocks, counts, sems, early = rest[count:]
+    q_out, new_out, bias_out, pick_out, blocks, counts, sems, early = rest[count:]
     me, rep = lax.axis_index("seq"), lax.axis_index("rep")
     heads = kv_ref.shape[1]
     copy = copier(sems)
@@ -89,12 +89,10 @@
     moves += [copy(q_ref, q_out), copy(new_ref, new_out)]
     copy = copier(early)
     first = [copy(blocks_ref, blocks), copy(counts_ref, counts)]
-    first.append(copy(own_state(state_ref, 1, split, loaded.shape[1]), loaded))
     for move in moves + first:
         move.start()
     for move in first:
         move.wait()
-    pack_state(loaded[...], pieces[1], heads * BLOCK)
     head_first = lax.axis_index("head") * new_ref.shape[2] + rep * heads
     rows = bias_out.shape[0] // heads
     keep_rep = pick_out.shape[2]
@@ -118,17 +116,13 @@
 
 
 def stage_state(count, split, state_ref, *rest):
-    outs, loaded, sems = rest[: count - 1], rest[count - 1], rest[count]
+    outs, loaded, sems = rest[:count], rest[count], rest[count + 1]
     copy = copier(sems)
-    steps_away = [0, *range(2, count)]
     run_all(
-        [
-            copy(own_state(state_ref, c, split, loaded.shape[2]), loaded.at[i])
-            for i, c in enumerate(steps_away)
-        ]
+        [copy(own_state(state_ref, c, split, loaded.shape[2]), loaded.at[c]) for c in range(count)]
     )
-    for i in range(count - 1):
-        pack_state(loaded[i], outs[i], 0)
+    for c in range(count):
+        pack_state(loaded[c], outs[c], 0)
 
 
 def dot_f32(a, b, contract):
@@ -160,7 +154,8 @@
 
 
 def attend(count, heads, q_ref, new_ref, bias_ref, pick_ref, *rest):
-    pieces, (out_ref, kept_ref, sent_ref) = rest[:count], rest[count:]
+    pieces, states = rest[:count], rest[count : 2 * count - 1]
+    outs, (kept_ref, sent_ref) = rest[2 * count - 1 : 3 * count - 1], rest[3 * count - 1 :]
     rep = lax.axis_index("rep")
     queries = query_rows(q_ref, heads)
     rows, hd = queries[0].shape
@@ -205,9 +200,12 @@
         total = total + weight
         summed = summed + weight.astype(BF).astype(F32) * fresh_values[step]
     result = (summed / total).astype(BF)
-    for j in range(2):
-        half = result[j * rows : (j + 1) * rows] if j < heads else jnp.zeros((rows, hd), BF)
-        out_ref[:, j * hd : (j + 1) * hd] = half
+    for c in range(count):
+        for j in range(2):
+            half = result[j * rows : (j + 1) * rows] if j < heads else jnp.zeros((rows, hd), BF)
+            outs[c][:rows, j * hd : (j + 1) * hd] = half
+        if c:
+            outs[c][rows:, :] = states[c - 1][...]
     tile = pick_ref.shape[4]
     for side, ref in ((1, sent_ref), (0, kept_ref)):
         for j in range(heads):
@@ -220,10 +218,10 @@
                 ref[j, k] = total.reshape(BLOCK, 2 * hd)
 
 
-def collect(count, heads, steps, group, slope_ref, base_ref, *rest):
+def collect(count, heads, steps, group, slope_ref, base_ref, home_ref, *rest):
     parts = rest[:1] + rest[1:count][::-1]
-    states = rest[count : 2 * count]
-    out_ref, mamba_ref, scratch = rest[2 * count :]
+    states = [home_ref, *parts[1:]]
+    out_ref, mamba_ref, scratch = rest[count:]
     me = lax.axis_index("seq")
     ns, part = slope_ref.shape[2:]
     for c in range(count):
@@ -408,36 +406,31 @@
     columns = out_weight.shape[1]
     half = heads * group * hd
     half_weight = pltpu.VMEM((half, columns), BF)
-    tall = heads * BLOCK
     *pieces, q_near, new_near, bias, picks = call(
-        functools.partial(stage, count, split),
-        [
-            shape((tall + (state_rows(part) if c == 1 else 0), width), BF)
-            for c in range(count)
-        ]
+        functools.partial(stage, count),
+        [shape((heads * BLOCK, width), BF)] * count
         + [
             shape(queries.shape, BF),
             shape(new_kv.shape, BF),
             shape((all_rows, count * BLOCK), F32),
             shape((reps, heads, keep_rep, count, 16, width), BF),
         ],
-        [HB] * 6,
+        [HB] * 5,
         [VM] * (count + 4),
         [
-            pltpu.VMEM((ns, part), F32),
             smem(blocks.shape, jnp.int32),
             smem(kept_counts.shape, jnp.int32),
             DMA((count * heads + 2,)),
-            DMA((3,)),
+            DMA((2,)),
         ],
-    )(prefill_kv, queries, new_kv, prefill_state, blocks, kept_counts)
+    )(prefill_kv, queries, new_kv, blocks, kept_counts)
     moved = [shift(pieces[c], "seq", c) for c in range(count - 1, 0, -1)][::-1]
-    home_state, *states = call(
+    states = call(
         functools.partial(stage_state, count, split),
-        [shape((state_rows(part), width), BF)] * (count - 1),
+        [shape((state_rows(part), width), BF)] * count,
         [HB],
-        [VM] * (count - 1),
-        [pltpu.VMEM((count - 1, ns, part), F32), DMA((count - 1,))],
+        [VM] * count,
+        [pltpu.VMEM((count, ns, part), F32), DMA((count,))],
     )(*after([prefill_state], pieces[0]))
     own_weight, other_weight, slope, base = call(
         functools.partial(prepare, count, split),
@@ -460,25 +453,26 @@
         ],
     )(*after([out_weight], pieces[0]), step_dt, step_input, step_bc, skip_gain, a_log)
 
-    states = after(states, own_weight)
-    states = [shift(states[c - 2], "seq", c) for c in range(count - 1, 1, -1)][::-1]
     *moved, own_weight = after([*moved[::-1], own_weight])
     kv = [pieces[0], *moved[::-1]]
     half_shape = (heads, keep_rep, BLOCK, width)
-    rows, kept, sent = call(
+    rows = steps * group
+    *sends, kept, sent = call(
         functools.partial(attend, count, heads),
-        [shape((steps * group, width), BF)] + [shape(half_shape, BF)] * 2,
-        [VM] * (4 + count),
-        [VM] * 3,
-    )(q_near, new_near, bias, picks, *kv)
-    gathered = [shift(rows, "seq", c) for c in range(count - 1, 0, -1)]
+        [shape((rows, width), BF)]
+        + [shape((rows + state_rows(part), width), BF)] * (count - 1)
+        + [shape(half_shape, BF)] * 2,
+        [VM] * (3 + 2 * count),
+        [VM] * (count + 2),
+    )(q_near, new_near, bias, picks, *kv, *states[1:])
+    gathered = [shift(sends[c], "seq", c) for c in range(count - 1, 0, -1)]
     attn, mamba = call(
         functools.partial(collect, count, heads, steps, group),
         [shape((steps * count, half), BF), shape((steps, count, 1, part), F32)],
-        [VM] * (2 + 2 * count),
+        [VM] * (3 + count),
         [VM] * 2,
         [pltpu.VMEM((heads, steps * count * group, hd), F32)],
-    )(slope, base, rows, *gathered, home_state, kv[1], *states)
+    )(slope, base, states[0], sends[0], *gathered)
     attn_other = shift(attn, "rep", 1)
     own_sum = call(
         project_own, shape((steps * count, columns), F32), [VM, VM], VM, us=0.7

time: 36.1 us -> 32.9 us (0.911)
  starting transfers between devices: 16.5 us -> 12.4 us
  waiting for transfers between devices: 9.21 us -> 10.2 us
    ppermute x12 -> x10, starting transfers between devices: 16.5 us -> 12.4 us  [shift(): return lax.ppermute(x, axis, [(i, i ^ c) for i in range(size)])]
    ppermute x12 -> x10, waiting for transfers between devices: 9.21 us -> 10.2 us  [shift(): return lax.ppermute(x, axis, [(i, i ^ c) for i in range(size)])]
  transfers between devices with their start and end apart: 12 -> 10, of which waited for: 5 -> 5; matrix products, arithmetic and copies ran while one was open for 0% -> 0% of each run, Pallas kernels for 21% -> 21%
where the time goes in v7:
time: 32.9 us; the launch traced here: 32.6 us
  starting transfers between devices  12.4 us (38%)
  waiting for transfers between devices  10.2 us (31%)
  Pallas kernels  9.35 us (28%)
  between operations  0.7 us (2%)
    ppermute x10, starting transfers between devices, shift(): return lax.ppermute(x, axis, [(i, i ^ c) for i in range(size)])  12.4 us
    ppermute x10, waiting for transfers between devices, shift(): return lax.ppermute(x, axis, [(i, i ^ c) for i in range(size)])  10.2 us
    pallas_call x1, Pallas kernels, per_device(): call(functools.partial(prepare, count, split), [half_weight, half_weight,...  3.76 us
    pallas_call x1, Pallas kernels, per_device(): call(functools.partial(stage, count), [shape((heads * BLOCK, width), BF)]...  1.18 us
    pallas_call x1, Pallas kernels, per_device(): call(functools.partial(stage_state, count, split), [shape((state_rows(par...  0.98 us
    pallas_call x1, Pallas kernels, per_device(): call(functools.partial(assemble, split), [shape((1, dec_heads, keep_rep,...  0.89 us
    pallas_call x1, Pallas kernels, per_device(): call(functools.partial(project_other, heads_count, count), [shape((steps,...  0.67 us
  transfers between devices with their start and end apart: 10, of which 5 were waited for; matrix products, arithmetic and copies ran while one was open for 0% of the time, Pallas kernels for 21%

profile of v7, /device:TPU:0, one launch (start us, length us, event | category | flops | bytes accessed | tf_op | source)
XLA Modules:
  0.0 32.6 jit_solution(16269931229076126689)
XLA Ops:
  0.6 1.2 %shard_map.139 = (bf16[256,256]{1,0:T(8,128)(2,1)S(1)}, bf16[256,256]{1,0:T(8,128)(2,1)S(1)}, bf16[256,256]{1,0:T(8,128)(2,1)S(1)}, bf16[256,256]{1,0:T(8,128)(2...) custom-call(bf16[4,2,128,256]{3,2,1,0:T(8,128)(2,1)} %kv_ref.1, ...), custom_call_target="tpu_custom_call" | custom-call | bytes 36000 | tf_op jit(solution)/shard_map/pallas_call | solution.py:409
  1.8 5.1 %collective-permute-start = (bf16[256,256]{1,0:T(8,128)(2,1)S(1)}, bf16[256,256]{1,0:T(8,128)(2,1)S(1)}, u32[]{:S(2)}, u32[]{:S(2)}) collective-permute-start(bf16[256,256]{1,0:T(8,128)(2,1)S(1)} %get-tuple-element.45), channel_id=1, source_target_pairs={{0,12},{4,8},{8,4},{12,0},{1,13},{5,9},{9,5},{13,1},{2,14},{6,10},... | collective-permute-start | bytes 393224 | tf_op jit(solution)/shard_map/ppermute | solution.py:22
  6.9 0.0 collective-permute-start.1
  6.9 0.6 %collective-permute-start.2 = (bf16[256,256]{1,0:T(8,128)(2,1)S(1)}, bf16[256,256]{1,0:T(8,128)(2,1)S(1)}, u32[]{:S(2)}, u32[]{:S(2)}) collective-permute-start(bf16[256,256]{1,0:T(8,128)(2,1)S(1)} %get-tuple-element.47), channel_id=1, source_target_pairs={{0,4},{4,0},{8,12},{12,8},{1,5},{5,1},{9,13},{13,9},{2,6},{6,2},{1... | collective-permute-start | bytes 393224 | tf_op jit(solution)/shard_map/ppermute | solution.py:22
  7.6 1.0 %shard_map.141 = (bf16[64,256]{1,0:T(8,128)(2,1)S(1)}, bf16[64,256]{1,0:T(8,128)(2,1)S(1)}, bf16[64,256]{1,0:T(8,128)(2,1)S(1)}, bf16[64,256]{1,0:T(8,128)(2,1)S(1)}) custom-call(f32[4,16,2048]{2,1,0:T(8,128)} %state_ref), custom_call_target="tpu_custom_call" | custom-call | bytes 36000 | tf_op jit(solution)/shard_map/pallas_call | solution.py:428
  8.6 3.8 %shard_map.140 = (bf16[2048,1024]{1,0:T(8,128)(2,1)S(1)}, bf16[2048,1024]{1,0:T(8,128)(2,1)S(1)}, f32[4,2,16,1024]{3,2,1,0:T(8,128)S(1)}, f32[4,2,1,1024]{3,2,1,0:T(1,128)S(1)}) custom-call(bf16[4096,1024]{1,0:T(8,128)(2,1)} %weight_hbm, f32[2,1,8192]{2,1,0:T(1,128)} %dt_hbm.1, bf16[2,8192]{1,0:T(2,128)(2,1)} %bitcast.3, f32[2,1,2,16]{3,2,1,0:T(2,128)} %bc_hbm.1, ...), custom_call_target="tpu_custom_call" | custom-call | bytes 36000 | tf_op jit(solution)/shard_map/pallas_call | solution.py:435
  12.3 0.0 collective-permute-done.rest_3_
  12.3 5.7 %collective-permute-done.1.rest_2_ = bf16[256,256]{1,0:T(8,128)(2,1)S(1)} collective-permute-done((bf16[256,256]{1,0:T(8,128)(2,1)S(1)}, bf16[256,256]{1,0:T(8,128)(2,1)S(1)}, u32[]{:S(2)}, u32[]{:S(2)}) %collective-permute-start.1) | collective-permute-done | bytes 131104 | tf_op jit(solution)/shard_map/ppermute | solution.py:22
  18.0 0.0 collective-permute-done.2.rest_1_
  18.0 0.5 %shard_map.142 = (bf16[16,256]{1,0:T(8,128)(2,1)S(1)}, bf16[80,256]{1,0:T(8,128)(2,1)S(1)}, bf16[80,256]{1,0:T(8,128)(2,1)S(1)}, bf16[80,256]{1,0:T(8,128)(2,1)S...) custom-call(bf16[2,1,32,128]{3,2,1,0:T(8,128)(2,1)S(1)} %get-tuple-element.40.q_ref, ...), custom_call_target="tpu_custom_call" | custom-call | bytes 36000 | tf_op jit(solution)/shard_map/pallas_call | solution.py:460
  18.5 2.5 %collective-permute-start.3 = (bf16[80,256]{1,0:T(8,128)(2,1)S(1)}, bf16[80,256]{1,0:T(8,128)(2,1)S(1)}, u32[]{:S(2)}, u32[]{:S(2)}) collective-permute-start(bf16[80,256]{1,0:T(8,128)(2,1)S(1)} %get-tuple-element.62), channel_id=1, source_target_pairs={{0,12},{4,8},{8,4},{12,0},{1,13},{5,9},{9,5},{13,1},{2,14},{6,10},... | collective-permute-start | bytes 122888 | tf_op jit(solution)/shard_map/ppermute | solution.py:22
  21.1 0.0 collective-permute-start.4
  21.1 1.9 %collective-permute-start.5 = (bf16[80,256]{1,0:T(8,128)(2,1)S(1)}, bf16[80,256]{1,0:T(8,128)(2,1)S(1)}, u32[]{:S(2)}, u32[]{:S(2)}) collective-permute-start(bf16[80,256]{1,0:T(8,128)(2,1)S(1)} %get-tuple-element.64), channel_id=1, source_target_pairs={{0,4},{4,0},{8,12},{12,8},{1,5},{5,1},{9,13},{13,9},{2,6},{6,2},{1... | collective-permute-start | bytes 122888 | tf_op jit(solution)/shard_map/ppermute | solution.py:22
  23.0 1.4 %collective-permute-done.3.rest_1_ = bf16[80,256]{1,0:T(8,128)(2,1)S(1)} collective-permute-done((bf16[80,256]{1,0:T(8,128)(2,1)S(1)}, bf16[80,256]{1,0:T(8,128)(2,1)S(1)}, u32[]{:S(2)}, u32[]{:S(2)}) %collective-permute-start.3) | collective-permute-done | bytes 40992 | tf_op jit(solution)/shard_map/ppermute | solution.py:22
  24.4 1.6 %collective-permute-done.4.rest_2_ = bf16[80,256]{1,0:T(8,128)(2,1)S(1)} collective-permute-done((bf16[80,256]{1,0:T(8,128)(2,1)S(1)}, bf16[80,256]{1,0:T(8,128)(2,1)S(1)}, u32[]{:S(2)}, u32[]{:S(2)}) %collective-permute-start.4) | collective-permute-done | bytes 40992 | tf_op jit(solution)/shard_map/ppermute | solution.py:22
  26.0 0.0 collective-permute-done.5.rest_3_
  26.0 0.1 shard_map.143
  26.1 0.1 collective-permute-start.7
  26.2 0.5 %collective-permute-start.6 = (bf16[8,2048]{1,0:T(8,128)(2,1)S(1)}, bf16[8,2048]{1,0:T(8,128)(2,1)S(1)}, u32[]{:S(2)}, u32[]{:S(2)}) collective-permute-start(bf16[8,2048]{1,0:T(8,128)(2,1)S(1)} %get-tuple-element.65.attn_ref), channel_id=1, source_target_pairs={{0,1},{1,0},{2,3},{3,2},{4,5},{5,4},{6,7},{7,6},{8,9},{9,8},{10,11... | collective-permute-start | bytes 98312 | tf_op jit(solution)/shard_map/ppermute | solution.py:22
  26.7 0.1 collective-permute-start.8
  26.8 0.6 %shard_map.144.acc_ref = f32[8,1024]{1,0:T(8,128)S(1)} custom-call(bf16[8,2048]{1,0:T(8,128)(2,1)S(1)} %get-tuple-element.65.attn_ref, bf16[2048,1024]{1,0:T(8,128)(2,1)S(1)} %get-tuple-element.66.weight_ref), custom_call_target="tpu_custom_call" | custom-call | bytes 25200 | tf_op jit(solution)/shard_map/pallas_call | solution.py:477
  27.4 0.2 collective-permute-done.6.attn_ref
  27.6 0.7 %shard_map.145 = (f32[2,2,1024]{2,1,0:T(2,128)S(1)}, f32[2,2,1024]{2,1,0:T(2,128)S(1)}) custom-call(f32[8,1024]{1,0:T(8,128)S(1)} %shard_map.144.acc_ref, bf16[8,2048]{1,0:T(8,128)(2,1)S(1)} %collective-permute-done.6.attn_ref, bf16[2048,1024]{1,0:T(8,128)(2,1)S(1)} %get-tuple-element.67.weight_ref), custom_call_target="tpu_custom_call" | custom-call | bytes 25200 | tf_op jit(solution)/shard_map/pallas_call | solution.py:481
  28.2 1.5 %collective-permute-start.9 = (f32[2,2,1024]{2,1,0:T(2,128)S(1)}, f32[2,2,1024]{2,1,0:T(2,128)S(1)}, u32[]{:S(2)}, u32[]{:S(2)}) collective-permute-start(f32[2,2,1024]{2,1,0:T(2,128)S(1)} %get-tuple-element.74), channel_id=1, source_target_pairs={{0,2},{2,0},{1,3},{3,1},{4,6},{6,4},{5,7},{7,5},{8,10},{10,8},{9,1... | collective-permute-start | bytes 49160 | tf_op jit(solution)/shard_map/ppermute | solution.py:22
  29.8 0.0 collective-permute-done.8.rest_0_
  29.8 0.0 collective-permute-done.7.got_ref
  29.8 0.9 %shard_map.146 = (bf16[1,4,1,128,256]{4,3,2,1,0:T(8,128)(2,1)}, f32[2,1,8192]{2,1,0:T(1,128)}) custom-call(bf16[2,1,128,256]{3,2,1,0:T(8,128)(2,1)S(1)} %get-tuple-element.69.kept_ref, bf16[2,1,128,256]{3,2,1,0:T(8,128)(2,1)S(1)} %collective-permute-done.7.got_ref, f32[2,4,1,1024]{3,2,1,0:T(1,128)S(1)} %get-tuple-element.71.mamba_ref, ...), custom_call_target="tpu_custom_call" | custom-call | bytes 36000 | tf_op jit(solution)/shard_map/pallas_call | solution.py:492
  30.7 1.3 %collective-permute-done.9.refs_1_ = f32[2,2,1024]{2,1,0:T(2,128)S(1)} collective-permute-done((f32[2,2,1024]{2,1,0:T(2,128)S(1)}, f32[2,2,1024]{2,1,0:T(2,128)S(1)}, u32[]{:S(2)}, u32[]{:S(2)}) %collective-permute-start.9) | collective-permute-done | bytes 16416 | tf_op jit(solution)/shard_map/ppermute | solution.py:22
  32.0 0.6 %shard_map.147 = bf16[2,2,1024]{2,1,0:T(2,128)(2,1)} custom-call(f32[2,2,1024]{2,1,0:T(2,128)S(1)} %get-tuple-element.68.refs_0_, f32[2,2,1024]{2,1,0:T(2,128)S(1)} %collective-permute-done.9.refs_1_), custom_call_target="tpu_custom_call" | custom-call | bytes 21600 | tf_op jit(solution)/shard_map/pallas_call | solution.py:503
Async XLA Ops:
  1.8 10.5 %collective-permute-start = (bf16[256,256]{1,0:T(8,128)(2,1)S(1)}, bf16[256,256]{1,0:T(8,128)(2,1)S(1)}, u32[]{:S(2)}, u32[]{:S(2)}) collective-permute-start(bf16[256,256]{1,0:T(8,128)(2,1)S(1)} %get-tuple-element.45), channel_id=1, source_target_pairs={{0,12},{4,8},{8,4},{12,0},{1,13},{5,9},{9,5},{13,1},{2,14},{6,10},... | collective-permute-start | bytes 393224 | tf_op jit(solution)/shard_map/ppermute | solution.py:22
  6.9 11.1 %collective-permute-start.1 = (bf16[256,256]{1,0:T(8,128)(2,1)S(1)}, bf16[256,256]{1,0:T(8,128)(2,1)S(1)}, u32[]{:S(2)}, u32[]{:S(2)}) collective-permute-start(bf16[256,256]{1,0:T(8,128)(2,1)S(1)} %get-tuple-element.46), channel_id=1, source_target_pairs={{0,8},{4,12},{8,0},{12,4},{1,9},{5,13},{9,1},{13,5},{2,10},{6,14},... | collective-permute-start | bytes 393224 | tf_op jit(solution)/shard_map/ppermute | solution.py:22
  6.9 11.1 %collective-permute-start.2 = (bf16[256,256]{1,0:T(8,128)(2,1)S(1)}, bf16[256,256]{1,0:T(8,128)(2,1)S(1)}, u32[]{:S(2)}, u32[]{:S(2)}) collective-permute-start(bf16[256,256]{1,0:T(8,128)(2,1)S(1)} %get-tuple-element.47), channel_id=1, source_target_pairs={{0,4},{4,0},{8,12},{12,8},{1,5},{5,1},{9,13},{13,9},{2,6},{6,2},{1... | collective-permute-start | bytes 393224 | tf_op jit(solution)/shard_map/ppermute | solution.py:22
  18.5 5.9 %collective-permute-start.3 = (bf16[80,256]{1,0:T(8,128)(2,1)S(1)}, bf16[80,256]{1,0:T(8,128)(2,1)S(1)}, u32[]{:S(2)}, u32[]{:S(2)}) collective-permute-start(bf16[80,256]{1,0:T(8,128)(2,1)S(1)} %get-tuple-element.62), channel_id=1, source_target_pairs={{0,12},{4,8},{8,4},{12,0},{1,13},{5,9},{9,5},{13,1},{2,14},{6,10},... | collective-permute-start | bytes 122888 | tf_op jit(solution)/shard_map/ppermute | solution.py:22
  21.1 4.9 %collective-permute-start.4 = (bf16[80,256]{1,0:T(8,128)(2,1)S(1)}, bf16[80,256]{1,0:T(8,128)(2,1)S(1)}, u32[]{:S(2)}, u32[]{:S(2)}) collective-permute-start(bf16[80,256]{1,0:T(8,128)(2,1)S(1)} %get-tuple-element.63), channel_id=1, source_target_pairs={{0,8},{4,12},{8,0},{12,4},{1,9},{5,13},{9,1},{13,5},{2,10},{6,14},... | collective-permute-start | bytes 122888 | tf_op jit(solution)/shard_map/ppermute | solution.py:22
  21.1 4.9 %collective-permute-start.5 = (bf16[80,256]{1,0:T(8,128)(2,1)S(1)}, bf16[80,256]{1,0:T(8,128)(2,1)S(1)}, u32[]{:S(2)}, u32[]{:S(2)}) collective-permute-start(bf16[80,256]{1,0:T(8,128)(2,1)S(1)} %get-tuple-element.64), channel_id=1, source_target_pairs={{0,4},{4,0},{8,12},{12,8},{1,5},{5,1},{9,13},{13,9},{2,6},{6,2},{1... | collective-permute-start | bytes 122888 | tf_op jit(solution)/shard_map/ppermute | solution.py:22
  26.1 3.7 %collective-permute-start.7 = (bf16[2,1,128,256]{3,2,1,0:T(8,128)(2,1)S(1)}, bf16[2,1,128,256]{3,2,1,0:T(8,128)(2,1)S(1)}, u32[]{:S(2)}, u32[]{:S(2)}) collective-permute-start(bf16[2,1,128,256]{3,2,1,0:T(8,128)(2,1)S(1)} %get-tuple-element.72), channel_id=1, source_target_pairs={{0,1},{1,0},{2,3},{3,2},{4,5},{5,4},{6,7},{7,6},{8,9},{9,8},{10,11... | collective-permute-start | bytes 393224 | tf_op jit(solution)/shard_map/ppermute | solution.py:22
  26.2 1.4 %collective-permute-start.6 = (bf16[8,2048]{1,0:T(8,128)(2,1)S(1)}, bf16[8,2048]{1,0:T(8,128)(2,1)S(1)}, u32[]{:S(2)}, u32[]{:S(2)}) collective-permute-start(bf16[8,2048]{1,0:T(8,128)(2,1)S(1)} %get-tuple-element.65.attn_ref), channel_id=1, source_target_pairs={{0,1},{1,0},{2,3},{3,2},{4,5},{5,4},{6,7},{7,6},{8,9},{9,8},{10,11... | collective-permute-start | bytes 98312 | tf_op jit(solution)/shard_map/ppermute | solution.py:22
  26.7 3.1 %collective-permute-start.8 = (f32[2,4,1,1024]{3,2,1,0:T(1,128)S(1)}, f32[2,4,1,1024]{3,2,1,0:T(1,128)S(1)}, u32[]{:S(2)}, u32[]{:S(2)}) collective-permute-start(f32[2,4,1,1024]{3,2,1,0:T(1,128)S(1)} %get-tuple-element.71.mamba_ref), channel_id=1, source_target_pairs={{0,1},{1,0},{2,3},{3,2},{4,5},{5,4},{6,7},{7,6},{8,9},{9,8},{10,11... | collective-permute-start | bytes 98312 | tf_op jit(solution)/shard_map/ppermute | solution.py:22
  28.2 3.8 %collective-permute-start.9 = (f32[2,2,1024]{2,1,0:T(2,128)S(1)}, f32[2,2,1024]{2,1,0:T(2,128)S(1)}, u32[]{:S(2)}, u32[]{:S(2)}) collective-permute-start(f32[2,2,1024]{2,1,0:T(2,128)S(1)} %get-tuple-element.74), channel_id=1, source_target_pairs={{0,2},{2,0},{1,3},{3,1},{4,6},{6,4},{5,7},{7,5},{8,10},{10,8},{9,1... | collective-permute-start | bytes 49160 | tf_op jit(solution)/shard_map/ppermute | solution.py:22

commit v8 on v7

--- a/solution.py
+++ b/solution.py
@@ -154,8 +154,8 @@
 
 
 def attend(count, heads, q_ref, new_ref, bias_ref, pick_ref, *rest):
-    pieces, states = rest[:count], rest[count : 2 * count - 1]
-    outs, (kept_ref, sent_ref) = rest[2 * count - 1 : 3 * count - 1], rest[3 * count - 1 :]
+    pieces, states = rest[:count], rest[count : 2 * count]
+    out_ref, kept_ref, sent_ref = rest[2 * count :]
     rep = lax.axis_index("rep")
     queries = query_rows(q_ref, heads)
     rows, hd = queries[0].shape
@@ -200,12 +200,12 @@
         total = total + weight
         summed = summed + weight.astype(BF).astype(F32) * fresh_values[step]
     result = (summed / total).astype(BF)
+    me = lax.axis_index("seq")
     for c in range(count):
         for j in range(2):
             half = result[j * rows : (j + 1) * rows] if j < heads else jnp.zeros((rows, hd), BF)
-            outs[c][:rows, j * hd : (j + 1) * hd] = half
-        if c:
-            outs[c][rows:, :] = states[c - 1][...]
+            out_ref[me ^ c, :rows, j * hd : (j + 1) * hd] = half
+        out_ref[me ^ c, rows:, :] = states[c][...]
     tile = pick_ref.shape[4]
     for side, ref in ((1, sent_ref), (0, kept_ref)):
         for j in range(heads):
@@ -218,11 +218,10 @@
                 ref[j, k] = total.reshape(BLOCK, 2 * hd)
 
 
-def collect(count, heads, steps, group, slope_ref, base_ref, home_ref, *rest):
-    parts = rest[:1] + rest[1:count][::-1]
-    states = [home_ref, *parts[1:]]
-    out_ref, mamba_ref, scratch = rest[count:]
+def collect(count, heads, steps, group, slope_ref, base_ref, got_ref, out_ref, mamba_ref, scratch):
     me = lax.axis_index("seq")
+    parts = [got_ref.at[me ^ c] for c in range(count)]
+    states = parts
     ns, part = slope_ref.shape[2:]
     for c in range(count):
         first = states[c].shape[0] - state_rows(part)
@@ -457,22 +456,20 @@
     kv = [pieces[0], *moved[::-1]]
     half_shape = (heads, keep_rep, BLOCK, width)
     rows = steps * group
-    *sends, kept, sent = call(
+    sends, kept, sent = call(
         functools.partial(attend, count, heads),
-        [shape((rows, width), BF)]
-        + [shape((rows + state_rows(part), width), BF)] * (count - 1)
-        + [shape(half_shape, BF)] * 2,
-        [VM] * (3 + 2 * count),
-        [VM] * (count + 2),
-    )(q_near, new_near, bias, picks, *kv, *states[1:])
-    gathered = [shift(sends[c], "seq", c) for c in range(count - 1, 0, -1)]
+        [shape((count, rows + state_rows(part), width), BF)] + [shape(half_shape, BF)] * 2,
+        [VM] * (4 + 2 * count),
+        [VM] * 3,
+    )(q_near, new_near, bias, picks, *kv, *states)
+    gathered = lax.all_to_all(sends, "seq", split_axis=0, concat_axis=0, tiled=True)
     attn, mamba = call(
         functools.partial(collect, count, heads, steps, group),
         [shape((steps * count, half), BF), shape((steps, count, 1, part), F32)],
-        [VM] * (3 + count),
+        [VM] * 3,
         [VM] * 2,
         [pltpu.VMEM((heads, steps * count * group, hd), F32)],
-    )(slope, base, states[0], sends[0], *gathered)
+    )(slope, base, gathered)
     attn_other = shift(attn, "rep", 1)
     own_sum = call(
         project_own, shape((steps * count, columns), F32), [VM, VM], VM, us=0.7

time: 32.9 us -> 35.7 us (1.085)
  blocking collectives: 0 us -> 10.3 us
  starting transfers between devices: 12.4 us -> 7.94 us
  waiting for transfers between devices: 10.2 us -> 7.18 us
    all_to_all x0 -> x1, blocking collectives: none -> 10.3 us  [per_device(): lax.all_to_all(sends, 'seq', split_axis=0, concat_axis=0, tiled=True)]
    ppermute x10 -> x7, starting transfers between devices: 12.4 us -> 7.94 us  [shift(): return lax.ppermute(x, axis, [(i, i ^ c) for i in range(size)])]
    ppermute x10 -> x7, waiting for transfers between devices: 10.2 us -> 7.18 us  [shift(): return lax.ppermute(x, axis, [(i, i ^ c) for i in range(size)])]
  transfers between devices with their start and end apart: 10 -> 7, of which waited for: 5 -> 3; matrix products, arithmetic and copies ran while one was open for 0% -> 0% of each run, Pallas kernels for 21% -> 20%
where the time goes in v8:
time: 35.7 us; the launch traced here: 35.4 us
  blocking collectives  10.3 us (29%)
  Pallas kernels  9.36 us (26%)
  starting transfers between devices  7.94 us (22%)
  waiting for transfers between devices  7.18 us (20%)
  between operations  0.7 us (2%)
    all_to_all x1, blocking collectives, per_device(): lax.all_to_all(sends, 'seq', split_axis=0, concat_axis=0, tiled=True)  10.3 us
    ppermute x7, starting transfers between devices, shift(): return lax.ppermute(x, axis, [(i, i ^ c) for i in range(size)])  7.94 us
    ppermute x7, waiting for transfers between devices, shift(): return lax.ppermute(x, axis, [(i, i ^ c) for i in range(size)])  7.18 us
    pallas_call x1, Pallas kernels, per_device(): call(functools.partial(prepare, count, split), [half_weight, half_weight,...  3.76 us
    pallas_call x1, Pallas kernels, per_device(): call(functools.partial(stage, count), [shape((heads * BLOCK, width), BF)]...  1.18 us
    pallas_call x1, Pallas kernels, per_device(): call(functools.partial(stage_state, count, split), [shape((state_rows(par...  0.98 us
    pallas_call x1, Pallas kernels, per_device(): call(functools.partial(assemble, split), [shape((1, dec_heads, keep_rep,...  0.89 us
  transfers between devices with their start and end apart: 7, of which 3 were waited for; matrix products, arithmetic and copies ran while one was open for 0% of the time, Pallas kernels for 20%

profile of v8, /device:TPU:0, one launch (start us, length us, event | category | flops | bytes accessed | tf_op | source)
XLA Modules:
  0.0 35.4 jit_solution(9004084140744496638)
XLA Ops:
  0.6 1.2 %shard_map.139 = (bf16[256,256]{1,0:T(8,128)(2,1)S(1)}, bf16[256,256]{1,0:T(8,128)(2,1)S(1)}, bf16[256,256]{1,0:T(8,128)(2,1)S(1)}, bf16[256,256]{1,0:T(8,128)(2...) custom-call(bf16[4,2,128,256]{3,2,1,0:T(8,128)(2,1)} %kv_ref.1, ...), custom_call_target="tpu_custom_call" | custom-call | bytes 36000 | tf_op jit(solution)/shard_map/pallas_call | solution.py:408
  1.8 5.1 %collective-permute-start = (bf16[256,256]{1,0:T(8,128)(2,1)S(1)}, bf16[256,256]{1,0:T(8,128)(2,1)S(1)}, u32[]{:S(2)}, u32[]{:S(2)}) collective-permute-start(bf16[256,256]{1,0:T(8,128)(2,1)S(1)} %get-tuple-element.42), channel_id=1, source_target_pairs={{0,12},{4,8},{8,4},{12,0},{1,13},{5,9},{9,5},{13,1},{2,14},{6,10},... | collective-permute-start | bytes 393224 | tf_op jit(solution)/shard_map/ppermute | solution.py:22
  6.9 0.0 collective-permute-start.1
  6.9 0.6 %collective-permute-start.2 = (bf16[256,256]{1,0:T(8,128)(2,1)S(1)}, bf16[256,256]{1,0:T(8,128)(2,1)S(1)}, u32[]{:S(2)}, u32[]{:S(2)}) collective-permute-start(bf16[256,256]{1,0:T(8,128)(2,1)S(1)} %get-tuple-element.44), channel_id=1, source_target_pairs={{0,4},{4,0},{8,12},{12,8},{1,5},{5,1},{9,13},{13,9},{2,6},{6,2},{1... | collective-permute-start | bytes 393224 | tf_op jit(solution)/shard_map/ppermute | solution.py:22
  7.6 1.0 %shard_map.141 = (bf16[64,256]{1,0:T(8,128)(2,1)S(1)}, bf16[64,256]{1,0:T(8,128)(2,1)S(1)}, bf16[64,256]{1,0:T(8,128)(2,1)S(1)}, bf16[64,256]{1,0:T(8,128)(2,1)S(1)}) custom-call(f32[4,16,2048]{2,1,0:T(8,128)} %state_ref), custom_call_target="tpu_custom_call" | custom-call | bytes 36000 | tf_op jit(solution)/shard_map/pallas_call | solution.py:427
  8.6 3.8 %shard_map.140 = (bf16[2048,1024]{1,0:T(8,128)(2,1)S(1)}, bf16[2048,1024]{1,0:T(8,128)(2,1)S(1)}, f32[4,2,16,1024]{3,2,1,0:T(8,128)S(1)}, f32[4,2,1,1024]{3,2,1,0:T(1,128)S(1)}) custom-call(bf16[4096,1024]{1,0:T(8,128)(2,1)} %weight_hbm, f32[2,1,8192]{2,1,0:T(1,128)} %dt_hbm.1, bf16[2,8192]{1,0:T(2,128)(2,1)} %bitcast.3, f32[2,1,2,16]{3,2,1,0:T(2,128)} %bc_hbm.1, ...), custom_call_target="tpu_custom_call" | custom-call | bytes 36000 | tf_op jit(solution)/shard_map/pallas_call | solution.py:434
  12.3 0.0 collective-permute-done.rest_3_
  12.3 5.7 %collective-permute-done.1.rest_2_ = bf16[256,256]{1,0:T(8,128)(2,1)S(1)} collective-permute-done((bf16[256,256]{1,0:T(8,128)(2,1)S(1)}, bf16[256,256]{1,0:T(8,128)(2,1)S(1)}, u32[]{:S(2)}, u32[]{:S(2)}) %collective-permute-start.1) | collective-permute-done | bytes 131104 | tf_op jit(solution)/shard_map/ppermute | solution.py:22
  18.0 0.0 collective-permute-done.2.rest_1_
  18.0 0.5 %shard_map.142 = (bf16[4,80,256]{2,1,0:T(8,128)(2,1)S(1)}, bf16[2,1,128,256]{3,2,1,0:T(8,128)(2,1)S(1)}, bf16[2,1,128,256]{3,2,1,0:T(8,128)(2,1)S(1)}) custom-call(bf16[2,1,32,128]{3,2,1,0:T(8,128)(2,1)S(1)} %get-tuple-element.37.q_ref, bf16[2,1,4,256]{3,2,1,0:T(4,128)(2,1)S(1)} %get-tuple-element.38.new_ref, f32[32,512]{1,0:T(8,128)S(1)} %get-tuple-element.39.bias_ref, ...), custom_call_target="tpu_custom_call" | custom-call | bytes 36000 | tf_op jit(solution)/shard_map/pallas_call | solution.py:459
  18.5 10.3 %all_to_all.5.got_ref = bf16[4,80,256]{2,1,0:T(8,128)(2,1)S(1)} all-to-all(bf16[4,80,256]{2,1,0:T(8,128)(2,1)S(1)} %get-tuple-element.58), channel_id=1, replica_groups=mesh['groups'=2,'seq'=4,'head'=2,'rep'=2] {'seq'}, dimensions={0} | all-to-all | bytes 327680 | tf_op jit(solution)/shard_map/all_to_all | solution.py:465
  28.8 0.1 shard_map.143
  28.9 0.1 collective-permute-start.4
  29.0 0.5 %collective-permute-start.3 = (bf16[8,2048]{1,0:T(8,128)(2,1)S(1)}, bf16[8,2048]{1,0:T(8,128)(2,1)S(1)}, u32[]{:S(2)}, u32[]{:S(2)}) collective-permute-start(bf16[8,2048]{1,0:T(8,128)(2,1)S(1)} %get-tuple-element.59.attn_ref), channel_id=1, source_target_pairs={{0,1},{1,0},{2,3},{3,2},{4,5},{5,4},{6,7},{7,6},{8,9},{9,8},{10,11... | collective-permute-start | bytes 98312 | tf_op jit(solution)/shard_map/ppermute | solution.py:22
  29.5 0.1 collective-permute-start.5
  29.6 0.6 %shard_map.144.acc_ref = f32[8,1024]{1,0:T(8,128)S(1)} custom-call(bf16[8,2048]{1,0:T(8,128)(2,1)S(1)} %get-tuple-element.59.attn_ref, bf16[2048,1024]{1,0:T(8,128)(2,1)S(1)} %get-tuple-element.60.weight_ref), custom_call_target="tpu_custom_call" | custom-call | bytes 25200 | tf_op jit(solution)/shard_map/pallas_call | solution.py:474
  30.2 0.2 collective-permute-done.3.attn_ref
  30.4 0.7 %shard_map.145 = (f32[2,2,1024]{2,1,0:T(2,128)S(1)}, f32[2,2,1024]{2,1,0:T(2,128)S(1)}) custom-call(f32[8,1024]{1,0:T(8,128)S(1)} %shard_map.144.acc_ref, bf16[8,2048]{1,0:T(8,128)(2,1)S(1)} %collective-permute-done.3.attn_ref, bf16[2048,1024]{1,0:T(8,128)(2,1)S(1)} %get-tuple-element.61.weight_ref), custom_call_target="tpu_custom_call" | custom-call | bytes 25200 | tf_op jit(solution)/shard_map/pallas_call | solution.py:478
  31.0 1.5 %collective-permute-start.6 = (f32[2,2,1024]{2,1,0:T(2,128)S(1)}, f32[2,2,1024]{2,1,0:T(2,128)S(1)}, u32[]{:S(2)}, u32[]{:S(2)}) collective-permute-start(f32[2,2,1024]{2,1,0:T(2,128)S(1)} %get-tuple-element.68), channel_id=1, source_target_pairs={{0,2},{2,0},{1,3},{3,1},{4,6},{6,4},{5,7},{7,5},{8,10},{10,8},{9,1... | collective-permute-start | bytes 49160 | tf_op jit(solution)/shard_map/ppermute | solution.py:22
  32.6 0.0 collective-permute-done.5.rest_0_
  32.6 0.0 collective-permute-done.4.got_ref
  32.6 0.9 %shard_map.146 = (bf16[1,4,1,128,256]{4,3,2,1,0:T(8,128)(2,1)}, f32[2,1,8192]{2,1,0:T(1,128)}) custom-call(bf16[2,1,128,256]{3,2,1,0:T(8,128)(2,1)S(1)} %get-tuple-element.63.kept_ref, bf16[2,1,128,256]{3,2,1,0:T(8,128)(2,1)S(1)} %collective-permute-done.4.got_ref, f32[2,4,1,1024]{3,2,1,0:T(1,128)S(1)} %get-tuple-element.65.mamba_ref, ...), custom_call_target="tpu_custom_call" | custom-call | bytes 36000 | tf_op jit(solution)/shard_map/pallas_call | solution.py:489
  33.5 1.3 %collective-permute-done.6.refs_1_ = f32[2,2,1024]{2,1,0:T(2,128)S(1)} collective-permute-done((f32[2,2,1024]{2,1,0:T(2,128)S(1)}, f32[2,2,1024]{2,1,0:T(2,128)S(1)}, u32[]{:S(2)}, u32[]{:S(2)}) %collective-permute-start.6) | collective-permute-done | bytes 16416 | tf_op jit(solution)/shard_map/ppermute | solution.py:22
  34.8 0.6 %shard_map.147 = bf16[2,2,1024]{2,1,0:T(2,128)(2,1)} custom-call(f32[2,2,1024]{2,1,0:T(2,128)S(1)} %get-tuple-element.62.refs_0_, f32[2,2,1024]{2,1,0:T(2,128)S(1)} %collective-permute-done.6.refs_1_), custom_call_target="tpu_custom_call" | custom-call | bytes 21600 | tf_op jit(solution)/shard_map/pallas_call | solution.py:500
Async XLA Ops:
  1.8 10.5 %collective-permute-start = (bf16[256,256]{1,0:T(8,128)(2,1)S(1)}, bf16[256,256]{1,0:T(8,128)(2,1)S(1)}, u32[]{:S(2)}, u32[]{:S(2)}) collective-permute-start(bf16[256,256]{1,0:T(8,128)(2,1)S(1)} %get-tuple-element.42), channel_id=1, source_target_pairs={{0,12},{4,8},{8,4},{12,0},{1,13},{5,9},{9,5},{13,1},{2,14},{6,10},... | collective-permute-start | bytes 393224 | tf_op jit(solution)/shard_map/ppermute | solution.py:22
  6.9 11.1 %collective-permute-start.1 = (bf16[256,256]{1,0:T(8,128)(2,1)S(1)}, bf16[256,256]{1,0:T(8,128)(2,1)S(1)}, u32[]{:S(2)}, u32[]{:S(2)}) collective-permute-start(bf16[256,256]{1,0:T(8,128)(2,1)S(1)} %get-tuple-element.43), channel_id=1, source_target_pairs={{0,8},{4,12},{8,0},{12,4},{1,9},{5,13},{9,1},{13,5},{2,10},{6,14},... | collective-permute-start | bytes 393224 | tf_op jit(solution)/shard_map/ppermute | solution.py:22
  6.9 11.1 %collective-permute-start.2 = (bf16[256,256]{1,0:T(8,128)(2,1)S(1)}, bf16[256,256]{1,0:T(8,128)(2,1)S(1)}, u32[]{:S(2)}, u32[]{:S(2)}) collective-permute-start(bf16[256,256]{1,0:T(8,128)(2,1)S(1)} %get-tuple-element.44), channel_id=1, source_target_pairs={{0,4},{4,0},{8,12},{12,8},{1,5},{5,1},{9,13},{13,9},{2,6},{6,2},{1... | collective-permute-start | bytes 393224 | tf_op jit(solution)/shard_map/ppermute | solution.py:22
  28.9 3.7 %collective-permute-start.4 = (bf16[2,1,128,256]{3,2,1,0:T(8,128)(2,1)S(1)}, bf16[2,1,128,256]{3,2,1,0:T(8,128)(2,1)S(1)}, u32[]{:S(2)}, u32[]{:S(2)}) collective-permute-start(bf16[2,1,128,256]{3,2,1,0:T(8,128)(2,1)S(1)} %get-tuple-element.66), channel_id=1, source_target_pairs={{0,1},{1,0},{2,3},{3,2},{4,5},{5,4},{6,7},{7,6},{8,9},{9,8},{10,11... | collective-permute-start | bytes 393224 | tf_op jit(solution)/shard_map/ppermute | solution.py:22
  29.0 1.4 %collective-permute-start.3 = (bf16[8,2048]{1,0:T(8,128)(2,1)S(1)}, bf16[8,2048]{1,0:T(8,128)(2,1)S(1)}, u32[]{:S(2)}, u32[]{:S(2)}) collective-permute-start(bf16[8,2048]{1,0:T(8,128)(2,1)S(1)} %get-tuple-element.59.attn_ref), channel_id=1, source_target_pairs={{0,1},{1,0},{2,3},{3,2},{4,5},{5,4},{6,7},{7,6},{8,9},{9,8},{10,11... | collective-permute-start | bytes 98312 | tf_op jit(solution)/shard_map/ppermute | solution.py:22
  29.5 3.1 %collective-permute-start.5 = (f32[2,4,1,1024]{3,2,1,0:T(1,128)S(1)}, f32[2,4,1,1024]{3,2,1,0:T(1,128)S(1)}, u32[]{:S(2)}, u32[]{:S(2)}) collective-permute-start(f32[2,4,1,1024]{3,2,1,0:T(1,128)S(1)} %get-tuple-element.65.mamba_ref), channel_id=1, source_target_pairs={{0,1},{1,0},{2,3},{3,2},{4,5},{5,4},{6,7},{7,6},{8,9},{9,8},{10,11... | collective-permute-start | bytes 98312 | tf_op jit(solution)/shard_map/ppermute | solution.py:22
  31.0 3.8 %collective-permute-start.6 = (f32[2,2,1024]{2,1,0:T(2,128)S(1)}, f32[2,2,1024]{2,1,0:T(2,128)S(1)}, u32[]{:S(2)}, u32[]{:S(2)}) collective-permute-start(f32[2,2,1024]{2,1,0:T(2,128)S(1)} %get-tuple-element.68), channel_id=1, source_target_pairs={{0,2},{2,0},{1,3},{3,1},{4,6},{6,4},{5,7},{7,5},{8,10},{10,8},{9,1... | collective-permute-start | bytes 49160 | tf_op jit(solution)/shard_map/ppermute | solution.py:22

commit v9 on v7

--- a/solution.py
+++ b/solution.py
@@ -76,23 +76,43 @@
     return state_ref.at[me ^ c]
 
 
-def stage(count, kv_ref, q_ref, new_ref, blocks_ref, counts_ref, *rest):
-    pieces = rest[:count]
-    q_out, new_out, bias_out, pick_out, blocks, counts, sems, early = rest[count:]
+def stage_blocks(count, kv_ref, *rest):
+    outs, sems = rest[:-1], rest[-1]
+    me = lax.axis_index("seq")
+    copy = copier(sems)
+    run_all(
+        [
+            copy(kv_ref.at[me ^ c, j], outs[c - 1].at[pl.ds(j * BLOCK, BLOCK)])
+            for c in range(count - 1, 0, -1)
+            for j in range(kv_ref.shape[1])
+        ]
+    )
+
+
+def stage_rest(count, split, kv_ref, q_ref, new_ref, state_ref, blocks_ref, counts_ref, *rest):
+    own_out, q_out, new_out, bias_out, pick_out = rest[:5]
+    states = rest[5 : 5 + count]
+    loaded, blocks, counts, sems, early = rest[5 + count :]
     me, rep = lax.axis_index("seq"), lax.axis_index("rep")
     heads = kv_ref.shape[1]
     copy = copier(sems)
-    moves = []
-    for c in range(count - 1, -1, -1):
-        for j in range(heads):
-            moves.append(copy(kv_ref.at[me ^ c, j], pieces[c].at[pl.ds(j * BLOCK, BLOCK)]))
+    moves = [copy(kv_ref.at[me, j], own_out.at[pl.ds(j * BLOCK, BLOCK)]) for j in range(heads)]
     moves += [copy(q_ref, q_out), copy(new_ref, new_out)]
     copy = copier(early)
     first = [copy(blocks_ref, blocks), copy(counts_ref, counts)]
-    for move in moves + first:
+    part = loaded.shape[2]
+    for c in range(count):
+        if split:
+            src = state_ref.at[me ^ c, :, pl.ds(pl.multiple_of(rep * part, 128), part)]
+        else:
+            src = state_ref.at[me ^ c]
+        first.append(copy(src, loaded.at[c]))
+    for move in first + moves:
         move.start()
     for move in first:
         move.wait()
+    for c in range(count):
+        pack_state(loaded[c], states[c], 0)
     head_first = lax.axis_index("head") * new_ref.shape[2] + rep * heads
     rows = bias_out.shape[0] // heads
     keep_rep = pick_out.shape[2]
@@ -113,16 +133,6 @@
             )
     for move in moves:
         move.wait()
-
-
-def stage_state(count, split, state_ref, *rest):
-    outs, loaded, sems = rest[:count], rest[count], rest[count + 1]
-    copy = copier(sems)
-    run_all(
-        [copy(own_state(state_ref, c, split, loaded.shape[2]), loaded.at[c]) for c in range(count)]
-    )
-    for c in range(count):
-        pack_state(loaded[c], outs[c], 0)
 
 
 def dot_f32(a, b, contract):
@@ -219,7 +229,7 @@
 
 
 def collect(count, heads, steps, group, slope_ref, base_ref, home_ref, *rest):
-    parts = rest[:1] + rest[1:count][::-1]
+    parts = [rest[0], rest[count - 1], *rest[1 : count - 1]]
     states = [home_ref, *parts[1:]]
     out_ref, mamba_ref, scratch = rest[count:]
     me = lax.axis_index("seq")
@@ -406,32 +416,35 @@
     columns = out_weight.shape[1]
     half = heads * group * hd
     half_weight = pltpu.VMEM((half, columns), BF)
-    *pieces, q_near, new_near, bias, picks = call(
-        functools.partial(stage, count),
-        [shape((heads * BLOCK, width), BF)] * count
-        + [
+    block_shape = shape((heads * BLOCK, width), BF)
+    pieces = call(
+        functools.partial(stage_blocks, count),
+        [block_shape] * (count - 1),
+        [HB],
+        [VM] * (count - 1),
+        [DMA(((count - 1) * heads,))],
+    )(prefill_kv)
+    moved = [shift(pieces[c - 1], "seq", c) for c in range(count - 1, 0, -1)][::-1]
+    own_piece, q_near, new_near, bias, picks, *states = call(
+        functools.partial(stage_rest, count, split),
+        [
+            block_shape,
             shape(queries.shape, BF),
             shape(new_kv.shape, BF),
             shape((all_rows, count * BLOCK), F32),
             shape((reps, heads, keep_rep, count, 16, width), BF),
-        ],
-        [HB] * 5,
-        [VM] * (count + 4),
+        ]
+        + [shape((state_rows(part), width), BF)] * count,
+        [HB] * 6,
+        [VM] * (5 + count),
         [
+            pltpu.VMEM((count, ns, part), F32),
             smem(blocks.shape, jnp.int32),
             smem(kept_counts.shape, jnp.int32),
-            DMA((count * heads + 2,)),
-            DMA((2,)),
+            DMA((heads + 2,)),
+            DMA((count + 2,)),
         ],
-    )(prefill_kv, queries, new_kv, blocks, kept_counts)
-    moved = [shift(pieces[c], "seq", c) for c in range(count - 1, 0, -1)][::-1]
-    states = call(
-        functools.partial(stage_state, count, split),
-        [shape((state_rows(part), width), BF)] * count,
-        [HB],
-        [VM] * count,
-        [pltpu.VMEM((count, ns, part), F32), DMA((count,))],
-    )(*after([prefill_state], pieces[0]))
+    )(*after([prefill_kv], pieces[0]), queries, new_kv, prefill_state, blocks, kept_counts)
     own_weight, other_weight, slope, base = call(
         functools.partial(prepare, count, split),
         [
@@ -454,7 +467,7 @@
     )(*after([out_weight], pieces[0]), step_dt, step_input, step_bc, skip_gain, a_log)
 
     *moved, own_weight = after([*moved[::-1], own_weight])
-    kv = [pieces[0], *moved[::-1]]
+    kv = [own_piece, *moved[::-1]]
     half_shape = (heads, keep_rep, BLOCK, width)
     rows = steps * group
     *sends, kept, sent = call(
@@ -465,7 +478,8 @@
         [VM] * (3 + 2 * count),
         [VM] * (count + 2),
     )(q_near, new_near, bias, picks, *kv, *states[1:])
-    gathered = [shift(sends[c], "seq", c) for c in range(count - 1, 0, -1)]
+    order = [*range(2, count), 1]
+    gathered = [shift(sends[c], "seq", c) for c in order]
     attn, mamba = call(
         functools.partial(collect, count, heads, steps, group),
         [shape((steps * count, half), BF), shape((steps, count, 1, part), F32)],

time: 32.9 us -> 31.9 us (0.970)
  starting transfers between devices: 12.4 us -> 11.5 us
    ppermute x10, starting transfers between devices: 12.4 us -> 11.5 us  [shift(): return lax.ppermute(x, axis, [(i, i ^ c) for i in range(size)])]
  transfers between devices with their start and end apart: 10 -> 10, of which waited for: 5 -> 6; matrix products, arithmetic and copies ran while one was open for 0% -> 0% of each run, Pallas kernels for 21% -> 22%
where the time goes in v9:
time: 31.9 us; the launch traced here: 31.7 us
  starting transfers between devices  11.5 us (36%)
  waiting for transfers between devices  10.1 us (32%)
  Pallas kernels  9.4 us (29%)
  between operations  0.71 us (2%)
    ppermute x10, starting transfers between devices, shift(): return lax.ppermute(x, axis, [(i, i ^ c) for i in range(size)])  11.5 us
    ppermute x10, waiting for transfers between devices, shift(): return lax.ppermute(x, axis, [(i, i ^ c) for i in range(size)])  10.1 us
    pallas_call x1, Pallas kernels, per_device(): call(functools.partial(prepare, count, split), [half_weight, half_weight,...  3.76 us
    pallas_call x1, Pallas kernels, per_device(): call(functools.partial(stage_rest, count, split), [block_shape, shape(que...  1.15 us
    pallas_call x1, Pallas kernels, per_device(): call(functools.partial(stage_blocks, count), [block_shape] * (count - 1),...  1.06 us
    pallas_call x1, Pallas kernels, per_device(): call(functools.partial(assemble, split), [shape((1, dec_heads, keep_rep,...  0.89 us
    pallas_call x1, Pallas kernels, per_device(): call(functools.partial(project_other, heads_count, count), [shape((steps,...  0.67 us
    pallas_call x1, Pallas kernels, per_device(): call(project_own, shape((steps * count, columns), F32), [VM, VM], VM, us=...  0.64 us
  transfers between devices with their start and end apart: 10, of which 6 were waited for; matrix products, arithmetic and copies ran while one was open for 0% of the time, Pallas kernels for 22%

profile of v9, /device:TPU:0, one launch (start us, length us, event | category | flops | bytes accessed | tf_op | source)
XLA Modules:
  0.0 31.7 jit_solution(2205385868584165687)
XLA Ops:
  0.6 1.1 %shard_map.139 = (bf16[256,256]{1,0:T(8,128)(2,1)S(1)}, bf16[256,256]{1,0:T(8,128)(2,1)S(1)}, bf16[256,256]{1,0:T(8,128)(2,1)S(1)}) custom-call(bf16[4,2,128,256]{3,2,1,0:T(8,128)(2,1)} %kv_ref.2), custom_call_target="tpu_custom_call" | custom-call | bytes 36000 | tf_op jit(solution)/shard_map/pallas_call | solution.py:420
  1.7 5.1 %collective-permute-start = (bf16[256,256]{1,0:T(8,128)(2,1)S(1)}, bf16[256,256]{1,0:T(8,128)(2,1)S(1)}, u32[]{:S(2)}, u32[]{:S(2)}) collective-permute-start(bf16[256,256]{1,0:T(8,128)(2,1)S(1)} %get-tuple-element.47), channel_id=1, source_target_pairs={{0,12},{4,8},{8,4},{12,0},{1,13},{5,9},{9,5},{13,1},{2,14},{6,10},... | collective-permute-start | bytes 393224 | tf_op jit(solution)/shard_map/ppermute | solution.py:22
  6.8 0.0 collective-permute-start.1
  6.8 0.6 %collective-permute-start.2 = (bf16[256,256]{1,0:T(8,128)(2,1)S(1)}, bf16[256,256]{1,0:T(8,128)(2,1)S(1)}, u32[]{:S(2)}, u32[]{:S(2)}) collective-permute-start(bf16[256,256]{1,0:T(8,128)(2,1)S(1)} %get-tuple-element.40), channel_id=1, source_target_pairs={{0,4},{4,0},{8,12},{12,8},{1,5},{5,1},{9,13},{13,9},{2,6},{6,2},{1... | collective-permute-start | bytes 393224 | tf_op jit(solution)/shard_map/ppermute | solution.py:22
  7.5 1.2 %shard_map.140 = (bf16[256,256]{1,0:T(8,128)(2,1)S(1)}, bf16[2,1,32,128]{3,2,1,0:T(8,128)(2,1)S(1)}, bf16[2,1,4,256]{3,2,1,0:T(4,128)(2,1)S(1)}, f32[32,512]{1,0...) custom-call(bf16[4,2,128,256]{3,2,1,0:T(8,128)(2,1)} %kv_ref.2, ...), custom_call_target="tpu_custom_call" | custom-call | bytes 36000 | tf_op jit(solution)/shard_map/pallas_call | solution.py:428
  8.6 3.8 %shard_map.141 = (bf16[2048,1024]{1,0:T(8,128)(2,1)S(1)}, bf16[2048,1024]{1,0:T(8,128)(2,1)S(1)}, f32[4,2,16,1024]{3,2,1,0:T(8,128)S(1)}, f32[4,2,1,1024]{3,2,1,0:T(1,128)S(1)}) custom-call(bf16[4096,1024]{1,0:T(8,128)(2,1)} %weight_hbm, f32[2,1,8192]{2,1,0:T(1,128)} %dt_hbm.1, bf16[2,8192]{1,0:T(2,128)(2,1)} %bitcast.3, f32[2,1,2,16]{3,2,1,0:T(2,128)} %bc_hbm.1, ...), custom_call_target="tpu_custom_call" | custom-call | bytes 36000 | tf_op jit(solution)/shard_map/pallas_call | solution.py:448
  12.4 0.0 collective-permute-done.rest_3_
  12.4 5.5 %collective-permute-done.1.rest_2_ = bf16[256,256]{1,0:T(8,128)(2,1)S(1)} collective-permute-done((bf16[256,256]{1,0:T(8,128)(2,1)S(1)}, bf16[256,256]{1,0:T(8,128)(2,1)S(1)}, u32[]{:S(2)}, u32[]{:S(2)}) %collective-permute-start.1) | collective-permute-done | bytes 131104 | tf_op jit(solution)/shard_map/ppermute | solution.py:22
  17.9 0.0 collective-permute-done.2.rest_1_
  17.9 0.5 %shard_map.142 = (bf16[16,256]{1,0:T(8,128)(2,1)S(1)}, bf16[80,256]{1,0:T(8,128)(2,1)S(1)}, bf16[80,256]{1,0:T(8,128)(2,1)S(1)}, bf16[80,256]{1,0:T(8,128)(2,1)S...) custom-call(bf16[2,1,32,128]{3,2,1,0:T(8,128)(2,1)S(1)} %get-tuple-element.42.q_ref, ...), custom_call_target="tpu_custom_call" | custom-call | bytes 36000 | tf_op jit(solution)/shard_map/pallas_call | solution.py:473
  18.4 0.1 collective-permute-start.3
  18.5 2.5 %collective-permute-start.4 = (bf16[80,256]{1,0:T(8,128)(2,1)S(1)}, bf16[80,256]{1,0:T(8,128)(2,1)S(1)}, u32[]{:S(2)}, u32[]{:S(2)}) collective-permute-start(bf16[80,256]{1,0:T(8,128)(2,1)S(1)} %get-tuple-element.63), channel_id=1, source_target_pairs={{0,12},{4,8},{8,4},{12,0},{1,13},{5,9},{9,5},{13,1},{2,14},{6,10},... | collective-permute-start | bytes 122888 | tf_op jit(solution)/shard_map/ppermute | solution.py:22
  21.0 0.9 %collective-permute-start.5 = (bf16[80,256]{1,0:T(8,128)(2,1)S(1)}, bf16[80,256]{1,0:T(8,128)(2,1)S(1)}, u32[]{:S(2)}, u32[]{:S(2)}) collective-permute-start(bf16[80,256]{1,0:T(8,128)(2,1)S(1)} %get-tuple-element.64), channel_id=1, source_target_pairs={{0,4},{4,0},{8,12},{12,8},{1,5},{5,1},{9,13},{13,9},{2,6},{6,2},{1... | collective-permute-start | bytes 122888 | tf_op jit(solution)/shard_map/ppermute | solution.py:22
  22.0 1.9 %collective-permute-done.3.rest_1_ = bf16[80,256]{1,0:T(8,128)(2,1)S(1)} collective-permute-done((bf16[80,256]{1,0:T(8,128)(2,1)S(1)}, bf16[80,256]{1,0:T(8,128)(2,1)S(1)}, u32[]{:S(2)}, u32[]{:S(2)}) %collective-permute-start.3) | collective-permute-done | bytes 40992 | tf_op jit(solution)/shard_map/ppermute | solution.py:22
  23.8 0.5 %collective-permute-done.4.rest_2_ = bf16[80,256]{1,0:T(8,128)(2,1)S(1)} collective-permute-done((bf16[80,256]{1,0:T(8,128)(2,1)S(1)}, bf16[80,256]{1,0:T(8,128)(2,1)S(1)}, u32[]{:S(2)}, u32[]{:S(2)}) %collective-permute-start.4) | collective-permute-done | bytes 40992 | tf_op jit(solution)/shard_map/ppermute | solution.py:22
  24.3 0.7 %collective-permute-done.5.rest_3_ = bf16[80,256]{1,0:T(8,128)(2,1)S(1)} collective-permute-done((bf16[80,256]{1,0:T(8,128)(2,1)S(1)}, bf16[80,256]{1,0:T(8,128)(2,1)S(1)}, u32[]{:S(2)}, u32[]{:S(2)}) %collective-permute-start.5) | collective-permute-done | bytes 40992 | tf_op jit(solution)/shard_map/ppermute | solution.py:22
  25.0 0.1 shard_map.143
  25.2 0.1 collective-permute-start.7
  25.2 0.5 %collective-permute-start.6 = (bf16[8,2048]{1,0:T(8,128)(2,1)S(1)}, bf16[8,2048]{1,0:T(8,128)(2,1)S(1)}, u32[]{:S(2)}, u32[]{:S(2)}) collective-permute-start(bf16[8,2048]{1,0:T(8,128)(2,1)S(1)} %get-tuple-element.65.attn_ref), channel_id=1, source_target_pairs={{0,1},{1,0},{2,3},{3,2},{4,5},{5,4},{6,7},{7,6},{8,9},{9,8},{10,11... | collective-permute-start | bytes 98312 | tf_op jit(solution)/shard_map/ppermute | solution.py:22
  25.7 0.1 collective-permute-start.8
  25.8 0.6 %shard_map.144.acc_ref = f32[8,1024]{1,0:T(8,128)S(1)} custom-call(bf16[8,2048]{1,0:T(8,128)(2,1)S(1)} %get-tuple-element.65.attn_ref, bf16[2048,1024]{1,0:T(8,128)(2,1)S(1)} %get-tuple-element.66.weight_ref), custom_call_target="tpu_custom_call" | custom-call | bytes 25200 | tf_op jit(solution)/shard_map/pallas_call | solution.py:491
  26.4 0.2 collective-permute-done.6.attn_ref
  26.6 0.7 %shard_map.145 = (f32[2,2,1024]{2,1,0:T(2,128)S(1)}, f32[2,2,1024]{2,1,0:T(2,128)S(1)}) custom-call(f32[8,1024]{1,0:T(8,128)S(1)} %shard_map.144.acc_ref, bf16[8,2048]{1,0:T(8,128)(2,1)S(1)} %collective-permute-done.6.attn_ref, bf16[2048,1024]{1,0:T(8,128)(2,1)S(1)} %get-tuple-element.67.weight_ref), custom_call_target="tpu_custom_call" | custom-call | bytes 25200 | tf_op jit(solution)/shard_map/pallas_call | solution.py:495
  27.3 1.5 %collective-permute-start.9 = (f32[2,2,1024]{2,1,0:T(2,128)S(1)}, f32[2,2,1024]{2,1,0:T(2,128)S(1)}, u32[]{:S(2)}, u32[]{:S(2)}) collective-permute-start(f32[2,2,1024]{2,1,0:T(2,128)S(1)} %get-tuple-element.74), channel_id=1, source_target_pairs={{0,2},{2,0},{1,3},{3,1},{4,6},{6,4},{5,7},{7,5},{8,10},{10,8},{9,1... | collective-permute-start | bytes 49160 | tf_op jit(solution)/shard_map/ppermute | solution.py:22
  28.8 0.0 collective-permute-done.8.rest_0_
  28.8 0.0 collective-permute-done.7.got_ref
  28.8 0.9 %shard_map.146 = (bf16[1,4,1,128,256]{4,3,2,1,0:T(8,128)(2,1)}, f32[2,1,8192]{2,1,0:T(1,128)}) custom-call(bf16[2,1,128,256]{3,2,1,0:T(8,128)(2,1)S(1)} %get-tuple-element.69.kept_ref, bf16[2,1,128,256]{3,2,1,0:T(8,128)(2,1)S(1)} %collective-permute-done.7.got_ref, f32[2,4,1,1024]{3,2,1,0:T(1,128)S(1)} %get-tuple-element.71.mamba_ref, ...), custom_call_target="tpu_custom_call" | custom-call | bytes 36000 | tf_op jit(solution)/shard_map/pallas_call | solution.py:506
  29.7 1.3 %collective-permute-done.9.refs_1_ = f32[2,2,1024]{2,1,0:T(2,128)S(1)} collective-permute-done((f32[2,2,1024]{2,1,0:T(2,128)S(1)}, f32[2,2,1024]{2,1,0:T(2,128)S(1)}, u32[]{:S(2)}, u32[]{:S(2)}) %collective-permute-start.9) | collective-permute-done | bytes 16416 | tf_op jit(solution)/shard_map/ppermute | solution.py:22
  31.1 0.6 %shard_map.147 = bf16[2,2,1024]{2,1,0:T(2,128)(2,1)} custom-call(f32[2,2,1024]{2,1,0:T(2,128)S(1)} %get-tuple-element.68.refs_0_, f32[2,2,1024]{2,1,0:T(2,128)S(1)} %collective-permute-done.9.refs_1_), custom_call_target="tpu_custom_call" | custom-call | bytes 21600 | tf_op jit(solution)/shard_map/pallas_call | solution.py:517
Async XLA Ops:
  1.7 10.7 %collective-permute-start = (bf16[256,256]{1,0:T(8,128)(2,1)S(1)}, bf16[256,256]{1,0:T(8,128)(2,1)S(1)}, u32[]{:S(2)}, u32[]{:S(2)}) collective-permute-start(bf16[256,256]{1,0:T(8,128)(2,1)S(1)} %get-tuple-element.47), channel_id=1, source_target_pairs={{0,12},{4,8},{8,4},{12,0},{1,13},{5,9},{9,5},{13,1},{2,14},{6,10},... | collective-permute-start | bytes 393224 | tf_op jit(solution)/shard_map/ppermute | solution.py:22
  6.8 11.1 %collective-permute-start.1 = (bf16[256,256]{1,0:T(8,128)(2,1)S(1)}, bf16[256,256]{1,0:T(8,128)(2,1)S(1)}, u32[]{:S(2)}, u32[]{:S(2)}) collective-permute-start(bf16[256,256]{1,0:T(8,128)(2,1)S(1)} %get-tuple-element.48), channel_id=1, source_target_pairs={{0,8},{4,12},{8,0},{12,4},{1,9},{5,13},{9,1},{13,5},{2,10},{6,14},... | collective-permute-start | bytes 393224 | tf_op jit(solution)/shard_map/ppermute | solution.py:22
  6.8 11.1 %collective-permute-start.2 = (bf16[256,256]{1,0:T(8,128)(2,1)S(1)}, bf16[256,256]{1,0:T(8,128)(2,1)S(1)}, u32[]{:S(2)}, u32[]{:S(2)}) collective-permute-start(bf16[256,256]{1,0:T(8,128)(2,1)S(1)} %get-tuple-element.40), channel_id=1, source_target_pairs={{0,4},{4,0},{8,12},{12,8},{1,5},{5,1},{9,13},{13,9},{2,6},{6,2},{1... | collective-permute-start | bytes 393224 | tf_op jit(solution)/shard_map/ppermute | solution.py:22
  18.4 5.4 %collective-permute-start.3 = (bf16[80,256]{1,0:T(8,128)(2,1)S(1)}, bf16[80,256]{1,0:T(8,128)(2,1)S(1)}, u32[]{:S(2)}, u32[]{:S(2)}) collective-permute-start(bf16[80,256]{1,0:T(8,128)(2,1)S(1)} %get-tuple-element.62), channel_id=1, source_target_pairs={{0,8},{4,12},{8,0},{12,4},{1,9},{5,13},{9,1},{13,5},{2,10},{6,14},... | collective-permute-start | bytes 122888 | tf_op jit(solution)/shard_map/ppermute | solution.py:22
  18.5 5.9 %collective-permute-start.4 = (bf16[80,256]{1,0:T(8,128)(2,1)S(1)}, bf16[80,256]{1,0:T(8,128)(2,1)S(1)}, u32[]{:S(2)}, u32[]{:S(2)}) collective-permute-start(bf16[80,256]{1,0:T(8,128)(2,1)S(1)} %get-tuple-element.63), channel_id=1, source_target_pairs={{0,12},{4,8},{8,4},{12,0},{1,13},{5,9},{9,5},{13,1},{2,14},{6,10},... | collective-permute-start | bytes 122888 | tf_op jit(solution)/shard_map/ppermute | solution.py:22
  21.0 4.0 %collective-permute-start.5 = (bf16[80,256]{1,0:T(8,128)(2,1)S(1)}, bf16[80,256]{1,0:T(8,128)(2,1)S(1)}, u32[]{:S(2)}, u32[]{:S(2)}) collective-permute-start(bf16[80,256]{1,0:T(8,128)(2,1)S(1)} %get-tuple-element.64), channel_id=1, source_target_pairs={{0,4},{4,0},{8,12},{12,8},{1,5},{5,1},{9,13},{13,9},{2,6},{6,2},{1... | collective-permute-start | bytes 122888 | tf_op jit(solution)/shard_map/ppermute | solution.py:22
  25.2 3.7 %collective-permute-start.7 = (bf16[2,1,128,256]{3,2,1,0:T(8,128)(2,1)S(1)}, bf16[2,1,128,256]{3,2,1,0:T(8,128)(2,1)S(1)}, u32[]{:S(2)}, u32[]{:S(2)}) collective-permute-start(bf16[2,1,128,256]{3,2,1,0:T(8,128)(2,1)S(1)} %get-tuple-element.72), channel_id=1, source_target_pairs={{0,1},{1,0},{2,3},{3,2},{4,5},{5,4},{6,7},{7,6},{8,9},{9,8},{10,11... | collective-permute-start | bytes 393224 | tf_op jit(solution)/shard_map/ppermute | solution.py:22
  25.2 1.4 %collective-permute-start.6 = (bf16[8,2048]{1,0:T(8,128)(2,1)S(1)}, bf16[8,2048]{1,0:T(8,128)(2,1)S(1)}, u32[]{:S(2)}, u32[]{:S(2)}) collective-permute-start(bf16[8,2048]{1,0:T(8,128)(2,1)S(1)} %get-tuple-element.65.attn_ref), channel_id=1, source_target_pairs={{0,1},{1,0},{2,3},{3,2},{4,5},{5,4},{6,7},{7,6},{8,9},{9,8},{10,11... | collective-permute-start | bytes 98312 | tf_op jit(solution)/shard_map/ppermute | solution.py:22
  25.7 3.1 %collective-permute-start.8 = (f32[2,4,1,1024]{3,2,1,0:T(1,128)S(1)}, f32[2,4,1,1024]{3,2,1,0:T(1,128)S(1)}, u32[]{:S(2)}, u32[]{:S(2)}) collective-permute-start(f32[2,4,1,1024]{3,2,1,0:T(1,128)S(1)} %get-tuple-element.71.mamba_ref), channel_id=1, source_target_pairs={{0,1},{1,0},{2,3},{3,2},{4,5},{5,4},{6,7},{7,6},{8,9},{9,8},{10,11... | collective-permute-start | bytes 98312 | tf_op jit(solution)/shard_map/ppermute | solution.py:22
  27.3 3.8 %collective-permute-start.9 = (f32[2,2,1024]{2,1,0:T(2,128)S(1)}, f32[2,2,1024]{2,1,0:T(2,128)S(1)}, u32[]{:S(2)}, u32[]{:S(2)}) collective-permute-start(f32[2,2,1024]{2,1,0:T(2,128)S(1)} %get-tuple-element.74), channel_id=1, source_target_pairs={{0,2},{2,0},{1,3},{3,1},{4,6},{6,4},{5,7},{7,5},{8,10},{10,8},{9,1... | collective-permute-start | bytes 49160 | tf_op jit(solution)/shard_map/ppermute | solution.py:22

commit v10 on v9

--- a/solution.py
+++ b/solution.py
@@ -9,6 +9,7 @@
 
 BLOCK = 128
 PIECES = 4
+CUTS = 4
 NEG = -1e30
 BF = jnp.bfloat16
 F32 = jnp.float32
@@ -80,11 +81,16 @@
     outs, sems = rest[:-1], rest[-1]
     me = lax.axis_index("seq")
     copy = copier(sems)
+    cut = BLOCK // CUTS
     run_all(
         [
-            copy(kv_ref.at[me ^ c, j], outs[c - 1].at[pl.ds(j * BLOCK, BLOCK)])
+            copy(
+                kv_ref.at[me ^ c, j, pl.ds(i * cut, cut)],
+                outs[c - 1].at[pl.ds(j * BLOCK + i * cut, cut)],
+            )
             for c in range(count - 1, 0, -1)
             for j in range(kv_ref.shape[1])
+            for i in range(CUTS)
         ]
     )
 
@@ -422,7 +428,7 @@
         [block_shape] * (count - 1),
         [HB],
         [VM] * (count - 1),
-        [DMA(((count - 1) * heads,))],
+        [DMA(((count - 1) * heads * CUTS,))],
     )(prefill_kv)
     moved = [shift(pieces[c - 1], "seq", c) for c in range(count - 1, 0, -1)][::-1]
     own_piece, q_near, new_near, bias, picks, *states = call(
@@ -480,6 +486,8 @@
     )(q_near, new_near, bias, picks, *kv, *states[1:])
     order = [*range(2, count), 1]
     gathered = [shift(sends[c], "seq", c) for c in order]
+    got = shift(sent, "rep", 1)
+    *gathered, got = after([*gathered, got])
     attn, mamba = call(
         functools.partial(collect, count, heads, steps, group),
         [shape((steps * count, half), BF), shape((steps, count, 1, part), F32)],
@@ -500,7 +508,7 @@
         us=0.7,
     )(own_sum, attn_other, other_weight)
     sums = [sums[0]] + [shift(sums[c], "head", c) for c in range(1, heads_count)]
-    got = shift(after([sent], mamba)[0], "rep", 1)
+    mamba = after([mamba], own_sum)[0]
     kept = after([kept], sums[0])[0]
     operands = [kept, got, mamba] + ([shift(mamba, "rep", 1)] if split else [])
     handoff, mamba_out = call(

time: 31.9 us -> 32.8 us (1.028)
  waiting for transfers between devices: 10.1 us -> 10.7 us
    ppermute x10, waiting for transfers between devices: 10.1 us -> 10.7 us  [shift(): return lax.ppermute(x, axis, [(i, i ^ c) for i in range(size)])]
  transfers between devices with their start and end apart: 10 -> 10, of which waited for: 6 -> 4; matrix products, arithmetic and copies ran while one was open for 0% -> 0% of each run, Pallas kernels for 22% -> 22%
where the time goes in v10:
time: 32.8 us; the launch traced here: 32.4 us
  starting transfers between devices  11.5 us (35%)
  waiting for transfers between devices  10.7 us (33%)
  Pallas kernels  9.51 us (29%)
  between operations  0.71 us (2%)
    ppermute x10, starting transfers between devices, shift(): return lax.ppermute(x, axis, [(i, i ^ c) for i in range(size)])  11.5 us
    ppermute x10, waiting for transfers between devices, shift(): return lax.ppermute(x, axis, [(i, i ^ c) for i in range(size)])  10.7 us
    pallas_call x1, Pallas kernels, per_device(): call(functools.partial(prepare, count, split), [half_weight, half_weight,...  3.76 us
    pallas_call x1, Pallas kernels, per_device(): call(functools.partial(stage_blocks, count), [block_shape] * (count - 1),...  1.16 us
    pallas_call x1, Pallas kernels, per_device(): call(functools.partial(stage_rest, count, split), [block_shape, shape(que...  1.15 us
    pallas_call x1, Pallas kernels, per_device(): call(functools.partial(assemble, split), [shape((1, dec_heads, keep_rep,...  0.89 us
    pallas_call x1, Pallas kernels, per_device(): call(functools.partial(project_other, heads_count, count), [shape((steps,...  0.67 us
  transfers between devices with their start and end apart: 10, of which 4 were waited for; matrix products, arithmetic and copies ran while one was open for 0% of the time, Pallas kernels for 22%

profile of v10, /device:TPU:0, one launch (start us, length us, event | category | flops | bytes accessed | tf_op | source)
XLA Modules:
  0.0 32.4 jit_solution(10165378390717092375)
XLA Ops:
  0.6 1.2 %shard_map.139 = (bf16[256,256]{1,0:T(8,128)(2,1)S(1)}, bf16[256,256]{1,0:T(8,128)(2,1)S(1)}, bf16[256,256]{1,0:T(8,128)(2,1)S(1)}) custom-call(bf16[4,2,128,256]{3,2,1,0:T(8,128)(2,1)} %kv_ref.2), custom_call_target="tpu_custom_call" | custom-call | bytes 36000 | tf_op jit(solution)/shard_map/pallas_call | solution.py:426
  1.8 5.1 %collective-permute-start = (bf16[256,256]{1,0:T(8,128)(2,1)S(1)}, bf16[256,256]{1,0:T(8,128)(2,1)S(1)}, u32[]{:S(2)}, u32[]{:S(2)}) collective-permute-start(bf16[256,256]{1,0:T(8,128)(2,1)S(1)} %get-tuple-element.51), channel_id=1, source_target_pairs={{0,12},{4,8},{8,4},{12,0},{1,13},{5,9},{9,5},{13,1},{2,14},{6,10},... | collective-permute-start | bytes 393224 | tf_op jit(solution)/shard_map/ppermute | solution.py:23
  6.9 0.0 collective-permute-start.1
  6.9 0.6 %collective-permute-start.2 = (bf16[256,256]{1,0:T(8,128)(2,1)S(1)}, bf16[256,256]{1,0:T(8,128)(2,1)S(1)}, u32[]{:S(2)}, u32[]{:S(2)}) collective-permute-start(bf16[256,256]{1,0:T(8,128)(2,1)S(1)} %get-tuple-element.44), channel_id=1, source_target_pairs={{0,4},{4,0},{8,12},{12,8},{1,5},{5,1},{9,13},{13,9},{2,6},{6,2},{1... | collective-permute-start | bytes 393224 | tf_op jit(solution)/shard_map/ppermute | solution.py:23
  7.6 1.2 %shard_map.140 = (bf16[256,256]{1,0:T(8,128)(2,1)S(1)}, bf16[2,1,32,128]{3,2,1,0:T(8,128)(2,1)S(1)}, bf16[2,1,4,256]{3,2,1,0:T(4,128)(2,1)S(1)}, f32[32,512]{1,0...) custom-call(bf16[4,2,128,256]{3,2,1,0:T(8,128)(2,1)} %kv_ref.2, ...), custom_call_target="tpu_custom_call" | custom-call | bytes 36000 | tf_op jit(solution)/shard_map/pallas_call | solution.py:434
  8.7 3.8 %shard_map.141 = (bf16[2048,1024]{1,0:T(8,128)(2,1)S(1)}, bf16[2048,1024]{1,0:T(8,128)(2,1)S(1)}, f32[4,2,16,1024]{3,2,1,0:T(8,128)S(1)}, f32[4,2,1,1024]{3,2,1,0:T(1,128)S(1)}) custom-call(bf16[4096,1024]{1,0:T(8,128)(2,1)} %weight_hbm, f32[2,1,8192]{2,1,0:T(1,128)} %dt_hbm.1, bf16[2,8192]{1,0:T(2,128)(2,1)} %bitcast.3, f32[2,1,2,16]{3,2,1,0:T(2,128)} %bc_hbm.1, ...), custom_call_target="tpu_custom_call" | custom-call | bytes 36000 | tf_op jit(solution)/shard_map/pallas_call | solution.py:454
  12.5 0.0 collective-permute-done.rest_3_
  12.5 5.5 %collective-permute-done.1.rest_2_ = bf16[256,256]{1,0:T(8,128)(2,1)S(1)} collective-permute-done((bf16[256,256]{1,0:T(8,128)(2,1)S(1)}, bf16[256,256]{1,0:T(8,128)(2,1)S(1)}, u32[]{:S(2)}, u32[]{:S(2)}) %collective-permute-start.1) | collective-permute-done | bytes 131104 | tf_op jit(solution)/shard_map/ppermute | solution.py:23
  18.0 0.0 collective-permute-done.2.rest_1_
  18.0 0.5 %shard_map.142 = (bf16[16,256]{1,0:T(8,128)(2,1)S(1)}, bf16[80,256]{1,0:T(8,128)(2,1)S(1)}, bf16[80,256]{1,0:T(8,128)(2,1)S(1)}, bf16[80,256]{1,0:T(8,128)(2,1)S...) custom-call(bf16[2,1,32,128]{3,2,1,0:T(8,128)(2,1)S(1)} %get-tuple-element.46.q_ref, ...), custom_call_target="tpu_custom_call" | custom-call | bytes 36000 | tf_op jit(solution)/shard_map/pallas_call | solution.py:479
  18.5 0.1 collective-permute-start.6
  18.6 0.1 collective-permute-start.3
  18.7 2.5 %collective-permute-start.4 = (bf16[80,256]{1,0:T(8,128)(2,1)S(1)}, bf16[80,256]{1,0:T(8,128)(2,1)S(1)}, u32[]{:S(2)}, u32[]{:S(2)}) collective-permute-start(bf16[80,256]{1,0:T(8,128)(2,1)S(1)} %get-tuple-element.67), channel_id=1, source_target_pairs={{0,12},{4,8},{8,4},{12,0},{1,13},{5,9},{9,5},{13,1},{2,14},{6,10},... | collective-permute-start | bytes 122888 | tf_op jit(solution)/shard_map/ppermute | solution.py:23
  21.2 0.9 %collective-permute-start.5 = (bf16[80,256]{1,0:T(8,128)(2,1)S(1)}, bf16[80,256]{1,0:T(8,128)(2,1)S(1)}, u32[]{:S(2)}, u32[]{:S(2)}) collective-permute-start(bf16[80,256]{1,0:T(8,128)(2,1)S(1)} %get-tuple-element.68), channel_id=1, source_target_pairs={{0,4},{4,0},{8,12},{12,8},{1,5},{5,1},{9,13},{13,9},{2,6},{6,2},{1... | collective-permute-start | bytes 122888 | tf_op jit(solution)/shard_map/ppermute | solution.py:23
  22.1 3.0 %collective-permute-done.3.rest_1_ = bf16[80,256]{1,0:T(8,128)(2,1)S(1)} collective-permute-done((bf16[80,256]{1,0:T(8,128)(2,1)S(1)}, bf16[80,256]{1,0:T(8,128)(2,1)S(1)}, u32[]{:S(2)}, u32[]{:S(2)}) %collective-permute-start.3) | collective-permute-done | bytes 40992 | tf_op jit(solution)/shard_map/ppermute | solution.py:23
  25.1 0.0 collective-permute-done.4.rest_2_
  25.1 0.8 %collective-permute-done.5.rest_3_ = bf16[80,256]{1,0:T(8,128)(2,1)S(1)} collective-permute-done((bf16[80,256]{1,0:T(8,128)(2,1)S(1)}, bf16[80,256]{1,0:T(8,128)(2,1)S(1)}, u32[]{:S(2)}, u32[]{:S(2)}) %collective-permute-start.5) | collective-permute-done | bytes 40992 | tf_op jit(solution)/shard_map/ppermute | solution.py:23
  25.9 0.0 collective-permute-done.6.got_ref
  25.9 0.1 shard_map.143
  26.0 0.1 collective-permute-start.7
  26.1 0.6 %shard_map.144.acc_ref = f32[8,1024]{1,0:T(8,128)S(1)} custom-call(bf16[8,2048]{1,0:T(8,128)(2,1)S(1)} %get-tuple-element.73.attn_ref, bf16[2048,1024]{1,0:T(8,128)(2,1)S(1)} %get-tuple-element.74.weight_ref), custom_call_target="tpu_custom_call" | custom-call | bytes 25200 | tf_op jit(solution)/shard_map/pallas_call | solution.py:499
  26.8 0.5 %collective-permute-start.8 = (f32[2,4,1,1024]{3,2,1,0:T(1,128)S(1)}, f32[2,4,1,1024]{3,2,1,0:T(1,128)S(1)}, u32[]{:S(2)}, u32[]{:S(2)}) collective-permute-start(f32[2,4,1,1024]{3,2,1,0:T(1,128)S(1)} %get-tuple-element.80.mamba_ref), channel_id=1, source_target_pairs={{0,1},{1,0},{2,3},{3,2},{4,5},{5,4},{6,7},{7,6},{8,9},{9,8},{10,11... | collective-permute-start | bytes 98312 | tf_op jit(solution)/shard_map/ppermute | solution.py:23
  27.3 0.0 collective-permute-done.7.attn_ref
  27.3 0.7 %shard_map.145 = (f32[2,2,1024]{2,1,0:T(2,128)S(1)}, f32[2,2,1024]{2,1,0:T(2,128)S(1)}) custom-call(f32[8,1024]{1,0:T(8,128)S(1)} %shard_map.144.acc_ref, bf16[8,2048]{1,0:T(8,128)(2,1)S(1)} %collective-permute-done.7.attn_ref, bf16[2048,1024]{1,0:T(8,128)(2,1)S(1)} %get-tuple-element.75.weight_ref), custom_call_target="tpu_custom_call" | custom-call | bytes 25200 | tf_op jit(solution)/shard_map/pallas_call | solution.py:503
  28.0 1.5 %collective-permute-start.9 = (f32[2,2,1024]{2,1,0:T(2,128)S(1)}, f32[2,2,1024]{2,1,0:T(2,128)S(1)}, u32[]{:S(2)}, u32[]{:S(2)}) collective-permute-start(f32[2,2,1024]{2,1,0:T(2,128)S(1)} %get-tuple-element.82), channel_id=1, source_target_pairs={{0,2},{2,0},{1,3},{3,1},{4,6},{6,4},{5,7},{7,5},{8,10},{10,8},{9,1... | collective-permute-start | bytes 49160 | tf_op jit(solution)/shard_map/ppermute | solution.py:23
  29.5 0.0 collective-permute-done.8.rest_0_
  29.5 0.9 %shard_map.146 = (bf16[1,4,1,128,256]{4,3,2,1,0:T(8,128)(2,1)}, f32[2,1,8192]{2,1,0:T(1,128)}) custom-call(bf16[2,1,128,256]{3,2,1,0:T(8,128)(2,1)S(1)} %get-tuple-element.77.kept_ref, bf16[2,1,128,256]{3,2,1,0:T(8,128)(2,1)S(1)} %collective-permute-done.6.got_ref, f32[2,4,1,1024]{3,2,1,0:T(1,128)S(1)} %get-tuple-element.80.mamba_ref, ...), custom_call_target="tpu_custom_call" | custom-call | bytes 36000 | tf_op jit(solution)/shard_map/pallas_call | solution.py:514
  30.4 1.3 %collective-permute-done.9.refs_1_ = f32[2,2,1024]{2,1,0:T(2,128)S(1)} collective-permute-done((f32[2,2,1024]{2,1,0:T(2,128)S(1)}, f32[2,2,1024]{2,1,0:T(2,128)S(1)}, u32[]{:S(2)}, u32[]{:S(2)}) %collective-permute-start.9) | collective-permute-done | bytes 16416 | tf_op jit(solution)/shard_map/ppermute | solution.py:23
  31.8 0.6 %shard_map.147 = bf16[2,2,1024]{2,1,0:T(2,128)(2,1)} custom-call(f32[2,2,1024]{2,1,0:T(2,128)S(1)} %get-tuple-element.76.refs_0_, f32[2,2,1024]{2,1,0:T(2,128)S(1)} %collective-permute-done.9.refs_1_), custom_call_target="tpu_custom_call" | custom-call | bytes 21600 | tf_op jit(solution)/shard_map/pallas_call | solution.py:525
Async XLA Ops:
  1.8 10.7 %collective-permute-start = (bf16[256,256]{1,0:T(8,128)(2,1)S(1)}, bf16[256,256]{1,0:T(8,128)(2,1)S(1)}, u32[]{:S(2)}, u32[]{:S(2)}) collective-permute-start(bf16[256,256]{1,0:T(8,128)(2,1)S(1)} %get-tuple-element.51), channel_id=1, source_target_pairs={{0,12},{4,8},{8,4},{12,0},{1,13},{5,9},{9,5},{13,1},{2,14},{6,10},... | collective-permute-start | bytes 393224 | tf_op jit(solution)/shard_map/ppermute | solution.py:23
  6.9 11.1 %collective-permute-start.1 = (bf16[256,256]{1,0:T(8,128)(2,1)S(1)}, bf16[256,256]{1,0:T(8,128)(2,1)S(1)}, u32[]{:S(2)}, u32[]{:S(2)}) collective-permute-start(bf16[256,256]{1,0:T(8,128)(2,1)S(1)} %get-tuple-element.52), channel_id=1, source_target_pairs={{0,8},{4,12},{8,0},{12,4},{1,9},{5,13},{9,1},{13,5},{2,10},{6,14},... | collective-permute-start | bytes 393224 | tf_op jit(solution)/shard_map/ppermute | solution.py:23
  6.9 11.1 %collective-permute-start.2 = (bf16[256,256]{1,0:T(8,128)(2,1)S(1)}, bf16[256,256]{1,0:T(8,128)(2,1)S(1)}, u32[]{:S(2)}, u32[]{:S(2)}) collective-permute-start(bf16[256,256]{1,0:T(8,128)(2,1)S(1)} %get-tuple-element.44), channel_id=1, source_target_pairs={{0,4},{4,0},{8,12},{12,8},{1,5},{5,1},{9,13},{13,9},{2,6},{6,2},{1... | collective-permute-start | bytes 393224 | tf_op jit(solution)/shard_map/ppermute | solution.py:23
  18.5 7.4 %collective-permute-start.6 = (bf16[2,1,128,256]{3,2,1,0:T(8,128)(2,1)S(1)}, bf16[2,1,128,256]{3,2,1,0:T(8,128)(2,1)S(1)}, u32[]{:S(2)}, u32[]{:S(2)}) collective-permute-start(bf16[2,1,128,256]{3,2,1,0:T(8,128)(2,1)S(1)} %get-tuple-element.69), channel_id=1, source_target_pairs={{0,1},{1,0},{2,3},{3,2},{4,5},{5,4},{6,7},{7,6},{8,9},{9,8},{10,11... | collective-permute-start | bytes 393224 | tf_op jit(solution)/shard_map/ppermute | solution.py:23
  18.6 6.6 %collective-permute-start.3 = (bf16[80,256]{1,0:T(8,128)(2,1)S(1)}, bf16[80,256]{1,0:T(8,128)(2,1)S(1)}, u32[]{:S(2)}, u32[]{:S(2)}) collective-permute-start(bf16[80,256]{1,0:T(8,128)(2,1)S(1)} %get-tuple-element.66), channel_id=1, source_target_pairs={{0,8},{4,12},{8,0},{12,4},{1,9},{5,13},{9,1},{13,5},{2,10},{6,14},... | collective-permute-start | bytes 122888 | tf_op jit(solution)/shard_map/ppermute | solution.py:23
  18.7 6.5 %collective-permute-start.4 = (bf16[80,256]{1,0:T(8,128)(2,1)S(1)}, bf16[80,256]{1,0:T(8,128)(2,1)S(1)}, u32[]{:S(2)}, u32[]{:S(2)}) collective-permute-start(bf16[80,256]{1,0:T(8,128)(2,1)S(1)} %get-tuple-element.67), channel_id=1, source_target_pairs={{0,12},{4,8},{8,4},{12,0},{1,13},{5,9},{9,5},{13,1},{2,14},{6,10},... | collective-permute-start | bytes 122888 | tf_op jit(solution)/shard_map/ppermute | solution.py:23
  21.2 4.7 %collective-permute-start.5 = (bf16[80,256]{1,0:T(8,128)(2,1)S(1)}, bf16[80,256]{1,0:T(8,128)(2,1)S(1)}, u32[]{:S(2)}, u32[]{:S(2)}) collective-permute-start(bf16[80,256]{1,0:T(8,128)(2,1)S(1)} %get-tuple-element.68), channel_id=1, source_target_pairs={{0,4},{4,0},{8,12},{12,8},{1,5},{5,1},{9,13},{13,9},{2,6},{6,2},{1... | collective-permute-start | bytes 122888 | tf_op jit(solution)/shard_map/ppermute | solution.py:23
  26.0 1.3 %collective-permute-start.7 = (bf16[8,2048]{1,0:T(8,128)(2,1)S(1)}, bf16[8,2048]{1,0:T(8,128)(2,1)S(1)}, u32[]{:S(2)}, u32[]{:S(2)}) collective-permute-start(bf16[8,2048]{1,0:T(8,128)(2,1)S(1)} %get-tuple-element.73.attn_ref), channel_id=1, source_target_pairs={{0,1},{1,0},{2,3},{3,2},{4,5},{5,4},{6,7},{7,6},{8,9},{9,8},{10,11... | collective-permute-start | bytes 98312 | tf_op jit(solution)/shard_map/ppermute | solution.py:23
  26.8 2.8 %collective-permute-start.8 = (f32[2,4,1,1024]{3,2,1,0:T(1,128)S(1)}, f32[2,4,1,1024]{3,2,1,0:T(1,128)S(1)}, u32[]{:S(2)}, u32[]{:S(2)}) collective-permute-start(f32[2,4,1,1024]{3,2,1,0:T(1,128)S(1)} %get-tuple-element.80.mamba_ref), channel_id=1, source_target_pairs={{0,1},{1,0},{2,3},{3,2},{4,5},{5,4},{6,7},{7,6},{8,9},{9,8},{10,11... | collective-permute-start | bytes 98312 | tf_op jit(solution)/shard_map/ppermute | solution.py:23
  28.0 3.8 %collective-permute-start.9 = (f32[2,2,1024]{2,1,0:T(2,128)S(1)}, f32[2,2,1024]{2,1,0:T(2,128)S(1)}, u32[]{:S(2)}, u32[]{:S(2)}) collective-permute-start(f32[2,2,1024]{2,1,0:T(2,128)S(1)} %get-tuple-element.82), channel_id=1, source_target_pairs={{0,2},{2,0},{1,3},{3,1},{4,6},{6,4},{5,7},{7,5},{8,10},{10,8},{9,1... | collective-permute-start | bytes 49160 | tf_op jit(solution)/shard_map/ppermute | solution.py:23

commit v11 on v9

--- a/solution.py
+++ b/solution.py
@@ -22,13 +22,14 @@
     return lax.ppermute(x, axis, [(i, i ^ c) for i in range(size)])
 
 
-def call(body, out_shape, in_specs, out_specs, scratch=(), us=1.0):
+def call(body, out_shape, in_specs, out_specs, scratch=(), us=1.0, aliases=None):
     return pl.pallas_call(
         body,
         out_shape=out_shape,
         in_specs=in_specs,
         out_specs=out_specs,
         scratch_shapes=list(scratch),
+        input_output_aliases=aliases or {},
         cost_estimate=pl.CostEstimate(
             flops=0, bytes_accessed=int(us * 3.6e4), transcendentals=0
         ),
@@ -89,10 +90,10 @@
     )
 
 
-def stage_rest(count, split, kv_ref, q_ref, new_ref, state_ref, blocks_ref, counts_ref, *rest):
-    own_out, q_out, new_out, bias_out, pick_out = rest[:5]
-    states = rest[5 : 5 + count]
-    loaded, blocks, counts, sems, early = rest[5 + count :]
+def stage_others(count, split, sources, outs, scratch):
+    kv_ref, q_ref, new_ref, state_ref, blocks_ref, counts_ref = sources
+    own_out, q_out, new_out, bias_out, pick_out, *states = outs
+    loaded, blocks, counts, sems, early = scratch
     me, rep = lax.axis_index("seq"), lax.axis_index("rep")
     heads = kv_ref.shape[1]
     copy = copier(sems)
@@ -133,6 +134,24 @@
             )
     for move in moves:
         move.wait()
+
+
+def stage_first(count, split, *refs):
+    sources, pieces, outs = refs[:6], refs[6 : 5 + count], refs[5 + count : 10 + 2 * count]
+    block_sems, *scratch = refs[10 + 2 * count :]
+    stage_blocks(count, sources[0], *pieces, block_sems)
+
+    @pl.when(lax.axis_index("rep") == 1)
+    def _():
+        stage_others(count, split, sources, outs, scratch)
+
+
+def stage_second(count, split, *refs):
+    sources, outs, scratch = refs[:6], refs[11 + count : 16 + 2 * count], refs[16 + 2 * count :]
+
+    @pl.when(lax.axis_index("rep") == 0)
+    def _():
+        stage_others(count, split, sources, outs, scratch)
 
 
 def dot_f32(a, b, contract):
@@ -417,34 +436,38 @@
     half = heads * group * hd
     half_weight = pltpu.VMEM((half, columns), BF)
     block_shape = shape((heads * BLOCK, width), BF)
-    pieces = call(
-        functools.partial(stage_blocks, count),
-        [block_shape] * (count - 1),
-        [HB],
-        [VM] * (count - 1),
-        [DMA(((count - 1) * heads,))],
-    )(prefill_kv)
+    sources = (prefill_kv, queries, new_kv, prefill_state, blocks, kept_counts)
+    other_shapes = [
+        block_shape,
+        shape(queries.shape, BF),
+        shape(new_kv.shape, BF),
+        shape((all_rows, count * BLOCK), F32),
+        shape((reps, heads, keep_rep, count, 16, width), BF),
+    ] + [shape((state_rows(part), width), BF)] * count
+    other_scratch = [
+        pltpu.VMEM((count, ns, part), F32),
+        smem(blocks.shape, jnp.int32),
+        smem(kept_counts.shape, jnp.int32),
+        DMA((heads + 2,)),
+        DMA((count + 2,)),
+    ]
+    staged = call(
+        functools.partial(stage_first, count, split),
+        [block_shape] * (count - 1) + other_shapes,
+        [HB] * 6,
+        [VM] * (2 * count + 4),
+        [DMA(((count - 1) * heads,)), *other_scratch],
+    )(*sources)
+    pieces, others = staged[: count - 1], staged[count - 1 :]
     moved = [shift(pieces[c - 1], "seq", c) for c in range(count - 1, 0, -1)][::-1]
     own_piece, q_near, new_near, bias, picks, *states = call(
-        functools.partial(stage_rest, count, split),
-        [
-            block_shape,
-            shape(queries.shape, BF),
-            shape(new_kv.shape, BF),
-            shape((all_rows, count * BLOCK), F32),
-            shape((reps, heads, keep_rep, count, 16, width), BF),
-        ]
-        + [shape((state_rows(part), width), BF)] * count,
-        [HB] * 6,
+        functools.partial(stage_second, count, split),
+        other_shapes,
+        [HB] * 6 + [VM] * (5 + count),
         [VM] * (5 + count),
-        [
-            pltpu.VMEM((count, ns, part), F32),
-            smem(blocks.shape, jnp.int32),
-            smem(kept_counts.shape, jnp.int32),
-            DMA((heads + 2,)),
-            DMA((count + 2,)),
-        ],
-    )(*after([prefill_kv], pieces[0]), queries, new_kv, prefill_state, blocks, kept_counts)
+        other_scratch,
+        aliases={6 + i: i for i in range(5 + count)},
+    )(*sources, *others)
     own_weight, other_weight, slope, base = call(
         functools.partial(prepare, count, split),
         [

time: 31.9 us -> 33.4 us (1.047)
  waiting for transfers between devices: 10.1 us -> 11.5 us
    ppermute x10, waiting for transfers between devices: 10.1 us -> 11.5 us  [shift(): return lax.ppermute(x, axis, [(i, i ^ c) for i in range(size)])]
  transfers between devices with their start and end apart: 10 -> 10, of which waited for: 6 -> 5; matrix products, arithmetic and copies ran while one was open for 0% -> 0% of each run, Pallas kernels for 22% -> 21%
where the time goes in v11:
time: 33.4 us; the launch traced here: 33.2 us
  starting transfers between devices  11.5 us (34%)
  waiting for transfers between devices  11.5 us (34%)
  Pallas kernels  9.5 us (28%)
  between operations  0.71 us (2%)
    ppermute x10, starting transfers between devices, shift(): return lax.ppermute(x, axis, [(i, i ^ c) for i in range(size)])  11.5 us
    ppermute x10, waiting for transfers between devices, shift(): return lax.ppermute(x, axis, [(i, i ^ c) for i in range(size)])  11.5 us
    pallas_call x1, Pallas kernels, per_device(): call(functools.partial(prepare, count, split), [half_weight, half_weight,...  3.74 us
    pallas_call x1, Pallas kernels, per_device(): call(functools.partial(stage_second, count, split), other_shapes, [HB] *...  1.16 us
    pallas_call x1, Pallas kernels, per_device(): call(functools.partial(stage_first, count, split), [block_shape] * (count...  1.16 us
    pallas_call x1, Pallas kernels, per_device(): call(functools.partial(assemble, split), [shape((1, dec_heads, keep_rep,...  0.89 us
  transfers between devices with their start and end apart: 10, of which 5 were waited for; matrix products, arithmetic and copies ran while one was open for 0% of the time, Pallas kernels for 21%

profile of v11, /device:TPU:0, one launch (start us, length us, event | category | flops | bytes accessed | tf_op | source)
XLA Modules:
  0.0 33.2 jit_solution(15348070996314671094)
XLA Ops:
  0.6 1.2 %shard_map.139 = (bf16[256,256]{1,0:T(8,128)(2,1)S(1)}, bf16[256,256]{1,0:T(8,128)(2,1)S(1)}, bf16[256,256]{1,0:T(8,128)(2,1)S(1)}, bf16[256,256]{1,0:T(8,128)(2...) custom-call(bf16[4,2,128,256]{3,2,1,0:T(8,128)(2,1)} %refs_0_.3, ...), custom_call_target="tpu_custom_call" | custom-call | bytes 36000 | tf_op jit(solution)/shard_map/pallas_call | solution.py:454
  1.8 5.1 %collective-permute-start = (bf16[256,256]{1,0:T(8,128)(2,1)S(1)}, bf16[256,256]{1,0:T(8,128)(2,1)S(1)}, u32[]{:S(2)}, u32[]{:S(2)}) collective-permute-start(bf16[256,256]{1,0:T(8,128)(2,1)S(1)} %get-tuple-element.62), channel_id=1, source_target_pairs={{0,12},{4,8},{8,4},{12,0},{1,13},{5,9},{9,5},{13,1},{2,14},{6,10},... | collective-permute-start | bytes 393224 | tf_op jit(solution)/shard_map/ppermute | solution.py:22
  6.9 0.0 collective-permute-start.1
  6.9 0.6 %collective-permute-start.2 = (bf16[256,256]{1,0:T(8,128)(2,1)S(1)}, bf16[256,256]{1,0:T(8,128)(2,1)S(1)}, u32[]{:S(2)}, u32[]{:S(2)}) collective-permute-start(bf16[256,256]{1,0:T(8,128)(2,1)S(1)} %get-tuple-element.64), channel_id=1, source_target_pairs={{0,4},{4,0},{8,12},{12,8},{1,5},{5,1},{9,13},{13,9},{2,6},{6,2},{1... | collective-permute-start | bytes 393224 | tf_op jit(solution)/shard_map/ppermute | solution.py:22
  7.6 3.7 %shard_map.141 = (bf16[2048,1024]{1,0:T(8,128)(2,1)S(1)}, bf16[2048,1024]{1,0:T(8,128)(2,1)S(1)}, f32[4,2,16,1024]{3,2,1,0:T(8,128)S(1)}, f32[4,2,1,1024]{3,2,1,0:T(1,128)S(1)}) custom-call(bf16[4096,1024]{1,0:T(8,128)(2,1)} %weight_hbm, f32[2,1,8192]{2,1,0:T(1,128)} %dt_hbm.1, bf16[2,8192]{1,0:T(2,128)(2,1)} %bitcast.3, f32[2,1,2,16]{3,2,1,0:T(2,128)} %bc_hbm.1, ...), custom_call_target="tpu_custom_call" | custom-call | bytes 36000 | tf_op jit(solution)/shard_map/pallas_call | solution.py:471
  11.3 1.2 %shard_map.140 = (bf16[256,256]{1,0:T(8,128)(2,1)S(1)}, bf16[2,1,32,128]{3,2,1,0:T(8,128)(2,1)S(1)}, bf16[2,1,4,256]{3,2,1,0:T(4,128)(2,1)S(1)}, f32[32,512]{1,0...) custom-call(bf16[4,2,128,256]{3,2,1,0:T(8,128)(2,1)} %refs_0_.3, ...), custom_call_target="tpu_custom_call", output_to_operand_aliasing={{0}: (6, {}), {1}: (7, {}), {2}: (8, {}), {3}: (9, {}), {4}... | custom-call | bytes 36000 | tf_op jit(solution)/shard_map/pallas_call | solution.py:463
  12.5 0.0 collective-permute-done.rest_3_
  12.5 6.6 %collective-permute-done.1.rest_2_ = bf16[256,256]{1,0:T(8,128)(2,1)S(1)} collective-permute-done((bf16[256,256]{1,0:T(8,128)(2,1)S(1)}, bf16[256,256]{1,0:T(8,128)(2,1)S(1)}, u32[]{:S(2)}, u32[]{:S(2)}) %collective-permute-start.1) | collective-permute-done | bytes 131104 | tf_op jit(solution)/shard_map/ppermute | solution.py:22
  19.0 0.0 collective-permute-done.2.rest_1_
  19.0 0.5 %shard_map.142 = (bf16[16,256]{1,0:T(8,128)(2,1)S(1)}, bf16[80,256]{1,0:T(8,128)(2,1)S(1)}, bf16[80,256]{1,0:T(8,128)(2,1)S(1)}, bf16[80,256]{1,0:T(8,128)(2,1)S...) custom-call(bf16[2,1,32,128]{3,2,1,0:T(8,128)(2,1)S(1)} %get-tuple-element.57.q_ref, ...), custom_call_target="tpu_custom_call" | custom-call | bytes 36000 | tf_op jit(solution)/shard_map/pallas_call | solution.py:496
  19.6 0.1 collective-permute-start.3
  19.6 2.5 %collective-permute-start.4 = (bf16[80,256]{1,0:T(8,128)(2,1)S(1)}, bf16[80,256]{1,0:T(8,128)(2,1)S(1)}, u32[]{:S(2)}, u32[]{:S(2)}) collective-permute-start(bf16[80,256]{1,0:T(8,128)(2,1)S(1)} %get-tuple-element.79), channel_id=1, source_target_pairs={{0,12},{4,8},{8,4},{12,0},{1,13},{5,9},{9,5},{13,1},{2,14},{6,10},... | collective-permute-start | bytes 122888 | tf_op jit(solution)/shard_map/ppermute | solution.py:22
  22.2 0.9 %collective-permute-start.5 = (bf16[80,256]{1,0:T(8,128)(2,1)S(1)}, bf16[80,256]{1,0:T(8,128)(2,1)S(1)}, u32[]{:S(2)}, u32[]{:S(2)}) collective-permute-start(bf16[80,256]{1,0:T(8,128)(2,1)S(1)} %get-tuple-element.80), channel_id=1, source_target_pairs={{0,4},{4,0},{8,12},{12,8},{1,5},{5,1},{9,13},{13,9},{2,6},{6,2},{1... | collective-permute-start | bytes 122888 | tf_op jit(solution)/shard_map/ppermute | solution.py:22
  23.1 2.7 %collective-permute-done.3.rest_1_ = bf16[80,256]{1,0:T(8,128)(2,1)S(1)} collective-permute-done((bf16[80,256]{1,0:T(8,128)(2,1)S(1)}, bf16[80,256]{1,0:T(8,128)(2,1)S(1)}, u32[]{:S(2)}, u32[]{:S(2)}) %collective-permute-start.3) | collective-permute-done | bytes 40992 | tf_op jit(solution)/shard_map/ppermute | solution.py:22
  25.8 0.0 collective-permute-done.4.rest_2_
  25.8 0.7 %collective-permute-done.5.rest_3_ = bf16[80,256]{1,0:T(8,128)(2,1)S(1)} collective-permute-done((bf16[80,256]{1,0:T(8,128)(2,1)S(1)}, bf16[80,256]{1,0:T(8,128)(2,1)S(1)}, u32[]{:S(2)}, u32[]{:S(2)}) %collective-permute-start.5) | collective-permute-done | bytes 40992 | tf_op jit(solution)/shard_map/ppermute | solution.py:22
  26.5 0.1 shard_map.143
  26.6 0.1 collective-permute-start.7
  26.7 0.5 %collective-permute-start.6 = (bf16[8,2048]{1,0:T(8,128)(2,1)S(1)}, bf16[8,2048]{1,0:T(8,128)(2,1)S(1)}, u32[]{:S(2)}, u32[]{:S(2)}) collective-permute-start(bf16[8,2048]{1,0:T(8,128)(2,1)S(1)} %get-tuple-element.81.attn_ref), channel_id=1, source_target_pairs={{0,1},{1,0},{2,3},{3,2},{4,5},{5,4},{6,7},{7,6},{8,9},{9,8},{10,11... | collective-permute-start | bytes 98312 | tf_op jit(solution)/shard_map/ppermute | solution.py:22
  27.2 0.1 collective-permute-start.8
  27.3 0.6 %shard_map.144.acc_ref = f32[8,1024]{1,0:T(8,128)S(1)} custom-call(bf16[8,2048]{1,0:T(8,128)(2,1)S(1)} %get-tuple-element.81.attn_ref, bf16[2048,1024]{1,0:T(8,128)(2,1)S(1)} %get-tuple-element.82.weight_ref), custom_call_target="tpu_custom_call" | custom-call | bytes 25200 | tf_op jit(solution)/shard_map/pallas_call | solution.py:514
  27.9 0.2 collective-permute-done.6.attn_ref
  28.1 0.7 %shard_map.145 = (f32[2,2,1024]{2,1,0:T(2,128)S(1)}, f32[2,2,1024]{2,1,0:T(2,128)S(1)}) custom-call(f32[8,1024]{1,0:T(8,128)S(1)} %shard_map.144.acc_ref, bf16[8,2048]{1,0:T(8,128)(2,1)S(1)} %collective-permute-done.6.attn_ref, bf16[2048,1024]{1,0:T(8,128)(2,1)S(1)} %get-tuple-element.83.weight_ref), custom_call_target="tpu_custom_call" | custom-call | bytes 25200 | tf_op jit(solution)/shard_map/pallas_call | solution.py:518
  28.8 1.5 %collective-permute-start.9 = (f32[2,2,1024]{2,1,0:T(2,128)S(1)}, f32[2,2,1024]{2,1,0:T(2,128)S(1)}, u32[]{:S(2)}, u32[]{:S(2)}) collective-permute-start(f32[2,2,1024]{2,1,0:T(2,128)S(1)} %get-tuple-element.90), channel_id=1, source_target_pairs={{0,2},{2,0},{1,3},{3,1},{4,6},{6,4},{5,7},{7,5},{8,10},{10,8},{9,1... | collective-permute-start | bytes 49160 | tf_op jit(solution)/shard_map/ppermute | solution.py:22
  30.3 0.0 collective-permute-done.8.rest_0_
  30.3 0.0 collective-permute-done.7.got_ref
  30.3 0.9 %shard_map.146 = (bf16[1,4,1,128,256]{4,3,2,1,0:T(8,128)(2,1)}, f32[2,1,8192]{2,1,0:T(1,128)}) custom-call(bf16[2,1,128,256]{3,2,1,0:T(8,128)(2,1)S(1)} %get-tuple-element.85.kept_ref, bf16[2,1,128,256]{3,2,1,0:T(8,128)(2,1)S(1)} %collective-permute-done.7.got_ref, f32[2,4,1,1024]{3,2,1,0:T(1,128)S(1)} %get-tuple-element.87.mamba_ref, ...), custom_call_target="tpu_custom_call" | custom-call | bytes 36000 | tf_op jit(solution)/shard_map/pallas_call | solution.py:529
  31.2 1.3 %collective-permute-done.9.refs_1_ = f32[2,2,1024]{2,1,0:T(2,128)S(1)} collective-permute-done((f32[2,2,1024]{2,1,0:T(2,128)S(1)}, f32[2,2,1024]{2,1,0:T(2,128)S(1)}, u32[]{:S(2)}, u32[]{:S(2)}) %collective-permute-start.9) | collective-permute-done | bytes 16416 | tf_op jit(solution)/shard_map/ppermute | solution.py:22
  32.5 0.6 %shard_map.147 = bf16[2,2,1024]{2,1,0:T(2,128)(2,1)} custom-call(f32[2,2,1024]{2,1,0:T(2,128)S(1)} %get-tuple-element.84.refs_0_, f32[2,2,1024]{2,1,0:T(2,128)S(1)} %collective-permute-done.9.refs_1_), custom_call_target="tpu_custom_call" | custom-call | bytes 21600 | tf_op jit(solution)/shard_map/pallas_call | solution.py:540
Async XLA Ops:
  1.8 10.7 %collective-permute-start = (bf16[256,256]{1,0:T(8,128)(2,1)S(1)}, bf16[256,256]{1,0:T(8,128)(2,1)S(1)}, u32[]{:S(2)}, u32[]{:S(2)}) collective-permute-start(bf16[256,256]{1,0:T(8,128)(2,1)S(1)} %get-tuple-element.62), channel_id=1, source_target_pairs={{0,12},{4,8},{8,4},{12,0},{1,13},{5,9},{9,5},{13,1},{2,14},{6,10},... | collective-permute-start | bytes 393224 | tf_op jit(solution)/shard_map/ppermute | solution.py:22
  6.9 12.1 %collective-permute-start.1 = (bf16[256,256]{1,0:T(8,128)(2,1)S(1)}, bf16[256,256]{1,0:T(8,128)(2,1)S(1)}, u32[]{:S(2)}, u32[]{:S(2)}) collective-permute-start(bf16[256,256]{1,0:T(8,128)(2,1)S(1)} %get-tuple-element.63), channel_id=1, source_target_pairs={{0,8},{4,12},{8,0},{12,4},{1,9},{5,13},{9,1},{13,5},{2,10},{6,14},... | collective-permute-start | bytes 393224 | tf_op jit(solution)/shard_map/ppermute | solution.py:22
  6.9 12.1 %collective-permute-start.2 = (bf16[256,256]{1,0:T(8,128)(2,1)S(1)}, bf16[256,256]{1,0:T(8,128)(2,1)S(1)}, u32[]{:S(2)}, u32[]{:S(2)}) collective-permute-start(bf16[256,256]{1,0:T(8,128)(2,1)S(1)} %get-tuple-element.64), channel_id=1, source_target_pairs={{0,4},{4,0},{8,12},{12,8},{1,5},{5,1},{9,13},{13,9},{2,6},{6,2},{1... | collective-permute-start | bytes 393224 | tf_op jit(solution)/shard_map/ppermute | solution.py:22
  19.6 6.3 %collective-permute-start.3 = (bf16[80,256]{1,0:T(8,128)(2,1)S(1)}, bf16[80,256]{1,0:T(8,128)(2,1)S(1)}, u32[]{:S(2)}, u32[]{:S(2)}) collective-permute-start(bf16[80,256]{1,0:T(8,128)(2,1)S(1)} %get-tuple-element.78), channel_id=1, source_target_pairs={{0,8},{4,12},{8,0},{12,4},{1,9},{5,13},{9,1},{13,5},{2,10},{6,14},... | collective-permute-start | bytes 122888 | tf_op jit(solution)/shard_map/ppermute | solution.py:22
  19.6 6.2 %collective-permute-start.4 = (bf16[80,256]{1,0:T(8,128)(2,1)S(1)}, bf16[80,256]{1,0:T(8,128)(2,1)S(1)}, u32[]{:S(2)}, u32[]{:S(2)}) collective-permute-start(bf16[80,256]{1,0:T(8,128)(2,1)S(1)} %get-tuple-element.79), channel_id=1, source_target_pairs={{0,12},{4,8},{8,4},{12,0},{1,13},{5,9},{9,5},{13,1},{2,14},{6,10},... | collective-permute-start | bytes 122888 | tf_op jit(solution)/shard_map/ppermute | solution.py:22
  22.2 4.3 %collective-permute-start.5 = (bf16[80,256]{1,0:T(8,128)(2,1)S(1)}, bf16[80,256]{1,0:T(8,128)(2,1)S(1)}, u32[]{:S(2)}, u32[]{:S(2)}) collective-permute-start(bf16[80,256]{1,0:T(8,128)(2,1)S(1)} %get-tuple-element.80), channel_id=1, source_target_pairs={{0,4},{4,0},{8,12},{12,8},{1,5},{5,1},{9,13},{13,9},{2,6},{6,2},{1... | collective-permute-start | bytes 122888 | tf_op jit(solution)/shard_map/ppermute | solution.py:22
  26.6 3.7 %collective-permute-start.7 = (bf16[2,1,128,256]{3,2,1,0:T(8,128)(2,1)S(1)}, bf16[2,1,128,256]{3,2,1,0:T(8,128)(2,1)S(1)}, u32[]{:S(2)}, u32[]{:S(2)}) collective-permute-start(bf16[2,1,128,256]{3,2,1,0:T(8,128)(2,1)S(1)} %get-tuple-element.88), channel_id=1, source_target_pairs={{0,1},{1,0},{2,3},{3,2},{4,5},{5,4},{6,7},{7,6},{8,9},{9,8},{10,11... | collective-permute-start | bytes 393224 | tf_op jit(solution)/shard_map/ppermute | solution.py:22
  26.7 1.4 %collective-permute-start.6 = (bf16[8,2048]{1,0:T(8,128)(2,1)S(1)}, bf16[8,2048]{1,0:T(8,128)(2,1)S(1)}, u32[]{:S(2)}, u32[]{:S(2)}) collective-permute-start(bf16[8,2048]{1,0:T(8,128)(2,1)S(1)} %get-tuple-element.81.attn_ref), channel_id=1, source_target_pairs={{0,1},{1,0},{2,3},{3,2},{4,5},{5,4},{6,7},{7,6},{8,9},{9,8},{10,11... | collective-permute-start | bytes 98312 | tf_op jit(solution)/shard_map/ppermute | solution.py:22
  27.2 3.1 %collective-permute-start.8 = (f32[2,4,1,1024]{3,2,1,0:T(1,128)S(1)}, f32[2,4,1,1024]{3,2,1,0:T(1,128)S(1)}, u32[]{:S(2)}, u32[]{:S(2)}) collective-permute-start(f32[2,4,1,1024]{3,2,1,0:T(1,128)S(1)} %get-tuple-element.87.mamba_ref), channel_id=1, source_target_pairs={{0,1},{1,0},{2,3},{3,2},{4,5},{5,4},{6,7},{7,6},{8,9},{9,8},{10,11... | collective-permute-start | bytes 98312 | tf_op jit(solution)/shard_map/ppermute | solution.py:22
  28.8 3.8 %collective-permute-start.9 = (f32[2,2,1024]{2,1,0:T(2,128)S(1)}, f32[2,2,1024]{2,1,0:T(2,128)S(1)}, u32[]{:S(2)}, u32[]{:S(2)}) collective-permute-start(f32[2,2,1024]{2,1,0:T(2,128)S(1)} %get-tuple-element.90), channel_id=1, source_target_pairs={{0,2},{2,0},{1,3},{3,1},{4,6},{6,4},{5,7},{7,5},{8,10},{10,8},{9,1... | collective-permute-start | bytes 49160 | tf_op jit(solution)/shard_map/ppermute | solution.py:22

commit v12 on v9

--- a/solution.py
+++ b/solution.py
@@ -164,8 +164,8 @@
 
 
 def attend(count, heads, q_ref, new_ref, bias_ref, pick_ref, *rest):
-    pieces, states = rest[:count], rest[count : 2 * count - 1]
-    outs, (kept_ref, sent_ref) = rest[2 * count - 1 : 3 * count - 1], rest[3 * count - 1 :]
+    pieces, states = rest[:count], rest[count : 2 * count - 2]
+    outs, (kept_ref, sent_ref) = rest[2 * count - 2 : 3 * count - 2], rest[3 * count - 2 :]
     rep = lax.axis_index("rep")
     queries = query_rows(q_ref, heads)
     rows, hd = queries[0].shape
@@ -214,8 +214,8 @@
         for j in range(2):
             half = result[j * rows : (j + 1) * rows] if j < heads else jnp.zeros((rows, hd), BF)
             outs[c][:rows, j * hd : (j + 1) * hd] = half
-        if c:
-            outs[c][rows:, :] = states[c - 1][...]
+        if c > 1:
+            outs[c][rows:, :] = states[c - 2][...]
     tile = pick_ref.shape[4]
     for side, ref in ((1, sent_ref), (0, kept_ref)):
         for j in range(heads):
@@ -228,9 +228,9 @@
                 ref[j, k] = total.reshape(BLOCK, 2 * hd)
 
 
-def collect(count, heads, steps, group, slope_ref, base_ref, home_ref, *rest):
+def collect(count, heads, steps, group, slope_ref, base_ref, home_ref, beside_ref, *rest):
     parts = [rest[0], rest[count - 1], *rest[1 : count - 1]]
-    states = [home_ref, *parts[1:]]
+    states = [home_ref, beside_ref, *parts[2:]]
     out_ref, mamba_ref, scratch = rest[count:]
     me = lax.axis_index("seq")
     ns, part = slope_ref.shape[2:]
@@ -466,27 +466,28 @@
         ],
     )(*after([out_weight], pieces[0]), step_dt, step_input, step_bc, skip_gain, a_log)
 
-    *moved, own_weight = after([*moved[::-1], own_weight])
+    beside = shift(states[1], "seq", 1)
+    *moved, beside, own_weight = after([*moved[::-1], beside, own_weight])
     kv = [own_piece, *moved[::-1]]
     half_shape = (heads, keep_rep, BLOCK, width)
     rows = steps * group
     *sends, kept, sent = call(
         functools.partial(attend, count, heads),
-        [shape((rows, width), BF)]
-        + [shape((rows + state_rows(part), width), BF)] * (count - 1)
+        [shape((rows, width), BF)] * 2
+        + [shape((rows + state_rows(part), width), BF)] * (count - 2)
         + [shape(half_shape, BF)] * 2,
-        [VM] * (3 + 2 * count),
+        [VM] * (2 + 2 * count),
         [VM] * (count + 2),
-    )(q_near, new_near, bias, picks, *kv, *states[1:])
+    )(q_near, new_near, bias, picks, *kv, *states[2:])
     order = [*range(2, count), 1]
     gathered = [shift(sends[c], "seq", c) for c in order]
     attn, mamba = call(
         functools.partial(collect, count, heads, steps, group),
         [shape((steps * count, half), BF), shape((steps, count, 1, part), F32)],
-        [VM] * (3 + count),
+        [VM] * (4 + count),
         [VM] * 2,
         [pltpu.VMEM((heads, steps * count * group, hd), F32)],
-    )(slope, base, states[0], sends[0], *gathered)
+    )(slope, base, states[0], beside, sends[0], *gathered)
     attn_other = shift(attn, "rep", 1)
     own_sum = call(
         project_own, shape((steps * count, columns), F32), [VM, VM], VM, us=0.7

time: 31.9 us -> 31.9 us (level)
  waiting for transfers between devices: 10.1 us -> 8.65 us
  starting transfers between devices: 11.5 us -> 12.9 us
    ppermute x10 -> x11, starting transfers between devices: 11.5 us -> 12.9 us  [shift(): return lax.ppermute(x, axis, [(i, i ^ c) for i in range(size)])]
    ppermute x10 -> x11, waiting for transfers between devices: 10.1 us -> 8.65 us  [shift(): return lax.ppermute(x, axis, [(i, i ^ c) for i in range(size)])]
  transfers between devices with their start and end apart: 10 -> 11, of which waited for: 6 -> 5; matrix products, arithmetic and copies ran while one was open for 0% -> 0% of each run, Pallas kernels for 22% -> 22%
where the time goes in v12:
time: 31.9 us; the launch traced here: 31.7 us
  starting transfers between devices  12.9 us (40%)
  Pallas kernels  9.39 us (29%)
  waiting for transfers between devices  8.65 us (27%)
  between operations  0.7 us (2%)
    ppermute x11, starting transfers between devices, shift(): return lax.ppermute(x, axis, [(i, i ^ c) for i in range(size)])  12.9 us
    ppermute x11, waiting for transfers between devices, shift(): return lax.ppermute(x, axis, [(i, i ^ c) for i in range(size)])  8.65 us
    pallas_call x1, Pallas kernels, per_device(): call(functools.partial(prepare, count, split), [half_weight, half_weight,...  3.74 us
    pallas_call x1, Pallas kernels, per_device(): call(functools.partial(stage_rest, count, split), [block_shape, shape(que...  1.15 us
    pallas_call x1, Pallas kernels, per_device(): call(functools.partial(stage_blocks, count), [block_shape] * (count - 1),...  1.06 us
    pallas_call x1, Pallas kernels, per_device(): call(functools.partial(assemble, split), [shape((1, dec_heads, keep_rep,...  0.89 us
    pallas_call x1, Pallas kernels, per_device(): call(functools.partial(project_other, heads_count, count), [shape((steps,...  0.67 us
    pallas_call x1, Pallas kernels, per_device(): call(project_own, shape((steps * count, columns), F32), [VM, VM], VM, us=...  0.64 us
  transfers between devices with their start and end apart: 11, of which 5 were waited for; matrix products, arithmetic and copies ran while one was open for 0% of the time, Pallas kernels for 22%

profile of v12, /device:TPU:0, one launch (start us, length us, event | category | flops | bytes accessed | tf_op | source)
XLA Modules:
  0.0 31.7 jit_solution(13475479591537318644)
XLA Ops:
  0.6 1.1 %shard_map.139 = (bf16[256,256]{1,0:T(8,128)(2,1)S(1)}, bf16[256,256]{1,0:T(8,128)(2,1)S(1)}, bf16[256,256]{1,0:T(8,128)(2,1)S(1)}) custom-call(bf16[4,2,128,256]{3,2,1,0:T(8,128)(2,1)} %kv_ref.2), custom_call_target="tpu_custom_call" | custom-call | bytes 36000 | tf_op jit(solution)/shard_map/pallas_call | solution.py:420
  1.7 5.1 %collective-permute-start = (bf16[256,256]{1,0:T(8,128)(2,1)S(1)}, bf16[256,256]{1,0:T(8,128)(2,1)S(1)}, u32[]{:S(2)}, u32[]{:S(2)}) collective-permute-start(bf16[256,256]{1,0:T(8,128)(2,1)S(1)} %get-tuple-element.48), channel_id=1, source_target_pairs={{0,12},{4,8},{8,4},{12,0},{1,13},{5,9},{9,5},{13,1},{2,14},{6,10},... | collective-permute-start | bytes 393224 | tf_op jit(solution)/shard_map/ppermute | solution.py:22
  6.8 0.0 collective-permute-start.1
  6.8 0.6 %collective-permute-start.2 = (bf16[256,256]{1,0:T(8,128)(2,1)S(1)}, bf16[256,256]{1,0:T(8,128)(2,1)S(1)}, u32[]{:S(2)}, u32[]{:S(2)}) collective-permute-start(bf16[256,256]{1,0:T(8,128)(2,1)S(1)} %get-tuple-element.41), channel_id=1, source_target_pairs={{0,4},{4,0},{8,12},{12,8},{1,5},{5,1},{9,13},{13,9},{2,6},{6,2},{1... | collective-permute-start | bytes 393224 | tf_op jit(solution)/shard_map/ppermute | solution.py:22
  7.5 1.2 %shard_map.140 = (bf16[256,256]{1,0:T(8,128)(2,1)S(1)}, bf16[2,1,32,128]{3,2,1,0:T(8,128)(2,1)S(1)}, bf16[2,1,4,256]{3,2,1,0:T(4,128)(2,1)S(1)}, f32[32,512]{1,0...) custom-call(bf16[4,2,128,256]{3,2,1,0:T(8,128)(2,1)} %kv_ref.2, ...), custom_call_target="tpu_custom_call" | custom-call | bytes 36000 | tf_op jit(solution)/shard_map/pallas_call | solution.py:428
  8.6 1.5 %collective-permute-start.3 = (bf16[64,256]{1,0:T(8,128)(2,1)S(1)}, bf16[64,256]{1,0:T(8,128)(2,1)S(1)}, u32[]{:S(2)}, u32[]{:S(2)}) collective-permute-start(bf16[64,256]{1,0:T(8,128)(2,1)S(1)} %get-tuple-element.50), channel_id=1, source_target_pairs={{0,4},{4,0},{8,12},{12,8},{1,5},{5,1},{9,13},{13,9},{2,6},{6,2},{1... | collective-permute-start | bytes 98312 | tf_op jit(solution)/shard_map/ppermute | solution.py:22
  10.1 3.7 %shard_map.141 = (bf16[2048,1024]{1,0:T(8,128)(2,1)S(1)}, bf16[2048,1024]{1,0:T(8,128)(2,1)S(1)}, f32[4,2,16,1024]{3,2,1,0:T(8,128)S(1)}, f32[4,2,1,1024]{3,2,1,0:T(1,128)S(1)}) custom-call(bf16[4096,1024]{1,0:T(8,128)(2,1)} %weight_hbm, f32[2,1,8192]{2,1,0:T(1,128)} %dt_hbm.1, bf16[2,8192]{1,0:T(2,128)(2,1)} %bitcast.3, f32[2,1,2,16]{3,2,1,0:T(2,128)} %bc_hbm.1, ...), custom_call_target="tpu_custom_call" | custom-call | bytes 36000 | tf_op jit(solution)/shard_map/pallas_call | solution.py:448
  13.8 2.1 %collective-permute-done.3.beside_ref = bf16[64,256]{1,0:T(8,128)(2,1)S(1)} collective-permute-done((bf16[64,256]{1,0:T(8,128)(2,1)S(1)}, bf16[64,256]{1,0:T(8,128)(2,1)S(1)}, u32[]{:S(2)}, u32[]{:S(2)}) %collective-permute-start.3) | collective-permute-done | bytes 32800 | tf_op jit(solution)/shard_map/ppermute | solution.py:22
  15.9 0.0 collective-permute-done.rest_3_
  15.9 1.9 %collective-permute-done.1.rest_2_ = bf16[256,256]{1,0:T(8,128)(2,1)S(1)} collective-permute-done((bf16[256,256]{1,0:T(8,128)(2,1)S(1)}, bf16[256,256]{1,0:T(8,128)(2,1)S(1)}, u32[]{:S(2)}, u32[]{:S(2)}) %collective-permute-start.1) | collective-permute-done | bytes 131104 | tf_op jit(solution)/shard_map/ppermute | solution.py:22
  17.9 0.0 collective-permute-done.2.rest_1_
  17.9 0.5 %shard_map.142 = (bf16[16,256]{1,0:T(8,128)(2,1)S(1)}, bf16[16,256]{1,0:T(8,128)(2,1)S(1)}, bf16[80,256]{1,0:T(8,128)(2,1)S(1)}, bf16[80,256]{1,0:T(8,128)(2,1)S...) custom-call(bf16[2,1,32,128]{3,2,1,0:T(8,128)(2,1)S(1)} %get-tuple-element.43.q_ref, ...), custom_call_target="tpu_custom_call" | custom-call | bytes 36000 | tf_op jit(solution)/shard_map/pallas_call | solution.py:474
  18.4 0.1 collective-permute-start.4
  18.5 2.9 %collective-permute-start.5 = (bf16[80,256]{1,0:T(8,128)(2,1)S(1)}, bf16[80,256]{1,0:T(8,128)(2,1)S(1)}, u32[]{:S(2)}, u32[]{:S(2)}) collective-permute-start(bf16[80,256]{1,0:T(8,128)(2,1)S(1)} %get-tuple-element.65), channel_id=1, source_target_pairs={{0,12},{4,8},{8,4},{12,0},{1,13},{5,9},{9,5},{13,1},{2,14},{6,10},... | collective-permute-start | bytes 122888 | tf_op jit(solution)/shard_map/ppermute | solution.py:22
  21.4 0.6 %collective-permute-start.6 = (bf16[16,256]{1,0:T(8,128)(2,1)S(1)}, bf16[16,256]{1,0:T(8,128)(2,1)S(1)}, u32[]{:S(2)}, u32[]{:S(2)}) collective-permute-start(bf16[16,256]{1,0:T(8,128)(2,1)S(1)} %get-tuple-element.66), channel_id=1, source_target_pairs={{0,4},{4,0},{8,12},{12,8},{1,5},{5,1},{9,13},{13,9},{2,6},{6,2},{1... | collective-permute-start | bytes 24584 | tf_op jit(solution)/shard_map/ppermute | solution.py:22
  21.9 3.1 %collective-permute-done.6.rest_3_ = bf16[16,256]{1,0:T(8,128)(2,1)S(1)} collective-permute-done((bf16[16,256]{1,0:T(8,128)(2,1)S(1)}, bf16[16,256]{1,0:T(8,128)(2,1)S(1)}, u32[]{:S(2)}, u32[]{:S(2)}) %collective-permute-start.6) | collective-permute-done | bytes 8224 | tf_op jit(solution)/shard_map/ppermute | solution.py:22
  25.0 0.0 collective-permute-done.4.rest_1_
  25.0 0.0 collective-permute-done.5.rest_2_
  25.0 0.1 shard_map.143
  25.2 0.1 collective-permute-start.8
  25.2 0.5 %collective-permute-start.7 = (bf16[8,2048]{1,0:T(8,128)(2,1)S(1)}, bf16[8,2048]{1,0:T(8,128)(2,1)S(1)}, u32[]{:S(2)}, u32[]{:S(2)}) collective-permute-start(bf16[8,2048]{1,0:T(8,128)(2,1)S(1)} %get-tuple-element.67.attn_ref), channel_id=1, source_target_pairs={{0,1},{1,0},{2,3},{3,2},{4,5},{5,4},{6,7},{7,6},{8,9},{9,8},{10,11... | collective-permute-start | bytes 98312 | tf_op jit(solution)/shard_map/ppermute | solution.py:22
  25.7 0.1 collective-permute-start.9
  25.8 0.6 %shard_map.144.acc_ref = f32[8,1024]{1,0:T(8,128)S(1)} custom-call(bf16[8,2048]{1,0:T(8,128)(2,1)S(1)} %get-tuple-element.67.attn_ref, bf16[2048,1024]{1,0:T(8,128)(2,1)S(1)} %get-tuple-element.68.weight_ref), custom_call_target="tpu_custom_call" | custom-call | bytes 25200 | tf_op jit(solution)/shard_map/pallas_call | solution.py:492
  26.4 0.2 collective-permute-done.7.attn_ref
  26.6 0.7 %shard_map.145 = (f32[2,2,1024]{2,1,0:T(2,128)S(1)}, f32[2,2,1024]{2,1,0:T(2,128)S(1)}) custom-call(f32[8,1024]{1,0:T(8,128)S(1)} %shard_map.144.acc_ref, bf16[8,2048]{1,0:T(8,128)(2,1)S(1)} %collective-permute-done.7.attn_ref, bf16[2048,1024]{1,0:T(8,128)(2,1)S(1)} %get-tuple-element.69.weight_ref), custom_call_target="tpu_custom_call" | custom-call | bytes 25200 | tf_op jit(solution)/shard_map/pallas_call | solution.py:496
  27.3 1.5 %collective-permute-start.10 = (f32[2,2,1024]{2,1,0:T(2,128)S(1)}, f32[2,2,1024]{2,1,0:T(2,128)S(1)}, u32[]{:S(2)}, u32[]{:S(2)}) collective-permute-start(f32[2,2,1024]{2,1,0:T(2,128)S(1)} %get-tuple-element.76), channel_id=1, source_target_pairs={{0,2},{2,0},{1,3},{3,1},{4,6},{6,4},{5,7},{7,5},{8,10},{10,8},{9,1... | collective-permute-start | bytes 49160 | tf_op jit(solution)/shard_map/ppermute | solution.py:22
  28.8 0.0 collective-permute-done.9.rest_0_
  28.8 0.0 collective-permute-done.8.got_ref
  28.8 0.9 %shard_map.146 = (bf16[1,4,1,128,256]{4,3,2,1,0:T(8,128)(2,1)}, f32[2,1,8192]{2,1,0:T(1,128)}) custom-call(bf16[2,1,128,256]{3,2,1,0:T(8,128)(2,1)S(1)} %get-tuple-element.71.kept_ref, bf16[2,1,128,256]{3,2,1,0:T(8,128)(2,1)S(1)} %collective-permute-done.8.got_ref, f32[2,4,1,1024]{3,2,1,0:T(1,128)S(1)} %get-tuple-element.73.mamba_ref, ...), custom_call_target="tpu_custom_call" | custom-call | bytes 36000 | tf_op jit(solution)/shard_map/pallas_call | solution.py:507
  29.7 1.3 %collective-permute-done.10.refs_1_ = f32[2,2,1024]{2,1,0:T(2,128)S(1)} collective-permute-done((f32[2,2,1024]{2,1,0:T(2,128)S(1)}, f32[2,2,1024]{2,1,0:T(2,128)S(1)}, u32[]{:S(2)}, u32[]{:S(2)}) %collective-permute-start.10) | collective-permute-done | bytes 16416 | tf_op jit(solution)/shard_map/ppermute | solution.py:22
  31.1 0.6 %shard_map.147 = bf16[2,2,1024]{2,1,0:T(2,128)(2,1)} custom-call(f32[2,2,1024]{2,1,0:T(2,128)S(1)} %get-tuple-element.70.refs_0_, f32[2,2,1024]{2,1,0:T(2,128)S(1)} %collective-permute-done.10.refs_1_), custom_call_target="tpu_custom_call" | custom-call | bytes 21600 | tf_op jit(solution)/shard_map/pallas_call | solution.py:518
Async XLA Ops:
  1.7 14.2 %collective-permute-start = (bf16[256,256]{1,0:T(8,128)(2,1)S(1)}, bf16[256,256]{1,0:T(8,128)(2,1)S(1)}, u32[]{:S(2)}, u32[]{:S(2)}) collective-permute-start(bf16[256,256]{1,0:T(8,128)(2,1)S(1)} %get-tuple-element.48), channel_id=1, source_target_pairs={{0,12},{4,8},{8,4},{12,0},{1,13},{5,9},{9,5},{13,1},{2,14},{6,10},... | collective-permute-start | bytes 393224 | tf_op jit(solution)/shard_map/ppermute | solution.py:22
  6.8 11.1 %collective-permute-start.1 = (bf16[256,256]{1,0:T(8,128)(2,1)S(1)}, bf16[256,256]{1,0:T(8,128)(2,1)S(1)}, u32[]{:S(2)}, u32[]{:S(2)}) collective-permute-start(bf16[256,256]{1,0:T(8,128)(2,1)S(1)} %get-tuple-element.49), channel_id=1, source_target_pairs={{0,8},{4,12},{8,0},{12,4},{1,9},{5,13},{9,1},{13,5},{2,10},{6,14},... | collective-permute-start | bytes 393224 | tf_op jit(solution)/shard_map/ppermute | solution.py:22
  6.8 11.1 %collective-permute-start.2 = (bf16[256,256]{1,0:T(8,128)(2,1)S(1)}, bf16[256,256]{1,0:T(8,128)(2,1)S(1)}, u32[]{:S(2)}, u32[]{:S(2)}) collective-permute-start(bf16[256,256]{1,0:T(8,128)(2,1)S(1)} %get-tuple-element.41), channel_id=1, source_target_pairs={{0,4},{4,0},{8,12},{12,8},{1,5},{5,1},{9,13},{13,9},{2,6},{6,2},{1... | collective-permute-start | bytes 393224 | tf_op jit(solution)/shard_map/ppermute | solution.py:22
  8.6 7.3 %collective-permute-start.3 = (bf16[64,256]{1,0:T(8,128)(2,1)S(1)}, bf16[64,256]{1,0:T(8,128)(2,1)S(1)}, u32[]{:S(2)}, u32[]{:S(2)}) collective-permute-start(bf16[64,256]{1,0:T(8,128)(2,1)S(1)} %get-tuple-element.50), channel_id=1, source_target_pairs={{0,4},{4,0},{8,12},{12,8},{1,5},{5,1},{9,13},{13,9},{2,6},{6,2},{1... | collective-permute-start | bytes 98312 | tf_op jit(solution)/shard_map/ppermute | solution.py:22
  18.4 6.6 %collective-permute-start.4 = (bf16[80,256]{1,0:T(8,128)(2,1)S(1)}, bf16[80,256]{1,0:T(8,128)(2,1)S(1)}, u32[]{:S(2)}, u32[]{:S(2)}) collective-permute-start(bf16[80,256]{1,0:T(8,128)(2,1)S(1)} %get-tuple-element.64), channel_id=1, source_target_pairs={{0,8},{4,12},{8,0},{12,4},{1,9},{5,13},{9,1},{13,5},{2,10},{6,14},... | collective-permute-start | bytes 122888 | tf_op jit(solution)/shard_map/ppermute | solution.py:22
  18.5 6.6 %collective-permute-start.5 = (bf16[80,256]{1,0:T(8,128)(2,1)S(1)}, bf16[80,256]{1,0:T(8,128)(2,1)S(1)}, u32[]{:S(2)}, u32[]{:S(2)}) collective-permute-start(bf16[80,256]{1,0:T(8,128)(2,1)S(1)} %get-tuple-element.65), channel_id=1, source_target_pairs={{0,12},{4,8},{8,4},{12,0},{1,13},{5,9},{9,5},{13,1},{2,14},{6,10},... | collective-permute-start | bytes 122888 | tf_op jit(solution)/shard_map/ppermute | solution.py:22
  21.4 3.7 %collective-permute-start.6 = (bf16[16,256]{1,0:T(8,128)(2,1)S(1)}, bf16[16,256]{1,0:T(8,128)(2,1)S(1)}, u32[]{:S(2)}, u32[]{:S(2)}) collective-permute-start(bf16[16,256]{1,0:T(8,128)(2,1)S(1)} %get-tuple-element.66), channel_id=1, source_target_pairs={{0,4},{4,0},{8,12},{12,8},{1,5},{5,1},{9,13},{13,9},{2,6},{6,2},{1... | collective-permute-start | bytes 24584 | tf_op jit(solution)/shard_map/ppermute | solution.py:22
  25.2 3.7 %collective-permute-start.8 = (bf16[2,1,128,256]{3,2,1,0:T(8,128)(2,1)S(1)}, bf16[2,1,128,256]{3,2,1,0:T(8,128)(2,1)S(1)}, u32[]{:S(2)}, u32[]{:S(2)}) collective-permute-start(bf16[2,1,128,256]{3,2,1,0:T(8,128)(2,1)S(1)} %get-tuple-element.74), channel_id=1, source_target_pairs={{0,1},{1,0},{2,3},{3,2},{4,5},{5,4},{6,7},{7,6},{8,9},{9,8},{10,11... | collective-permute-start | bytes 393224 | tf_op jit(solution)/shard_map/ppermute | solution.py:22
  25.2 1.4 %collective-permute-start.7 = (bf16[8,2048]{1,0:T(8,128)(2,1)S(1)}, bf16[8,2048]{1,0:T(8,128)(2,1)S(1)}, u32[]{:S(2)}, u32[]{:S(2)}) collective-permute-start(bf16[8,2048]{1,0:T(8,128)(2,1)S(1)} %get-tuple-element.67.attn_ref), channel_id=1, source_target_pairs={{0,1},{1,0},{2,3},{3,2},{4,5},{5,4},{6,7},{7,6},{8,9},{9,8},{10,11... | collective-permute-start | bytes 98312 | tf_op jit(solution)/shard_map/ppermute | solution.py:22
  25.7 3.1 %collective-permute-start.9 = (f32[2,4,1,1024]{3,2,1,0:T(1,128)S(1)}, f32[2,4,1,1024]{3,2,1,0:T(1,128)S(1)}, u32[]{:S(2)}, u32[]{:S(2)}) collective-permute-start(f32[2,4,1,1024]{3,2,1,0:T(1,128)S(1)} %get-tuple-element.73.mamba_ref), channel_id=1, source_target_pairs={{0,1},{1,0},{2,3},{3,2},{4,5},{5,4},{6,7},{7,6},{8,9},{9,8},{10,11... | collective-permute-start | bytes 98312 | tf_op jit(solution)/shard_map/ppermute | solution.py:22
  27.3 3.8 %collective-permute-start.10 = (f32[2,2,1024]{2,1,0:T(2,128)S(1)}, f32[2,2,1024]{2,1,0:T(2,128)S(1)}, u32[]{:S(2)}, u32[]{:S(2)}) collective-permute-start(f32[2,2,1024]{2,1,0:T(2,128)S(1)} %get-tuple-element.76), channel_id=1, source_target_pairs={{0,2},{2,0},{1,3},{3,1},{4,6},{6,4},{5,7},{7,5},{8,10},{10,8},{9,1... | collective-permute-start | bytes 49160 | tf_op jit(solution)/shard_map/ppermute | solution.py:22

commit v13 on v9

--- a/solution.py
+++ b/solution.py
@@ -20,6 +20,18 @@
 def shift(x, axis, c):
     size = lax.axis_size(axis)
     return lax.ppermute(x, axis, [(i, i ^ c) for i in range(size)])
+
+
+def across(x, c):
+    count, reps = lax.axis_size("seq"), lax.axis_size("rep")
+    pairs = [
+        (s * reps + r, (s ^ c) * reps + (r ^ 1)) for s in range(count) for r in range(reps)
+    ]
+    return lax.ppermute(x, ("seq", "rep"), pairs)
+
+
+def served():
+    return 1 - lax.axis_index("rep")
 
 
 def call(body, out_shape, in_specs, out_specs, scratch=(), us=1.0):
@@ -113,7 +125,7 @@
         move.wait()
     for c in range(count):
         pack_state(loaded[c], states[c], 0)
-    head_first = lax.axis_index("head") * new_ref.shape[2] + rep * heads
+    head_first = lax.axis_index("head") * new_ref.shape[2] + served() * heads
     rows = bias_out.shape[0] // heads
     keep_rep = pick_out.shape[2]
     for j in range(heads):
@@ -140,12 +152,11 @@
 
 
 def query_rows(q_ref, heads):
-    rep = lax.axis_index("rep")
     steps, _, q_heads, _ = q_ref.shape
     own_q = q_heads // 2
     group = own_q // heads
     q_all = [q_ref[step, 0].astype(F32) for step in range(steps)]
-    q_all = [jnp.where(rep == 0, q[:own_q], q[own_q:]) for q in q_all]
+    q_all = [jnp.where(served() == 0, q[:own_q], q[own_q:]) for q in q_all]
     return [
         jnp.concatenate([x[j * group : (j + 1) * group] for x in q_all], axis=0)
         for j in range(heads)
@@ -166,7 +177,6 @@
 def attend(count, heads, q_ref, new_ref, bias_ref, pick_ref, *rest):
     pieces, states = rest[:count], rest[count : 2 * count - 1]
     outs, (kept_ref, sent_ref) = rest[2 * count - 1 : 3 * count - 1], rest[3 * count - 1 :]
-    rep = lax.axis_index("rep")
     queries = query_rows(q_ref, heads)
     rows, hd = queries[0].shape
     steps = q_ref.shape[0]
@@ -186,7 +196,7 @@
     top = jnp.max(scores, axis=1, keepdims=True)
     for step in range(steps):
         both = new_ref[step, 0].astype(F32)
-        fresh = jnp.where(rep == 0, both[:heads], both[heads:])
+        fresh = jnp.where(served() == 0, both[:heads], both[heads:])
         wide = jnp.concatenate(
             [jnp.broadcast_to(fresh[j : j + 1], (rows, 2 * hd)) for j in range(heads)], axis=0
         )
@@ -308,7 +318,7 @@
         copy(gain_hbm, gain_ref),
         copy(log_hbm, log_ref),
     ]
-    copy, which = copier(weight_sems), lax.axis_index("rep")
+    copy, which = copier(weight_sems), served()
     weights = weight_half(weight_hbm, own_ref, which, copy)
     weights += weight_half(weight_hbm, other_ref, 1 - which, copy)
     for move in first + weights:
@@ -357,8 +367,8 @@
     heads = kept_ref.shape[0]
     copy = copier(sems)
     moves = [
-        copy(kept_ref, handoff_ref.at[0, pl.ds(rep * heads, heads)]),
-        copy(got_ref, handoff_ref.at[0, pl.ds((1 - rep) * heads, heads)]),
+        copy(kept_ref, handoff_ref.at[0, pl.ds((1 - rep) * heads, heads)]),
+        copy(got_ref, handoff_ref.at[0, pl.ds(rep * heads, heads)]),
     ]
     steps, count, _, part = mamba_ref.shape
     for step in range(steps):
@@ -424,7 +434,7 @@
         [VM] * (count - 1),
         [DMA(((count - 1) * heads,))],
     )(prefill_kv)
-    moved = [shift(pieces[c - 1], "seq", c) for c in range(count - 1, 0, -1)][::-1]
+    moved = [across(pieces[c - 1], c) for c in range(count - 1, 0, -1)][::-1]
     own_piece, q_near, new_near, bias, picks, *states = call(
         functools.partial(stage_rest, count, split),
         [
@@ -466,7 +476,8 @@
         ],
     )(*after([out_weight], pieces[0]), step_dt, step_input, step_bc, skip_gain, a_log)
 
-    *moved, own_weight = after([*moved[::-1], own_weight])
+    own_piece = shift(own_piece, "rep", 1)
+    *moved, own_piece, own_weight = after([*moved[::-1], own_piece, own_weight])
     kv = [own_piece, *moved[::-1]]
     half_shape = (heads, keep_rep, BLOCK, width)
     rows = steps * group

time: 31.9 us -> 32.8 us (1.028)
  waiting for transfers between devices: 10.1 us -> 11.2 us
    ppermute x0 -> x3, waiting for transfers between devices: none -> 6.13 us  [across(): return lax.ppermute(x, ('seq', 'rep'), pairs)]
    ppermute x10 -> x8, starting transfers between devices: 11.5 us -> 5.81 us  [shift(): return lax.ppermute(x, axis, [(i, i ^ c) for i in range(size)])]
    ppermute x0 -> x3, starting transfers between devices: none -> 5.48 us  [across(): return lax.ppermute(x, ('seq', 'rep'), pairs)]
    ppermute x10 -> x8, waiting for transfers between devices: 10.1 us -> 5.09 us  [shift(): return lax.ppermute(x, axis, [(i, i ^ c) for i in range(size)])]
  transfers between devices with their start and end apart: 10 -> 11, of which waited for: 6 -> 5; matrix products, arithmetic and copies ran while one was open for 0% -> 0% of each run, Pallas kernels for 22% -> 22%
where the time goes in v13:
time: 32.8 us; the launch traced here: 32.6 us
  starting transfers between devices  11.3 us (34%)
  waiting for transfers between devices  11.2 us (34%)
  Pallas kernels  9.4 us (29%)
  between operations  0.71 us (2%)
    ppermute x3, waiting for transfers between devices, across(): return lax.ppermute(x, ('seq', 'rep'), pairs)  6.13 us
    ppermute x8, starting transfers between devices, shift(): return lax.ppermute(x, axis, [(i, i ^ c) for i in range(size)])  5.81 us
    ppermute x3, starting transfers between devices, across(): return lax.ppermute(x, ('seq', 'rep'), pairs)  5.48 us
    ppermute x8, waiting for transfers between devices, shift(): return lax.ppermute(x, axis, [(i, i ^ c) for i in range(size)])  5.09 us
    pallas_call x1, Pallas kernels, per_device(): call(functools.partial(prepare, count, split), [half_weight, half_weight,...  3.76 us
    pallas_call x1, Pallas kernels, per_device(): call(functools.partial(stage_rest, count, split), [block_shape, shape(que...  1.15 us
    pallas_call x1, Pallas kernels, per_device(): call(functools.partial(stage_blocks, count), [block_shape] * (count - 1),...  1.06 us
    pallas_call x1, Pallas kernels, per_device(): call(functools.partial(assemble, split), [shape((1, dec_heads, keep_rep,...  0.89 us
  transfers between devices with their start and end apart: 11, of which 5 were waited for; matrix products, arithmetic and copies ran while one was open for 0% of the time, Pallas kernels for 22%

profile of v13, /device:TPU:0, one launch (start us, length us, event | category | flops | bytes accessed | tf_op | source)
XLA Modules:
  0.0 32.6 jit_solution(5022597400129278363)
XLA Ops:
  0.6 1.1 %shard_map.139 = (bf16[256,256]{1,0:T(8,128)(2,1)S(1)}, bf16[256,256]{1,0:T(8,128)(2,1)S(1)}, bf16[256,256]{1,0:T(8,128)(2,1)S(1)}) custom-call(bf16[4,2,128,256]{3,2,1,0:T(8,128)(2,1)} %kv_ref.2), custom_call_target="tpu_custom_call" | custom-call | bytes 36000 | tf_op jit(solution)/shard_map/pallas_call | solution.py:430
  1.7 4.6 %collective-permute-start = (bf16[256,256]{1,0:T(8,128)(2,1)S(1)}, bf16[256,256]{1,0:T(8,128)(2,1)S(1)}, u32[]{:S(2)}, u32[]{:S(2)}) collective-permute-start(bf16[256,256]{1,0:T(8,128)(2,1)S(1)} %get-tuple-element.47), channel_id=1, source_target_pairs={{0,13},{1,12},{4,9},{5,8},{8,5},{9,4},{12,1},{13,0},{2,15},{3,14},... | collective-permute-start | bytes 393224 | tf_op jit(solution)/shard_map/ppermute | solution.py:30
  6.3 0.0 collective-permute-start.1
  6.3 0.9 %collective-permute-start.2 = (bf16[256,256]{1,0:T(8,128)(2,1)S(1)}, bf16[256,256]{1,0:T(8,128)(2,1)S(1)}, u32[]{:S(2)}, u32[]{:S(2)}) collective-permute-start(bf16[256,256]{1,0:T(8,128)(2,1)S(1)} %get-tuple-element.41), channel_id=1, source_target_pairs={{0,5},{1,4},{4,1},{5,0},{8,13},{9,12},{12,9},{13,8},{2,7},{3,6},{6... | collective-permute-start | bytes 393224 | tf_op jit(solution)/shard_map/ppermute | solution.py:30
  7.2 1.2 %shard_map.140 = (bf16[256,256]{1,0:T(8,128)(2,1)S(1)}, bf16[2,1,32,128]{3,2,1,0:T(8,128)(2,1)S(1)}, bf16[2,1,4,256]{3,2,1,0:T(4,128)(2,1)S(1)}, f32[32,512]{1,0...) custom-call(bf16[4,2,128,256]{3,2,1,0:T(8,128)(2,1)} %kv_ref.2, ...), custom_call_target="tpu_custom_call" | custom-call | bytes 36000 | tf_op jit(solution)/shard_map/pallas_call | solution.py:438
  8.3 0.1 collective-permute-start.3
  8.4 3.8 %shard_map.141 = (bf16[2048,1024]{1,0:T(8,128)(2,1)S(1)}, bf16[2048,1024]{1,0:T(8,128)(2,1)S(1)}, f32[4,2,16,1024]{3,2,1,0:T(8,128)S(1)}, f32[4,2,1,1024]{3,2,1,0:T(1,128)S(1)}) custom-call(bf16[4096,1024]{1,0:T(8,128)(2,1)} %weight_hbm, f32[2,1,8192]{2,1,0:T(1,128)} %dt_hbm.1, bf16[2,8192]{1,0:T(2,128)(2,1)} %bitcast.3, f32[2,1,2,16]{3,2,1,0:T(2,128)} %bc_hbm.1, ...), custom_call_target="tpu_custom_call" | custom-call | bytes 36000 | tf_op jit(solution)/shard_map/pallas_call | solution.py:458
  12.2 0.0 collective-permute-done.rest_3_
  12.2 6.1 %collective-permute-done.1.rest_2_ = bf16[256,256]{1,0:T(8,128)(2,1)S(1)} collective-permute-done((bf16[256,256]{1,0:T(8,128)(2,1)S(1)}, bf16[256,256]{1,0:T(8,128)(2,1)S(1)}, u32[]{:S(2)}, u32[]{:S(2)}) %collective-permute-start.1) | collective-permute-done | bytes 131104 | tf_op jit(solution)/shard_map/ppermute | solution.py:30
  18.3 0.0 collective-permute-done.2.rest_1_
  18.3 0.0 collective-permute-done.3.rest_0_
  18.3 0.5 %shard_map.142 = (bf16[16,256]{1,0:T(8,128)(2,1)S(1)}, bf16[80,256]{1,0:T(8,128)(2,1)S(1)}, bf16[80,256]{1,0:T(8,128)(2,1)S(1)}, bf16[80,256]{1,0:T(8,128)(2,1)S...) custom-call(bf16[2,1,32,128]{3,2,1,0:T(8,128)(2,1)S(1)} %get-tuple-element.43.q_ref, ...), custom_call_target="tpu_custom_call" | custom-call | bytes 36000 | tf_op jit(solution)/shard_map/pallas_call | solution.py:484
  18.8 0.1 collective-permute-start.4
  18.9 2.7 %collective-permute-start.5 = (bf16[80,256]{1,0:T(8,128)(2,1)S(1)}, bf16[80,256]{1,0:T(8,128)(2,1)S(1)}, u32[]{:S(2)}, u32[]{:S(2)}) collective-permute-start(bf16[80,256]{1,0:T(8,128)(2,1)S(1)} %get-tuple-element.65), channel_id=1, source_target_pairs={{0,12},{4,8},{8,4},{12,0},{1,13},{5,9},{9,5},{13,1},{2,14},{6,10},... | collective-permute-start | bytes 122888 | tf_op jit(solution)/shard_map/ppermute | solution.py:22
  21.6 0.8 %collective-permute-start.6 = (bf16[80,256]{1,0:T(8,128)(2,1)S(1)}, bf16[80,256]{1,0:T(8,128)(2,1)S(1)}, u32[]{:S(2)}, u32[]{:S(2)}) collective-permute-start(bf16[80,256]{1,0:T(8,128)(2,1)S(1)} %get-tuple-element.66), channel_id=1, source_target_pairs={{0,4},{4,0},{8,12},{12,8},{1,5},{5,1},{9,13},{13,9},{2,6},{6,2},{1... | collective-permute-start | bytes 122888 | tf_op jit(solution)/shard_map/ppermute | solution.py:22
  22.4 2.8 %collective-permute-done.4.rest_1_ = bf16[80,256]{1,0:T(8,128)(2,1)S(1)} collective-permute-done((bf16[80,256]{1,0:T(8,128)(2,1)S(1)}, bf16[80,256]{1,0:T(8,128)(2,1)S(1)}, u32[]{:S(2)}, u32[]{:S(2)}) %collective-permute-start.4) | collective-permute-done | bytes 40992 | tf_op jit(solution)/shard_map/ppermute | solution.py:22
  25.2 0.0 collective-permute-done.5.rest_2_
  25.2 0.7 %collective-permute-done.6.rest_3_ = bf16[80,256]{1,0:T(8,128)(2,1)S(1)} collective-permute-done((bf16[80,256]{1,0:T(8,128)(2,1)S(1)}, bf16[80,256]{1,0:T(8,128)(2,1)S(1)}, u32[]{:S(2)}, u32[]{:S(2)}) %collective-permute-start.6) | collective-permute-done | bytes 40992 | tf_op jit(solution)/shard_map/ppermute | solution.py:22
  26.0 0.1 shard_map.143
  26.1 0.1 collective-permute-start.8
  26.2 0.5 %collective-permute-start.7 = (bf16[8,2048]{1,0:T(8,128)(2,1)S(1)}, bf16[8,2048]{1,0:T(8,128)(2,1)S(1)}, u32[]{:S(2)}, u32[]{:S(2)}) collective-permute-start(bf16[8,2048]{1,0:T(8,128)(2,1)S(1)} %get-tuple-element.67.attn_ref), channel_id=1, source_target_pairs={{0,1},{1,0},{2,3},{3,2},{4,5},{5,4},{6,7},{7,6},{8,9},{9,8},{10,11... | collective-permute-start | bytes 98312 | tf_op jit(solution)/shard_map/ppermute | solution.py:22
  26.7 0.1 collective-permute-start.9
  26.7 0.6 %shard_map.144.acc_ref = f32[8,1024]{1,0:T(8,128)S(1)} custom-call(bf16[8,2048]{1,0:T(8,128)(2,1)S(1)} %get-tuple-element.67.attn_ref, bf16[2048,1024]{1,0:T(8,128)(2,1)S(1)} %get-tuple-element.68.weight_ref), custom_call_target="tpu_custom_call" | custom-call | bytes 25200 | tf_op jit(solution)/shard_map/pallas_call | solution.py:502
  27.4 0.2 collective-permute-done.7.attn_ref
  27.6 0.7 %shard_map.145 = (f32[2,2,1024]{2,1,0:T(2,128)S(1)}, f32[2,2,1024]{2,1,0:T(2,128)S(1)}) custom-call(f32[8,1024]{1,0:T(8,128)S(1)} %shard_map.144.acc_ref, bf16[8,2048]{1,0:T(8,128)(2,1)S(1)} %collective-permute-done.7.attn_ref, bf16[2048,1024]{1,0:T(8,128)(2,1)S(1)} %get-tuple-element.69.weight_ref), custom_call_target="tpu_custom_call" | custom-call | bytes 25200 | tf_op jit(solution)/shard_map/pallas_call | solution.py:506
  28.2 1.5 %collective-permute-start.10 = (f32[2,2,1024]{2,1,0:T(2,128)S(1)}, f32[2,2,1024]{2,1,0:T(2,128)S(1)}, u32[]{:S(2)}, u32[]{:S(2)}) collective-permute-start(f32[2,2,1024]{2,1,0:T(2,128)S(1)} %get-tuple-element.76), channel_id=1, source_target_pairs={{0,2},{2,0},{1,3},{3,1},{4,6},{6,4},{5,7},{7,5},{8,10},{10,8},{9,1... | collective-permute-start | bytes 49160 | tf_op jit(solution)/shard_map/ppermute | solution.py:22
  29.8 0.0 collective-permute-done.9.rest_0_
  29.8 0.0 collective-permute-done.8.got_ref
  29.8 0.9 %shard_map.146 = (bf16[1,4,1,128,256]{4,3,2,1,0:T(8,128)(2,1)}, f32[2,1,8192]{2,1,0:T(1,128)}) custom-call(bf16[2,1,128,256]{3,2,1,0:T(8,128)(2,1)S(1)} %get-tuple-element.71.kept_ref, bf16[2,1,128,256]{3,2,1,0:T(8,128)(2,1)S(1)} %collective-permute-done.8.got_ref, f32[2,4,1,1024]{3,2,1,0:T(1,128)S(1)} %get-tuple-element.73.mamba_ref, ...), custom_call_target="tpu_custom_call" | custom-call | bytes 36000 | tf_op jit(solution)/shard_map/pallas_call | solution.py:517
  30.7 1.3 %collective-permute-done.10.refs_1_ = f32[2,2,1024]{2,1,0:T(2,128)S(1)} collective-permute-done((f32[2,2,1024]{2,1,0:T(2,128)S(1)}, f32[2,2,1024]{2,1,0:T(2,128)S(1)}, u32[]{:S(2)}, u32[]{:S(2)}) %collective-permute-start.10) | collective-permute-done | bytes 16416 | tf_op jit(solution)/shard_map/ppermute | solution.py:22
  32.0 0.6 %shard_map.147 = bf16[2,2,1024]{2,1,0:T(2,128)(2,1)} custom-call(f32[2,2,1024]{2,1,0:T(2,128)S(1)} %get-tuple-element.70.refs_0_, f32[2,2,1024]{2,1,0:T(2,128)S(1)} %collective-permute-done.10.refs_1_), custom_call_target="tpu_custom_call" | custom-call | bytes 21600 | tf_op jit(solution)/shard_map/pallas_call | solution.py:528
Async XLA Ops:
  1.7 10.5 %collective-permute-start = (bf16[256,256]{1,0:T(8,128)(2,1)S(1)}, bf16[256,256]{1,0:T(8,128)(2,1)S(1)}, u32[]{:S(2)}, u32[]{:S(2)}) collective-permute-start(bf16[256,256]{1,0:T(8,128)(2,1)S(1)} %get-tuple-element.47), channel_id=1, source_target_pairs={{0,13},{1,12},{4,9},{5,8},{8,5},{9,4},{12,1},{13,0},{2,15},{3,14},... | collective-permute-start | bytes 393224 | tf_op jit(solution)/shard_map/ppermute | solution.py:30
  6.3 12.1 %collective-permute-start.1 = (bf16[256,256]{1,0:T(8,128)(2,1)S(1)}, bf16[256,256]{1,0:T(8,128)(2,1)S(1)}, u32[]{:S(2)}, u32[]{:S(2)}) collective-permute-start(bf16[256,256]{1,0:T(8,128)(2,1)S(1)} %get-tuple-element.48), channel_id=1, source_target_pairs={{0,9},{1,8},{4,13},{5,12},{8,1},{9,0},{12,5},{13,4},{2,11},{3,10},... | collective-permute-start | bytes 393224 | tf_op jit(solution)/shard_map/ppermute | solution.py:30
  6.3 12.1 %collective-permute-start.2 = (bf16[256,256]{1,0:T(8,128)(2,1)S(1)}, bf16[256,256]{1,0:T(8,128)(2,1)S(1)}, u32[]{:S(2)}, u32[]{:S(2)}) collective-permute-start(bf16[256,256]{1,0:T(8,128)(2,1)S(1)} %get-tuple-element.41), channel_id=1, source_target_pairs={{0,5},{1,4},{4,1},{5,0},{8,13},{9,12},{12,9},{13,8},{2,7},{3,6},{6... | collective-permute-start | bytes 393224 | tf_op jit(solution)/shard_map/ppermute | solution.py:30
  8.3 10.0 %collective-permute-start.3 = (bf16[256,256]{1,0:T(8,128)(2,1)S(1)}, bf16[256,256]{1,0:T(8,128)(2,1)S(1)}, u32[]{:S(2)}, u32[]{:S(2)}) collective-permute-start(bf16[256,256]{1,0:T(8,128)(2,1)S(1)} %get-tuple-element.49), channel_id=1, source_target_pairs={{0,1},{1,0},{2,3},{3,2},{4,5},{5,4},{6,7},{7,6},{8,9},{9,8},{10,11... | collective-permute-start | bytes 393224 | tf_op jit(solution)/shard_map/ppermute | solution.py:22
  18.8 6.4 %collective-permute-start.4 = (bf16[80,256]{1,0:T(8,128)(2,1)S(1)}, bf16[80,256]{1,0:T(8,128)(2,1)S(1)}, u32[]{:S(2)}, u32[]{:S(2)}) collective-permute-start(bf16[80,256]{1,0:T(8,128)(2,1)S(1)} %get-tuple-element.64), channel_id=1, source_target_pairs={{0,8},{4,12},{8,0},{12,4},{1,9},{5,13},{9,1},{13,5},{2,10},{6,14},... | collective-permute-start | bytes 122888 | tf_op jit(solution)/shard_map/ppermute | solution.py:22
  18.9 6.3 %collective-permute-start.5 = (bf16[80,256]{1,0:T(8,128)(2,1)S(1)}, bf16[80,256]{1,0:T(8,128)(2,1)S(1)}, u32[]{:S(2)}, u32[]{:S(2)}) collective-permute-start(bf16[80,256]{1,0:T(8,128)(2,1)S(1)} %get-tuple-element.65), channel_id=1, source_target_pairs={{0,12},{4,8},{8,4},{12,0},{1,13},{5,9},{9,5},{13,1},{2,14},{6,10},... | collective-permute-start | bytes 122888 | tf_op jit(solution)/shard_map/ppermute | solution.py:22
  21.6 4.4 %collective-permute-start.6 = (bf16[80,256]{1,0:T(8,128)(2,1)S(1)}, bf16[80,256]{1,0:T(8,128)(2,1)S(1)}, u32[]{:S(2)}, u32[]{:S(2)}) collective-permute-start(bf16[80,256]{1,0:T(8,128)(2,1)S(1)} %get-tuple-element.66), channel_id=1, source_target_pairs={{0,4},{4,0},{8,12},{12,8},{1,5},{5,1},{9,13},{13,9},{2,6},{6,2},{1... | collective-permute-start | bytes 122888 | tf_op jit(solution)/shard_map/ppermute | solution.py:22
  26.1 3.7 %collective-permute-start.8 = (bf16[2,1,128,256]{3,2,1,0:T(8,128)(2,1)S(1)}, bf16[2,1,128,256]{3,2,1,0:T(8,128)(2,1)S(1)}, u32[]{:S(2)}, u32[]{:S(2)}) collective-permute-start(bf16[2,1,128,256]{3,2,1,0:T(8,128)(2,1)S(1)} %get-tuple-element.74), channel_id=1, source_target_pairs={{0,1},{1,0},{2,3},{3,2},{4,5},{5,4},{6,7},{7,6},{8,9},{9,8},{10,11... | collective-permute-start | bytes 393224 | tf_op jit(solution)/shard_map/ppermute | solution.py:22
  26.2 1.4 %collective-permute-start.7 = (bf16[8,2048]{1,0:T(8,128)(2,1)S(1)}, bf16[8,2048]{1,0:T(8,128)(2,1)S(1)}, u32[]{:S(2)}, u32[]{:S(2)}) collective-permute-start(bf16[8,2048]{1,0:T(8,128)(2,1)S(1)} %get-tuple-element.67.attn_ref), channel_id=1, source_target_pairs={{0,1},{1,0},{2,3},{3,2},{4,5},{5,4},{6,7},{7,6},{8,9},{9,8},{10,11... | collective-permute-start | bytes 98312 | tf_op jit(solution)/shard_map/ppermute | solution.py:22
  26.7 3.1 %collective-permute-start.9 = (f32[2,4,1,1024]{3,2,1,0:T(1,128)S(1)}, f32[2,4,1,1024]{3,2,1,0:T(1,128)S(1)}, u32[]{:S(2)}, u32[]{:S(2)}) collective-permute-start(f32[2,4,1,1024]{3,2,1,0:T(1,128)S(1)} %get-tuple-element.73.mamba_ref), channel_id=1, source_target_pairs={{0,1},{1,0},{2,3},{3,2},{4,5},{5,4},{6,7},{7,6},{8,9},{9,8},{10,11... | collective-permute-start | bytes 98312 | tf_op jit(solution)/shard_map/ppermute | solution.py:22
  28.2 3.8 %collective-permute-start.10 = (f32[2,2,1024]{2,1,0:T(2,128)S(1)}, f32[2,2,1024]{2,1,0:T(2,128)S(1)}, u32[]{:S(2)}, u32[]{:S(2)}) collective-permute-start(f32[2,2,1024]{2,1,0:T(2,128)S(1)} %get-tuple-element.76), channel_id=1, source_target_pairs={{0,2},{2,0},{1,3},{3,1},{4,6},{6,4},{5,7},{7,5},{8,10},{10,8},{9,1... | collective-permute-start | bytes 49160 | tf_op jit(solution)/shard_map/ppermute | solution.py:22

commit v14 on v12

--- a/solution.py
+++ b/solution.py
@@ -112,7 +112,7 @@
     for move in first:
         move.wait()
     for c in range(count):
-        pack_state(loaded[c], states[c], 0)
+        pack_state(loaded[c], states[c], states[c].shape[0] - state_rows(part))
     head_first = lax.axis_index("head") * new_ref.shape[2] + rep * heads
     rows = bias_out.shape[0] // heads
     keep_rep = pick_out.shape[2]
@@ -434,7 +434,7 @@
             shape((all_rows, count * BLOCK), F32),
             shape((reps, heads, keep_rep, count, 16, width), BF),
         ]
-        + [shape((state_rows(part), width), BF)] * count,
+        + [shape((state_rows(part) + (32 if c == 1 else 0), width), BF) for c in range(count)],
         [HB] * 6,
         [VM] * (5 + count),
         [
@@ -466,8 +466,8 @@
         ],
     )(*after([out_weight], pieces[0]), step_dt, step_input, step_bc, skip_gain, a_log)
 
-    beside = shift(states[1], "seq", 1)
-    *moved, beside, own_weight = after([*moved[::-1], beside, own_weight])
+    beside = shift(after(states[1:2], own_weight)[0], "seq", 1)
+    *moved, own_weight = after([*moved[::-1], own_weight])
     kv = [own_piece, *moved[::-1]]
     half_shape = (heads, keep_rep, BLOCK, width)
     rows = steps * group

time: 31.9 us -> 31.7 us (level)
  transfers between devices with their start and end apart: 11 -> 11, of which waited for: 5 -> 4; matrix products, arithmetic and copies ran while one was open for 0% -> 0% of each run, Pallas kernels for 22% -> 24%
where the time goes in v14:
time: 31.7 us; the launch traced here: 31.5 us
  starting transfers between devices  12.9 us (41%)
  Pallas kernels  9.4 us (30%)
  waiting for transfers between devices  8.45 us (27%)
  between operations  0.7 us (2%)
    ppermute x11, starting transfers between devices, shift(): return lax.ppermute(x, axis, [(i, i ^ c) for i in range(size)])  12.9 us
    ppermute x11, waiting for transfers between devices, shift(): return lax.ppermute(x, axis, [(i, i ^ c) for i in range(size)])  8.45 us
    pallas_call x1, Pallas kernels, per_device(): call(functools.partial(prepare, count, split), [half_weight, half_weight,...  3.76 us
    pallas_call x1, Pallas kernels, per_device(): call(functools.partial(stage_rest, count, split), [block_shape, shape(que...  1.15 us
    pallas_call x1, Pallas kernels, per_device(): call(functools.partial(stage_blocks, count), [block_shape] * (count - 1),...  1.06 us
    pallas_call x1, Pallas kernels, per_device(): call(functools.partial(assemble, split), [shape((1, dec_heads, keep_rep,...  0.89 us
    pallas_call x1, Pallas kernels, per_device(): call(functools.partial(project_other, heads_count, count), [shape((steps,...  0.67 us
    pallas_call x1, Pallas kernels, per_device(): call(project_own, shape((steps * count, columns), F32), [VM, VM], VM, us=...  0.64 us
  transfers between devices with their start and end apart: 11, of which 4 were waited for; matrix products, arithmetic and copies ran while one was open for 0% of the time, Pallas kernels for 24%

profile of v14, /device:TPU:0, one launch (start us, length us, event | category | flops | bytes accessed | tf_op | source)
XLA Modules:
  0.0 31.5 jit_solution(13255702200531270746)
XLA Ops:
  0.6 1.1 %shard_map.139 = (bf16[256,256]{1,0:T(8,128)(2,1)S(1)}, bf16[256,256]{1,0:T(8,128)(2,1)S(1)}, bf16[256,256]{1,0:T(8,128)(2,1)S(1)}) custom-call(bf16[4,2,128,256]{3,2,1,0:T(8,128)(2,1)} %kv_ref.2), custom_call_target="tpu_custom_call" | custom-call | bytes 36000 | tf_op jit(solution)/shard_map/pallas_call | solution.py:420
  1.7 5.1 %collective-permute-start = (bf16[256,256]{1,0:T(8,128)(2,1)S(1)}, bf16[256,256]{1,0:T(8,128)(2,1)S(1)}, u32[]{:S(2)}, u32[]{:S(2)}) collective-permute-start(bf16[256,256]{1,0:T(8,128)(2,1)S(1)} %get-tuple-element.48), channel_id=1, source_target_pairs={{0,12},{4,8},{8,4},{12,0},{1,13},{5,9},{9,5},{13,1},{2,14},{6,10},... | collective-permute-start | bytes 393224 | tf_op jit(solution)/shard_map/ppermute | solution.py:22
  6.8 0.0 collective-permute-start.1
  6.8 0.6 %collective-permute-start.2 = (bf16[256,256]{1,0:T(8,128)(2,1)S(1)}, bf16[256,256]{1,0:T(8,128)(2,1)S(1)}, u32[]{:S(2)}, u32[]{:S(2)}) collective-permute-start(bf16[256,256]{1,0:T(8,128)(2,1)S(1)} %get-tuple-element.41), channel_id=1, source_target_pairs={{0,4},{4,0},{8,12},{12,8},{1,5},{5,1},{9,13},{13,9},{2,6},{6,2},{1... | collective-permute-start | bytes 393224 | tf_op jit(solution)/shard_map/ppermute | solution.py:22
  7.5 1.2 %shard_map.140 = (bf16[256,256]{1,0:T(8,128)(2,1)S(1)}, bf16[2,1,32,128]{3,2,1,0:T(8,128)(2,1)S(1)}, bf16[2,1,4,256]{3,2,1,0:T(4,128)(2,1)S(1)}, f32[32,512]{1,0...) custom-call(bf16[4,2,128,256]{3,2,1,0:T(8,128)(2,1)} %kv_ref.2, ...), custom_call_target="tpu_custom_call" | custom-call | bytes 36000 | tf_op jit(solution)/shard_map/pallas_call | solution.py:428
  8.6 3.8 %shard_map.141 = (bf16[2048,1024]{1,0:T(8,128)(2,1)S(1)}, bf16[2048,1024]{1,0:T(8,128)(2,1)S(1)}, f32[4,2,16,1024]{3,2,1,0:T(8,128)S(1)}, f32[4,2,1,1024]{3,2,1,0:T(1,128)S(1)}) custom-call(bf16[4096,1024]{1,0:T(8,128)(2,1)} %weight_hbm, f32[2,1,8192]{2,1,0:T(1,128)} %dt_hbm.1, bf16[2,8192]{1,0:T(2,128)(2,1)} %bitcast.3, f32[2,1,2,16]{3,2,1,0:T(2,128)} %bc_hbm.1, ...), custom_call_target="tpu_custom_call" | custom-call | bytes 36000 | tf_op jit(solution)/shard_map/pallas_call | solution.py:448
  12.4 1.5 %collective-permute-start.3 = (bf16[96,256]{1,0:T(8,128)(2,1)S(1)}, bf16[96,256]{1,0:T(8,128)(2,1)S(1)}, u32[]{:S(2)}, u32[]{:S(2)}) collective-permute-start(bf16[96,256]{1,0:T(8,128)(2,1)S(1)} %get-tuple-element.62), channel_id=1, source_target_pairs={{0,4},{4,0},{8,12},{12,8},{1,5},{5,1},{9,13},{13,9},{2,6},{6,2},{1... | collective-permute-start | bytes 147464 | tf_op jit(solution)/shard_map/ppermute | solution.py:22
  13.8 0.0 collective-permute-done.rest_3_
  13.8 4.2 %collective-permute-done.1.rest_2_ = bf16[256,256]{1,0:T(8,128)(2,1)S(1)} collective-permute-done((bf16[256,256]{1,0:T(8,128)(2,1)S(1)}, bf16[256,256]{1,0:T(8,128)(2,1)S(1)}, u32[]{:S(2)}, u32[]{:S(2)}) %collective-permute-start.1) | collective-permute-done | bytes 131104 | tf_op jit(solution)/shard_map/ppermute | solution.py:22
  18.0 0.0 collective-permute-done.2.rest_1_
  18.0 0.5 %shard_map.142 = (bf16[16,256]{1,0:T(8,128)(2,1)S(1)}, bf16[16,256]{1,0:T(8,128)(2,1)S(1)}, bf16[80,256]{1,0:T(8,128)(2,1)S(1)}, bf16[80,256]{1,0:T(8,128)(2,1)S...) custom-call(bf16[2,1,32,128]{3,2,1,0:T(8,128)(2,1)S(1)} %get-tuple-element.43.q_ref, ...), custom_call_target="tpu_custom_call" | custom-call | bytes 36000 | tf_op jit(solution)/shard_map/pallas_call | solution.py:474
  18.5 0.1 collective-permute-start.4
  18.6 2.6 %collective-permute-start.5 = (bf16[80,256]{1,0:T(8,128)(2,1)S(1)}, bf16[80,256]{1,0:T(8,128)(2,1)S(1)}, u32[]{:S(2)}, u32[]{:S(2)}) collective-permute-start(bf16[80,256]{1,0:T(8,128)(2,1)S(1)} %get-tuple-element.65), channel_id=1, source_target_pairs={{0,12},{4,8},{8,4},{12,0},{1,13},{5,9},{9,5},{13,1},{2,14},{6,10},... | collective-permute-start | bytes 122888 | tf_op jit(solution)/shard_map/ppermute | solution.py:22
  21.2 0.9 %collective-permute-start.6 = (bf16[16,256]{1,0:T(8,128)(2,1)S(1)}, bf16[16,256]{1,0:T(8,128)(2,1)S(1)}, u32[]{:S(2)}, u32[]{:S(2)}) collective-permute-start(bf16[16,256]{1,0:T(8,128)(2,1)S(1)} %get-tuple-element.66), channel_id=1, source_target_pairs={{0,4},{4,0},{8,12},{12,8},{1,5},{5,1},{9,13},{13,9},{2,6},{6,2},{1... | collective-permute-start | bytes 24584 | tf_op jit(solution)/shard_map/ppermute | solution.py:22
  22.1 0.0 collective-permute-done.3.beside_ref
  22.1 2.8 %collective-permute-done.6.rest_3_ = bf16[16,256]{1,0:T(8,128)(2,1)S(1)} collective-permute-done((bf16[16,256]{1,0:T(8,128)(2,1)S(1)}, bf16[16,256]{1,0:T(8,128)(2,1)S(1)}, u32[]{:S(2)}, u32[]{:S(2)}) %collective-permute-start.6) | collective-permute-done | bytes 8224 | tf_op jit(solution)/shard_map/ppermute | solution.py:22
  24.8 0.0 collective-permute-done.4.rest_1_
  24.8 0.0 collective-permute-done.5.rest_2_
  24.8 0.1 shard_map.143
  25.0 0.1 collective-permute-start.8
  25.0 0.5 %collective-permute-start.7 = (bf16[8,2048]{1,0:T(8,128)(2,1)S(1)}, bf16[8,2048]{1,0:T(8,128)(2,1)S(1)}, u32[]{:S(2)}, u32[]{:S(2)}) collective-permute-start(bf16[8,2048]{1,0:T(8,128)(2,1)S(1)} %get-tuple-element.67.attn_ref), channel_id=1, source_target_pairs={{0,1},{1,0},{2,3},{3,2},{4,5},{5,4},{6,7},{7,6},{8,9},{9,8},{10,11... | collective-permute-start | bytes 98312 | tf_op jit(solution)/shard_map/ppermute | solution.py:22
  25.5 0.1 collective-permute-start.9
  25.6 0.6 %shard_map.144.acc_ref = f32[8,1024]{1,0:T(8,128)S(1)} custom-call(bf16[8,2048]{1,0:T(8,128)(2,1)S(1)} %get-tuple-element.67.attn_ref, bf16[2048,1024]{1,0:T(8,128)(2,1)S(1)} %get-tuple-element.68.weight_ref), custom_call_target="tpu_custom_call" | custom-call | bytes 25200 | tf_op jit(solution)/shard_map/pallas_call | solution.py:492
  26.3 0.2 collective-permute-done.7.attn_ref
  26.4 0.7 %shard_map.145 = (f32[2,2,1024]{2,1,0:T(2,128)S(1)}, f32[2,2,1024]{2,1,0:T(2,128)S(1)}) custom-call(f32[8,1024]{1,0:T(8,128)S(1)} %shard_map.144.acc_ref, bf16[8,2048]{1,0:T(8,128)(2,1)S(1)} %collective-permute-done.7.attn_ref, bf16[2048,1024]{1,0:T(8,128)(2,1)S(1)} %get-tuple-element.69.weight_ref), custom_call_target="tpu_custom_call" | custom-call | bytes 25200 | tf_op jit(solution)/shard_map/pallas_call | solution.py:496
  27.1 1.5 %collective-permute-start.10 = (f32[2,2,1024]{2,1,0:T(2,128)S(1)}, f32[2,2,1024]{2,1,0:T(2,128)S(1)}, u32[]{:S(2)}, u32[]{:S(2)}) collective-permute-start(f32[2,2,1024]{2,1,0:T(2,128)S(1)} %get-tuple-element.76), channel_id=1, source_target_pairs={{0,2},{2,0},{1,3},{3,1},{4,6},{6,4},{5,7},{7,5},{8,10},{10,8},{9,1... | collective-permute-start | bytes 49160 | tf_op jit(solution)/shard_map/ppermute | solution.py:22
  28.6 0.0 collective-permute-done.9.rest_0_
  28.6 0.0 collective-permute-done.8.got_ref
  28.6 0.9 %shard_map.146 = (bf16[1,4,1,128,256]{4,3,2,1,0:T(8,128)(2,1)}, f32[2,1,8192]{2,1,0:T(1,128)}) custom-call(bf16[2,1,128,256]{3,2,1,0:T(8,128)(2,1)S(1)} %get-tuple-element.71.kept_ref, bf16[2,1,128,256]{3,2,1,0:T(8,128)(2,1)S(1)} %collective-permute-done.8.got_ref, f32[2,4,1,1024]{3,2,1,0:T(1,128)S(1)} %get-tuple-element.73.mamba_ref, ...), custom_call_target="tpu_custom_call" | custom-call | bytes 36000 | tf_op jit(solution)/shard_map/pallas_call | solution.py:507
  29.5 1.3 %collective-permute-done.10.refs_1_ = f32[2,2,1024]{2,1,0:T(2,128)S(1)} collective-permute-done((f32[2,2,1024]{2,1,0:T(2,128)S(1)}, f32[2,2,1024]{2,1,0:T(2,128)S(1)}, u32[]{:S(2)}, u32[]{:S(2)}) %collective-permute-start.10) | collective-permute-done | bytes 16416 | tf_op jit(solution)/shard_map/ppermute | solution.py:22
  30.9 0.6 %shard_map.147 = bf16[2,2,1024]{2,1,0:T(2,128)(2,1)} custom-call(f32[2,2,1024]{2,1,0:T(2,128)S(1)} %get-tuple-element.70.refs_0_, f32[2,2,1024]{2,1,0:T(2,128)S(1)} %collective-permute-done.10.refs_1_), custom_call_target="tpu_custom_call" | custom-call | bytes 21600 | tf_op jit(solution)/shard_map/pallas_call | solution.py:518
Async XLA Ops:
  1.7 12.1 %collective-permute-start = (bf16[256,256]{1,0:T(8,128)(2,1)S(1)}, bf16[256,256]{1,0:T(8,128)(2,1)S(1)}, u32[]{:S(2)}, u32[]{:S(2)}) collective-permute-start(bf16[256,256]{1,0:T(8,128)(2,1)S(1)} %get-tuple-element.48), channel_id=1, source_target_pairs={{0,12},{4,8},{8,4},{12,0},{1,13},{5,9},{9,5},{13,1},{2,14},{6,10},... | collective-permute-start | bytes 393224 | tf_op jit(solution)/shard_map/ppermute | solution.py:22
  6.8 11.2 %collective-permute-start.1 = (bf16[256,256]{1,0:T(8,128)(2,1)S(1)}, bf16[256,256]{1,0:T(8,128)(2,1)S(1)}, u32[]{:S(2)}, u32[]{:S(2)}) collective-permute-start(bf16[256,256]{1,0:T(8,128)(2,1)S(1)} %get-tuple-element.49), channel_id=1, source_target_pairs={{0,8},{4,12},{8,0},{12,4},{1,9},{5,13},{9,1},{13,5},{2,10},{6,14},... | collective-permute-start | bytes 393224 | tf_op jit(solution)/shard_map/ppermute | solution.py:22
  6.8 11.2 %collective-permute-start.2 = (bf16[256,256]{1,0:T(8,128)(2,1)S(1)}, bf16[256,256]{1,0:T(8,128)(2,1)S(1)}, u32[]{:S(2)}, u32[]{:S(2)}) collective-permute-start(bf16[256,256]{1,0:T(8,128)(2,1)S(1)} %get-tuple-element.41), channel_id=1, source_target_pairs={{0,4},{4,0},{8,12},{12,8},{1,5},{5,1},{9,13},{13,9},{2,6},{6,2},{1... | collective-permute-start | bytes 393224 | tf_op jit(solution)/shard_map/ppermute | solution.py:22
  12.4 9.7 %collective-permute-start.3 = (bf16[96,256]{1,0:T(8,128)(2,1)S(1)}, bf16[96,256]{1,0:T(8,128)(2,1)S(1)}, u32[]{:S(2)}, u32[]{:S(2)}) collective-permute-start(bf16[96,256]{1,0:T(8,128)(2,1)S(1)} %get-tuple-element.62), channel_id=1, source_target_pairs={{0,4},{4,0},{8,12},{12,8},{1,5},{5,1},{9,13},{13,9},{2,6},{6,2},{1... | collective-permute-start | bytes 147464 | tf_op jit(solution)/shard_map/ppermute | solution.py:22
  18.5 6.3 %collective-permute-start.4 = (bf16[80,256]{1,0:T(8,128)(2,1)S(1)}, bf16[80,256]{1,0:T(8,128)(2,1)S(1)}, u32[]{:S(2)}, u32[]{:S(2)}) collective-permute-start(bf16[80,256]{1,0:T(8,128)(2,1)S(1)} %get-tuple-element.64), channel_id=1, source_target_pairs={{0,8},{4,12},{8,0},{12,4},{1,9},{5,13},{9,1},{13,5},{2,10},{6,14},... | collective-permute-start | bytes 122888 | tf_op jit(solution)/shard_map/ppermute | solution.py:22
  18.6 6.3 %collective-permute-start.5 = (bf16[80,256]{1,0:T(8,128)(2,1)S(1)}, bf16[80,256]{1,0:T(8,128)(2,1)S(1)}, u32[]{:S(2)}, u32[]{:S(2)}) collective-permute-start(bf16[80,256]{1,0:T(8,128)(2,1)S(1)} %get-tuple-element.65), channel_id=1, source_target_pairs={{0,12},{4,8},{8,4},{12,0},{1,13},{5,9},{9,5},{13,1},{2,14},{6,10},... | collective-permute-start | bytes 122888 | tf_op jit(solution)/shard_map/ppermute | solution.py:22
  21.2 3.7 %collective-permute-start.6 = (bf16[16,256]{1,0:T(8,128)(2,1)S(1)}, bf16[16,256]{1,0:T(8,128)(2,1)S(1)}, u32[]{:S(2)}, u32[]{:S(2)}) collective-permute-start(bf16[16,256]{1,0:T(8,128)(2,1)S(1)} %get-tuple-element.66), channel_id=1, source_target_pairs={{0,4},{4,0},{8,12},{12,8},{1,5},{5,1},{9,13},{13,9},{2,6},{6,2},{1... | collective-permute-start | bytes 24584 | tf_op jit(solution)/shard_map/ppermute | solution.py:22
  25.0 3.7 %collective-permute-start.8 = (bf16[2,1,128,256]{3,2,1,0:T(8,128)(2,1)S(1)}, bf16[2,1,128,256]{3,2,1,0:T(8,128)(2,1)S(1)}, u32[]{:S(2)}, u32[]{:S(2)}) collective-permute-start(bf16[2,1,128,256]{3,2,1,0:T(8,128)(2,1)S(1)} %get-tuple-element.74), channel_id=1, source_target_pairs={{0,1},{1,0},{2,3},{3,2},{4,5},{5,4},{6,7},{7,6},{8,9},{9,8},{10,11... | collective-permute-start | bytes 393224 | tf_op jit(solution)/shard_map/ppermute | solution.py:22
  25.0 1.4 %collective-permute-start.7 = (bf16[8,2048]{1,0:T(8,128)(2,1)S(1)}, bf16[8,2048]{1,0:T(8,128)(2,1)S(1)}, u32[]{:S(2)}, u32[]{:S(2)}) collective-permute-start(bf16[8,2048]{1,0:T(8,128)(2,1)S(1)} %get-tuple-element.67.attn_ref), channel_id=1, source_target_pairs={{0,1},{1,0},{2,3},{3,2},{4,5},{5,4},{6,7},{7,6},{8,9},{9,8},{10,11... | collective-permute-start | bytes 98312 | tf_op jit(solution)/shard_map/ppermute | solution.py:22
  25.5 3.1 %collective-permute-start.9 = (f32[2,4,1,1024]{3,2,1,0:T(1,128)S(1)}, f32[2,4,1,1024]{3,2,1,0:T(1,128)S(1)}, u32[]{:S(2)}, u32[]{:S(2)}) collective-permute-start(f32[2,4,1,1024]{3,2,1,0:T(1,128)S(1)} %get-tuple-element.73.mamba_ref), channel_id=1, source_target_pairs={{0,1},{1,0},{2,3},{3,2},{4,5},{5,4},{6,7},{7,6},{8,9},{9,8},{10,11... | collective-permute-start | bytes 98312 | tf_op jit(solution)/shard_map/ppermute | solution.py:22
  27.1 3.8 %collective-permute-start.10 = (f32[2,2,1024]{2,1,0:T(2,128)S(1)}, f32[2,2,1024]{2,1,0:T(2,128)S(1)}, u32[]{:S(2)}, u32[]{:S(2)}) collective-permute-start(f32[2,2,1024]{2,1,0:T(2,128)S(1)} %get-tuple-element.76), channel_id=1, source_target_pairs={{0,2},{2,0},{1,3},{3,1},{4,6},{6,4},{5,7},{7,5},{8,10},{10,8},{9,1... | collective-permute-start | bytes 49160 | tf_op jit(solution)/shard_map/ppermute | solution.py:22

commit v15 on v14

--- a/solution.py
+++ b/solution.py
@@ -163,9 +163,9 @@
     return dot_f32(weights, values, ((1,), (0,)))
 
 
-def attend(count, heads, q_ref, new_ref, bias_ref, pick_ref, *rest):
+def attend(count, heads, q_ref, new_ref, bias_ref, *rest):
     pieces, states = rest[:count], rest[count : 2 * count - 2]
-    outs, (kept_ref, sent_ref) = rest[2 * count - 2 : 3 * count - 2], rest[3 * count - 2 :]
+    outs = rest[2 * count - 2 :]
     rep = lax.axis_index("rep")
     queries = query_rows(q_ref, heads)
     rows, hd = queries[0].shape
@@ -216,16 +216,21 @@
             outs[c][:rows, j * hd : (j + 1) * hd] = half
         if c > 1:
             outs[c][rows:, :] = states[c - 2][...]
+
+
+def select(count, heads, pick_ref, *rest):
+    pieces, (kept_ref, sent_ref) = rest[:count], rest[count:]
+    width = pieces[0].shape[1]
     tile = pick_ref.shape[4]
     for side, ref in ((1, sent_ref), (0, kept_ref)):
         for j in range(heads):
             for k in range(ref.shape[1]):
                 total = None
                 for c in range(count):
-                    piece = pieces[c][j * BLOCK : (j + 1) * BLOCK, :].reshape(-1, tile, 2 * hd)
+                    piece = pieces[c][j * BLOCK : (j + 1) * BLOCK, :].reshape(-1, tile, width)
                     term = piece * pick_ref[side, j, k, c][None]
                     total = term if total is None else total + term
-                ref[j, k] = total.reshape(BLOCK, 2 * hd)
+                ref[j, k] = total.reshape(BLOCK, width)
 
 
 def collect(count, heads, steps, group, slope_ref, base_ref, home_ref, beside_ref, *rest):
@@ -471,14 +476,19 @@
     kv = [own_piece, *moved[::-1]]
     half_shape = (heads, keep_rep, BLOCK, width)
     rows = steps * group
-    *sends, kept, sent = call(
+    sends = call(
         functools.partial(attend, count, heads),
         [shape((rows, width), BF)] * 2
-        + [shape((rows + state_rows(part), width), BF)] * (count - 2)
-        + [shape(half_shape, BF)] * 2,
-        [VM] * (2 + 2 * count),
-        [VM] * (count + 2),
-    )(q_near, new_near, bias, picks, *kv, *states[2:])
+        + [shape((rows + state_rows(part), width), BF)] * (count - 2),
+        [VM] * (1 + 2 * count),
+        [VM] * count,
+    )(q_near, new_near, bias, *kv, *states[2:])
+    kept, sent = call(
+        functools.partial(select, count, heads),
+        [shape(half_shape, BF)] * 2,
+        [VM] * (1 + count),
+        [VM] * 2,
+    )(*after([picks], sends[0]), *kv)
     order = [*range(2, count), 1]
     gathered = [shift(sends[c], "seq", c) for c in order]
     attn, mamba = call(

time: 31.7 us -> 32.8 us (1.035)
  waiting for transfers between devices: 8.45 us -> 9.15 us
  starting transfers between devices: 12.9 us -> 13.3 us
    ppermute x11, waiting for transfers between devices: 8.45 us -> 9.15 us  [shift(): return lax.ppermute(x, axis, [(i, i ^ c) for i in range(size)])]
    ppermute x11, starting transfers between devices: 12.9 us -> 13.3 us  [shift(): return lax.ppermute(x, axis, [(i, i ^ c) for i in range(size)])]
  transfers between devices with their start and end apart: 11 -> 11, of which waited for: 4 -> 5; matrix products, arithmetic and copies ran while one was open for 0% -> 0% of each run, Pallas kernels for 24% -> 23%
where the time goes in v15:
time: 32.8 us; the launch traced here: 32.6 us
  starting transfers between devices  13.3 us (41%)
  Pallas kernels  9.45 us (29%)
  waiting for transfers between devices  9.15 us (28%)
  between operations  0.7 us (2%)
    ppermute x11, starting transfers between devices, shift(): return lax.ppermute(x, axis, [(i, i ^ c) for i in range(size)])  13.3 us
    ppermute x11, waiting for transfers between devices, shift(): return lax.ppermute(x, axis, [(i, i ^ c) for i in range(size)])  9.15 us
    pallas_call x1, Pallas kernels, per_device(): call(functools.partial(prepare, count, split), [half_weight, half_weight,...  3.74 us
    pallas_call x1, Pallas kernels, per_device(): call(functools.partial(stage_rest, count, split), [block_shape, shape(que...  1.17 us
    pallas_call x1, Pallas kernels, per_device(): call(functools.partial(stage_blocks, count), [block_shape] * (count - 1),...  1.06 us
    pallas_call x1, Pallas kernels, per_device(): call(functools.partial(assemble, split), [shape((1, dec_heads, keep_rep,...  0.89 us
    pallas_call x1, Pallas kernels, per_device(): call(functools.partial(project_other, heads_count, count), [shape((steps,...  0.67 us
  transfers between devices with their start and end apart: 11, of which 5 were waited for; matrix products, arithmetic and copies ran while one was open for 0% of the time, Pallas kernels for 23%

profile of v15, /device:TPU:0, one launch (start us, length us, event | category | flops | bytes accessed | tf_op | source)
XLA Modules:
  0.0 32.6 jit_solution(15550802335096795105)
XLA Ops:
  0.6 1.1 %shard_map.139 = (bf16[256,256]{1,0:T(8,128)(2,1)S(1)}, bf16[256,256]{1,0:T(8,128)(2,1)S(1)}, bf16[256,256]{1,0:T(8,128)(2,1)S(1)}) custom-call(bf16[4,2,128,256]{3,2,1,0:T(8,128)(2,1)} %kv_ref.2), custom_call_target="tpu_custom_call" | custom-call | bytes 36000 | tf_op jit(solution)/shard_map/pallas_call | solution.py:425
  1.7 3.1 %collective-permute-start.2 = (bf16[256,256]{1,0:T(8,128)(2,1)S(1)}, bf16[256,256]{1,0:T(8,128)(2,1)S(1)}, u32[]{:S(2)}, u32[]{:S(2)}) collective-permute-start(bf16[256,256]{1,0:T(8,128)(2,1)S(1)} %get-tuple-element.42), channel_id=1, source_target_pairs={{0,4},{4,0},{8,12},{12,8},{1,5},{5,1},{9,13},{13,9},{2,6},{6,2},{1... | collective-permute-start | bytes 393224 | tf_op jit(solution)/shard_map/ppermute | solution.py:22
  4.8 2.5 %collective-permute-start = (bf16[256,256]{1,0:T(8,128)(2,1)S(1)}, bf16[256,256]{1,0:T(8,128)(2,1)S(1)}, u32[]{:S(2)}, u32[]{:S(2)}) collective-permute-start(bf16[256,256]{1,0:T(8,128)(2,1)S(1)} %get-tuple-element.49), channel_id=1, source_target_pairs={{0,12},{4,8},{8,4},{12,0},{1,13},{5,9},{9,5},{13,1},{2,14},{6,10},... | collective-permute-start | bytes 393224 | tf_op jit(solution)/shard_map/ppermute | solution.py:22
  7.3 0.1 collective-permute-start.1
  7.4 3.7 %shard_map.141 = (bf16[2048,1024]{1,0:T(8,128)(2,1)S(1)}, bf16[2048,1024]{1,0:T(8,128)(2,1)S(1)}, f32[4,2,16,1024]{3,2,1,0:T(8,128)S(1)}, f32[4,2,1,1024]{3,2,1,0:T(1,128)S(1)}) custom-call(bf16[4096,1024]{1,0:T(8,128)(2,1)} %weight_hbm, f32[2,1,8192]{2,1,0:T(1,128)} %dt_hbm.1, bf16[2,8192]{1,0:T(2,128)(2,1)} %bitcast.3, f32[2,1,2,16]{3,2,1,0:T(2,128)} %bc_hbm.1, ...), custom_call_target="tpu_custom_call" | custom-call | bytes 36000 | tf_op jit(solution)/shard_map/pallas_call | solution.py:453
  11.1 1.2 %shard_map.140 = (bf16[256,256]{1,0:T(8,128)(2,1)S(1)}, bf16[2,1,32,128]{3,2,1,0:T(8,128)(2,1)S(1)}, bf16[2,1,4,256]{3,2,1,0:T(4,128)(2,1)S(1)}, f32[32,512]{1,0...) custom-call(bf16[4,2,128,256]{3,2,1,0:T(8,128)(2,1)} %kv_ref.2, ...), custom_call_target="tpu_custom_call" | custom-call | bytes 36000 | tf_op jit(solution)/shard_map/pallas_call | solution.py:433
  12.3 1.9 %collective-permute-start.3 = (bf16[96,256]{1,0:T(8,128)(2,1)S(1)}, bf16[96,256]{1,0:T(8,128)(2,1)S(1)}, u32[]{:S(2)}, u32[]{:S(2)}) collective-permute-start(bf16[96,256]{1,0:T(8,128)(2,1)S(1)} %get-tuple-element.65), channel_id=1, source_target_pairs={{0,4},{4,0},{8,12},{12,8},{1,5},{5,1},{9,13},{13,9},{2,6},{6,2},{1... | collective-permute-start | bytes 147464 | tf_op jit(solution)/shard_map/ppermute | solution.py:22
  14.2 0.0 collective-permute-done.2.rest_1_
  14.2 0.4 %collective-permute-done.rest_3_ = bf16[256,256]{1,0:T(8,128)(2,1)S(1)} collective-permute-done((bf16[256,256]{1,0:T(8,128)(2,1)S(1)}, bf16[256,256]{1,0:T(8,128)(2,1)S(1)}, u32[]{:S(2)}, u32[]{:S(2)}) %collective-permute-start) | collective-permute-done | bytes 131104 | tf_op jit(solution)/shard_map/ppermute | solution.py:22
  14.5 4.5 %collective-permute-done.1.rest_2_ = bf16[256,256]{1,0:T(8,128)(2,1)S(1)} collective-permute-done((bf16[256,256]{1,0:T(8,128)(2,1)S(1)}, bf16[256,256]{1,0:T(8,128)(2,1)S(1)}, u32[]{:S(2)}, u32[]{:S(2)}) %collective-permute-start.1) | collective-permute-done | bytes 131104 | tf_op jit(solution)/shard_map/ppermute | solution.py:22
  19.0 0.5 %shard_map.142 = (bf16[16,256]{1,0:T(8,128)(2,1)S(1)}, bf16[16,256]{1,0:T(8,128)(2,1)S(1)}, bf16[80,256]{1,0:T(8,128)(2,1)S(1)}, bf16[80,256]{1,0:T(8,128)(2,1)S(1)}) custom-call(bf16[2,1,32,128]{3,2,1,0:T(8,128)(2,1)S(1)} %get-tuple-element.45.q_ref, bf16[2,1,4,256]{3,2,1,0:T(4,128)(2,1)S(1)} %get-tuple-element.46.new_ref, ...), custom_call_target="tpu_custom_call" | custom-call | bytes 36000 | tf_op jit(solution)/shard_map/pallas_call | solution.py:479
  19.5 0.2 collective-permute-start.4
  19.6 2.6 %collective-permute-start.5 = (bf16[80,256]{1,0:T(8,128)(2,1)S(1)}, bf16[80,256]{1,0:T(8,128)(2,1)S(1)}, u32[]{:S(2)}, u32[]{:S(2)}) collective-permute-start(bf16[80,256]{1,0:T(8,128)(2,1)S(1)} %get-tuple-element.67), channel_id=1, source_target_pairs={{0,12},{4,8},{8,4},{12,0},{1,13},{5,9},{9,5},{13,1},{2,14},{6,10},... | collective-permute-start | bytes 122888 | tf_op jit(solution)/shard_map/ppermute | solution.py:22
  22.3 0.8 %collective-permute-start.6 = (bf16[16,256]{1,0:T(8,128)(2,1)S(1)}, bf16[16,256]{1,0:T(8,128)(2,1)S(1)}, u32[]{:S(2)}, u32[]{:S(2)}) collective-permute-start(bf16[16,256]{1,0:T(8,128)(2,1)S(1)} %get-tuple-element.68), channel_id=1, source_target_pairs={{0,4},{4,0},{8,12},{12,8},{1,5},{5,1},{9,13},{13,9},{2,6},{6,2},{1... | collective-permute-start | bytes 24584 | tf_op jit(solution)/shard_map/ppermute | solution.py:22
  23.0 0.1 shard_map.143
  23.1 0.0 collective-permute-done.3.beside_ref
  23.1 2.8 %collective-permute-done.6.rest_3_ = bf16[16,256]{1,0:T(8,128)(2,1)S(1)} collective-permute-done((bf16[16,256]{1,0:T(8,128)(2,1)S(1)}, bf16[16,256]{1,0:T(8,128)(2,1)S(1)}, u32[]{:S(2)}, u32[]{:S(2)}) %collective-permute-start.6) | collective-permute-done | bytes 8224 | tf_op jit(solution)/shard_map/ppermute | solution.py:22
  25.9 0.0 collective-permute-done.4.rest_1_
  25.9 0.0 collective-permute-done.5.rest_2_
  25.9 0.1 shard_map.144
  26.1 0.1 collective-permute-start.8
  26.1 0.5 %collective-permute-start.7 = (bf16[8,2048]{1,0:T(8,128)(2,1)S(1)}, bf16[8,2048]{1,0:T(8,128)(2,1)S(1)}, u32[]{:S(2)}, u32[]{:S(2)}) collective-permute-start(bf16[8,2048]{1,0:T(8,128)(2,1)S(1)} %get-tuple-element.69.attn_ref), channel_id=1, source_target_pairs={{0,1},{1,0},{2,3},{3,2},{4,5},{5,4},{6,7},{7,6},{8,9},{9,8},{10,11... | collective-permute-start | bytes 98312 | tf_op jit(solution)/shard_map/ppermute | solution.py:22
  26.6 0.1 collective-permute-start.9
  26.7 0.6 %shard_map.145.acc_ref = f32[8,1024]{1,0:T(8,128)S(1)} custom-call(bf16[8,2048]{1,0:T(8,128)(2,1)S(1)} %get-tuple-element.69.attn_ref, bf16[2048,1024]{1,0:T(8,128)(2,1)S(1)} %get-tuple-element.70.weight_ref), custom_call_target="tpu_custom_call" | custom-call | bytes 25200 | tf_op jit(solution)/shard_map/pallas_call | solution.py:502
  27.4 0.2 collective-permute-done.7.attn_ref
  27.5 0.7 %shard_map.146 = (f32[2,2,1024]{2,1,0:T(2,128)S(1)}, f32[2,2,1024]{2,1,0:T(2,128)S(1)}) custom-call(f32[8,1024]{1,0:T(8,128)S(1)} %shard_map.145.acc_ref, bf16[8,2048]{1,0:T(8,128)(2,1)S(1)} %collective-permute-done.7.attn_ref, bf16[2048,1024]{1,0:T(8,128)(2,1)S(1)} %get-tuple-element.71.weight_ref), custom_call_target="tpu_custom_call" | custom-call | bytes 25200 | tf_op jit(solution)/shard_map/pallas_call | solution.py:506
  28.2 1.5 %collective-permute-start.10 = (f32[2,2,1024]{2,1,0:T(2,128)S(1)}, f32[2,2,1024]{2,1,0:T(2,128)S(1)}, u32[]{:S(2)}, u32[]{:S(2)}) collective-permute-start(f32[2,2,1024]{2,1,0:T(2,128)S(1)} %get-tuple-element.78), channel_id=1, source_target_pairs={{0,2},{2,0},{1,3},{3,1},{4,6},{6,4},{5,7},{7,5},{8,10},{10,8},{9,1... | collective-permute-start | bytes 49160 | tf_op jit(solution)/shard_map/ppermute | solution.py:22
  29.7 0.0 collective-permute-done.9.rest_0_
  29.7 0.0 collective-permute-done.8.got_ref
  29.7 0.9 %shard_map.147 = (bf16[1,4,1,128,256]{4,3,2,1,0:T(8,128)(2,1)}, f32[2,1,8192]{2,1,0:T(1,128)}) custom-call(bf16[2,1,128,256]{3,2,1,0:T(8,128)(2,1)S(1)} %get-tuple-element.73.kept_ref, bf16[2,1,128,256]{3,2,1,0:T(8,128)(2,1)S(1)} %collective-permute-done.8.got_ref, f32[2,4,1,1024]{3,2,1,0:T(1,128)S(1)} %get-tuple-element.75.mamba_ref, ...), custom_call_target="tpu_custom_call" | custom-call | bytes 36000 | tf_op jit(solution)/shard_map/pallas_call | solution.py:517
  30.6 1.3 %collective-permute-done.10.refs_1_ = f32[2,2,1024]{2,1,0:T(2,128)S(1)} collective-permute-done((f32[2,2,1024]{2,1,0:T(2,128)S(1)}, f32[2,2,1024]{2,1,0:T(2,128)S(1)}, u32[]{:S(2)}, u32[]{:S(2)}) %collective-permute-start.10) | collective-permute-done | bytes 16416 | tf_op jit(solution)/shard_map/ppermute | solution.py:22
  32.0 0.6 %shard_map.148 = bf16[2,2,1024]{2,1,0:T(2,128)(2,1)} custom-call(f32[2,2,1024]{2,1,0:T(2,128)S(1)} %get-tuple-element.72.refs_0_, f32[2,2,1024]{2,1,0:T(2,128)S(1)} %collective-permute-done.10.refs_1_), custom_call_target="tpu_custom_call" | custom-call | bytes 21600 | tf_op jit(solution)/shard_map/pallas_call | solution.py:528
Async XLA Ops:
  1.7 12.5 %collective-permute-start.2 = (bf16[256,256]{1,0:T(8,128)(2,1)S(1)}, bf16[256,256]{1,0:T(8,128)(2,1)S(1)}, u32[]{:S(2)}, u32[]{:S(2)}) collective-permute-start(bf16[256,256]{1,0:T(8,128)(2,1)S(1)} %get-tuple-element.42), channel_id=1, source_target_pairs={{0,4},{4,0},{8,12},{12,8},{1,5},{5,1},{9,13},{13,9},{2,6},{6,2},{1... | collective-permute-start | bytes 393224 | tf_op jit(solution)/shard_map/ppermute | solution.py:22
  4.8 9.7 %collective-permute-start = (bf16[256,256]{1,0:T(8,128)(2,1)S(1)}, bf16[256,256]{1,0:T(8,128)(2,1)S(1)}, u32[]{:S(2)}, u32[]{:S(2)}) collective-permute-start(bf16[256,256]{1,0:T(8,128)(2,1)S(1)} %get-tuple-element.49), channel_id=1, source_target_pairs={{0,12},{4,8},{8,4},{12,0},{1,13},{5,9},{9,5},{13,1},{2,14},{6,10},... | collective-permute-start | bytes 393224 | tf_op jit(solution)/shard_map/ppermute | solution.py:22
  7.3 11.8 %collective-permute-start.1 = (bf16[256,256]{1,0:T(8,128)(2,1)S(1)}, bf16[256,256]{1,0:T(8,128)(2,1)S(1)}, u32[]{:S(2)}, u32[]{:S(2)}) collective-permute-start(bf16[256,256]{1,0:T(8,128)(2,1)S(1)} %get-tuple-element.50), channel_id=1, source_target_pairs={{0,8},{4,12},{8,0},{12,4},{1,9},{5,13},{9,1},{13,5},{2,10},{6,14},... | collective-permute-start | bytes 393224 | tf_op jit(solution)/shard_map/ppermute | solution.py:22
  12.3 10.8 %collective-permute-start.3 = (bf16[96,256]{1,0:T(8,128)(2,1)S(1)}, bf16[96,256]{1,0:T(8,128)(2,1)S(1)}, u32[]{:S(2)}, u32[]{:S(2)}) collective-permute-start(bf16[96,256]{1,0:T(8,128)(2,1)S(1)} %get-tuple-element.65), channel_id=1, source_target_pairs={{0,4},{4,0},{8,12},{12,8},{1,5},{5,1},{9,13},{13,9},{2,6},{6,2},{1... | collective-permute-start | bytes 147464 | tf_op jit(solution)/shard_map/ppermute | solution.py:22
  19.5 6.4 %collective-permute-start.4 = (bf16[80,256]{1,0:T(8,128)(2,1)S(1)}, bf16[80,256]{1,0:T(8,128)(2,1)S(1)}, u32[]{:S(2)}, u32[]{:S(2)}) collective-permute-start(bf16[80,256]{1,0:T(8,128)(2,1)S(1)} %get-tuple-element.66), channel_id=1, source_target_pairs={{0,8},{4,12},{8,0},{12,4},{1,9},{5,13},{9,1},{13,5},{2,10},{6,14},... | collective-permute-start | bytes 122888 | tf_op jit(solution)/shard_map/ppermute | solution.py:22
  19.6 6.3 %collective-permute-start.5 = (bf16[80,256]{1,0:T(8,128)(2,1)S(1)}, bf16[80,256]{1,0:T(8,128)(2,1)S(1)}, u32[]{:S(2)}, u32[]{:S(2)}) collective-permute-start(bf16[80,256]{1,0:T(8,128)(2,1)S(1)} %get-tuple-element.67), channel_id=1, source_target_pairs={{0,12},{4,8},{8,4},{12,0},{1,13},{5,9},{9,5},{13,1},{2,14},{6,10},... | collective-permute-start | bytes 122888 | tf_op jit(solution)/shard_map/ppermute | solution.py:22
  22.3 3.7 %collective-permute-start.6 = (bf16[16,256]{1,0:T(8,128)(2,1)S(1)}, bf16[16,256]{1,0:T(8,128)(2,1)S(1)}, u32[]{:S(2)}, u32[]{:S(2)}) collective-permute-start(bf16[16,256]{1,0:T(8,128)(2,1)S(1)} %get-tuple-element.68), channel_id=1, source_target_pairs={{0,4},{4,0},{8,12},{12,8},{1,5},{5,1},{9,13},{13,9},{2,6},{6,2},{1... | collective-permute-start | bytes 24584 | tf_op jit(solution)/shard_map/ppermute | solution.py:22
  26.1 3.7 %collective-permute-start.8 = (bf16[2,1,128,256]{3,2,1,0:T(8,128)(2,1)S(1)}, bf16[2,1,128,256]{3,2,1,0:T(8,128)(2,1)S(1)}, u32[]{:S(2)}, u32[]{:S(2)}) collective-permute-start(bf16[2,1,128,256]{3,2,1,0:T(8,128)(2,1)S(1)} %get-tuple-element.76), channel_id=1, source_target_pairs={{0,1},{1,0},{2,3},{3,2},{4,5},{5,4},{6,7},{7,6},{8,9},{9,8},{10,11... | collective-permute-start | bytes 393224 | tf_op jit(solution)/shard_map/ppermute | solution.py:22
  26.1 1.4 %collective-permute-start.7 = (bf16[8,2048]{1,0:T(8,128)(2,1)S(1)}, bf16[8,2048]{1,0:T(8,128)(2,1)S(1)}, u32[]{:S(2)}, u32[]{:S(2)}) collective-permute-start(bf16[8,2048]{1,0:T(8,128)(2,1)S(1)} %get-tuple-element.69.attn_ref), channel_id=1, source_target_pairs={{0,1},{1,0},{2,3},{3,2},{4,5},{5,4},{6,7},{7,6},{8,9},{9,8},{10,11... | collective-permute-start | bytes 98312 | tf_op jit(solution)/shard_map/ppermute | solution.py:22
  26.6 3.1 %collective-permute-start.9 = (f32[2,4,1,1024]{3,2,1,0:T(1,128)S(1)}, f32[2,4,1,1024]{3,2,1,0:T(1,128)S(1)}, u32[]{:S(2)}, u32[]{:S(2)}) collective-permute-start(f32[2,4,1,1024]{3,2,1,0:T(1,128)S(1)} %get-tuple-element.75.mamba_ref), channel_id=1, source_target_pairs={{0,1},{1,0},{2,3},{3,2},{4,5},{5,4},{6,7},{7,6},{8,9},{9,8},{10,11... | collective-permute-start | bytes 98312 | tf_op jit(solution)/shard_map/ppermute | solution.py:22
  28.2 3.8 %collective-permute-start.10 = (f32[2,2,1024]{2,1,0:T(2,128)S(1)}, f32[2,2,1024]{2,1,0:T(2,128)S(1)}, u32[]{:S(2)}, u32[]{:S(2)}) collective-permute-start(f32[2,2,1024]{2,1,0:T(2,128)S(1)} %get-tuple-element.78), channel_id=1, source_target_pairs={{0,2},{2,0},{1,3},{3,1},{4,6},{6,4},{5,7},{7,5},{8,10},{10,8},{9,1... | collective-permute-start | bytes 49160 | tf_op jit(solution)/shard_map/ppermute | solution.py:22

commit v16 on v14

--- a/solution.py
+++ b/solution.py
@@ -164,7 +164,8 @@
 
 
 def attend(count, heads, q_ref, new_ref, bias_ref, pick_ref, *rest):
-    pieces, states = rest[:count], rest[count : 2 * count - 2]
+    pieces = [*rest[:2], *rest[2:count][::-1]]
+    states = rest[count : 2 * count - 2]
     outs, (kept_ref, sent_ref) = rest[2 * count - 2 : 3 * count - 2], rest[3 * count - 2 :]
     rep = lax.axis_index("rep")
     queries = query_rows(q_ref, heads)
@@ -467,8 +468,8 @@
     )(*after([out_weight], pieces[0]), step_dt, step_input, step_bc, skip_gain, a_log)
 
     beside = shift(after(states[1:2], own_weight)[0], "seq", 1)
-    *moved, own_weight = after([*moved[::-1], own_weight])
-    kv = [own_piece, *moved[::-1]]
+    *moved, own_weight = after([*moved, own_weight])
+    kv = [own_piece, moved[0], *moved[:0:-1]]
     half_shape = (heads, keep_rep, BLOCK, width)
     rows = steps * group
     *sends, kept, sent = call(

time: 31.7 us -> 33.7 us (1.063)
  starting transfers between devices: 12.9 us -> 14 us
  waiting for transfers between devices: 8.45 us -> 9.33 us
    ppermute x11, starting transfers between devices: 12.9 us -> 14 us  [shift(): return lax.ppermute(x, axis, [(i, i ^ c) for i in range(size)])]
    ppermute x11, waiting for transfers between devices: 8.45 us -> 9.33 us  [shift(): return lax.ppermute(x, axis, [(i, i ^ c) for i in range(size)])]
  transfers between devices with their start and end apart: 11 -> 11, of which waited for: 4 -> 6; matrix products, arithmetic and copies ran while one was open for 0% -> 0% of each run, Pallas kernels for 24% -> 23%
where the time goes in v16:
time: 33.7 us; the launch traced here: 33.4 us
  starting transfers between devices  14 us (42%)
  Pallas kernels  9.4 us (28%)
  waiting for transfers between devices  9.33 us (28%)
  between operations  0.69 us (2%)
    ppermute x11, starting transfers between devices, shift(): return lax.ppermute(x, axis, [(i, i ^ c) for i in range(size)])  14 us
    ppermute x11, waiting for transfers between devices, shift(): return lax.ppermute(x, axis, [(i, i ^ c) for i in range(size)])  9.33 us
    pallas_call x1, Pallas kernels, per_device(): call(functools.partial(prepare, count, split), [half_weight, half_weight,...  3.76 us
    pallas_call x1, Pallas kernels, per_device(): call(functools.partial(stage_rest, count, split), [block_shape, shape(que...  1.15 us
    pallas_call x1, Pallas kernels, per_device(): call(functools.partial(stage_blocks, count), [block_shape] * (count - 1),...  1.06 us
    pallas_call x1, Pallas kernels, per_device(): call(functools.partial(assemble, split), [shape((1, dec_heads, keep_rep,...  0.89 us
  transfers between devices with their start and end apart: 11, of which 6 were waited for; matrix products, arithmetic and copies ran while one was open for 0% of the time, Pallas kernels for 23%

profile of v16, /device:TPU:0, one launch (start us, length us, event | category | flops | bytes accessed | tf_op | source)
XLA Modules:
  0.0 33.4 jit_solution(8098765768838772333)
XLA Ops:
  0.6 1.1 %shard_map.139 = (bf16[256,256]{1,0:T(8,128)(2,1)S(1)}, bf16[256,256]{1,0:T(8,128)(2,1)S(1)}, bf16[256,256]{1,0:T(8,128)(2,1)S(1)}) custom-call(bf16[4,2,128,256]{3,2,1,0:T(8,128)(2,1)} %kv_ref.2), custom_call_target="tpu_custom_call" | custom-call | bytes 36000 | tf_op jit(solution)/shard_map/pallas_call | solution.py:421
  1.7 4.1 %collective-permute-start.1 = (bf16[256,256]{1,0:T(8,128)(2,1)S(1)}, bf16[256,256]{1,0:T(8,128)(2,1)S(1)}, u32[]{:S(2)}, u32[]{:S(2)}) collective-permute-start(bf16[256,256]{1,0:T(8,128)(2,1)S(1)} %get-tuple-element.48), channel_id=1, source_target_pairs={{0,8},{4,12},{8,0},{12,4},{1,9},{5,13},{9,1},{13,5},{2,10},{6,14},... | collective-permute-start | bytes 393224 | tf_op jit(solution)/shard_map/ppermute | solution.py:22
  5.8 1.3 %collective-permute-start.2 = (bf16[256,256]{1,0:T(8,128)(2,1)S(1)}, bf16[256,256]{1,0:T(8,128)(2,1)S(1)}, u32[]{:S(2)}, u32[]{:S(2)}) collective-permute-start(bf16[256,256]{1,0:T(8,128)(2,1)S(1)} %get-tuple-element.49), channel_id=1, source_target_pairs={{0,12},{4,8},{8,4},{12,0},{1,13},{5,9},{9,5},{13,1},{2,14},{6,10},... | collective-permute-start | bytes 393224 | tf_op jit(solution)/shard_map/ppermute | solution.py:22
  7.1 0.2 collective-permute-start
  7.4 1.2 %shard_map.140 = (bf16[256,256]{1,0:T(8,128)(2,1)S(1)}, bf16[2,1,32,128]{3,2,1,0:T(8,128)(2,1)S(1)}, bf16[2,1,4,256]{3,2,1,0:T(4,128)(2,1)S(1)}, f32[32,512]{1,0...) custom-call(bf16[4,2,128,256]{3,2,1,0:T(8,128)(2,1)} %kv_ref.2, ...), custom_call_target="tpu_custom_call" | custom-call | bytes 36000 | tf_op jit(solution)/shard_map/pallas_call | solution.py:429
  8.5 3.8 %shard_map.141 = (bf16[2048,1024]{1,0:T(8,128)(2,1)S(1)}, bf16[2048,1024]{1,0:T(8,128)(2,1)S(1)}, f32[4,2,16,1024]{3,2,1,0:T(8,128)S(1)}, f32[4,2,1,1024]{3,2,1,0:T(1,128)S(1)}) custom-call(bf16[4096,1024]{1,0:T(8,128)(2,1)} %weight_hbm, f32[2,1,8192]{2,1,0:T(1,128)} %dt_hbm.1, bf16[2,8192]{1,0:T(2,128)(2,1)} %bitcast.3, f32[2,1,2,16]{3,2,1,0:T(2,128)} %bc_hbm.1, ...), custom_call_target="tpu_custom_call" | custom-call | bytes 36000 | tf_op jit(solution)/shard_map/pallas_call | solution.py:449
  12.3 1.9 %collective-permute-start.3 = (bf16[96,256]{1,0:T(8,128)(2,1)S(1)}, bf16[96,256]{1,0:T(8,128)(2,1)S(1)}, u32[]{:S(2)}, u32[]{:S(2)}) collective-permute-start(bf16[96,256]{1,0:T(8,128)(2,1)S(1)} %get-tuple-element.62), channel_id=1, source_target_pairs={{0,4},{4,0},{8,12},{12,8},{1,5},{5,1},{9,13},{13,9},{2,6},{6,2},{1... | collective-permute-start | bytes 147464 | tf_op jit(solution)/shard_map/ppermute | solution.py:22
  14.2 1.6 %collective-permute-done.1.rest_3_ = bf16[256,256]{1,0:T(8,128)(2,1)S(1)} collective-permute-done((bf16[256,256]{1,0:T(8,128)(2,1)S(1)}, bf16[256,256]{1,0:T(8,128)(2,1)S(1)}, u32[]{:S(2)}, u32[]{:S(2)}) %collective-permute-start.1) | collective-permute-done | bytes 131104 | tf_op jit(solution)/shard_map/ppermute | solution.py:22
  15.8 0.0 collective-permute-done.2.rest_2_
  15.8 1.0 %collective-permute-done.rest_1_ = bf16[256,256]{1,0:T(8,128)(2,1)S(1)} collective-permute-done((bf16[256,256]{1,0:T(8,128)(2,1)S(1)}, bf16[256,256]{1,0:T(8,128)(2,1)S(1)}, u32[]{:S(2)}, u32[]{:S(2)}) %collective-permute-start) | collective-permute-done | bytes 131104 | tf_op jit(solution)/shard_map/ppermute | solution.py:22
  16.8 0.5 %shard_map.142 = (bf16[16,256]{1,0:T(8,128)(2,1)S(1)}, bf16[16,256]{1,0:T(8,128)(2,1)S(1)}, bf16[80,256]{1,0:T(8,128)(2,1)S(1)}, bf16[80,256]{1,0:T(8,128)(2,1)S...) custom-call(bf16[2,1,32,128]{3,2,1,0:T(8,128)(2,1)S(1)} %get-tuple-element.43.q_ref, ...), custom_call_target="tpu_custom_call" | custom-call | bytes 36000 | tf_op jit(solution)/shard_map/pallas_call | solution.py:475
  17.3 3.6 %collective-permute-start.4 = (bf16[80,256]{1,0:T(8,128)(2,1)S(1)}, bf16[80,256]{1,0:T(8,128)(2,1)S(1)}, u32[]{:S(2)}, u32[]{:S(2)}) collective-permute-start(bf16[80,256]{1,0:T(8,128)(2,1)S(1)} %get-tuple-element.64), channel_id=1, source_target_pairs={{0,8},{4,12},{8,0},{12,4},{1,9},{5,13},{9,1},{13,5},{2,10},{6,14},... | collective-permute-start | bytes 122888 | tf_op jit(solution)/shard_map/ppermute | solution.py:22
  21.0 0.4 %collective-permute-start.5 = (bf16[80,256]{1,0:T(8,128)(2,1)S(1)}, bf16[80,256]{1,0:T(8,128)(2,1)S(1)}, u32[]{:S(2)}, u32[]{:S(2)}) collective-permute-start(bf16[80,256]{1,0:T(8,128)(2,1)S(1)} %get-tuple-element.65), channel_id=1, source_target_pairs={{0,12},{4,8},{8,4},{12,0},{1,13},{5,9},{9,5},{13,1},{2,14},{6,10},... | collective-permute-start | bytes 122888 | tf_op jit(solution)/shard_map/ppermute | solution.py:22
  21.4 0.2 collective-permute-start.6
  21.6 0.0 collective-permute-done.3.beside_ref
  21.6 3.4 %collective-permute-done.6.rest_3_ = bf16[16,256]{1,0:T(8,128)(2,1)S(1)} collective-permute-done((bf16[16,256]{1,0:T(8,128)(2,1)S(1)}, bf16[16,256]{1,0:T(8,128)(2,1)S(1)}, u32[]{:S(2)}, u32[]{:S(2)}) %collective-permute-start.6) | collective-permute-done | bytes 8224 | tf_op jit(solution)/shard_map/ppermute | solution.py:22
  25.1 0.0 collective-permute-done.4.rest_1_
  25.1 1.7 %collective-permute-done.5.rest_2_ = bf16[80,256]{1,0:T(8,128)(2,1)S(1)} collective-permute-done((bf16[80,256]{1,0:T(8,128)(2,1)S(1)}, bf16[80,256]{1,0:T(8,128)(2,1)S(1)}, u32[]{:S(2)}, u32[]{:S(2)}) %collective-permute-start.5) | collective-permute-done | bytes 40992 | tf_op jit(solution)/shard_map/ppermute | solution.py:22
  26.8 0.1 shard_map.143
  26.9 0.1 collective-permute-start.8
  27.0 0.5 %collective-permute-start.7 = (bf16[8,2048]{1,0:T(8,128)(2,1)S(1)}, bf16[8,2048]{1,0:T(8,128)(2,1)S(1)}, u32[]{:S(2)}, u32[]{:S(2)}) collective-permute-start(bf16[8,2048]{1,0:T(8,128)(2,1)S(1)} %get-tuple-element.67.attn_ref), channel_id=1, source_target_pairs={{0,1},{1,0},{2,3},{3,2},{4,5},{5,4},{6,7},{7,6},{8,9},{9,8},{10,11... | collective-permute-start | bytes 98312 | tf_op jit(solution)/shard_map/ppermute | solution.py:22
  27.5 0.1 collective-permute-start.9
  27.6 0.6 %shard_map.144.acc_ref = f32[8,1024]{1,0:T(8,128)S(1)} custom-call(bf16[8,2048]{1,0:T(8,128)(2,1)S(1)} %get-tuple-element.67.attn_ref, bf16[2048,1024]{1,0:T(8,128)(2,1)S(1)} %get-tuple-element.68.weight_ref), custom_call_target="tpu_custom_call" | custom-call | bytes 25200 | tf_op jit(solution)/shard_map/pallas_call | solution.py:493
  28.2 0.2 collective-permute-done.7.attn_ref
  28.4 0.7 %shard_map.145 = (f32[2,2,1024]{2,1,0:T(2,128)S(1)}, f32[2,2,1024]{2,1,0:T(2,128)S(1)}) custom-call(f32[8,1024]{1,0:T(8,128)S(1)} %shard_map.144.acc_ref, bf16[8,2048]{1,0:T(8,128)(2,1)S(1)} %collective-permute-done.7.attn_ref, bf16[2048,1024]{1,0:T(8,128)(2,1)S(1)} %get-tuple-element.69.weight_ref), custom_call_target="tpu_custom_call" | custom-call | bytes 25200 | tf_op jit(solution)/shard_map/pallas_call | solution.py:497
  29.0 1.5 %collective-permute-start.10 = (f32[2,2,1024]{2,1,0:T(2,128)S(1)}, f32[2,2,1024]{2,1,0:T(2,128)S(1)}, u32[]{:S(2)}, u32[]{:S(2)}) collective-permute-start(f32[2,2,1024]{2,1,0:T(2,128)S(1)} %get-tuple-element.76), channel_id=1, source_target_pairs={{0,2},{2,0},{1,3},{3,1},{4,6},{6,4},{5,7},{7,5},{8,10},{10,8},{9,1... | collective-permute-start | bytes 49160 | tf_op jit(solution)/shard_map/ppermute | solution.py:22
  30.6 0.0 collective-permute-done.9.rest_0_
  30.6 0.0 collective-permute-done.8.got_ref
  30.6 0.9 %shard_map.146 = (bf16[1,4,1,128,256]{4,3,2,1,0:T(8,128)(2,1)}, f32[2,1,8192]{2,1,0:T(1,128)}) custom-call(bf16[2,1,128,256]{3,2,1,0:T(8,128)(2,1)S(1)} %get-tuple-element.71.kept_ref, bf16[2,1,128,256]{3,2,1,0:T(8,128)(2,1)S(1)} %collective-permute-done.8.got_ref, f32[2,4,1,1024]{3,2,1,0:T(1,128)S(1)} %get-tuple-element.73.mamba_ref, ...), custom_call_target="tpu_custom_call" | custom-call | bytes 36000 | tf_op jit(solution)/shard_map/pallas_call | solution.py:508
  31.5 1.3 %collective-permute-done.10.refs_1_ = f32[2,2,1024]{2,1,0:T(2,128)S(1)} collective-permute-done((f32[2,2,1024]{2,1,0:T(2,128)S(1)}, f32[2,2,1024]{2,1,0:T(2,128)S(1)}, u32[]{:S(2)}, u32[]{:S(2)}) %collective-permute-start.10) | collective-permute-done | bytes 16416 | tf_op jit(solution)/shard_map/ppermute | solution.py:22
  32.8 0.6 %shard_map.147 = bf16[2,2,1024]{2,1,0:T(2,128)(2,1)} custom-call(f32[2,2,1024]{2,1,0:T(2,128)S(1)} %get-tuple-element.70.refs_0_, f32[2,2,1024]{2,1,0:T(2,128)S(1)} %collective-permute-done.10.refs_1_), custom_call_target="tpu_custom_call" | custom-call | bytes 21600 | tf_op jit(solution)/shard_map/pallas_call | solution.py:519
Async XLA Ops:
  1.7 14.1 %collective-permute-start.1 = (bf16[256,256]{1,0:T(8,128)(2,1)S(1)}, bf16[256,256]{1,0:T(8,128)(2,1)S(1)}, u32[]{:S(2)}, u32[]{:S(2)}) collective-permute-start(bf16[256,256]{1,0:T(8,128)(2,1)S(1)} %get-tuple-element.48), channel_id=1, source_target_pairs={{0,8},{4,12},{8,0},{12,4},{1,9},{5,13},{9,1},{13,5},{2,10},{6,14},... | collective-permute-start | bytes 393224 | tf_op jit(solution)/shard_map/ppermute | solution.py:22
  5.8 10.0 %collective-permute-start.2 = (bf16[256,256]{1,0:T(8,128)(2,1)S(1)}, bf16[256,256]{1,0:T(8,128)(2,1)S(1)}, u32[]{:S(2)}, u32[]{:S(2)}) collective-permute-start(bf16[256,256]{1,0:T(8,128)(2,1)S(1)} %get-tuple-element.49), channel_id=1, source_target_pairs={{0,12},{4,8},{8,4},{12,0},{1,13},{5,9},{9,5},{13,1},{2,14},{6,10},... | collective-permute-start | bytes 393224 | tf_op jit(solution)/shard_map/ppermute | solution.py:22
  7.1 9.7 %collective-permute-start = (bf16[256,256]{1,0:T(8,128)(2,1)S(1)}, bf16[256,256]{1,0:T(8,128)(2,1)S(1)}, u32[]{:S(2)}, u32[]{:S(2)}) collective-permute-start(bf16[256,256]{1,0:T(8,128)(2,1)S(1)} %get-tuple-element.41), channel_id=1, source_target_pairs={{0,4},{4,0},{8,12},{12,8},{1,5},{5,1},{9,13},{13,9},{2,6},{6,2},{1... | collective-permute-start | bytes 393224 | tf_op jit(solution)/shard_map/ppermute | solution.py:22
  12.3 9.3 %collective-permute-start.3 = (bf16[96,256]{1,0:T(8,128)(2,1)S(1)}, bf16[96,256]{1,0:T(8,128)(2,1)S(1)}, u32[]{:S(2)}, u32[]{:S(2)}) collective-permute-start(bf16[96,256]{1,0:T(8,128)(2,1)S(1)} %get-tuple-element.62), channel_id=1, source_target_pairs={{0,4},{4,0},{8,12},{12,8},{1,5},{5,1},{9,13},{13,9},{2,6},{6,2},{1... | collective-permute-start | bytes 147464 | tf_op jit(solution)/shard_map/ppermute | solution.py:22
  17.3 7.7 %collective-permute-start.4 = (bf16[80,256]{1,0:T(8,128)(2,1)S(1)}, bf16[80,256]{1,0:T(8,128)(2,1)S(1)}, u32[]{:S(2)}, u32[]{:S(2)}) collective-permute-start(bf16[80,256]{1,0:T(8,128)(2,1)S(1)} %get-tuple-element.64), channel_id=1, source_target_pairs={{0,8},{4,12},{8,0},{12,4},{1,9},{5,13},{9,1},{13,5},{2,10},{6,14},... | collective-permute-start | bytes 122888 | tf_op jit(solution)/shard_map/ppermute | solution.py:22
  21.0 5.8 %collective-permute-start.5 = (bf16[80,256]{1,0:T(8,128)(2,1)S(1)}, bf16[80,256]{1,0:T(8,128)(2,1)S(1)}, u32[]{:S(2)}, u32[]{:S(2)}) collective-permute-start(bf16[80,256]{1,0:T(8,128)(2,1)S(1)} %get-tuple-element.65), channel_id=1, source_target_pairs={{0,12},{4,8},{8,4},{12,0},{1,13},{5,9},{9,5},{13,1},{2,14},{6,10},... | collective-permute-start | bytes 122888 | tf_op jit(solution)/shard_map/ppermute | solution.py:22
  21.4 3.7 %collective-permute-start.6 = (bf16[16,256]{1,0:T(8,128)(2,1)S(1)}, bf16[16,256]{1,0:T(8,128)(2,1)S(1)}, u32[]{:S(2)}, u32[]{:S(2)}) collective-permute-start(bf16[16,256]{1,0:T(8,128)(2,1)S(1)} %get-tuple-element.66), channel_id=1, source_target_pairs={{0,4},{4,0},{8,12},{12,8},{1,5},{5,1},{9,13},{13,9},{2,6},{6,2},{1... | collective-permute-start | bytes 24584 | tf_op jit(solution)/shard_map/ppermute | solution.py:22
  26.9 3.7 %collective-permute-start.8 = (bf16[2,1,128,256]{3,2,1,0:T(8,128)(2,1)S(1)}, bf16[2,1,128,256]{3,2,1,0:T(8,128)(2,1)S(1)}, u32[]{:S(2)}, u32[]{:S(2)}) collective-permute-start(bf16[2,1,128,256]{3,2,1,0:T(8,128)(2,1)S(1)} %get-tuple-element.74), channel_id=1, source_target_pairs={{0,1},{1,0},{2,3},{3,2},{4,5},{5,4},{6,7},{7,6},{8,9},{9,8},{10,11... | collective-permute-start | bytes 393224 | tf_op jit(solution)/shard_map/ppermute | solution.py:22
  27.0 1.4 %collective-permute-start.7 = (bf16[8,2048]{1,0:T(8,128)(2,1)S(1)}, bf16[8,2048]{1,0:T(8,128)(2,1)S(1)}, u32[]{:S(2)}, u32[]{:S(2)}) collective-permute-start(bf16[8,2048]{1,0:T(8,128)(2,1)S(1)} %get-tuple-element.67.attn_ref), channel_id=1, source_target_pairs={{0,1},{1,0},{2,3},{3,2},{4,5},{5,4},{6,7},{7,6},{8,9},{9,8},{10,11... | collective-permute-start | bytes 98312 | tf_op jit(solution)/shard_map/ppermute | solution.py:22
  27.5 3.1 %collective-permute-start.9 = (f32[2,4,1,1024]{3,2,1,0:T(1,128)S(1)}, f32[2,4,1,1024]{3,2,1,0:T(1,128)S(1)}, u32[]{:S(2)}, u32[]{:S(2)}) collective-permute-start(f32[2,4,1,1024]{3,2,1,0:T(1,128)S(1)} %get-tuple-element.73.mamba_ref), channel_id=1, source_target_pairs={{0,1},{1,0},{2,3},{3,2},{4,5},{5,4},{6,7},{7,6},{8,9},{9,8},{10,11... | collective-permute-start | bytes 98312 | tf_op jit(solution)/shard_map/ppermute | solution.py:22
  29.0 3.8 %collective-permute-start.10 = (f32[2,2,1024]{2,1,0:T(2,128)S(1)}, f32[2,2,1024]{2,1,0:T(2,128)S(1)}, u32[]{:S(2)}, u32[]{:S(2)}) collective-permute-start(f32[2,2,1024]{2,1,0:T(2,128)S(1)} %get-tuple-element.76), channel_id=1, source_target_pairs={{0,2},{2,0},{1,3},{3,1},{4,6},{6,4},{5,7},{7,5},{8,10},{10,8},{9,1... | collective-permute-start | bytes 49160 | tf_op jit(solution)/shard_map/ppermute | solution.py:22

commit v17 on v14

--- a/solution.py
+++ b/solution.py
@@ -76,14 +76,14 @@
     return state_ref.at[me ^ c]
 
 
-def stage_blocks(count, kv_ref, *rest):
+def stage_blocks(partners, kv_ref, *rest):
     outs, sems = rest[:-1], rest[-1]
     me = lax.axis_index("seq")
     copy = copier(sems)
     run_all(
         [
-            copy(kv_ref.at[me ^ c, j], outs[c - 1].at[pl.ds(j * BLOCK, BLOCK)])
-            for c in range(count - 1, 0, -1)
+            copy(kv_ref.at[me ^ c, j], outs[i].at[pl.ds(j * BLOCK, BLOCK)])
+            for i, c in enumerate(partners)
             for j in range(kv_ref.shape[1])
         ]
     )
@@ -417,13 +417,17 @@
     half = heads * group * hd
     half_weight = pltpu.VMEM((half, columns), BF)
     block_shape = shape((heads * BLOCK, width), BF)
-    pieces = call(
-        functools.partial(stage_blocks, count),
-        [block_shape] * (count - 1),
-        [HB],
-        [VM] * (count - 1),
-        [DMA(((count - 1) * heads,))],
-    )(prefill_kv)
+    pieces = {}
+    for partners in ([count - 1], range(count - 2, 0, -1)):
+        staged = call(
+            functools.partial(stage_blocks, partners),
+            [block_shape] * len(partners),
+            [HB],
+            [VM] * len(partners),
+            [DMA((len(partners) * heads,))],
+        )(prefill_kv)
+        pieces.update(zip(partners, staged))
+    pieces = [pieces[c] for c in range(1, count)]
     moved = [shift(pieces[c - 1], "seq", c) for c in range(count - 1, 0, -1)][::-1]
     own_piece, q_near, new_near, bias, picks, *states = call(
         functools.partial(stage_rest, count, split),

time: 31.7 us -> 31.6 us (level)
  waiting for transfers between devices: 8.45 us -> 7.33 us
  Pallas kernels: 9.4 us -> 10.2 us
    ppermute x11, waiting for transfers between devices: 8.45 us -> 7.33 us  [shift(): return lax.ppermute(x, axis, [(i, i ^ c) for i in range(size)])]
    pallas_call x1 -> x2, Pallas kernels: 1.06 us -> 1.87 us  [per_device(): call(functools.partial(stage_blocks, partners), [block_shape] * len(partn...]
  transfers between devices with their start and end apart: 11 -> 11, of which waited for: 4 -> 4; matrix products, arithmetic and copies ran while one was open for 0% -> 0% of each run, Pallas kernels for 24% -> 27%
where the time goes in v17:
time: 31.6 us; the launch traced here: 31.3 us
  starting transfers between devices  13.1 us (41%)
  Pallas kernels  10.2 us (32%)
  waiting for transfers between devices  7.33 us (23%)
  between operations  0.72 us (2%)
    ppermute x11, starting transfers between devices, shift(): return lax.ppermute(x, axis, [(i, i ^ c) for i in range(size)])  13.1 us
    ppermute x11, waiting for transfers between devices, shift(): return lax.ppermute(x, axis, [(i, i ^ c) for i in range(size)])  7.33 us
    pallas_call x1, Pallas kernels, per_device(): call(functools.partial(prepare, count, split), [half_weight, half_weight,...  3.76 us
    pallas_call x2, Pallas kernels, per_device(): call(functools.partial(stage_blocks, partners), [block_shape] * len(partn...  1.87 us
    pallas_call x1, Pallas kernels, per_device(): call(functools.partial(stage_rest, count, split), [block_shape, shape(que...  1.15 us
    pallas_call x1, Pallas kernels, per_device(): call(functools.partial(assemble, split), [shape((1, dec_heads, keep_rep,...  0.89 us
    pallas_call x1, Pallas kernels, per_device(): call(functools.partial(project_other, heads_count, count), [shape((steps,...  0.67 us
    pallas_call x1, Pallas kernels, per_device(): call(project_own, shape((steps * count, columns), F32), [VM, VM], VM, us=...  0.64 us
  transfers between devices with their start and end apart: 11, of which 4 were waited for; matrix products, arithmetic and copies ran while one was open for 0% of the time, Pallas kernels for 27%

profile of v17, /device:TPU:0, one launch (start us, length us, event | category | flops | bytes accessed | tf_op | source)
XLA Modules:
  0.0 31.3 jit_solution(4952850328728700707)
XLA Ops:
  0.6 0.9 %shard_map.141 = bf16[256,256]{1,0:T(8,128)(2,1)S(1)} custom-call(bf16[4,2,128,256]{3,2,1,0:T(8,128)(2,1)} %kv_ref.4), custom_call_target="tpu_custom_call" | custom-call | bytes 36000 | tf_op jit(solution)/shard_map/pallas_call | solution.py:422
  1.5 5.1 %collective-permute-start = (bf16[256,256]{1,0:T(8,128)(2,1)S(1)}, bf16[256,256]{1,0:T(8,128)(2,1)S(1)}, u32[]{:S(2)}, u32[]{:S(2)}) collective-permute-start(bf16[256,256]{1,0:T(8,128)(2,1)S(1)} %shard_map.141), channel_id=1, source_target_pairs={{0,12},{4,8},{8,4},{12,0},{1,13},{5,9},{9,5},{13,1},{2,14},{6,10},... | collective-permute-start | bytes 393224 | tf_op jit(solution)/shard_map/ppermute | solution.py:22
  6.7 1.0 %shard_map.139 = (bf16[256,256]{1,0:T(8,128)(2,1)S(1)}, bf16[256,256]{1,0:T(8,128)(2,1)S(1)}) custom-call(bf16[4,2,128,256]{3,2,1,0:T(8,128)(2,1)} %kv_ref.4), custom_call_target="tpu_custom_call" | custom-call | bytes 36000 | tf_op jit(solution)/shard_map/pallas_call | solution.py:422
  7.6 0.1 collective-permute-start.1
  7.7 0.6 %collective-permute-start.2 = (bf16[256,256]{1,0:T(8,128)(2,1)S(1)}, bf16[256,256]{1,0:T(8,128)(2,1)S(1)}, u32[]{:S(2)}, u32[]{:S(2)}) collective-permute-start(bf16[256,256]{1,0:T(8,128)(2,1)S(1)} %get-tuple-element.40), channel_id=1, source_target_pairs={{0,4},{4,0},{8,12},{12,8},{1,5},{5,1},{9,13},{13,9},{2,6},{6,2},{1... | collective-permute-start | bytes 393224 | tf_op jit(solution)/shard_map/ppermute | solution.py:22
  8.3 1.2 %shard_map.140 = (bf16[256,256]{1,0:T(8,128)(2,1)S(1)}, bf16[2,1,32,128]{3,2,1,0:T(8,128)(2,1)S(1)}, bf16[2,1,4,256]{3,2,1,0:T(4,128)(2,1)S(1)}, f32[32,512]{1,0...) custom-call(bf16[4,2,128,256]{3,2,1,0:T(8,128)(2,1)} %kv_ref.4, ...), custom_call_target="tpu_custom_call" | custom-call | bytes 36000 | tf_op jit(solution)/shard_map/pallas_call | solution.py:432
  9.4 3.8 %shard_map.142 = (bf16[2048,1024]{1,0:T(8,128)(2,1)S(1)}, bf16[2048,1024]{1,0:T(8,128)(2,1)S(1)}, f32[4,2,16,1024]{3,2,1,0:T(8,128)S(1)}, f32[4,2,1,1024]{3,2,1,0:T(1,128)S(1)}) custom-call(bf16[4096,1024]{1,0:T(8,128)(2,1)} %weight_hbm, f32[2,1,8192]{2,1,0:T(1,128)} %dt_hbm.1, bf16[2,8192]{1,0:T(2,128)(2,1)} %bitcast.3, f32[2,1,2,16]{3,2,1,0:T(2,128)} %bc_hbm.1, ...), custom_call_target="tpu_custom_call" | custom-call | bytes 36000 | tf_op jit(solution)/shard_map/pallas_call | solution.py:452
  13.2 1.6 %collective-permute-start.3 = (bf16[96,256]{1,0:T(8,128)(2,1)S(1)}, bf16[96,256]{1,0:T(8,128)(2,1)S(1)}, u32[]{:S(2)}, u32[]{:S(2)}) collective-permute-start(bf16[96,256]{1,0:T(8,128)(2,1)S(1)} %get-tuple-element.60), channel_id=1, source_target_pairs={{0,4},{4,0},{8,12},{12,8},{1,5},{5,1},{9,13},{13,9},{2,6},{6,2},{1... | collective-permute-start | bytes 147464 | tf_op jit(solution)/shard_map/ppermute | solution.py:22
  14.8 0.0 collective-permute-done.rest_3_
  14.8 3.0 %collective-permute-done.1.rest_2_ = bf16[256,256]{1,0:T(8,128)(2,1)S(1)} collective-permute-done((bf16[256,256]{1,0:T(8,128)(2,1)S(1)}, bf16[256,256]{1,0:T(8,128)(2,1)S(1)}, u32[]{:S(2)}, u32[]{:S(2)}) %collective-permute-start.1) | collective-permute-done | bytes 131104 | tf_op jit(solution)/shard_map/ppermute | solution.py:22
  17.8 0.0 collective-permute-done.2.rest_1_
  17.8 0.5 %shard_map.143 = (bf16[16,256]{1,0:T(8,128)(2,1)S(1)}, bf16[16,256]{1,0:T(8,128)(2,1)S(1)}, bf16[80,256]{1,0:T(8,128)(2,1)S(1)}, bf16[80,256]{1,0:T(8,128)(2,1)S...) custom-call(bf16[2,1,32,128]{3,2,1,0:T(8,128)(2,1)S(1)} %get-tuple-element.42.q_ref, ...), custom_call_target="tpu_custom_call" | custom-call | bytes 36000 | tf_op jit(solution)/shard_map/pallas_call | solution.py:478
  18.3 0.1 collective-permute-start.4
  18.4 2.6 %collective-permute-start.5 = (bf16[80,256]{1,0:T(8,128)(2,1)S(1)}, bf16[80,256]{1,0:T(8,128)(2,1)S(1)}, u32[]{:S(2)}, u32[]{:S(2)}) collective-permute-start(bf16[80,256]{1,0:T(8,128)(2,1)S(1)} %get-tuple-element.63), channel_id=1, source_target_pairs={{0,12},{4,8},{8,4},{12,0},{1,13},{5,9},{9,5},{13,1},{2,14},{6,10},... | collective-permute-start | bytes 122888 | tf_op jit(solution)/shard_map/ppermute | solution.py:22
  21.0 0.9 %collective-permute-start.6 = (bf16[16,256]{1,0:T(8,128)(2,1)S(1)}, bf16[16,256]{1,0:T(8,128)(2,1)S(1)}, u32[]{:S(2)}, u32[]{:S(2)}) collective-permute-start(bf16[16,256]{1,0:T(8,128)(2,1)S(1)} %get-tuple-element.64), channel_id=1, source_target_pairs={{0,4},{4,0},{8,12},{12,8},{1,5},{5,1},{9,13},{13,9},{2,6},{6,2},{1... | collective-permute-start | bytes 24584 | tf_op jit(solution)/shard_map/ppermute | solution.py:22
  21.9 0.0 collective-permute-done.3.beside_ref
  21.9 2.8 %collective-permute-done.6.rest_3_ = bf16[16,256]{1,0:T(8,128)(2,1)S(1)} collective-permute-done((bf16[16,256]{1,0:T(8,128)(2,1)S(1)}, bf16[16,256]{1,0:T(8,128)(2,1)S(1)}, u32[]{:S(2)}, u32[]{:S(2)}) %collective-permute-start.6) | collective-permute-done | bytes 8224 | tf_op jit(solution)/shard_map/ppermute | solution.py:22
  24.7 0.0 collective-permute-done.4.rest_1_
  24.7 0.0 collective-permute-done.5.rest_2_
  24.7 0.1 shard_map.144
  24.8 0.1 collective-permute-start.8
  24.9 0.5 %collective-permute-start.7 = (bf16[8,2048]{1,0:T(8,128)(2,1)S(1)}, bf16[8,2048]{1,0:T(8,128)(2,1)S(1)}, u32[]{:S(2)}, u32[]{:S(2)}) collective-permute-start(bf16[8,2048]{1,0:T(8,128)(2,1)S(1)} %get-tuple-element.65.attn_ref), channel_id=1, source_target_pairs={{0,1},{1,0},{2,3},{3,2},{4,5},{5,4},{6,7},{7,6},{8,9},{9,8},{10,11... | collective-permute-start | bytes 98312 | tf_op jit(solution)/shard_map/ppermute | solution.py:22
  25.4 0.1 collective-permute-start.9
  25.4 0.6 %shard_map.145.acc_ref = f32[8,1024]{1,0:T(8,128)S(1)} custom-call(bf16[8,2048]{1,0:T(8,128)(2,1)S(1)} %get-tuple-element.65.attn_ref, bf16[2048,1024]{1,0:T(8,128)(2,1)S(1)} %get-tuple-element.66.weight_ref), custom_call_target="tpu_custom_call" | custom-call | bytes 25200 | tf_op jit(solution)/shard_map/pallas_call | solution.py:496
  26.1 0.2 collective-permute-done.7.attn_ref
  26.3 0.7 %shard_map.146 = (f32[2,2,1024]{2,1,0:T(2,128)S(1)}, f32[2,2,1024]{2,1,0:T(2,128)S(1)}) custom-call(f32[8,1024]{1,0:T(8,128)S(1)} %shard_map.145.acc_ref, bf16[8,2048]{1,0:T(8,128)(2,1)S(1)} %collective-permute-done.7.attn_ref, bf16[2048,1024]{1,0:T(8,128)(2,1)S(1)} %get-tuple-element.67.weight_ref), custom_call_target="tpu_custom_call" | custom-call | bytes 25200 | tf_op jit(solution)/shard_map/pallas_call | solution.py:500
  26.9 1.5 %collective-permute-start.10 = (f32[2,2,1024]{2,1,0:T(2,128)S(1)}, f32[2,2,1024]{2,1,0:T(2,128)S(1)}, u32[]{:S(2)}, u32[]{:S(2)}) collective-permute-start(f32[2,2,1024]{2,1,0:T(2,128)S(1)} %get-tuple-element.74), channel_id=1, source_target_pairs={{0,2},{2,0},{1,3},{3,1},{4,6},{6,4},{5,7},{7,5},{8,10},{10,8},{9,1... | collective-permute-start | bytes 49160 | tf_op jit(solution)/shard_map/ppermute | solution.py:22
  28.5 0.0 collective-permute-done.9.rest_0_
  28.5 0.0 collective-permute-done.8.got_ref
  28.5 0.9 %shard_map.147 = (bf16[1,4,1,128,256]{4,3,2,1,0:T(8,128)(2,1)}, f32[2,1,8192]{2,1,0:T(1,128)}) custom-call(bf16[2,1,128,256]{3,2,1,0:T(8,128)(2,1)S(1)} %get-tuple-element.69.kept_ref, bf16[2,1,128,256]{3,2,1,0:T(8,128)(2,1)S(1)} %collective-permute-done.8.got_ref, f32[2,4,1,1024]{3,2,1,0:T(1,128)S(1)} %get-tuple-element.71.mamba_ref, ...), custom_call_target="tpu_custom_call" | custom-call | bytes 36000 | tf_op jit(solution)/shard_map/pallas_call | solution.py:511
  29.4 1.3 %collective-permute-done.10.refs_1_ = f32[2,2,1024]{2,1,0:T(2,128)S(1)} collective-permute-done((f32[2,2,1024]{2,1,0:T(2,128)S(1)}, f32[2,2,1024]{2,1,0:T(2,128)S(1)}, u32[]{:S(2)}, u32[]{:S(2)}) %collective-permute-start.10) | collective-permute-done | bytes 16416 | tf_op jit(solution)/shard_map/ppermute | solution.py:22
  30.7 0.6 %shard_map.148 = bf16[2,2,1024]{2,1,0:T(2,128)(2,1)} custom-call(f32[2,2,1024]{2,1,0:T(2,128)S(1)} %get-tuple-element.68.refs_0_, f32[2,2,1024]{2,1,0:T(2,128)S(1)} %collective-permute-done.10.refs_1_), custom_call_target="tpu_custom_call" | custom-call | bytes 21600 | tf_op jit(solution)/shard_map/pallas_call | solution.py:522
Async XLA Ops:
  1.5 13.3 %collective-permute-start = (bf16[256,256]{1,0:T(8,128)(2,1)S(1)}, bf16[256,256]{1,0:T(8,128)(2,1)S(1)}, u32[]{:S(2)}, u32[]{:S(2)}) collective-permute-start(bf16[256,256]{1,0:T(8,128)(2,1)S(1)} %shard_map.141), channel_id=1, source_target_pairs={{0,12},{4,8},{8,4},{12,0},{1,13},{5,9},{9,5},{13,1},{2,14},{6,10},... | collective-permute-start | bytes 393224 | tf_op jit(solution)/shard_map/ppermute | solution.py:22
  7.6 10.2 %collective-permute-start.1 = (bf16[256,256]{1,0:T(8,128)(2,1)S(1)}, bf16[256,256]{1,0:T(8,128)(2,1)S(1)}, u32[]{:S(2)}, u32[]{:S(2)}) collective-permute-start(bf16[256,256]{1,0:T(8,128)(2,1)S(1)} %get-tuple-element.47), channel_id=1, source_target_pairs={{0,8},{4,12},{8,0},{12,4},{1,9},{5,13},{9,1},{13,5},{2,10},{6,14},... | collective-permute-start | bytes 393224 | tf_op jit(solution)/shard_map/ppermute | solution.py:22
  7.7 10.1 %collective-permute-start.2 = (bf16[256,256]{1,0:T(8,128)(2,1)S(1)}, bf16[256,256]{1,0:T(8,128)(2,1)S(1)}, u32[]{:S(2)}, u32[]{:S(2)}) collective-permute-start(bf16[256,256]{1,0:T(8,128)(2,1)S(1)} %get-tuple-element.40), channel_id=1, source_target_pairs={{0,4},{4,0},{8,12},{12,8},{1,5},{5,1},{9,13},{13,9},{2,6},{6,2},{1... | collective-permute-start | bytes 393224 | tf_op jit(solution)/shard_map/ppermute | solution.py:22
  13.2 8.7 %collective-permute-start.3 = (bf16[96,256]{1,0:T(8,128)(2,1)S(1)}, bf16[96,256]{1,0:T(8,128)(2,1)S(1)}, u32[]{:S(2)}, u32[]{:S(2)}) collective-permute-start(bf16[96,256]{1,0:T(8,128)(2,1)S(1)} %get-tuple-element.60), channel_id=1, source_target_pairs={{0,4},{4,0},{8,12},{12,8},{1,5},{5,1},{9,13},{13,9},{2,6},{6,2},{1... | collective-permute-start | bytes 147464 | tf_op jit(solution)/shard_map/ppermute | solution.py:22
  18.3 6.3 %collective-permute-start.4 = (bf16[80,256]{1,0:T(8,128)(2,1)S(1)}, bf16[80,256]{1,0:T(8,128)(2,1)S(1)}, u32[]{:S(2)}, u32[]{:S(2)}) collective-permute-start(bf16[80,256]{1,0:T(8,128)(2,1)S(1)} %get-tuple-element.62), channel_id=1, source_target_pairs={{0,8},{4,12},{8,0},{12,4},{1,9},{5,13},{9,1},{13,5},{2,10},{6,14},... | collective-permute-start | bytes 122888 | tf_op jit(solution)/shard_map/ppermute | solution.py:22
  18.4 6.2 %collective-permute-start.5 = (bf16[80,256]{1,0:T(8,128)(2,1)S(1)}, bf16[80,256]{1,0:T(8,128)(2,1)S(1)}, u32[]{:S(2)}, u32[]{:S(2)}) collective-permute-start(bf16[80,256]{1,0:T(8,128)(2,1)S(1)} %get-tuple-element.63), channel_id=1, source_target_pairs={{0,12},{4,8},{8,4},{12,0},{1,13},{5,9},{9,5},{13,1},{2,14},{6,10},... | collective-permute-start | bytes 122888 | tf_op jit(solution)/shard_map/ppermute | solution.py:22
  21.0 3.7 %collective-permute-start.6 = (bf16[16,256]{1,0:T(8,128)(2,1)S(1)}, bf16[16,256]{1,0:T(8,128)(2,1)S(1)}, u32[]{:S(2)}, u32[]{:S(2)}) collective-permute-start(bf16[16,256]{1,0:T(8,128)(2,1)S(1)} %get-tuple-element.64), channel_id=1, source_target_pairs={{0,4},{4,0},{8,12},{12,8},{1,5},{5,1},{9,13},{13,9},{2,6},{6,2},{1... | collective-permute-start | bytes 24584 | tf_op jit(solution)/shard_map/ppermute | solution.py:22
  24.8 3.7 %collective-permute-start.8 = (bf16[2,1,128,256]{3,2,1,0:T(8,128)(2,1)S(1)}, bf16[2,1,128,256]{3,2,1,0:T(8,128)(2,1)S(1)}, u32[]{:S(2)}, u32[]{:S(2)}) collective-permute-start(bf16[2,1,128,256]{3,2,1,0:T(8,128)(2,1)S(1)} %get-tuple-element.72), channel_id=1, source_target_pairs={{0,1},{1,0},{2,3},{3,2},{4,5},{5,4},{6,7},{7,6},{8,9},{9,8},{10,11... | collective-permute-start | bytes 393224 | tf_op jit(solution)/shard_map/ppermute | solution.py:22
  24.9 1.4 %collective-permute-start.7 = (bf16[8,2048]{1,0:T(8,128)(2,1)S(1)}, bf16[8,2048]{1,0:T(8,128)(2,1)S(1)}, u32[]{:S(2)}, u32[]{:S(2)}) collective-permute-start(bf16[8,2048]{1,0:T(8,128)(2,1)S(1)} %get-tuple-element.65.attn_ref), channel_id=1, source_target_pairs={{0,1},{1,0},{2,3},{3,2},{4,5},{5,4},{6,7},{7,6},{8,9},{9,8},{10,11... | collective-permute-start | bytes 98312 | tf_op jit(solution)/shard_map/ppermute | solution.py:22
  25.4 3.1 %collective-permute-start.9 = (f32[2,4,1,1024]{3,2,1,0:T(1,128)S(1)}, f32[2,4,1,1024]{3,2,1,0:T(1,128)S(1)}, u32[]{:S(2)}, u32[]{:S(2)}) collective-permute-start(f32[2,4,1,1024]{3,2,1,0:T(1,128)S(1)} %get-tuple-element.71.mamba_ref), channel_id=1, source_target_pairs={{0,1},{1,0},{2,3},{3,2},{4,5},{5,4},{6,7},{7,6},{8,9},{9,8},{10,11... | collective-permute-start | bytes 98312 | tf_op jit(solution)/shard_map/ppermute | solution.py:22
  26.9 3.8 %collective-permute-start.10 = (f32[2,2,1024]{2,1,0:T(2,128)S(1)}, f32[2,2,1024]{2,1,0:T(2,128)S(1)}, u32[]{:S(2)}, u32[]{:S(2)}) collective-permute-start(f32[2,2,1024]{2,1,0:T(2,128)S(1)} %get-tuple-element.74), channel_id=1, source_target_pairs={{0,2},{2,0},{1,3},{3,1},{4,6},{6,4},{5,7},{7,5},{8,10},{10,8},{9,1... | collective-permute-start | bytes 49160 | tf_op jit(solution)/shard_map/ppermute | solution.py:22

commit v18 on v17

--- a/solution.py
+++ b/solution.py
@@ -428,7 +428,7 @@
         )(prefill_kv)
         pieces.update(zip(partners, staged))
     pieces = [pieces[c] for c in range(1, count)]
-    moved = [shift(pieces[c - 1], "seq", c) for c in range(count - 1, 0, -1)][::-1]
+    moved = [shift(pieces[c - 1], "seq", c) for c in range(count - 1, 1, -1)][::-1]
     own_piece, q_near, new_near, bias, picks, *states = call(
         functools.partial(stage_rest, count, split),
         [
@@ -470,6 +470,7 @@
         ],
     )(*after([out_weight], pieces[0]), step_dt, step_input, step_bc, skip_gain, a_log)
 
+    moved = [shift(after(pieces[:1], own_weight)[0], "seq", 1), *moved]
     beside = shift(after(states[1:2], own_weight)[0], "seq", 1)
     *moved, own_weight = after([*moved[::-1], own_weight])
     kv = [own_piece, *moved[::-1]]

time: 31.6 us -> 33.6 us (1.063)
  waiting for transfers between devices: 7.33 us -> 9.38 us
    ppermute x11, waiting for transfers between devices: 7.33 us -> 9.38 us  [shift(): return lax.ppermute(x, axis, [(i, i ^ c) for i in range(size)])]
  transfers between devices with their start and end apart: 11 -> 11, of which waited for: 4 -> 5; matrix products, arithmetic and copies ran while one was open for 0% -> 0% of each run, Pallas kernels for 27% -> 26%
where the time goes in v18:
time: 33.6 us; the launch traced here: 33.4 us
  starting transfers between devices  13.1 us (39%)
  Pallas kernels  10.2 us (30%)
  waiting for transfers between devices  9.38 us (28%)
  between operations  0.71 us (2%)
    ppermute x11, starting transfers between devices, shift(): return lax.ppermute(x, axis, [(i, i ^ c) for i in range(size)])  13.1 us
    ppermute x11, waiting for transfers between devices, shift(): return lax.ppermute(x, axis, [(i, i ^ c) for i in range(size)])  9.38 us
    pallas_call x1, Pallas kernels, per_device(): call(functools.partial(prepare, count, split), [half_weight, half_weight,...  3.76 us
    pallas_call x2, Pallas kernels, per_device(): call(functools.partial(stage_blocks, partners), [block_shape] * len(partn...  1.87 us
    pallas_call x1, Pallas kernels, per_device(): call(functools.partial(stage_rest, count, split), [block_shape, shape(que...  1.15 us
    pallas_call x1, Pallas kernels, per_device(): call(functools.partial(assemble, split), [shape((1, dec_heads, keep_rep,...  0.89 us
  transfers between devices with their start and end apart: 11, of which 5 were waited for; matrix products, arithmetic and copies ran while one was open for 0% of the time, Pallas kernels for 26%

profile of v18, /device:TPU:0, one launch (start us, length us, event | category | flops | bytes accessed | tf_op | source)
XLA Modules:
  0.0 33.4 jit_solution(11095852608764373439)
XLA Ops:
  0.6 0.9 %shard_map.141 = bf16[256,256]{1,0:T(8,128)(2,1)S(1)} custom-call(bf16[4,2,128,256]{3,2,1,0:T(8,128)(2,1)} %kv_ref.4), custom_call_target="tpu_custom_call" | custom-call | bytes 36000 | tf_op jit(solution)/shard_map/pallas_call | solution.py:422
  1.5 5.1 %collective-permute-start = (bf16[256,256]{1,0:T(8,128)(2,1)S(1)}, bf16[256,256]{1,0:T(8,128)(2,1)S(1)}, u32[]{:S(2)}, u32[]{:S(2)}) collective-permute-start(bf16[256,256]{1,0:T(8,128)(2,1)S(1)} %shard_map.141), channel_id=1, source_target_pairs={{0,12},{4,8},{8,4},{12,0},{1,13},{5,9},{9,5},{13,1},{2,14},{6,10},... | collective-permute-start | bytes 393224 | tf_op jit(solution)/shard_map/ppermute | solution.py:22
  6.7 1.0 %shard_map.139 = (bf16[256,256]{1,0:T(8,128)(2,1)S(1)}, bf16[256,256]{1,0:T(8,128)(2,1)S(1)}) custom-call(bf16[4,2,128,256]{3,2,1,0:T(8,128)(2,1)} %kv_ref.4), custom_call_target="tpu_custom_call" | custom-call | bytes 36000 | tf_op jit(solution)/shard_map/pallas_call | solution.py:422
  7.6 0.1 collective-permute-start.1
  7.7 3.8 %shard_map.142 = (bf16[2048,1024]{1,0:T(8,128)(2,1)S(1)}, bf16[2048,1024]{1,0:T(8,128)(2,1)S(1)}, f32[4,2,16,1024]{3,2,1,0:T(8,128)S(1)}, f32[4,2,1,1024]{3,2,1,0:T(1,128)S(1)}) custom-call(bf16[4096,1024]{1,0:T(8,128)(2,1)} %weight_hbm, f32[2,1,8192]{2,1,0:T(1,128)} %dt_hbm.1, bf16[2,8192]{1,0:T(2,128)(2,1)} %bitcast.3, f32[2,1,2,16]{3,2,1,0:T(2,128)} %bc_hbm.1, ...), custom_call_target="tpu_custom_call" | custom-call | bytes 36000 | tf_op jit(solution)/shard_map/pallas_call | solution.py:452
  11.5 0.6 %collective-permute-start.2 = (bf16[256,256]{1,0:T(8,128)(2,1)S(1)}, bf16[256,256]{1,0:T(8,128)(2,1)S(1)}, u32[]{:S(2)}, u32[]{:S(2)}) collective-permute-start(bf16[256,256]{1,0:T(8,128)(2,1)S(1)} %get-tuple-element.51), channel_id=1, source_target_pairs={{0,4},{4,0},{8,12},{12,8},{1,5},{5,1},{9,13},{13,9},{2,6},{6,2},{1... | collective-permute-start | bytes 393224 | tf_op jit(solution)/shard_map/ppermute | solution.py:22
  12.1 1.2 %shard_map.140 = (bf16[256,256]{1,0:T(8,128)(2,1)S(1)}, bf16[2,1,32,128]{3,2,1,0:T(8,128)(2,1)S(1)}, bf16[2,1,4,256]{3,2,1,0:T(4,128)(2,1)S(1)}, f32[32,512]{1,0...) custom-call(bf16[4,2,128,256]{3,2,1,0:T(8,128)(2,1)} %kv_ref.4, ...), custom_call_target="tpu_custom_call" | custom-call | bytes 36000 | tf_op jit(solution)/shard_map/pallas_call | solution.py:432
  13.3 1.5 %collective-permute-start.3 = (bf16[96,256]{1,0:T(8,128)(2,1)S(1)}, bf16[96,256]{1,0:T(8,128)(2,1)S(1)}, u32[]{:S(2)}, u32[]{:S(2)}) collective-permute-start(bf16[96,256]{1,0:T(8,128)(2,1)S(1)} %get-tuple-element.62), channel_id=1, source_target_pairs={{0,4},{4,0},{8,12},{12,8},{1,5},{5,1},{9,13},{13,9},{2,6},{6,2},{1... | collective-permute-start | bytes 147464 | tf_op jit(solution)/shard_map/ppermute | solution.py:22
  14.8 0.0 collective-permute-done.rest_3_
  14.8 3.0 %collective-permute-done.1.rest_2_ = bf16[256,256]{1,0:T(8,128)(2,1)S(1)} collective-permute-done((bf16[256,256]{1,0:T(8,128)(2,1)S(1)}, bf16[256,256]{1,0:T(8,128)(2,1)S(1)}, u32[]{:S(2)}, u32[]{:S(2)}) %collective-permute-start.1) | collective-permute-done | bytes 131104 | tf_op jit(solution)/shard_map/ppermute | solution.py:22
  17.8 2.0 %collective-permute-done.2.rest_1_ = bf16[256,256]{1,0:T(8,128)(2,1)S(1)} collective-permute-done((bf16[256,256]{1,0:T(8,128)(2,1)S(1)}, bf16[256,256]{1,0:T(8,128)(2,1)S(1)}, u32[]{:S(2)}, u32[]{:S(2)}) %collective-permute-start.2) | collective-permute-done | bytes 131104 | tf_op jit(solution)/shard_map/ppermute | solution.py:22
  19.8 0.5 %shard_map.143 = (bf16[16,256]{1,0:T(8,128)(2,1)S(1)}, bf16[16,256]{1,0:T(8,128)(2,1)S(1)}, bf16[80,256]{1,0:T(8,128)(2,1)S(1)}, bf16[80,256]{1,0:T(8,128)(2,1)S...) custom-call(bf16[2,1,32,128]{3,2,1,0:T(8,128)(2,1)S(1)} %get-tuple-element.43.q_ref, ...), custom_call_target="tpu_custom_call" | custom-call | bytes 36000 | tf_op jit(solution)/shard_map/pallas_call | solution.py:479
  20.3 0.5 %collective-permute-start.4 = (bf16[80,256]{1,0:T(8,128)(2,1)S(1)}, bf16[80,256]{1,0:T(8,128)(2,1)S(1)}, u32[]{:S(2)}, u32[]{:S(2)}) collective-permute-start(bf16[80,256]{1,0:T(8,128)(2,1)S(1)} %get-tuple-element.64), channel_id=1, source_target_pairs={{0,8},{4,12},{8,0},{12,4},{1,9},{5,13},{9,1},{13,5},{2,10},{6,14},... | collective-permute-start | bytes 122888 | tf_op jit(solution)/shard_map/ppermute | solution.py:22
  20.8 2.0 %collective-permute-start.5 = (bf16[80,256]{1,0:T(8,128)(2,1)S(1)}, bf16[80,256]{1,0:T(8,128)(2,1)S(1)}, u32[]{:S(2)}, u32[]{:S(2)}) collective-permute-start(bf16[80,256]{1,0:T(8,128)(2,1)S(1)} %get-tuple-element.65), channel_id=1, source_target_pairs={{0,12},{4,8},{8,4},{12,0},{1,13},{5,9},{9,5},{13,1},{2,14},{6,10},... | collective-permute-start | bytes 122888 | tf_op jit(solution)/shard_map/ppermute | solution.py:22
  22.8 1.1 %collective-permute-start.6 = (bf16[16,256]{1,0:T(8,128)(2,1)S(1)}, bf16[16,256]{1,0:T(8,128)(2,1)S(1)}, u32[]{:S(2)}, u32[]{:S(2)}) collective-permute-start(bf16[16,256]{1,0:T(8,128)(2,1)S(1)} %get-tuple-element.66), channel_id=1, source_target_pairs={{0,4},{4,0},{8,12},{12,8},{1,5},{5,1},{9,13},{13,9},{2,6},{6,2},{1... | collective-permute-start | bytes 24584 | tf_op jit(solution)/shard_map/ppermute | solution.py:22
  23.9 0.0 collective-permute-done.3.beside_ref
  23.9 2.8 %collective-permute-done.6.rest_3_ = bf16[16,256]{1,0:T(8,128)(2,1)S(1)} collective-permute-done((bf16[16,256]{1,0:T(8,128)(2,1)S(1)}, bf16[16,256]{1,0:T(8,128)(2,1)S(1)}, u32[]{:S(2)}, u32[]{:S(2)}) %collective-permute-start.6) | collective-permute-done | bytes 8224 | tf_op jit(solution)/shard_map/ppermute | solution.py:22
  26.7 0.0 collective-permute-done.4.rest_1_
  26.7 0.0 collective-permute-done.5.rest_2_
  26.7 0.1 shard_map.144
  26.8 0.1 collective-permute-start.8
  26.9 0.5 %collective-permute-start.7 = (bf16[8,2048]{1,0:T(8,128)(2,1)S(1)}, bf16[8,2048]{1,0:T(8,128)(2,1)S(1)}, u32[]{:S(2)}, u32[]{:S(2)}) collective-permute-start(bf16[8,2048]{1,0:T(8,128)(2,1)S(1)} %get-tuple-element.67.attn_ref), channel_id=1, source_target_pairs={{0,1},{1,0},{2,3},{3,2},{4,5},{5,4},{6,7},{7,6},{8,9},{9,8},{10,11... | collective-permute-start | bytes 98312 | tf_op jit(solution)/shard_map/ppermute | solution.py:22
  27.4 0.1 collective-permute-start.9
  27.5 0.6 %shard_map.145.acc_ref = f32[8,1024]{1,0:T(8,128)S(1)} custom-call(bf16[8,2048]{1,0:T(8,128)(2,1)S(1)} %get-tuple-element.67.attn_ref, bf16[2048,1024]{1,0:T(8,128)(2,1)S(1)} %get-tuple-element.68.weight_ref), custom_call_target="tpu_custom_call" | custom-call | bytes 25200 | tf_op jit(solution)/shard_map/pallas_call | solution.py:497
  28.1 0.2 collective-permute-done.7.attn_ref
  28.3 0.7 %shard_map.146 = (f32[2,2,1024]{2,1,0:T(2,128)S(1)}, f32[2,2,1024]{2,1,0:T(2,128)S(1)}) custom-call(f32[8,1024]{1,0:T(8,128)S(1)} %shard_map.145.acc_ref, bf16[8,2048]{1,0:T(8,128)(2,1)S(1)} %collective-permute-done.7.attn_ref, bf16[2048,1024]{1,0:T(8,128)(2,1)S(1)} %get-tuple-element.69.weight_ref), custom_call_target="tpu_custom_call" | custom-call | bytes 25200 | tf_op jit(solution)/shard_map/pallas_call | solution.py:501
  29.0 1.5 %collective-permute-start.10 = (f32[2,2,1024]{2,1,0:T(2,128)S(1)}, f32[2,2,1024]{2,1,0:T(2,128)S(1)}, u32[]{:S(2)}, u32[]{:S(2)}) collective-permute-start(f32[2,2,1024]{2,1,0:T(2,128)S(1)} %get-tuple-element.76), channel_id=1, source_target_pairs={{0,2},{2,0},{1,3},{3,1},{4,6},{6,4},{5,7},{7,5},{8,10},{10,8},{9,1... | collective-permute-start | bytes 49160 | tf_op jit(solution)/shard_map/ppermute | solution.py:22
  30.5 0.0 collective-permute-done.9.rest_0_
  30.5 0.0 collective-permute-done.8.got_ref
  30.5 0.9 %shard_map.147 = (bf16[1,4,1,128,256]{4,3,2,1,0:T(8,128)(2,1)}, f32[2,1,8192]{2,1,0:T(1,128)}) custom-call(bf16[2,1,128,256]{3,2,1,0:T(8,128)(2,1)S(1)} %get-tuple-element.71.kept_ref, bf16[2,1,128,256]{3,2,1,0:T(8,128)(2,1)S(1)} %collective-permute-done.8.got_ref, f32[2,4,1,1024]{3,2,1,0:T(1,128)S(1)} %get-tuple-element.73.mamba_ref, ...), custom_call_target="tpu_custom_call" | custom-call | bytes 36000 | tf_op jit(solution)/shard_map/pallas_call | solution.py:512
  31.4 1.3 %collective-permute-done.10.refs_1_ = f32[2,2,1024]{2,1,0:T(2,128)S(1)} collective-permute-done((f32[2,2,1024]{2,1,0:T(2,128)S(1)}, f32[2,2,1024]{2,1,0:T(2,128)S(1)}, u32[]{:S(2)}, u32[]{:S(2)}) %collective-permute-start.10) | collective-permute-done | bytes 16416 | tf_op jit(solution)/shard_map/ppermute | solution.py:22
  32.8 0.6 %shard_map.148 = bf16[2,2,1024]{2,1,0:T(2,128)(2,1)} custom-call(f32[2,2,1024]{2,1,0:T(2,128)S(1)} %get-tuple-element.70.refs_0_, f32[2,2,1024]{2,1,0:T(2,128)S(1)} %collective-permute-done.10.refs_1_), custom_call_target="tpu_custom_call" | custom-call | bytes 21600 | tf_op jit(solution)/shard_map/pallas_call | solution.py:523
Async XLA Ops:
  1.5 13.3 %collective-permute-start = (bf16[256,256]{1,0:T(8,128)(2,1)S(1)}, bf16[256,256]{1,0:T(8,128)(2,1)S(1)}, u32[]{:S(2)}, u32[]{:S(2)}) collective-permute-start(bf16[256,256]{1,0:T(8,128)(2,1)S(1)} %shard_map.141), channel_id=1, source_target_pairs={{0,12},{4,8},{8,4},{12,0},{1,13},{5,9},{9,5},{13,1},{2,14},{6,10},... | collective-permute-start | bytes 393224 | tf_op jit(solution)/shard_map/ppermute | solution.py:22
  7.6 10.2 %collective-permute-start.1 = (bf16[256,256]{1,0:T(8,128)(2,1)S(1)}, bf16[256,256]{1,0:T(8,128)(2,1)S(1)}, u32[]{:S(2)}, u32[]{:S(2)}) collective-permute-start(bf16[256,256]{1,0:T(8,128)(2,1)S(1)} %get-tuple-element.48), channel_id=1, source_target_pairs={{0,8},{4,12},{8,0},{12,4},{1,9},{5,13},{9,1},{13,5},{2,10},{6,14},... | collective-permute-start | bytes 393224 | tf_op jit(solution)/shard_map/ppermute | solution.py:22
  11.5 8.4 %collective-permute-start.2 = (bf16[256,256]{1,0:T(8,128)(2,1)S(1)}, bf16[256,256]{1,0:T(8,128)(2,1)S(1)}, u32[]{:S(2)}, u32[]{:S(2)}) collective-permute-start(bf16[256,256]{1,0:T(8,128)(2,1)S(1)} %get-tuple-element.51), channel_id=1, source_target_pairs={{0,4},{4,0},{8,12},{12,8},{1,5},{5,1},{9,13},{13,9},{2,6},{6,2},{1... | collective-permute-start | bytes 393224 | tf_op jit(solution)/shard_map/ppermute | solution.py:22
  13.3 10.6 %collective-permute-start.3 = (bf16[96,256]{1,0:T(8,128)(2,1)S(1)}, bf16[96,256]{1,0:T(8,128)(2,1)S(1)}, u32[]{:S(2)}, u32[]{:S(2)}) collective-permute-start(bf16[96,256]{1,0:T(8,128)(2,1)S(1)} %get-tuple-element.62), channel_id=1, source_target_pairs={{0,4},{4,0},{8,12},{12,8},{1,5},{5,1},{9,13},{13,9},{2,6},{6,2},{1... | collective-permute-start | bytes 147464 | tf_op jit(solution)/shard_map/ppermute | solution.py:22
  20.3 6.4 %collective-permute-start.4 = (bf16[80,256]{1,0:T(8,128)(2,1)S(1)}, bf16[80,256]{1,0:T(8,128)(2,1)S(1)}, u32[]{:S(2)}, u32[]{:S(2)}) collective-permute-start(bf16[80,256]{1,0:T(8,128)(2,1)S(1)} %get-tuple-element.64), channel_id=1, source_target_pairs={{0,8},{4,12},{8,0},{12,4},{1,9},{5,13},{9,1},{13,5},{2,10},{6,14},... | collective-permute-start | bytes 122888 | tf_op jit(solution)/shard_map/ppermute | solution.py:22
  20.8 5.9 %collective-permute-start.5 = (bf16[80,256]{1,0:T(8,128)(2,1)S(1)}, bf16[80,256]{1,0:T(8,128)(2,1)S(1)}, u32[]{:S(2)}, u32[]{:S(2)}) collective-permute-start(bf16[80,256]{1,0:T(8,128)(2,1)S(1)} %get-tuple-element.65), channel_id=1, source_target_pairs={{0,12},{4,8},{8,4},{12,0},{1,13},{5,9},{9,5},{13,1},{2,14},{6,10},... | collective-permute-start | bytes 122888 | tf_op jit(solution)/shard_map/ppermute | solution.py:22
  22.8 3.9 %collective-permute-start.6 = (bf16[16,256]{1,0:T(8,128)(2,1)S(1)}, bf16[16,256]{1,0:T(8,128)(2,1)S(1)}, u32[]{:S(2)}, u32[]{:S(2)}) collective-permute-start(bf16[16,256]{1,0:T(8,128)(2,1)S(1)} %get-tuple-element.66), channel_id=1, source_target_pairs={{0,4},{4,0},{8,12},{12,8},{1,5},{5,1},{9,13},{13,9},{2,6},{6,2},{1... | collective-permute-start | bytes 24584 | tf_op jit(solution)/shard_map/ppermute | solution.py:22
  26.8 3.7 %collective-permute-start.8 = (bf16[2,1,128,256]{3,2,1,0:T(8,128)(2,1)S(1)}, bf16[2,1,128,256]{3,2,1,0:T(8,128)(2,1)S(1)}, u32[]{:S(2)}, u32[]{:S(2)}) collective-permute-start(bf16[2,1,128,256]{3,2,1,0:T(8,128)(2,1)S(1)} %get-tuple-element.74), channel_id=1, source_target_pairs={{0,1},{1,0},{2,3},{3,2},{4,5},{5,4},{6,7},{7,6},{8,9},{9,8},{10,11... | collective-permute-start | bytes 393224 | tf_op jit(solution)/shard_map/ppermute | solution.py:22
  26.9 1.4 %collective-permute-start.7 = (bf16[8,2048]{1,0:T(8,128)(2,1)S(1)}, bf16[8,2048]{1,0:T(8,128)(2,1)S(1)}, u32[]{:S(2)}, u32[]{:S(2)}) collective-permute-start(bf16[8,2048]{1,0:T(8,128)(2,1)S(1)} %get-tuple-element.67.attn_ref), channel_id=1, source_target_pairs={{0,1},{1,0},{2,3},{3,2},{4,5},{5,4},{6,7},{7,6},{8,9},{9,8},{10,11... | collective-permute-start | bytes 98312 | tf_op jit(solution)/shard_map/ppermute | solution.py:22
  27.4 3.1 %collective-permute-start.9 = (f32[2,4,1,1024]{3,2,1,0:T(1,128)S(1)}, f32[2,4,1,1024]{3,2,1,0:T(1,128)S(1)}, u32[]{:S(2)}, u32[]{:S(2)}) collective-permute-start(f32[2,4,1,1024]{3,2,1,0:T(1,128)S(1)} %get-tuple-element.73.mamba_ref), channel_id=1, source_target_pairs={{0,1},{1,0},{2,3},{3,2},{4,5},{5,4},{6,7},{7,6},{8,9},{9,8},{10,11... | collective-permute-start | bytes 98312 | tf_op jit(solution)/shard_map/ppermute | solution.py:22
  29.0 3.8 %collective-permute-start.10 = (f32[2,2,1024]{2,1,0:T(2,128)S(1)}, f32[2,2,1024]{2,1,0:T(2,128)S(1)}, u32[]{:S(2)}, u32[]{:S(2)}) collective-permute-start(f32[2,2,1024]{2,1,0:T(2,128)S(1)} %get-tuple-element.76), channel_id=1, source_target_pairs={{0,2},{2,0},{1,3},{3,1},{4,6},{6,4},{5,7},{7,5},{8,10},{10,8},{9,1... | collective-permute-start | bytes 49160 | tf_op jit(solution)/shard_map/ppermute | solution.py:22

commit v19 on v18

--- a/solution.py
+++ b/solution.py
@@ -470,7 +470,7 @@
         ],
     )(*after([out_weight], pieces[0]), step_dt, step_input, step_bc, skip_gain, a_log)
 
-    moved = [shift(after(pieces[:1], own_weight)[0], "seq", 1), *moved]
+    moved = [shift(after(pieces[:1], own_piece)[0], "seq", 1), *moved]
     beside = shift(after(states[1:2], own_weight)[0], "seq", 1)
     *moved, own_weight = after([*moved[::-1], own_weight])
     kv = [own_piece, *moved[::-1]]

time: 33.6 us -> 31.6 us (0.940)
  waiting for transfers between devices: 9.38 us -> 7.32 us
    ppermute x11, waiting for transfers between devices: 9.38 us -> 7.32 us  [shift(): return lax.ppermute(x, axis, [(i, i ^ c) for i in range(size)])]
  transfers between devices with their start and end apart: 11 -> 11, of which waited for: 5 -> 4; matrix products, arithmetic and copies ran while one was open for 0% -> 0% of each run, Pallas kernels for 26% -> 27%
where the time goes in v19:
time: 31.6 us; the launch traced here: 31.3 us
  starting transfers between devices  13.1 us (41%)
  Pallas kernels  10.2 us (32%)
  waiting for transfers between devices  7.32 us (23%)
  between operations  0.72 us (2%)
    ppermute x11, starting transfers between devices, shift(): return lax.ppermute(x, axis, [(i, i ^ c) for i in range(size)])  13.1 us
    ppermute x11, waiting for transfers between devices, shift(): return lax.ppermute(x, axis, [(i, i ^ c) for i in range(size)])  7.32 us
    pallas_call x1, Pallas kernels, per_device(): call(functools.partial(prepare, count, split), [half_weight, half_weight,...  3.74 us
    pallas_call x2, Pallas kernels, per_device(): call(functools.partial(stage_blocks, partners), [block_shape] * len(partn...  1.87 us
    pallas_call x1, Pallas kernels, per_device(): call(functools.partial(stage_rest, count, split), [block_shape, shape(que...  1.17 us
    pallas_call x1, Pallas kernels, per_device(): call(functools.partial(assemble, split), [shape((1, dec_heads, keep_rep,...  0.89 us
    pallas_call x1, Pallas kernels, per_device(): call(functools.partial(project_other, heads_count, count), [shape((steps,...  0.67 us
    pallas_call x1, Pallas kernels, per_device(): call(project_own, shape((steps * count, columns), F32), [VM, VM], VM, us=...  0.64 us
  transfers between devices with their start and end apart: 11, of which 4 were waited for; matrix products, arithmetic and copies ran while one was open for 0% of the time, Pallas kernels for 27%

profile of v19, /device:TPU:0, one launch (start us, length us, event | category | flops | bytes accessed | tf_op | source)
XLA Modules:
  0.0 31.3 jit_solution(2832449963810622132)
XLA Ops:
  0.6 0.9 %shard_map.141 = bf16[256,256]{1,0:T(8,128)(2,1)S(1)} custom-call(bf16[4,2,128,256]{3,2,1,0:T(8,128)(2,1)} %kv_ref.4), custom_call_target="tpu_custom_call" | custom-call | bytes 36000 | tf_op jit(solution)/shard_map/pallas_call | solution.py:422
  1.5 5.1 %collective-permute-start = (bf16[256,256]{1,0:T(8,128)(2,1)S(1)}, bf16[256,256]{1,0:T(8,128)(2,1)S(1)}, u32[]{:S(2)}, u32[]{:S(2)}) collective-permute-start(bf16[256,256]{1,0:T(8,128)(2,1)S(1)} %shard_map.141), channel_id=1, source_target_pairs={{0,12},{4,8},{8,4},{12,0},{1,13},{5,9},{9,5},{13,1},{2,14},{6,10},... | collective-permute-start | bytes 393224 | tf_op jit(solution)/shard_map/ppermute | solution.py:22
  6.7 1.0 %shard_map.139 = (bf16[256,256]{1,0:T(8,128)(2,1)S(1)}, bf16[256,256]{1,0:T(8,128)(2,1)S(1)}) custom-call(bf16[4,2,128,256]{3,2,1,0:T(8,128)(2,1)} %kv_ref.4), custom_call_target="tpu_custom_call" | custom-call | bytes 36000 | tf_op jit(solution)/shard_map/pallas_call | solution.py:422
  7.6 0.1 collective-permute-start.1
  7.7 1.2 %shard_map.140 = (bf16[256,256]{1,0:T(8,128)(2,1)S(1)}, bf16[2,1,32,128]{3,2,1,0:T(8,128)(2,1)S(1)}, bf16[2,1,4,256]{3,2,1,0:T(4,128)(2,1)S(1)}, f32[32,512]{1,0...) custom-call(bf16[4,2,128,256]{3,2,1,0:T(8,128)(2,1)} %kv_ref.4, ...), custom_call_target="tpu_custom_call" | custom-call | bytes 36000 | tf_op jit(solution)/shard_map/pallas_call | solution.py:432
  8.9 0.6 %collective-permute-start.2 = (bf16[256,256]{1,0:T(8,128)(2,1)S(1)}, bf16[256,256]{1,0:T(8,128)(2,1)S(1)}, u32[]{:S(2)}, u32[]{:S(2)}) collective-permute-start(bf16[256,256]{1,0:T(8,128)(2,1)S(1)} %get-tuple-element.49), channel_id=1, source_target_pairs={{0,4},{4,0},{8,12},{12,8},{1,5},{5,1},{9,13},{13,9},{2,6},{6,2},{1... | collective-permute-start | bytes 393224 | tf_op jit(solution)/shard_map/ppermute | solution.py:22
  9.5 3.7 %shard_map.142 = (bf16[2048,1024]{1,0:T(8,128)(2,1)S(1)}, bf16[2048,1024]{1,0:T(8,128)(2,1)S(1)}, f32[4,2,16,1024]{3,2,1,0:T(8,128)S(1)}, f32[4,2,1,1024]{3,2,1,0:T(1,128)S(1)}) custom-call(bf16[4096,1024]{1,0:T(8,128)(2,1)} %weight_hbm, f32[2,1,8192]{2,1,0:T(1,128)} %dt_hbm.1, bf16[2,8192]{1,0:T(2,128)(2,1)} %bitcast.3, f32[2,1,2,16]{3,2,1,0:T(2,128)} %bc_hbm.1, ...), custom_call_target="tpu_custom_call" | custom-call | bytes 36000 | tf_op jit(solution)/shard_map/pallas_call | solution.py:452
  13.3 1.5 %collective-permute-start.3 = (bf16[96,256]{1,0:T(8,128)(2,1)S(1)}, bf16[96,256]{1,0:T(8,128)(2,1)S(1)}, u32[]{:S(2)}, u32[]{:S(2)}) collective-permute-start(bf16[96,256]{1,0:T(8,128)(2,1)S(1)} %get-tuple-element.62), channel_id=1, source_target_pairs={{0,4},{4,0},{8,12},{12,8},{1,5},{5,1},{9,13},{13,9},{2,6},{6,2},{1... | collective-permute-start | bytes 147464 | tf_op jit(solution)/shard_map/ppermute | solution.py:22
  14.8 0.0 collective-permute-done.rest_3_
  14.8 3.0 %collective-permute-done.1.rest_2_ = bf16[256,256]{1,0:T(8,128)(2,1)S(1)} collective-permute-done((bf16[256,256]{1,0:T(8,128)(2,1)S(1)}, bf16[256,256]{1,0:T(8,128)(2,1)S(1)}, u32[]{:S(2)}, u32[]{:S(2)}) %collective-permute-start.1) | collective-permute-done | bytes 131104 | tf_op jit(solution)/shard_map/ppermute | solution.py:22
  17.8 0.0 collective-permute-done.2.rest_1_
  17.8 0.5 %shard_map.143 = (bf16[16,256]{1,0:T(8,128)(2,1)S(1)}, bf16[16,256]{1,0:T(8,128)(2,1)S(1)}, bf16[80,256]{1,0:T(8,128)(2,1)S(1)}, bf16[80,256]{1,0:T(8,128)(2,1)S...) custom-call(bf16[2,1,32,128]{3,2,1,0:T(8,128)(2,1)S(1)} %get-tuple-element.43.q_ref, ...), custom_call_target="tpu_custom_call" | custom-call | bytes 36000 | tf_op jit(solution)/shard_map/pallas_call | solution.py:479
  18.3 0.1 collective-permute-start.4
  18.4 2.6 %collective-permute-start.5 = (bf16[80,256]{1,0:T(8,128)(2,1)S(1)}, bf16[80,256]{1,0:T(8,128)(2,1)S(1)}, u32[]{:S(2)}, u32[]{:S(2)}) collective-permute-start(bf16[80,256]{1,0:T(8,128)(2,1)S(1)} %get-tuple-element.65), channel_id=1, source_target_pairs={{0,12},{4,8},{8,4},{12,0},{1,13},{5,9},{9,5},{13,1},{2,14},{6,10},... | collective-permute-start | bytes 122888 | tf_op jit(solution)/shard_map/ppermute | solution.py:22
  21.0 0.9 %collective-permute-start.6 = (bf16[16,256]{1,0:T(8,128)(2,1)S(1)}, bf16[16,256]{1,0:T(8,128)(2,1)S(1)}, u32[]{:S(2)}, u32[]{:S(2)}) collective-permute-start(bf16[16,256]{1,0:T(8,128)(2,1)S(1)} %get-tuple-element.66), channel_id=1, source_target_pairs={{0,4},{4,0},{8,12},{12,8},{1,5},{5,1},{9,13},{13,9},{2,6},{6,2},{1... | collective-permute-start | bytes 24584 | tf_op jit(solution)/shard_map/ppermute | solution.py:22
  21.9 0.0 collective-permute-done.3.beside_ref
  21.9 2.8 %collective-permute-done.6.rest_3_ = bf16[16,256]{1,0:T(8,128)(2,1)S(1)} collective-permute-done((bf16[16,256]{1,0:T(8,128)(2,1)S(1)}, bf16[16,256]{1,0:T(8,128)(2,1)S(1)}, u32[]{:S(2)}, u32[]{:S(2)}) %collective-permute-start.6) | collective-permute-done | bytes 8224 | tf_op jit(solution)/shard_map/ppermute | solution.py:22
  24.7 0.0 collective-permute-done.4.rest_1_
  24.7 0.0 collective-permute-done.5.rest_2_
  24.7 0.1 shard_map.144
  24.8 0.1 collective-permute-start.8
  24.9 0.5 %collective-permute-start.7 = (bf16[8,2048]{1,0:T(8,128)(2,1)S(1)}, bf16[8,2048]{1,0:T(8,128)(2,1)S(1)}, u32[]{:S(2)}, u32[]{:S(2)}) collective-permute-start(bf16[8,2048]{1,0:T(8,128)(2,1)S(1)} %get-tuple-element.67.attn_ref), channel_id=1, source_target_pairs={{0,1},{1,0},{2,3},{3,2},{4,5},{5,4},{6,7},{7,6},{8,9},{9,8},{10,11... | collective-permute-start | bytes 98312 | tf_op jit(solution)/shard_map/ppermute | solution.py:22
  25.4 0.1 collective-permute-start.9
  25.4 0.6 %shard_map.145.acc_ref = f32[8,1024]{1,0:T(8,128)S(1)} custom-call(bf16[8,2048]{1,0:T(8,128)(2,1)S(1)} %get-tuple-element.67.attn_ref, bf16[2048,1024]{1,0:T(8,128)(2,1)S(1)} %get-tuple-element.68.weight_ref), custom_call_target="tpu_custom_call" | custom-call | bytes 25200 | tf_op jit(solution)/shard_map/pallas_call | solution.py:497
  26.1 0.2 collective-permute-done.7.attn_ref
  26.3 0.7 %shard_map.146 = (f32[2,2,1024]{2,1,0:T(2,128)S(1)}, f32[2,2,1024]{2,1,0:T(2,128)S(1)}) custom-call(f32[8,1024]{1,0:T(8,128)S(1)} %shard_map.145.acc_ref, bf16[8,2048]{1,0:T(8,128)(2,1)S(1)} %collective-permute-done.7.attn_ref, bf16[2048,1024]{1,0:T(8,128)(2,1)S(1)} %get-tuple-element.69.weight_ref), custom_call_target="tpu_custom_call" | custom-call | bytes 25200 | tf_op jit(solution)/shard_map/pallas_call | solution.py:501
  26.9 1.5 %collective-permute-start.10 = (f32[2,2,1024]{2,1,0:T(2,128)S(1)}, f32[2,2,1024]{2,1,0:T(2,128)S(1)}, u32[]{:S(2)}, u32[]{:S(2)}) collective-permute-start(f32[2,2,1024]{2,1,0:T(2,128)S(1)} %get-tuple-element.76), channel_id=1, source_target_pairs={{0,2},{2,0},{1,3},{3,1},{4,6},{6,4},{5,7},{7,5},{8,10},{10,8},{9,1... | collective-permute-start | bytes 49160 | tf_op jit(solution)/shard_map/ppermute | solution.py:22
  28.5 0.0 collective-permute-done.9.rest_0_
  28.5 0.0 collective-permute-done.8.got_ref
  28.5 0.9 %shard_map.147 = (bf16[1,4,1,128,256]{4,3,2,1,0:T(8,128)(2,1)}, f32[2,1,8192]{2,1,0:T(1,128)}) custom-call(bf16[2,1,128,256]{3,2,1,0:T(8,128)(2,1)S(1)} %get-tuple-element.71.kept_ref, bf16[2,1,128,256]{3,2,1,0:T(8,128)(2,1)S(1)} %collective-permute-done.8.got_ref, f32[2,4,1,1024]{3,2,1,0:T(1,128)S(1)} %get-tuple-element.73.mamba_ref, ...), custom_call_target="tpu_custom_call" | custom-call | bytes 36000 | tf_op jit(solution)/shard_map/pallas_call | solution.py:512
  29.4 1.3 %collective-permute-done.10.refs_1_ = f32[2,2,1024]{2,1,0:T(2,128)S(1)} collective-permute-done((f32[2,2,1024]{2,1,0:T(2,128)S(1)}, f32[2,2,1024]{2,1,0:T(2,128)S(1)}, u32[]{:S(2)}, u32[]{:S(2)}) %collective-permute-start.10) | collective-permute-done | bytes 16416 | tf_op jit(solution)/shard_map/ppermute | solution.py:22
  30.7 0.6 %shard_map.148 = bf16[2,2,1024]{2,1,0:T(2,128)(2,1)} custom-call(f32[2,2,1024]{2,1,0:T(2,128)S(1)} %get-tuple-element.70.refs_0_, f32[2,2,1024]{2,1,0:T(2,128)S(1)} %collective-permute-done.10.refs_1_), custom_call_target="tpu_custom_call" | custom-call | bytes 21600 | tf_op jit(solution)/shard_map/pallas_call | solution.py:523
Async XLA Ops:
  1.5 13.3 %collective-permute-start = (bf16[256,256]{1,0:T(8,128)(2,1)S(1)}, bf16[256,256]{1,0:T(8,128)(2,1)S(1)}, u32[]{:S(2)}, u32[]{:S(2)}) collective-permute-start(bf16[256,256]{1,0:T(8,128)(2,1)S(1)} %shard_map.141), channel_id=1, source_target_pairs={{0,12},{4,8},{8,4},{12,0},{1,13},{5,9},{9,5},{13,1},{2,14},{6,10},... | collective-permute-start | bytes 393224 | tf_op jit(solution)/shard_map/ppermute | solution.py:22
  7.6 10.2 %collective-permute-start.1 = (bf16[256,256]{1,0:T(8,128)(2,1)S(1)}, bf16[256,256]{1,0:T(8,128)(2,1)S(1)}, u32[]{:S(2)}, u32[]{:S(2)}) collective-permute-start(bf16[256,256]{1,0:T(8,128)(2,1)S(1)} %get-tuple-element.48), channel_id=1, source_target_pairs={{0,8},{4,12},{8,0},{12,4},{1,9},{5,13},{9,1},{13,5},{2,10},{6,14},... | collective-permute-start | bytes 393224 | tf_op jit(solution)/shard_map/ppermute | solution.py:22
  8.9 8.9 %collective-permute-start.2 = (bf16[256,256]{1,0:T(8,128)(2,1)S(1)}, bf16[256,256]{1,0:T(8,128)(2,1)S(1)}, u32[]{:S(2)}, u32[]{:S(2)}) collective-permute-start(bf16[256,256]{1,0:T(8,128)(2,1)S(1)} %get-tuple-element.49), channel_id=1, source_target_pairs={{0,4},{4,0},{8,12},{12,8},{1,5},{5,1},{9,13},{13,9},{2,6},{6,2},{1... | collective-permute-start | bytes 393224 | tf_op jit(solution)/shard_map/ppermute | solution.py:22
  13.3 8.6 %collective-permute-start.3 = (bf16[96,256]{1,0:T(8,128)(2,1)S(1)}, bf16[96,256]{1,0:T(8,128)(2,1)S(1)}, u32[]{:S(2)}, u32[]{:S(2)}) collective-permute-start(bf16[96,256]{1,0:T(8,128)(2,1)S(1)} %get-tuple-element.62), channel_id=1, source_target_pairs={{0,4},{4,0},{8,12},{12,8},{1,5},{5,1},{9,13},{13,9},{2,6},{6,2},{1... | collective-permute-start | bytes 147464 | tf_op jit(solution)/shard_map/ppermute | solution.py:22
  18.3 6.3 %collective-permute-start.4 = (bf16[80,256]{1,0:T(8,128)(2,1)S(1)}, bf16[80,256]{1,0:T(8,128)(2,1)S(1)}, u32[]{:S(2)}, u32[]{:S(2)}) collective-permute-start(bf16[80,256]{1,0:T(8,128)(2,1)S(1)} %get-tuple-element.64), channel_id=1, source_target_pairs={{0,8},{4,12},{8,0},{12,4},{1,9},{5,13},{9,1},{13,5},{2,10},{6,14},... | collective-permute-start | bytes 122888 | tf_op jit(solution)/shard_map/ppermute | solution.py:22
  18.4 6.2 %collective-permute-start.5 = (bf16[80,256]{1,0:T(8,128)(2,1)S(1)}, bf16[80,256]{1,0:T(8,128)(2,1)S(1)}, u32[]{:S(2)}, u32[]{:S(2)}) collective-permute-start(bf16[80,256]{1,0:T(8,128)(2,1)S(1)} %get-tuple-element.65), channel_id=1, source_target_pairs={{0,12},{4,8},{8,4},{12,0},{1,13},{5,9},{9,5},{13,1},{2,14},{6,10},... | collective-permute-start | bytes 122888 | tf_op jit(solution)/shard_map/ppermute | solution.py:22
  21.0 3.7 %collective-permute-start.6 = (bf16[16,256]{1,0:T(8,128)(2,1)S(1)}, bf16[16,256]{1,0:T(8,128)(2,1)S(1)}, u32[]{:S(2)}, u32[]{:S(2)}) collective-permute-start(bf16[16,256]{1,0:T(8,128)(2,1)S(1)} %get-tuple-element.66), channel_id=1, source_target_pairs={{0,4},{4,0},{8,12},{12,8},{1,5},{5,1},{9,13},{13,9},{2,6},{6,2},{1... | collective-permute-start | bytes 24584 | tf_op jit(solution)/shard_map/ppermute | solution.py:22
  24.8 3.7 %collective-permute-start.8 = (bf16[2,1,128,256]{3,2,1,0:T(8,128)(2,1)S(1)}, bf16[2,1,128,256]{3,2,1,0:T(8,128)(2,1)S(1)}, u32[]{:S(2)}, u32[]{:S(2)}) collective-permute-start(bf16[2,1,128,256]{3,2,1,0:T(8,128)(2,1)S(1)} %get-tuple-element.74), channel_id=1, source_target_pairs={{0,1},{1,0},{2,3},{3,2},{4,5},{5,4},{6,7},{7,6},{8,9},{9,8},{10,11... | collective-permute-start | bytes 393224 | tf_op jit(solution)/shard_map/ppermute | solution.py:22
  24.9 1.4 %collective-permute-start.7 = (bf16[8,2048]{1,0:T(8,128)(2,1)S(1)}, bf16[8,2048]{1,0:T(8,128)(2,1)S(1)}, u32[]{:S(2)}, u32[]{:S(2)}) collective-permute-start(bf16[8,2048]{1,0:T(8,128)(2,1)S(1)} %get-tuple-element.67.attn_ref), channel_id=1, source_target_pairs={{0,1},{1,0},{2,3},{3,2},{4,5},{5,4},{6,7},{7,6},{8,9},{9,8},{10,11... | collective-permute-start | bytes 98312 | tf_op jit(solution)/shard_map/ppermute | solution.py:22
  25.4 3.1 %collective-permute-start.9 = (f32[2,4,1,1024]{3,2,1,0:T(1,128)S(1)}, f32[2,4,1,1024]{3,2,1,0:T(1,128)S(1)}, u32[]{:S(2)}, u32[]{:S(2)}) collective-permute-start(f32[2,4,1,1024]{3,2,1,0:T(1,128)S(1)} %get-tuple-element.73.mamba_ref), channel_id=1, source_target_pairs={{0,1},{1,0},{2,3},{3,2},{4,5},{5,4},{6,7},{7,6},{8,9},{9,8},{10,11... | collective-permute-start | bytes 98312 | tf_op jit(solution)/shard_map/ppermute | solution.py:22
  26.9 3.8 %collective-permute-start.10 = (f32[2,2,1024]{2,1,0:T(2,128)S(1)}, f32[2,2,1024]{2,1,0:T(2,128)S(1)}, u32[]{:S(2)}, u32[]{:S(2)}) collective-permute-start(f32[2,2,1024]{2,1,0:T(2,128)S(1)} %get-tuple-element.76), channel_id=1, source_target_pairs={{0,2},{2,0},{1,3},{3,1},{4,6},{6,4},{5,7},{7,5},{8,10},{10,8},{9,1... | collective-permute-start | bytes 49160 | tf_op jit(solution)/shard_map/ppermute | solution.py:22

commit v20 on v19

--- a/solution.py
+++ b/solution.py
@@ -491,7 +491,7 @@
         [shape((steps * count, half), BF), shape((steps, count, 1, part), F32)],
         [VM] * (4 + count),
         [VM] * 2,
-        [pltpu.VMEM((heads, steps * count * group, hd), F32)],
+        [pltpu.VMEM((heads, (steps * count + 1) * group, hd), F32)],
     )(slope, base, states[0], beside, sends[0], *gathered)
     attn_other = shift(attn, "rep", 1)
     own_sum = call(

time: 31.6 us -> 31.6 us (level)
  no operation moved by 1% of the time
where the time goes in v20:
time: 31.6 us; the launch traced here: 31.3 us
  starting transfers between devices  13.1 us (41%)
  Pallas kernels  10.2 us (32%)
  waiting for transfers between devices  7.32 us (23%)
  between operations  0.72 us (2%)
    ppermute x11, starting transfers between devices, shift(): return lax.ppermute(x, axis, [(i, i ^ c) for i in range(size)])  13.1 us
    ppermute x11, waiting for transfers between devices, shift(): return lax.ppermute(x, axis, [(i, i ^ c) for i in range(size)])  7.32 us
    pallas_call x1, Pallas kernels, per_device(): call(functools.partial(prepare, count, split), [half_weight, half_weight,...  3.74 us
    pallas_call x2, Pallas kernels, per_device(): call(functools.partial(stage_blocks, partners), [block_shape] * len(partn...  1.87 us
    pallas_call x1, Pallas kernels, per_device(): call(functools.partial(stage_rest, count, split), [block_shape, shape(que...  1.17 us
    pallas_call x1, Pallas kernels, per_device(): call(functools.partial(assemble, split), [shape((1, dec_heads, keep_rep,...  0.89 us
    pallas_call x1, Pallas kernels, per_device(): call(functools.partial(project_other, heads_count, count), [shape((steps,...  0.67 us
    pallas_call x1, Pallas kernels, per_device(): call(project_own, shape((steps * count, columns), F32), [VM, VM], VM, us=...  0.64 us
  transfers between devices with their start and end apart: 11, of which 4 were waited for; matrix products, arithmetic and copies ran while one was open for 0% of the time, Pallas kernels for 27%

profile of v20, /device:TPU:0, one launch (start us, length us, event | category | flops | bytes accessed | tf_op | source)
XLA Modules:
  0.0 31.3 jit_solution(7802540078398863510)
XLA Ops:
  0.6 0.9 %shard_map.141 = bf16[256,256]{1,0:T(8,128)(2,1)S(1)} custom-call(bf16[4,2,128,256]{3,2,1,0:T(8,128)(2,1)} %kv_ref.4), custom_call_target="tpu_custom_call" | custom-call | bytes 36000 | tf_op jit(solution)/shard_map/pallas_call | solution.py:422
  1.5 5.1 %collective-permute-start = (bf16[256,256]{1,0:T(8,128)(2,1)S(1)}, bf16[256,256]{1,0:T(8,128)(2,1)S(1)}, u32[]{:S(2)}, u32[]{:S(2)}) collective-permute-start(bf16[256,256]{1,0:T(8,128)(2,1)S(1)} %shard_map.141), channel_id=1, source_target_pairs={{0,12},{4,8},{8,4},{12,0},{1,13},{5,9},{9,5},{13,1},{2,14},{6,10},... | collective-permute-start | bytes 393224 | tf_op jit(solution)/shard_map/ppermute | solution.py:22
  6.7 1.0 %shard_map.139 = (bf16[256,256]{1,0:T(8,128)(2,1)S(1)}, bf16[256,256]{1,0:T(8,128)(2,1)S(1)}) custom-call(bf16[4,2,128,256]{3,2,1,0:T(8,128)(2,1)} %kv_ref.4), custom_call_target="tpu_custom_call" | custom-call | bytes 36000 | tf_op jit(solution)/shard_map/pallas_call | solution.py:422
  7.6 0.1 collective-permute-start.1
  7.7 1.2 %shard_map.140 = (bf16[256,256]{1,0:T(8,128)(2,1)S(1)}, bf16[2,1,32,128]{3,2,1,0:T(8,128)(2,1)S(1)}, bf16[2,1,4,256]{3,2,1,0:T(4,128)(2,1)S(1)}, f32[32,512]{1,0...) custom-call(bf16[4,2,128,256]{3,2,1,0:T(8,128)(2,1)} %kv_ref.4, ...), custom_call_target="tpu_custom_call" | custom-call | bytes 36000 | tf_op jit(solution)/shard_map/pallas_call | solution.py:432
  8.9 0.6 %collective-permute-start.2 = (bf16[256,256]{1,0:T(8,128)(2,1)S(1)}, bf16[256,256]{1,0:T(8,128)(2,1)S(1)}, u32[]{:S(2)}, u32[]{:S(2)}) collective-permute-start(bf16[256,256]{1,0:T(8,128)(2,1)S(1)} %get-tuple-element.49), channel_id=1, source_target_pairs={{0,4},{4,0},{8,12},{12,8},{1,5},{5,1},{9,13},{13,9},{2,6},{6,2},{1... | collective-permute-start | bytes 393224 | tf_op jit(solution)/shard_map/ppermute | solution.py:22
  9.5 3.7 %shard_map.142 = (bf16[2048,1024]{1,0:T(8,128)(2,1)S(1)}, bf16[2048,1024]{1,0:T(8,128)(2,1)S(1)}, f32[4,2,16,1024]{3,2,1,0:T(8,128)S(1)}, f32[4,2,1,1024]{3,2,1,0:T(1,128)S(1)}) custom-call(bf16[4096,1024]{1,0:T(8,128)(2,1)} %weight_hbm, f32[2,1,8192]{2,1,0:T(1,128)} %dt_hbm.1, bf16[2,8192]{1,0:T(2,128)(2,1)} %bitcast.3, f32[2,1,2,16]{3,2,1,0:T(2,128)} %bc_hbm.1, ...), custom_call_target="tpu_custom_call" | custom-call | bytes 36000 | tf_op jit(solution)/shard_map/pallas_call | solution.py:452
  13.3 1.5 %collective-permute-start.3 = (bf16[96,256]{1,0:T(8,128)(2,1)S(1)}, bf16[96,256]{1,0:T(8,128)(2,1)S(1)}, u32[]{:S(2)}, u32[]{:S(2)}) collective-permute-start(bf16[96,256]{1,0:T(8,128)(2,1)S(1)} %get-tuple-element.62), channel_id=1, source_target_pairs={{0,4},{4,0},{8,12},{12,8},{1,5},{5,1},{9,13},{13,9},{2,6},{6,2},{1... | collective-permute-start | bytes 147464 | tf_op jit(solution)/shard_map/ppermute | solution.py:22
  14.8 0.0 collective-permute-done.rest_3_
  14.8 3.0 %collective-permute-done.1.rest_2_ = bf16[256,256]{1,0:T(8,128)(2,1)S(1)} collective-permute-done((bf16[256,256]{1,0:T(8,128)(2,1)S(1)}, bf16[256,256]{1,0:T(8,128)(2,1)S(1)}, u32[]{:S(2)}, u32[]{:S(2)}) %collective-permute-start.1) | collective-permute-done | bytes 131104 | tf_op jit(solution)/shard_map/ppermute | solution.py:22
  17.8 0.0 collective-permute-done.2.rest_1_
  17.8 0.5 %shard_map.143 = (bf16[16,256]{1,0:T(8,128)(2,1)S(1)}, bf16[16,256]{1,0:T(8,128)(2,1)S(1)}, bf16[80,256]{1,0:T(8,128)(2,1)S(1)}, bf16[80,256]{1,0:T(8,128)(2,1)S...) custom-call(bf16[2,1,32,128]{3,2,1,0:T(8,128)(2,1)S(1)} %get-tuple-element.43.q_ref, ...), custom_call_target="tpu_custom_call" | custom-call | bytes 36000 | tf_op jit(solution)/shard_map/pallas_call | solution.py:479
  18.3 0.1 collective-permute-start.4
  18.4 2.6 %collective-permute-start.5 = (bf16[80,256]{1,0:T(8,128)(2,1)S(1)}, bf16[80,256]{1,0:T(8,128)(2,1)S(1)}, u32[]{:S(2)}, u32[]{:S(2)}) collective-permute-start(bf16[80,256]{1,0:T(8,128)(2,1)S(1)} %get-tuple-element.65), channel_id=1, source_target_pairs={{0,12},{4,8},{8,4},{12,0},{1,13},{5,9},{9,5},{13,1},{2,14},{6,10},... | collective-permute-start | bytes 122888 | tf_op jit(solution)/shard_map/ppermute | solution.py:22
  21.0 0.9 %collective-permute-start.6 = (bf16[16,256]{1,0:T(8,128)(2,1)S(1)}, bf16[16,256]{1,0:T(8,128)(2,1)S(1)}, u32[]{:S(2)}, u32[]{:S(2)}) collective-permute-start(bf16[16,256]{1,0:T(8,128)(2,1)S(1)} %get-tuple-element.66), channel_id=1, source_target_pairs={{0,4},{4,0},{8,12},{12,8},{1,5},{5,1},{9,13},{13,9},{2,6},{6,2},{1... | collective-permute-start | bytes 24584 | tf_op jit(solution)/shard_map/ppermute | solution.py:22
  21.9 0.0 collective-permute-done.3.beside_ref
  21.9 2.8 %collective-permute-done.6.rest_3_ = bf16[16,256]{1,0:T(8,128)(2,1)S(1)} collective-permute-done((bf16[16,256]{1,0:T(8,128)(2,1)S(1)}, bf16[16,256]{1,0:T(8,128)(2,1)S(1)}, u32[]{:S(2)}, u32[]{:S(2)}) %collective-permute-start.6) | collective-permute-done | bytes 8224 | tf_op jit(solution)/shard_map/ppermute | solution.py:22
  24.7 0.0 collective-permute-done.4.rest_1_
  24.7 0.0 collective-permute-done.5.rest_2_
  24.7 0.1 shard_map.144
  24.8 0.1 collective-permute-start.8
  24.9 0.5 %collective-permute-start.7 = (bf16[8,2048]{1,0:T(8,128)(2,1)S(1)}, bf16[8,2048]{1,0:T(8,128)(2,1)S(1)}, u32[]{:S(2)}, u32[]{:S(2)}) collective-permute-start(bf16[8,2048]{1,0:T(8,128)(2,1)S(1)} %get-tuple-element.67.attn_ref), channel_id=1, source_target_pairs={{0,1},{1,0},{2,3},{3,2},{4,5},{5,4},{6,7},{7,6},{8,9},{9,8},{10,11... | collective-permute-start | bytes 98312 | tf_op jit(solution)/shard_map/ppermute | solution.py:22
  25.4 0.1 collective-permute-start.9
  25.4 0.6 %shard_map.145.acc_ref = f32[8,1024]{1,0:T(8,128)S(1)} custom-call(bf16[8,2048]{1,0:T(8,128)(2,1)S(1)} %get-tuple-element.67.attn_ref, bf16[2048,1024]{1,0:T(8,128)(2,1)S(1)} %get-tuple-element.68.weight_ref), custom_call_target="tpu_custom_call" | custom-call | bytes 25200 | tf_op jit(solution)/shard_map/pallas_call | solution.py:497
  26.1 0.2 collective-permute-done.7.attn_ref
  26.3 0.7 %shard_map.146 = (f32[2,2,1024]{2,1,0:T(2,128)S(1)}, f32[2,2,1024]{2,1,0:T(2,128)S(1)}) custom-call(f32[8,1024]{1,0:T(8,128)S(1)} %shard_map.145.acc_ref, bf16[8,2048]{1,0:T(8,128)(2,1)S(1)} %collective-permute-done.7.attn_ref, bf16[2048,1024]{1,0:T(8,128)(2,1)S(1)} %get-tuple-element.69.weight_ref), custom_call_target="tpu_custom_call" | custom-call | bytes 25200 | tf_op jit(solution)/shard_map/pallas_call | solution.py:501
  26.9 1.5 %collective-permute-start.10 = (f32[2,2,1024]{2,1,0:T(2,128)S(1)}, f32[2,2,1024]{2,1,0:T(2,128)S(1)}, u32[]{:S(2)}, u32[]{:S(2)}) collective-permute-start(f32[2,2,1024]{2,1,0:T(2,128)S(1)} %get-tuple-element.76), channel_id=1, source_target_pairs={{0,2},{2,0},{1,3},{3,1},{4,6},{6,4},{5,7},{7,5},{8,10},{10,8},{9,1... | collective-permute-start | bytes 49160 | tf_op jit(solution)/shard_map/ppermute | solution.py:22
  28.5 0.0 collective-permute-done.9.rest_0_
  28.5 0.0 collective-permute-done.8.got_ref
  28.5 0.9 %shard_map.147 = (bf16[1,4,1,128,256]{4,3,2,1,0:T(8,128)(2,1)}, f32[2,1,8192]{2,1,0:T(1,128)}) custom-call(bf16[2,1,128,256]{3,2,1,0:T(8,128)(2,1)S(1)} %get-tuple-element.71.kept_ref, bf16[2,1,128,256]{3,2,1,0:T(8,128)(2,1)S(1)} %collective-permute-done.8.got_ref, f32[2,4,1,1024]{3,2,1,0:T(1,128)S(1)} %get-tuple-element.73.mamba_ref, ...), custom_call_target="tpu_custom_call" | custom-call | bytes 36000 | tf_op jit(solution)/shard_map/pallas_call | solution.py:512
  29.4 1.3 %collective-permute-done.10.refs_1_ = f32[2,2,1024]{2,1,0:T(2,128)S(1)} collective-permute-done((f32[2,2,1024]{2,1,0:T(2,128)S(1)}, f32[2,2,1024]{2,1,0:T(2,128)S(1)}, u32[]{:S(2)}, u32[]{:S(2)}) %collective-permute-start.10) | collective-permute-done | bytes 16416 | tf_op jit(solution)/shard_map/ppermute | solution.py:22
  30.7 0.6 %shard_map.148 = bf16[2,2,1024]{2,1,0:T(2,128)(2,1)} custom-call(f32[2,2,1024]{2,1,0:T(2,128)S(1)} %get-tuple-element.70.refs_0_, f32[2,2,1024]{2,1,0:T(2,128)S(1)} %collective-permute-done.10.refs_1_), custom_call_target="tpu_custom_call" | custom-call | bytes 21600 | tf_op jit(solution)/shard_map/pallas_call | solution.py:523
Async XLA Ops:
  1.5 13.3 %collective-permute-start = (bf16[256,256]{1,0:T(8,128)(2,1)S(1)}, bf16[256,256]{1,0:T(8,128)(2,1)S(1)}, u32[]{:S(2)}, u32[]{:S(2)}) collective-permute-start(bf16[256,256]{1,0:T(8,128)(2,1)S(1)} %shard_map.141), channel_id=1, source_target_pairs={{0,12},{4,8},{8,4},{12,0},{1,13},{5,9},{9,5},{13,1},{2,14},{6,10},... | collective-permute-start | bytes 393224 | tf_op jit(solution)/shard_map/ppermute | solution.py:22
  7.6 10.2 %collective-permute-start.1 = (bf16[256,256]{1,0:T(8,128)(2,1)S(1)}, bf16[256,256]{1,0:T(8,128)(2,1)S(1)}, u32[]{:S(2)}, u32[]{:S(2)}) collective-permute-start(bf16[256,256]{1,0:T(8,128)(2,1)S(1)} %get-tuple-element.48), channel_id=1, source_target_pairs={{0,8},{4,12},{8,0},{12,4},{1,9},{5,13},{9,1},{13,5},{2,10},{6,14},... | collective-permute-start | bytes 393224 | tf_op jit(solution)/shard_map/ppermute | solution.py:22
  8.9 8.9 %collective-permute-start.2 = (bf16[256,256]{1,0:T(8,128)(2,1)S(1)}, bf16[256,256]{1,0:T(8,128)(2,1)S(1)}, u32[]{:S(2)}, u32[]{:S(2)}) collective-permute-start(bf16[256,256]{1,0:T(8,128)(2,1)S(1)} %get-tuple-element.49), channel_id=1, source_target_pairs={{0,4},{4,0},{8,12},{12,8},{1,5},{5,1},{9,13},{13,9},{2,6},{6,2},{1... | collective-permute-start | bytes 393224 | tf_op jit(solution)/shard_map/ppermute | solution.py:22
  13.3 8.6 %collective-permute-start.3 = (bf16[96,256]{1,0:T(8,128)(2,1)S(1)}, bf16[96,256]{1,0:T(8,128)(2,1)S(1)}, u32[]{:S(2)}, u32[]{:S(2)}) collective-permute-start(bf16[96,256]{1,0:T(8,128)(2,1)S(1)} %get-tuple-element.62), channel_id=1, source_target_pairs={{0,4},{4,0},{8,12},{12,8},{1,5},{5,1},{9,13},{13,9},{2,6},{6,2},{1... | collective-permute-start | bytes 147464 | tf_op jit(solution)/shard_map/ppermute | solution.py:22
  18.3 6.3 %collective-permute-start.4 = (bf16[80,256]{1,0:T(8,128)(2,1)S(1)}, bf16[80,256]{1,0:T(8,128)(2,1)S(1)}, u32[]{:S(2)}, u32[]{:S(2)}) collective-permute-start(bf16[80,256]{1,0:T(8,128)(2,1)S(1)} %get-tuple-element.64), channel_id=1, source_target_pairs={{0,8},{4,12},{8,0},{12,4},{1,9},{5,13},{9,1},{13,5},{2,10},{6,14},... | collective-permute-start | bytes 122888 | tf_op jit(solution)/shard_map/ppermute | solution.py:22
  18.4 6.2 %collective-permute-start.5 = (bf16[80,256]{1,0:T(8,128)(2,1)S(1)}, bf16[80,256]{1,0:T(8,128)(2,1)S(1)}, u32[]{:S(2)}, u32[]{:S(2)}) collective-permute-start(bf16[80,256]{1,0:T(8,128)(2,1)S(1)} %get-tuple-element.65), channel_id=1, source_target_pairs={{0,12},{4,8},{8,4},{12,0},{1,13},{5,9},{9,5},{13,1},{2,14},{6,10},... | collective-permute-start | bytes 122888 | tf_op jit(solution)/shard_map/ppermute | solution.py:22
  21.0 3.7 %collective-permute-start.6 = (bf16[16,256]{1,0:T(8,128)(2,1)S(1)}, bf16[16,256]{1,0:T(8,128)(2,1)S(1)}, u32[]{:S(2)}, u32[]{:S(2)}) collective-permute-start(bf16[16,256]{1,0:T(8,128)(2,1)S(1)} %get-tuple-element.66), channel_id=1, source_target_pairs={{0,4},{4,0},{8,12},{12,8},{1,5},{5,1},{9,13},{13,9},{2,6},{6,2},{1... | collective-permute-start | bytes 24584 | tf_op jit(solution)/shard_map/ppermute | solution.py:22
  24.8 3.7 %collective-permute-start.8 = (bf16[2,1,128,256]{3,2,1,0:T(8,128)(2,1)S(1)}, bf16[2,1,128,256]{3,2,1,0:T(8,128)(2,1)S(1)}, u32[]{:S(2)}, u32[]{:S(2)}) collective-permute-start(bf16[2,1,128,256]{3,2,1,0:T(8,128)(2,1)S(1)} %get-tuple-element.74), channel_id=1, source_target_pairs={{0,1},{1,0},{2,3},{3,2},{4,5},{5,4},{6,7},{7,6},{8,9},{9,8},{10,11... | collective-permute-start | bytes 393224 | tf_op jit(solution)/shard_map/ppermute | solution.py:22
  24.9 1.4 %collective-permute-start.7 = (bf16[8,2048]{1,0:T(8,128)(2,1)S(1)}, bf16[8,2048]{1,0:T(8,128)(2,1)S(1)}, u32[]{:S(2)}, u32[]{:S(2)}) collective-permute-start(bf16[8,2048]{1,0:T(8,128)(2,1)S(1)} %get-tuple-element.67.attn_ref), channel_id=1, source_target_pairs={{0,1},{1,0},{2,3},{3,2},{4,5},{5,4},{6,7},{7,6},{8,9},{9,8},{10,11... | collective-permute-start | bytes 98312 | tf_op jit(solution)/shard_map/ppermute | solution.py:22
  25.4 3.1 %collective-permute-start.9 = (f32[2,4,1,1024]{3,2,1,0:T(1,128)S(1)}, f32[2,4,1,1024]{3,2,1,0:T(1,128)S(1)}, u32[]{:S(2)}, u32[]{:S(2)}) collective-permute-start(f32[2,4,1,1024]{3,2,1,0:T(1,128)S(1)} %get-tuple-element.73.mamba_ref), channel_id=1, source_target_pairs={{0,1},{1,0},{2,3},{3,2},{4,5},{5,4},{6,7},{7,6},{8,9},{9,8},{10,11... | collective-permute-start | bytes 98312 | tf_op jit(solution)/shard_map/ppermute | solution.py:22
  26.9 3.8 %collective-permute-start.10 = (f32[2,2,1024]{2,1,0:T(2,128)S(1)}, f32[2,2,1024]{2,1,0:T(2,128)S(1)}, u32[]{:S(2)}, u32[]{:S(2)}) collective-permute-start(f32[2,2,1024]{2,1,0:T(2,128)S(1)} %get-tuple-element.76), channel_id=1, source_target_pairs={{0,2},{2,0},{1,3},{3,1},{4,6},{6,4},{5,7},{7,5},{8,10},{10,8},{9,1... | collective-permute-start | bytes 49160 | tf_op jit(solution)/shard_map/ppermute | solution.py:22

commit v21 on v20

--- a/solution.py
+++ b/solution.py
@@ -507,6 +507,7 @@
     )(own_sum, attn_other, other_weight)
     sums = [sums[0]] + [shift(sums[c], "head", c) for c in range(1, heads_count)]
     got = shift(after([sent], mamba)[0], "rep", 1)
+    mamba = after([mamba], own_sum)[0]
     kept = after([kept], sums[0])[0]
     operands = [kept, got, mamba] + ([shift(mamba, "rep", 1)] if split else [])
     handoff, mamba_out = call(

time: 31.6 us -> 31.6 us (level)
  no operation moved by 1% of the time
where the time goes in v21:
time: 31.6 us; the launch traced here: 31.3 us
  starting transfers between devices  13.1 us (41%)
  Pallas kernels  10.2 us (32%)
  waiting for transfers between devices  7.3 us (23%)
  between operations  0.72 us (2%)
    ppermute x11, starting transfers between devices, shift(): return lax.ppermute(x, axis, [(i, i ^ c) for i in range(size)])  13.1 us
    ppermute x11, waiting for transfers between devices, shift(): return lax.ppermute(x, axis, [(i, i ^ c) for i in range(size)])  7.3 us
    pallas_call x1, Pallas kernels, per_device(): call(functools.partial(prepare, count, split), [half_weight, half_weight,...  3.74 us
    pallas_call x2, Pallas kernels, per_device(): call(functools.partial(stage_blocks, partners), [block_shape] * len(partn...  1.87 us
    pallas_call x1, Pallas kernels, per_device(): call(functools.partial(stage_rest, count, split), [block_shape, shape(que...  1.17 us
    pallas_call x1, Pallas kernels, per_device(): call(functools.partial(assemble, split), [shape((1, dec_heads, keep_rep,...  0.89 us
    pallas_call x1, Pallas kernels, per_device(): call(functools.partial(project_other, heads_count, count), [shape((steps,...  0.67 us
    pallas_call x1, Pallas kernels, per_device(): call(project_own, shape((steps * count, columns), F32), [VM, VM], VM, us=...  0.64 us
  transfers between devices with their start and end apart: 11, of which 4 were waited for; matrix products, arithmetic and copies ran while one was open for 0% of the time, Pallas kernels for 27%

profile of v21, /device:TPU:0, one launch (start us, length us, event | category | flops | bytes accessed | tf_op | source)
XLA Modules:
  0.0 31.3 jit_solution(10832673823557362527)
XLA Ops:
  0.6 0.9 %shard_map.141 = bf16[256,256]{1,0:T(8,128)(2,1)S(1)} custom-call(bf16[4,2,128,256]{3,2,1,0:T(8,128)(2,1)} %kv_ref.4), custom_call_target="tpu_custom_call" | custom-call | bytes 36000 | tf_op jit(solution)/shard_map/pallas_call | solution.py:422
  1.5 5.1 %collective-permute-start = (bf16[256,256]{1,0:T(8,128)(2,1)S(1)}, bf16[256,256]{1,0:T(8,128)(2,1)S(1)}, u32[]{:S(2)}, u32[]{:S(2)}) collective-permute-start(bf16[256,256]{1,0:T(8,128)(2,1)S(1)} %shard_map.141), channel_id=1, source_target_pairs={{0,12},{4,8},{8,4},{12,0},{1,13},{5,9},{9,5},{13,1},{2,14},{6,10},... | collective-permute-start | bytes 393224 | tf_op jit(solution)/shard_map/ppermute | solution.py:22
  6.7 1.0 %shard_map.139 = (bf16[256,256]{1,0:T(8,128)(2,1)S(1)}, bf16[256,256]{1,0:T(8,128)(2,1)S(1)}) custom-call(bf16[4,2,128,256]{3,2,1,0:T(8,128)(2,1)} %kv_ref.4), custom_call_target="tpu_custom_call" | custom-call | bytes 36000 | tf_op jit(solution)/shard_map/pallas_call | solution.py:422
  7.6 0.1 collective-permute-start.1
  7.7 1.2 %shard_map.140 = (bf16[256,256]{1,0:T(8,128)(2,1)S(1)}, bf16[2,1,32,128]{3,2,1,0:T(8,128)(2,1)S(1)}, bf16[2,1,4,256]{3,2,1,0:T(4,128)(2,1)S(1)}, f32[32,512]{1,0...) custom-call(bf16[4,2,128,256]{3,2,1,0:T(8,128)(2,1)} %kv_ref.4, ...), custom_call_target="tpu_custom_call" | custom-call | bytes 36000 | tf_op jit(solution)/shard_map/pallas_call | solution.py:432
  8.9 0.6 %collective-permute-start.2 = (bf16[256,256]{1,0:T(8,128)(2,1)S(1)}, bf16[256,256]{1,0:T(8,128)(2,1)S(1)}, u32[]{:S(2)}, u32[]{:S(2)}) collective-permute-start(bf16[256,256]{1,0:T(8,128)(2,1)S(1)} %get-tuple-element.50), channel_id=1, source_target_pairs={{0,4},{4,0},{8,12},{12,8},{1,5},{5,1},{9,13},{13,9},{2,6},{6,2},{1... | collective-permute-start | bytes 393224 | tf_op jit(solution)/shard_map/ppermute | solution.py:22
  9.5 3.7 %shard_map.142 = (bf16[2048,1024]{1,0:T(8,128)(2,1)S(1)}, bf16[2048,1024]{1,0:T(8,128)(2,1)S(1)}, f32[4,2,16,1024]{3,2,1,0:T(8,128)S(1)}, f32[4,2,1,1024]{3,2,1,0:T(1,128)S(1)}) custom-call(bf16[4096,1024]{1,0:T(8,128)(2,1)} %weight_hbm, f32[2,1,8192]{2,1,0:T(1,128)} %dt_hbm.1, bf16[2,8192]{1,0:T(2,128)(2,1)} %bitcast.3, f32[2,1,2,16]{3,2,1,0:T(2,128)} %bc_hbm.1, ...), custom_call_target="tpu_custom_call" | custom-call | bytes 36000 | tf_op jit(solution)/shard_map/pallas_call | solution.py:452
  13.3 1.5 %collective-permute-start.3 = (bf16[96,256]{1,0:T(8,128)(2,1)S(1)}, bf16[96,256]{1,0:T(8,128)(2,1)S(1)}, u32[]{:S(2)}, u32[]{:S(2)}) collective-permute-start(bf16[96,256]{1,0:T(8,128)(2,1)S(1)} %get-tuple-element.63), channel_id=1, source_target_pairs={{0,4},{4,0},{8,12},{12,8},{1,5},{5,1},{9,13},{13,9},{2,6},{6,2},{1... | collective-permute-start | bytes 147464 | tf_op jit(solution)/shard_map/ppermute | solution.py:22
  14.8 0.0 collective-permute-done.rest_3_
  14.8 3.0 %collective-permute-done.1.rest_2_ = bf16[256,256]{1,0:T(8,128)(2,1)S(1)} collective-permute-done((bf16[256,256]{1,0:T(8,128)(2,1)S(1)}, bf16[256,256]{1,0:T(8,128)(2,1)S(1)}, u32[]{:S(2)}, u32[]{:S(2)}) %collective-permute-start.1) | collective-permute-done | bytes 131104 | tf_op jit(solution)/shard_map/ppermute | solution.py:22
  17.8 0.0 collective-permute-done.2.rest_1_
  17.8 0.5 %shard_map.143 = (bf16[16,256]{1,0:T(8,128)(2,1)S(1)}, bf16[16,256]{1,0:T(8,128)(2,1)S(1)}, bf16[80,256]{1,0:T(8,128)(2,1)S(1)}, bf16[80,256]{1,0:T(8,128)(2,1)S...) custom-call(bf16[2,1,32,128]{3,2,1,0:T(8,128)(2,1)S(1)} %get-tuple-element.44.q_ref, ...), custom_call_target="tpu_custom_call" | custom-call | bytes 36000 | tf_op jit(solution)/shard_map/pallas_call | solution.py:479
  18.3 0.1 collective-permute-start.4
  18.4 2.6 %collective-permute-start.5 = (bf16[80,256]{1,0:T(8,128)(2,1)S(1)}, bf16[80,256]{1,0:T(8,128)(2,1)S(1)}, u32[]{:S(2)}, u32[]{:S(2)}) collective-permute-start(bf16[80,256]{1,0:T(8,128)(2,1)S(1)} %get-tuple-element.66), channel_id=1, source_target_pairs={{0,12},{4,8},{8,4},{12,0},{1,13},{5,9},{9,5},{13,1},{2,14},{6,10},... | collective-permute-start | bytes 122888 | tf_op jit(solution)/shard_map/ppermute | solution.py:22
  21.0 0.9 %collective-permute-start.6 = (bf16[16,256]{1,0:T(8,128)(2,1)S(1)}, bf16[16,256]{1,0:T(8,128)(2,1)S(1)}, u32[]{:S(2)}, u32[]{:S(2)}) collective-permute-start(bf16[16,256]{1,0:T(8,128)(2,1)S(1)} %get-tuple-element.67), channel_id=1, source_target_pairs={{0,4},{4,0},{8,12},{12,8},{1,5},{5,1},{9,13},{13,9},{2,6},{6,2},{1... | collective-permute-start | bytes 24584 | tf_op jit(solution)/shard_map/ppermute | solution.py:22
  21.9 0.0 collective-permute-done.3.beside_ref
  21.9 2.8 %collective-permute-done.6.rest_3_ = bf16[16,256]{1,0:T(8,128)(2,1)S(1)} collective-permute-done((bf16[16,256]{1,0:T(8,128)(2,1)S(1)}, bf16[16,256]{1,0:T(8,128)(2,1)S(1)}, u32[]{:S(2)}, u32[]{:S(2)}) %collective-permute-start.6) | collective-permute-done | bytes 8224 | tf_op jit(solution)/shard_map/ppermute | solution.py:22
  24.7 0.0 collective-permute-done.4.rest_1_
  24.7 0.0 collective-permute-done.5.rest_2_
  24.7 0.1 shard_map.144
  24.8 0.1 collective-permute-start.8
  24.9 0.5 %collective-permute-start.7 = (bf16[8,2048]{1,0:T(8,128)(2,1)S(1)}, bf16[8,2048]{1,0:T(8,128)(2,1)S(1)}, u32[]{:S(2)}, u32[]{:S(2)}) collective-permute-start(bf16[8,2048]{1,0:T(8,128)(2,1)S(1)} %get-tuple-element.68.attn_ref), channel_id=1, source_target_pairs={{0,1},{1,0},{2,3},{3,2},{4,5},{5,4},{6,7},{7,6},{8,9},{9,8},{10,11... | collective-permute-start | bytes 98312 | tf_op jit(solution)/shard_map/ppermute | solution.py:22
  25.4 0.6 %shard_map.145.acc_ref = f32[8,1024]{1,0:T(8,128)S(1)} custom-call(bf16[8,2048]{1,0:T(8,128)(2,1)S(1)} %get-tuple-element.68.attn_ref, bf16[2048,1024]{1,0:T(8,128)(2,1)S(1)} %get-tuple-element.69.weight_ref), custom_call_target="tpu_custom_call" | custom-call | bytes 25200 | tf_op jit(solution)/shard_map/pallas_call | solution.py:497
  26.0 0.1 collective-permute-start.9
  26.1 0.1 collective-permute-done.7.attn_ref
  26.3 0.7 %shard_map.146 = (f32[2,2,1024]{2,1,0:T(2,128)S(1)}, f32[2,2,1024]{2,1,0:T(2,128)S(1)}) custom-call(f32[8,1024]{1,0:T(8,128)S(1)} %shard_map.145.acc_ref, bf16[8,2048]{1,0:T(8,128)(2,1)S(1)} %collective-permute-done.7.attn_ref, bf16[2048,1024]{1,0:T(8,128)(2,1)S(1)} %get-tuple-element.70.weight_ref), custom_call_target="tpu_custom_call" | custom-call | bytes 25200 | tf_op jit(solution)/shard_map/pallas_call | solution.py:501
  26.9 1.5 %collective-permute-start.10 = (f32[2,2,1024]{2,1,0:T(2,128)S(1)}, f32[2,2,1024]{2,1,0:T(2,128)S(1)}, u32[]{:S(2)}, u32[]{:S(2)}) collective-permute-start(f32[2,2,1024]{2,1,0:T(2,128)S(1)} %get-tuple-element.78), channel_id=1, source_target_pairs={{0,2},{2,0},{1,3},{3,1},{4,6},{6,4},{5,7},{7,5},{8,10},{10,8},{9,1... | collective-permute-start | bytes 49160 | tf_op jit(solution)/shard_map/ppermute | solution.py:22
  28.5 0.0 collective-permute-done.9.rest_0_
  28.5 0.0 collective-permute-done.8.got_ref
  28.5 0.9 %shard_map.147 = (bf16[1,4,1,128,256]{4,3,2,1,0:T(8,128)(2,1)}, f32[2,1,8192]{2,1,0:T(1,128)}) custom-call(bf16[2,1,128,256]{3,2,1,0:T(8,128)(2,1)S(1)} %get-tuple-element.72.kept_ref, bf16[2,1,128,256]{3,2,1,0:T(8,128)(2,1)S(1)} %collective-permute-done.8.got_ref, f32[2,4,1,1024]{3,2,1,0:T(1,128)S(1)} %get-tuple-element.76.mamba_ref, ...), custom_call_target="tpu_custom_call" | custom-call | bytes 36000 | tf_op jit(solution)/shard_map/pallas_call | solution.py:513
  29.4 1.3 %collective-permute-done.10.refs_1_ = f32[2,2,1024]{2,1,0:T(2,128)S(1)} collective-permute-done((f32[2,2,1024]{2,1,0:T(2,128)S(1)}, f32[2,2,1024]{2,1,0:T(2,128)S(1)}, u32[]{:S(2)}, u32[]{:S(2)}) %collective-permute-start.10) | collective-permute-done | bytes 16416 | tf_op jit(solution)/shard_map/ppermute | solution.py:22
  30.7 0.6 %shard_map.148 = bf16[2,2,1024]{2,1,0:T(2,128)(2,1)} custom-call(f32[2,2,1024]{2,1,0:T(2,128)S(1)} %get-tuple-element.71.refs_0_, f32[2,2,1024]{2,1,0:T(2,128)S(1)} %collective-permute-done.10.refs_1_), custom_call_target="tpu_custom_call" | custom-call | bytes 21600 | tf_op jit(solution)/shard_map/pallas_call | solution.py:524
Async XLA Ops:
  1.5 13.3 %collective-permute-start = (bf16[256,256]{1,0:T(8,128)(2,1)S(1)}, bf16[256,256]{1,0:T(8,128)(2,1)S(1)}, u32[]{:S(2)}, u32[]{:S(2)}) collective-permute-start(bf16[256,256]{1,0:T(8,128)(2,1)S(1)} %shard_map.141), channel_id=1, source_target_pairs={{0,12},{4,8},{8,4},{12,0},{1,13},{5,9},{9,5},{13,1},{2,14},{6,10},... | collective-permute-start | bytes 393224 | tf_op jit(solution)/shard_map/ppermute | solution.py:22
  7.6 10.2 %collective-permute-start.1 = (bf16[256,256]{1,0:T(8,128)(2,1)S(1)}, bf16[256,256]{1,0:T(8,128)(2,1)S(1)}, u32[]{:S(2)}, u32[]{:S(2)}) collective-permute-start(bf16[256,256]{1,0:T(8,128)(2,1)S(1)} %get-tuple-element.49), channel_id=1, source_target_pairs={{0,8},{4,12},{8,0},{12,4},{1,9},{5,13},{9,1},{13,5},{2,10},{6,14},... | collective-permute-start | bytes 393224 | tf_op jit(solution)/shard_map/ppermute | solution.py:22
  8.9 8.9 %collective-permute-start.2 = (bf16[256,256]{1,0:T(8,128)(2,1)S(1)}, bf16[256,256]{1,0:T(8,128)(2,1)S(1)}, u32[]{:S(2)}, u32[]{:S(2)}) collective-permute-start(bf16[256,256]{1,0:T(8,128)(2,1)S(1)} %get-tuple-element.50), channel_id=1, source_target_pairs={{0,4},{4,0},{8,12},{12,8},{1,5},{5,1},{9,13},{13,9},{2,6},{6,2},{1... | collective-permute-start | bytes 393224 | tf_op jit(solution)/shard_map/ppermute | solution.py:22
  13.3 8.6 %collective-permute-start.3 = (bf16[96,256]{1,0:T(8,128)(2,1)S(1)}, bf16[96,256]{1,0:T(8,128)(2,1)S(1)}, u32[]{:S(2)}, u32[]{:S(2)}) collective-permute-start(bf16[96,256]{1,0:T(8,128)(2,1)S(1)} %get-tuple-element.63), channel_id=1, source_target_pairs={{0,4},{4,0},{8,12},{12,8},{1,5},{5,1},{9,13},{13,9},{2,6},{6,2},{1... | collective-permute-start | bytes 147464 | tf_op jit(solution)/shard_map/ppermute | solution.py:22
  18.3 6.3 %collective-permute-start.4 = (bf16[80,256]{1,0:T(8,128)(2,1)S(1)}, bf16[80,256]{1,0:T(8,128)(2,1)S(1)}, u32[]{:S(2)}, u32[]{:S(2)}) collective-permute-start(bf16[80,256]{1,0:T(8,128)(2,1)S(1)} %get-tuple-element.65), channel_id=1, source_target_pairs={{0,8},{4,12},{8,0},{12,4},{1,9},{5,13},{9,1},{13,5},{2,10},{6,14},... | collective-permute-start | bytes 122888 | tf_op jit(solution)/shard_map/ppermute | solution.py:22
  18.4 6.2 %collective-permute-start.5 = (bf16[80,256]{1,0:T(8,128)(2,1)S(1)}, bf16[80,256]{1,0:T(8,128)(2,1)S(1)}, u32[]{:S(2)}, u32[]{:S(2)}) collective-permute-start(bf16[80,256]{1,0:T(8,128)(2,1)S(1)} %get-tuple-element.66), channel_id=1, source_target_pairs={{0,12},{4,8},{8,4},{12,0},{1,13},{5,9},{9,5},{13,1},{2,14},{6,10},... | collective-permute-start | bytes 122888 | tf_op jit(solution)/shard_map/ppermute | solution.py:22
  21.0 3.7 %collective-permute-start.6 = (bf16[16,256]{1,0:T(8,128)(2,1)S(1)}, bf16[16,256]{1,0:T(8,128)(2,1)S(1)}, u32[]{:S(2)}, u32[]{:S(2)}) collective-permute-start(bf16[16,256]{1,0:T(8,128)(2,1)S(1)} %get-tuple-element.67), channel_id=1, source_target_pairs={{0,4},{4,0},{8,12},{12,8},{1,5},{5,1},{9,13},{13,9},{2,6},{6,2},{1... | collective-permute-start | bytes 24584 | tf_op jit(solution)/shard_map/ppermute | solution.py:22
  24.8 3.7 %collective-permute-start.8 = (bf16[2,1,128,256]{3,2,1,0:T(8,128)(2,1)S(1)}, bf16[2,1,128,256]{3,2,1,0:T(8,128)(2,1)S(1)}, u32[]{:S(2)}, u32[]{:S(2)}) collective-permute-start(bf16[2,1,128,256]{3,2,1,0:T(8,128)(2,1)S(1)} %get-tuple-element.75), channel_id=1, source_target_pairs={{0,1},{1,0},{2,3},{3,2},{4,5},{5,4},{6,7},{7,6},{8,9},{9,8},{10,11... | collective-permute-start | bytes 393224 | tf_op jit(solution)/shard_map/ppermute | solution.py:22
  24.9 1.4 %collective-permute-start.7 = (bf16[8,2048]{1,0:T(8,128)(2,1)S(1)}, bf16[8,2048]{1,0:T(8,128)(2,1)S(1)}, u32[]{:S(2)}, u32[]{:S(2)}) collective-permute-start(bf16[8,2048]{1,0:T(8,128)(2,1)S(1)} %get-tuple-element.68.attn_ref), channel_id=1, source_target_pairs={{0,1},{1,0},{2,3},{3,2},{4,5},{5,4},{6,7},{7,6},{8,9},{9,8},{10,11... | collective-permute-start | bytes 98312 | tf_op jit(solution)/shard_map/ppermute | solution.py:22
  26.0 2.5 %collective-permute-start.9 = (f32[2,4,1,1024]{3,2,1,0:T(1,128)S(1)}, f32[2,4,1,1024]{3,2,1,0:T(1,128)S(1)}, u32[]{:S(2)}, u32[]{:S(2)}) collective-permute-start(f32[2,4,1,1024]{3,2,1,0:T(1,128)S(1)} %get-tuple-element.76.mamba_ref), channel_id=1, source_target_pairs={{0,1},{1,0},{2,3},{3,2},{4,5},{5,4},{6,7},{7,6},{8,9},{9,8},{10,11... | collective-permute-start | bytes 98312 | tf_op jit(solution)/shard_map/ppermute | solution.py:22
  26.9 3.8 %collective-permute-start.10 = (f32[2,2,1024]{2,1,0:T(2,128)S(1)}, f32[2,2,1024]{2,1,0:T(2,128)S(1)}, u32[]{:S(2)}, u32[]{:S(2)}) collective-permute-start(f32[2,2,1024]{2,1,0:T(2,128)S(1)} %get-tuple-element.78), channel_id=1, source_target_pairs={{0,2},{2,0},{1,3},{3,1},{4,6},{6,4},{5,7},{7,5},{8,10},{10,8},{9,1... | collective-permute-start | bytes 49160 | tf_op jit(solution)/shard_map/ppermute | solution.py:22
